TPU v7x, 32 devices: a whole 2x2x4 slice. The times are simulated.
32 devices in a mesh: lat: 8 (over y, x, core), chan: 4 (over z).
Axes of the slice: x: 2, y: 2, z: 4, core: 2. Of those that a mesh axis runs over, the one named last changes fastest.
Arguments:
- grid_field: float32 [16, 1440, 256], P('lat', 'chan'), may hold values from -6 to 6
- filters: float32 [16, 4, 3, 5], P('lat'), may hold values from -1.5 to 1.5
- disco_weight: float32 [4, 256], replicated, may hold values from -3 to 3
- band_start: int32 [16], P('lat'), may hold values from -2 to 0
- band_reach: int32 [16], P('lat'), may hold values from 1 to 3
- spec_weight: float32 [256, 256], replicated, may hold values from -0.375 to 0.375
- degree_gain: float32 [360, 256], replicated, may hold values from 0.5 to 2
- cotangent: float32 [16, 1440, 256], P('lat', 'chan'), may hold values from -6 to 6
Outputs:
- output: float32 [16, 1440, 256], P('lat', 'chan')
- grad_input: float32 [16, 1440, 256], P('lat', 'chan')
- grad_weight: float32 [256, 256], replicated
Inputs may be any that keep to these rules, and one draw needn't show every extreme that they name: The block of latitude i covers rows i + band_start[i] to i + band_start[i] + 2. Rows of a block at or past band_reach[i] are padding.
All inputs are finite; a program needn't handle non-finite values.
Results may differ from a plain program's by a relative error of at most 0.0003.
Values sent between devices are 32-bit elements; how exact they have to be, the bound alone decides.
No kernel may reach another device: no remote copies, remote signals or barrier semaphores. Data moves between devices by JAX's collectives and lax.ppermute only.
A program may use at most 64 MiB of HBM per device.

v0:
```python
import math

import jax
import jax.numpy as jnp
from jax import lax
from jax.sharding import PartitionSpec as P

L = 360
M = 256
WIN = 3
HMAX = 2
KLON = 5
POLAR = 720


highest = lax.Precision.HIGHEST
upper_bound = 2.0**32
lower_factor = 2.0 ** (-32)
log_step = 32.0 * math.log(2.0)


def extended(x, sides, width, wrap):
    for axis, dim in sides:
        count, length = (lax.axis_size(axis), x.shape[dim])
        up = [(i, (i + 1) % count) for i in range(count if wrap else count - 1)]
        down = [(j, i) for i, j in up]
        last = lax.slice_in_dim(x, length - width, length, axis=dim)
        initial = lax.slice_in_dim(x, 0, width, axis=dim)
        before = lax.ppermute(last, axis, up)
        after = lax.ppermute(initial, axis, down)
        x = jnp.concatenate([before, x, after], axis=dim)
    return x


def grid_tables(lat_total):
    first_row = (POLAR - lat_total) // 2
    colatitude = math.pi * (jnp.arange(lat_total, dtype=jnp.float32) + float(first_row)) / POLAR
    quad_weight = 2.0 * math.pi * math.pi / POLAR * jnp.sin(colatitude)
    return (colatitude, quad_weight)


def log_norms(order_count):
    order_index = jnp.arange(order_count, dtype=jnp.float32)
    log_terms = jnp.where(
        order_index > 0.0,
        jnp.log((2.0 * order_index + 1.0) / jnp.maximum(2.0 * order_index, 1.0)),
        0.0,
    )
    return -0.5 * math.log(4.0 * math.pi) + 0.5 * jnp.cumsum(log_terms)


def block_length(degree_count):
    best = 1
    for candidate in range(1, 41):
        if degree_count % candidate == 0:
            best = candidate
    return best


def legendre_orders(colatitude, orders, log_norm, degree_count):
    cosine = jnp.cos(colatitude)[None, :]
    log_sine = jnp.log(jnp.sin(colatitude))[None, :]
    order_f = orders.astype(jnp.float32)[:, None]
    norm_start = jnp.exp(log_norm)[:, None] + jnp.zeros_like(cosine)
    zeros_state = jnp.zeros((orders.shape[0], colatitude.shape[0]), jnp.float32)
    span = block_length(degree_count)

    def advance_block(carry, block_first):
        previous, second, log_scale = carry
        produced = []
        for offset in range(span):
            degree = block_first + offset
            degree_f = degree.astype(jnp.float32)
            step_factor = jnp.where(
                degree > orders[:, None],
                jnp.sqrt(
                    jnp.maximum(4.0 * degree_f * degree_f - 1.0, 0.0)
                    / jnp.maximum(degree_f * degree_f - order_f * order_f, 1.0)
                ),
                0.0,
            )
            lower_degree = degree_f - 1.0
            back_factor = jnp.sqrt(
                jnp.maximum(lower_degree * lower_degree - order_f * order_f, 0.0)
                / (4.0 * lower_degree * lower_degree - 1.0)
            )
            current = jnp.where(
                degree == orders[:, None],
                norm_start,
                step_factor * (cosine * previous - back_factor * second),
            )
            too_large = jnp.abs(current) > upper_bound
            current = jnp.where(too_large, current * lower_factor, current)
            previous = jnp.where(too_large, previous * lower_factor, previous)
            log_scale = jnp.where(too_large, log_scale + log_step, log_scale)
            produced.append(current * jnp.exp(log_scale))
            second = previous
            previous = current
        return ((previous, second, log_scale), jnp.stack(produced, axis=0))

    start_state = (zeros_state, zeros_state, order_f * log_sine)
    block_firsts = jnp.arange(0, degree_count, span, dtype=jnp.int32)
    _, tables = lax.scan(advance_block, start_state, block_firsts)
    return tables.reshape(degree_count, orders.shape[0], colatitude.shape[0])


def filter_coeff(filters, disco_weight, band_reach):
    summed = jnp.einsum("ikrt,kc->irtc", filters, disco_weight, precision=highest)
    live_rows = jnp.arange(filters.shape[2], dtype=jnp.int32)[None, :] < band_reach[:, None]
    return jnp.where(live_rows[:, :, None, None], summed, 0.0)


def wave_table(lon_index, order_index, lon_total):
    angle = (lon_index[:, None] * order_index[None, :] % lon_total).astype(jnp.float32) * (
        2.0 * math.pi / lon_total
    )
    return jnp.stack([jnp.cos(angle), -jnp.sin(angle)], axis=2)


def extend_rows(block):
    return extended(block, (("lat", 0),), HMAX, False)


def extend_cols(block):
    return extended(block, (("chan", 1),), KLON // 2, True)


def to_modes(grid_side):
    return lax.all_to_all(grid_side, "lat", split_axis=0, concat_axis=1, tiled=True)


def to_grid(mode_side):
    return lax.all_to_all(mode_side, "lat", split_axis=1, concat_axis=0, tiled=True)


def body(
    grid_field, filters, disco_weight, band_start, band_reach, spec_weight, degree_gain, cotangent
):
    band_rows, lon_local, chan_count = grid_field.shape
    lat_devices = lax.axis_size("lat")
    chan_devices = lax.axis_size("chan")
    lat_total = band_rows * lat_devices
    lon_total = lon_local * chan_devices
    chan_orders = M // chan_devices
    own_count = chan_orders // lat_devices
    order_base = lax.axis_index("chan") * chan_orders
    order_start = order_base + lax.axis_index("lat") * own_count
    lon_base = lax.axis_index("chan") * lon_local
    lon_mine = lon_base + jnp.arange(lon_local, dtype=jnp.int32)
    chan_order_index = order_base + jnp.arange(chan_orders, dtype=jnp.int32)
    half_taps = KLON // 2
    colatitude, quad_weight = grid_tables(lat_total)
    orders = order_start + jnp.arange(own_count, dtype=jnp.int32)
    log_norm = lax.dynamic_slice_in_dim(log_norms(M), order_start, own_count)
    legendre_rows = legendre_orders(colatitude, orders, log_norm, L)
    order_weight = jnp.where(chan_order_index == 0, 1.0, 2.0).astype(jnp.float32)[
        :, None, None, None
    ]
    quad_column = quad_weight[None, :, None, None]
    gain_column = degree_gain[:, None, None, :]

    def analyze(field):
        empty = jnp.zeros((chan_orders, band_rows, 2, chan_count), jnp.float32)
        piece = lax.all_gather(field, "chan", axis=1, tiled=True)
        lons = jnp.arange(piece.shape[1], dtype=jnp.int32)
        table = wave_table(lons, chan_order_index, lon_total)
        return empty + jnp.einsum("inc,nmp->mipc", piece, table, precision=highest)

    def compose(spec):
        empty = jnp.zeros((band_rows, lon_local, chan_count), jnp.float32)
        piece = lax.all_gather(spec, "chan", axis=0, tiled=True)
        order_part = jnp.arange(piece.shape[0], dtype=jnp.int32)
        table = wave_table(lon_mine, order_part, lon_total)
        return empty + jnp.einsum("mipc,nmp->inc", piece, table, precision=highest)

    coefficient = filter_coeff(filters, disco_weight, band_reach)
    padded = extend_cols(extend_rows(grid_field))
    row_index = (
        jnp.arange(band_rows, dtype=jnp.int32)[:, None]
        + HMAX
        + band_start[:, None]
        + jnp.arange(WIN, dtype=jnp.int32)[None, :]
    )
    flat_index = row_index.reshape(-1)
    windows = jnp.take(padded, flat_index, axis=0).reshape(
        band_rows, WIN, lon_local + 2 * half_taps, chan_count
    )
    local_out = jnp.zeros_like(grid_field)
    for tap_index in range(KLON):
        local_out = local_out + jnp.sum(
            coefficient[:, :, tap_index, None, :]
            * windows[:, :, tap_index : tap_index + lon_local, :],
            axis=1,
        )
    spectrum = analyze(grid_field) / lon_total
    modes = to_modes(spectrum) * quad_column
    degree = jnp.einsum("lmj,mjpc->lmpc", legendre_rows, modes, precision=highest)
    mixed_modes = jnp.einsum("lmpc,cd->lmpd", degree, spec_weight, precision=highest) * gain_column
    synthesis = to_grid(jnp.einsum("lmj,lmpd->mjpd", legendre_rows, mixed_modes, precision=highest))
    spectral = compose(synthesis * order_weight)
    hidden = local_out + spectral
    output = grid_field + jax.nn.silu(hidden)
    gate_value = jax.nn.sigmoid(hidden)
    error = cotangent * (gate_value * (1.0 + hidden * (1.0 - gate_value)))
    error_modes = to_modes(analyze(error) * order_weight)
    gained = (
        jnp.einsum("lmj,mjpd->lmpd", legendre_rows, error_modes, precision=highest) * gain_column
    )
    weight_part = jnp.einsum("lmpc,lmpd->cd", degree, gained, precision=highest)
    grad_weight = lax.psum(weight_part, ("lat", "chan"))
    degree_grad = jnp.einsum("lmpd,cd->lmpc", gained, spec_weight, precision=highest)
    spectrum_grad = to_grid(
        quad_column * jnp.einsum("lmj,lmpc->mjpc", legendre_rows, degree_grad, precision=highest)
    )
    spectral_grad = compose(spectrum_grad) / lon_total
    contrib = jnp.zeros((band_rows, WIN, lon_local + 2 * half_taps, chan_count), jnp.float32)
    for tap_index in range(KLON):
        contrib = contrib.at[:, :, tap_index : tap_index + lon_local, :].add(
            error[:, None, :, :] * coefficient[:, :, tap_index, None, :]
        )
    selector = (
        flat_index[:, None] == jnp.arange(band_rows + 2 * HMAX, dtype=jnp.int32)[None, :]
    ).astype(jnp.float32)
    spread = jnp.einsum(
        "qr,qlc->rlc",
        selector,
        contrib.reshape(band_rows * WIN, lon_local + 2 * half_taps, chan_count),
        precision=highest,
    )
    col_edges = jnp.concatenate([spread[:, :half_taps], spread[:, lon_local + half_taps :]], axis=1)
    col_arrived = extend_cols(col_edges)
    inner = spread[:, half_taps : lon_local + half_taps]
    inner = inner.at[:, :half_taps].add(col_arrived[:, :half_taps])
    inner = inner.at[:, lon_local - half_taps :].add(col_arrived[:, 3 * half_taps :])
    row_edges = jnp.concatenate([inner[:HMAX], inner[band_rows + HMAX :]], axis=0)
    row_arrived = extend_rows(row_edges)
    core = inner[HMAX : band_rows + HMAX]
    core = core.at[:HMAX].add(row_arrived[:HMAX])
    core = core.at[band_rows - HMAX :].add(row_arrived[3 * HMAX :])
    grad_input = cotangent + core + spectral_grad
    return (output, grad_input, grad_weight)


def solution(mesh):
    in_specs = (
        P("lat", "chan", None),
        P("lat", None, None, None),
        P(),
        P("lat"),
        P("lat"),
        P(),
        P(),
        P("lat", "chan", None),
    )
    out_specs = (P("lat", "chan", None), P("lat", "chan", None), P())
    return jax.shard_map(body, mesh=mesh, in_specs=in_specs, out_specs=out_specs, check_vma=False)
```

profile of v0, /device:TPU:0, one launch (start us, length us, event | category | flops | bytes accessed | tf_op | source)
XLA Modules:
  0.0 733.9 jit_solution(14275465959651504235)
XLA Ops:
  9.2 4.0 collective-permute-start
  14.1 354.3 %while.34 = (s32[]{:T(128)}, f32[8,16]{1,0:T(8,128)S(1)}, f32[8,16]{1,0:T(8,128)S(1)}, f32[8,16]{1,0:T(8,128)S(1)}, f32[9,40,8,16]{1,0,3,2:T(8,128)}, /*index=5*...) while((s32[]{:T(128)}, f32[8,16]{1,0:T(8,128)S(1)}, ...), condition=%wide.region_8.9_spmd.clone.clone.clone.clone, body=%wide.region_7.8_spmd.clone.clone.clone.clone.sunk | while | flops 101954 | bytes 221555 | solution.py:103
  373.5 3.9 fusion.240
  378.3 5.3 all-to-all-start
  384.0 6.4 all-to-all-done
  390.6 4.8 fusion.263
  395.5 4.8 fusion.209
  404.7 4.0 all-to-all-start.1
  410.0 5.7 all-to-all-done.1
  433.1 11.8 %all-gather.7.cloned.1.call-done = f32[256,2,2,256]{3,0,2,1:T(8,128)} async-done(((f32[64,2,2,256]{3,0,2,1:T(8,128)}), f32[256,2,2,256]{3,0,2,1:T(8,128)}) %all-gather.7.cloned.1.call-update) | async-done | bytes 1048592 | tf_op jit(solution)/shard_map/all_gather | solution.py:171
  444.9 4.9 multiply_multiply_fusion
  454.1 11.4 %scatter-add.25 = f32[2,3,364,256]{3,2,1,0:T(8,128)S(1)} dynamic-update-slice(f32[2,3,364,256]{3,2,1,0:T(8,128)S(1)} %scatter-add.24, f32[2,3,360,256]{3,2,1,0:T(8,128)} %multiply_add_fusion, s32[]{:T(128)} %constant.739.clone.1, s32[]{:T(128)} %constant.739.clone.1, s32[]{:T(128)} %constant.762.clone.1, s32[]{:T(128)} %constant.739.clone.1) | dynamic-update-slice | bytes 4423684 | tf_op jit(solution)/shard_map/scatter-add | solution.py:218
  467.2 11.4 %scatter-add.26 = f32[2,3,364,256]{3,2,1,0:T(8,128)S(1)} dynamic-update-slice(f32[2,3,364,256]{3,2,1,0:T(8,128)S(1)} %scatter-add.25, f32[2,3,360,256]{3,2,1,0:T(8,128)} %slice_add_fusion.2, s32[]{:T(128)} %constant.739.clone.1, s32[]{:T(128)} %constant.739.clone.1, s32[]{:T(128)} %constant.738.clone.1, s32[]{:T(128)} %constant.739.clone.1) | dynamic-update-slice | bytes 4423684 | tf_op jit(solution)/shard_map/scatter-add | solution.py:218
  478.6 31.1 %all-gather.9.cloned.1.call-done = f32[2,1440,256]{2,1,0:T(8,128)} async-done(((f32[2,360,256]{2,1,0:T(8,128)}), f32[2,1440,256]{2,1,0:T(8,128)}) %all-gather.9.cloned.1.call-update) | async-done | bytes 2949136 | tf_op jit(solution)/shard_map/all_gather | solution.py:164
  509.7 3.9 fusion.237
  514.5 4.0 all-to-all-start.2
  520.2 11.5 %scatter-add.29 = f32[2,3,364,256]{3,2,1,0:T(8,128)S(1)} dynamic-update-slice(f32[2,3,364,256]{3,2,1,0:T(8,128)S(1)} %scatter-add.26, f32[2,3,360,256]{3,2,1,0:T(8,128)} %slice_add_fusion.1, s32[]{:T(128)} %constant.739.clone.1, s32[]{:T(128)} %constant.739.clone.1, s32[]{:T(128)} %constant.763.clone.1, s32[]{:T(128)} %constant.739.clone.1) | dynamic-update-slice | bytes 4423684 | tf_op jit(solution)/shard_map/scatter-add | solution.py:218
  535.4 5.8 fusion.266
  541.1 4.8 fusion.213
  550.0 4.1 all-to-all-start.3
  555.8 11.4 %scatter-add.30 = f32[2,3,364,256]{3,2,1,0:T(8,128)S(1)} dynamic-update-slice(f32[2,3,364,256]{3,2,1,0:T(8,128)S(1)} %scatter-add.29, f32[2,3,360,256]{3,2,1,0:T(8,128)} %slice_add_fusion, s32[]{:T(128)} %constant.739.clone.1, s32[]{:T(128)} %constant.739.clone.1, s32[]{:T(128)} %constant.764.clone.1, s32[]{:T(128)} %constant.739.clone.1) | dynamic-update-slice | bytes 4423684 | tf_op jit(solution)/shard_map/scatter-add | solution.py:218
  571.8 3.8 collective-permute-start.5
  582.0 10.6 %fusion.243 = f32[256,256]{1,0:T(8,128)} fusion(f32[8,2,256,360]{2,3,1,0:T(8,128)S(1)} %bitcast.512, f32[360,256]{1,0:T(8,128)S(1)} %copy-done.14, f32[8,2,256,360]{2,3,1,0:T(8,128)S(1)} %bitcast.510), kind=kOutput, calls=%fused_computation.529 | convolution fusion | flops 4531322880 | bytes 12427264 | tf_op jit(solution)/shard_map/lmpc,lmpd->cd/dot_general | solution.py:209
  600.4 124.9 %all-reduce.3.cloned.1.call-done = f32[256,256]{1,0:T(8,128)} async-done(((f32[256,256]{1,0:T(8,128)}), f32[256,256]{1,0:T(8,128)}) %all-reduce.3.cloned.1.call-update) | async-done | bytes 262160 | tf_op jit(solution)/shard_map/psum | solution.py:210
  (1291 shorter events, 183.7 us)
Async XLA Ops:
  7.2 388.3 %copy-start = (f32[256,256]{1,0:T(8,128)S(1)}, f32[256,256]{1,0:T(8,128)}, u32[]{:S(2)}) copy-start(f32[256,256]{1,0:T(8,128)} %param.37) | copy-start | bytes 786436
  7.2 366.3 %all-gather.5.cloned.1.call-start = ((), (), s32[]{:S(2)}) async-start(), calls=%async_computation.4 | async-start | bytes 3686400 | tf_op jit(solution)/shard_map/all_gather | solution.py:164
  7.9 409.6 %collective-permute-start.1 = (f32[2,360,256]{2,1,0:T(8,128)}, f32[2,360,256]{2,1,0:T(8,128)}, u32[]{:S(2)}, u32[]{:S(2)}) collective-permute-start(f32[2,360,256]{2,1,0:T(8,128)} %param.32), channel_id=1, source_target_pairs={{4,0},{8,4},{12,8},{16,12},{20,16},{24,20},{28,24},{5,1},{9,5},{13... | collective-permute-start | bytes 2211848 | tf_op jit(solution)/shard_map/ppermute | solution.py:30
  9.2 399.6 %collective-permute-start = (f32[2,360,256]{2,1,0:T(8,128)}, f32[2,360,256]{2,1,0:T(8,128)}, u32[]{:S(2)}, u32[]{:S(2)}) collective-permute-start(f32[2,360,256]{2,1,0:T(8,128)} %param.32), channel_id=1, source_target_pairs={{0,4},{4,8},{8,12},{12,16},{16,20},{20,24},{24,28},{1,5},{5,9},{9,... | collective-permute-start | bytes 2211848 | tf_op jit(solution)/shard_map/ppermute | solution.py:29
  14.1 354.3 %copy-start.19 = (s32[2]{0:T(128)S(1)}, s32[2]{0:T(128)}, u32[]{:S(2)}) copy-start(s32[2]{0:T(128)} %param.35) | copy-start | bytes 28
  14.1 354.6 %copy-start.20 = (s32[2]{0:T(128)S(1)}, s32[2]{0:T(128)}, u32[]{:S(2)}) copy-start(s32[2]{0:T(128)} %param.36) | copy-start | bytes 28
  14.1 354.7 %copy-start.17 = (f32[2,4,3,5]{3,1,2,0:T(4,128)S(1)}, f32[2,4,3,5]{3,1,2,0:T(4,128)}, u32[]{:S(2)}) copy-start(f32[2,4,3,5]{3,1,2,0:T(4,128)} %param.33) | copy-start | bytes 1444
  14.1 354.7 %copy-start.18 = (f32[4,256]{1,0:T(4,128)S(1)}, f32[4,256]{1,0:T(4,128)}, u32[]{:S(2)}) copy-start(f32[4,256]{1,0:T(4,128)} %param.34) | copy-start | bytes 12292
  378.3 12.1 %all-to-all-start = ((f32[64,2,2,256]{3,1,2,0:T(2,128)}), f32[64,2,2,256]{3,1,2,0:T(2,128)S(1)}, u32[]{:S(2)}, u32[]{:S(2)}) async-start(f32[64,2,2,256]{3,1,2,0:T(2,128)} %copy.221), calls=%async_computation | async-start | bytes 524288 | tf_op jit(solution)/shard_map/all_to_all | solution.py:129
  404.7 11.0 %all-to-all-start.1 = ((f32[8,16,2,256]{3,2,0,1:T(2,128)}), f32[8,16,2,256]{3,2,0,1:T(2,128)}, u32[]{:S(2)}, u32[]{:S(2)}) async-start(f32[8,16,2,256]{3,2,0,1:T(2,128)} %copy.223), calls=%async_computation.1 | async-start | bytes 524288 | tf_op jit(solution)/shard_map/all_to_all | solution.py:133
  408.7 36.2 %all-gather.7.cloned.1.call-start = ((), (), s32[]{:S(2)}) async-start(), calls=%async_computation.5 | async-start | bytes 1310720 | tf_op jit(solution)/shard_map/all_gather | solution.py:171
  417.4 92.3 %all-gather.9.cloned.1.call-start = ((), (), s32[]{:S(2)}) async-start(), calls=%async_computation.6 | async-start | bytes 3686400 | tf_op jit(solution)/shard_map/all_gather | solution.py:164
  418.7 5.5 collective-permute-start.2
  420.4 3.9 collective-permute-start.3
  514.5 17.3 %all-to-all-start.2 = ((f32[64,2,2,256]{3,1,2,0:T(2,128)}), f32[64,2,2,256]{3,1,2,0:T(2,128)}, u32[]{:S(2)}, u32[]{:S(2)}) async-start(f32[64,2,2,256]{3,1,2,0:T(2,128)} %copy.230), calls=%async_computation.2 | async-start | bytes 524288 | tf_op jit(solution)/shard_map/all_to_all | solution.py:129
  550.0 17.2 %all-to-all-start.3 = ((f32[8,16,2,256]{3,2,0,1:T(2,128)}), f32[8,16,2,256]{3,2,0,1:T(2,128)S(1)}, u32[]{:S(2)}, u32[]{:S(2)}) async-start(f32[8,16,2,256]{3,2,0,1:T(2,128)} %copy.232), calls=%async_computation.3 | async-start | bytes 524288 | tf_op jit(solution)/shard_map/all_to_all | solution.py:133
  554.1 41.1 %all-gather.11.cloned.1.call-start = ((), (), s32[]{:S(2)}) async-start(), calls=%async_computation.7 | async-start | bytes 1310720 | tf_op jit(solution)/shard_map/all_gather | solution.py:171
  567.9 157.4 %all-reduce.3.cloned.1.call-start = ((), (), s32[]{:S(2)}) async-start(), calls=%async_computation.8 | async-start | bytes 524288 | tf_op jit(solution)/shard_map/psum | solution.py:210
  570.8 5.5 collective-permute-start.4
  571.8 5.3 collective-permute-start.5
  578.3 19.6 %collective-permute-start.6 = (f32[2,360,256]{2,1,0:T(8,128)}, f32[2,360,256]{2,1,0:T(8,128)}, u32[]{:S(2)}, u32[]{:S(2)}) collective-permute-start(f32[2,360,256]{2,1,0:T(8,128)} %get-tuple-element.1004), channel_id=1, source_target_pairs={{0,4},{4,8},{8,12},{12,16},{16,20},{20,24},{24,28},{1,5},{5,9},{9,... | collective-permute-start | bytes 2211848 | tf_op jit(solution)/shard_map/ppermute | solution.py:29
  580.5 14.7 %copy-start.9 = (f32[360,256,1]{1,0,2:T(8,128)S(1)}, f32[360,256,1]{1,0,2:T(8,128)}, u32[]{:S(2)}) copy-start(f32[360,256,1]{1,0,2:T(8,128)} %get-tuple-element.1015) | copy-start | bytes 1105924
  580.5 14.7 %copy-start.11 = (f32[360,256,1]{1,0,2:T(8,128)S(1)}, f32[360,256,1]{1,0,2:T(8,128)}, u32[]{:S(2)}) copy-start(f32[360,256,1]{1,0,2:T(8,128)} %get-tuple-element.1016) | copy-start | bytes 1105924
  580.5 17.4 %collective-permute-start.7 = (f32[2,360,256]{2,1,0:T(8,128)}, f32[2,360,256]{2,1,0:T(8,128)}, u32[]{:S(2)}, u32[]{:S(2)}) collective-permute-start(f32[2,360,256]{2,1,0:T(8,128)} %get-tuple-element.1005), channel_id=1, source_target_pairs={{4,0},{8,4},{12,8},{16,12},{20,16},{24,20},{28,24},{5,1},{9,5},{13... | collective-permute-start | bytes 2211848 | tf_op jit(solution)/shard_map/ppermute | solution.py:30
  (18 other events, 149.8 us)
Sparse Core Ops, SparseCore 0:
  9.6 62.9 all-gather.4
  417.5 27.3 all-gather.6
  449.9 59.7 all-gather.8
  568.0 27.1 all-gather.10
  600.6 124.7 all-reduce.2
where the time goes:
time: 746 us; the launch traced here: 734 us
  loops' own time  241 us (32%)
  waiting for transfers between devices  186 us (25%)
  local copies, waits for them, and re-layouts  149 us (20%)
  matrix products  55.7 us (7%)
  other arithmetic  52.7 us (7%)
  starting transfers between devices  34.4 us (5%)
  between operations  14.9 us (2%)
    another operation x1, loops' own time, legendre_orders(): _, tables = lax.scan(advance_block, start_state, block_firsts)  241 us
    psum x1, waiting for transfers between devices, body(): grad_weight = lax.psum(weight_part, ('lat', 'chan'))  125 us
    another operation x369, local copies, waits for them, and re-layouts, advance_block(): return ((previous, second, log_scale), jnp.stack(produced, axis=0))  53.3 us
    scatter-add x5, local copies, waits for them, and re-layouts, body(): contrib.at[:, :, tap_index:tap_index + lon_local, :]  45.9 us
    all_gather x2, waiting for transfers between devices, analyze(): piece = lax.all_gather(field, 'chan', axis=1, tiled=True)  31.1 us
    dynamic_update_slice x9, local copies, waits for them, and re-layouts, legendre_orders(): _, tables = lax.scan(advance_block, start_state, block_firsts)  26.3 us
  transfers between devices with their start and end apart: 17, of which 9 were waited for; matrix products, arithmetic and copies ran while one was open for 31% of the time, Pallas kernels for 0%

commit v1 on v0

v1 whole, which is shorter than its diff:
```python
import functools
import math

import jax
import jax.numpy as jnp
import ml_dtypes
import numpy as np
from jax import lax
from jax.experimental import pallas as pl
from jax.experimental.pallas import tpu as pltpu
from jax.sharding import PartitionSpec as P

L = 360
M = 256
WIN = 3
HMAX = 2
KLON = 5
POLAR = 720
SPAN = 2 * HMAX + 1
LANES = 128
HALF = 64
MIB = 2**20


highest = lax.Precision.HIGHEST
upper_bound = 2.0**32
lower_factor = 2.0 ** (-32)
log_step = 32.0 * math.log(2.0)

f32 = jnp.float32
bf16 = jnp.bfloat16
VMEM = pltpu.VMEM


@functools.lru_cache(maxsize=None)
def wave_tables(lon_total, own_count):
    orders = np.arange(M).reshape(-1, own_count)
    angle = (orders[:, :, None] * np.arange(lon_total)) % lon_total * (2.0 * np.pi / lon_total)
    table = np.stack([np.cos(angle), -np.sin(angle)], axis=1).reshape(2 * M, lon_total)
    high = table.astype(ml_dtypes.bfloat16)
    low = (table - high.astype(np.float64)).astype(ml_dtypes.bfloat16)
    return high, low


def grid_tables(lat_total):
    first_row = (POLAR - lat_total) // 2
    colatitude = math.pi * (jnp.arange(lat_total, dtype=f32) + float(first_row)) / POLAR
    quad_weight = 2.0 * math.pi * math.pi / POLAR * jnp.sin(colatitude)
    return (colatitude, quad_weight)


def log_norms(order_count):
    order_index = jnp.arange(order_count, dtype=f32)
    log_terms = jnp.where(
        order_index > 0.0,
        jnp.log((2.0 * order_index + 1.0) / jnp.maximum(2.0 * order_index, 1.0)),
        0.0,
    )
    return -0.5 * math.log(4.0 * math.pi) + 0.5 * jnp.cumsum(log_terms)


def split(x):
    high = x.astype(bf16)
    return high, (x - high.astype(f32)).astype(bf16)


def dot_split(a, b, dims):
    (ah, al), (bh, bl) = split(a), split(b)
    dot = lambda u, v: lax.dot_general(u, v, (dims, ((), ())), preferred_element_type=f32)
    return dot(ah, bh) + (dot(ah, bl) + dot(al, bh))


def lower_lanes(shape):
    return lax.broadcasted_iota(jnp.int32, shape, len(shape) - 1) < HALF


def swap(x):
    return pltpu.roll(x, HALF, x.ndim - 1)


def pair(first, second, odd):
    low = lower_lanes(first.shape)
    return jnp.where(low, swap(first), second) if odd else jnp.where(low, first, swap(second))


def call(kernel, out_shape, in_specs, scratch=(), flops=0, limit=48):
    return pl.pallas_call(
        kernel,
        out_shape=out_shape,
        in_specs=in_specs,
        out_specs=jax.tree.map(lambda _: pl.BlockSpec(memory_space=VMEM), out_shape),
        scratch_shapes=list(scratch),
        compiler_params=pltpu.CompilerParams(vmem_limit_bytes=limit * MIB),
    )


def vmem(count):
    return [pl.BlockSpec(memory_space=VMEM)] * count


smem = pl.BlockSpec(memory_space=pltpu.SMEM)


def struct(*shape, dtype=f32):
    return jax.ShapeDtypeStruct(shape, dtype)


def pack_kernel(x_ref, o_ref):
    for part in range(o_ref.shape[0]):
        lanes = pl.ds(part // 2 * LANES, LANES)
        o_ref[part] = pair(x_ref[0, :, lanes], x_ref[1, :, lanes], part % 2)


def unpack_kernel(p_ref, o_ref):
    for group in range(p_ref.shape[0] // 2):
        lanes = pl.ds(group * LANES, LANES)
        first, second = p_ref[2 * group], p_ref[2 * group + 1]
        for row in range(2):
            o_ref[row, :, lanes] = pair(first, second, row)


def pack(x, parts):
    return call(pack_kernel, struct(parts, x.shape[1], LANES), vmem(1))(x)


def unpack(p):
    return call(unpack_kernel, struct(2, p.shape[1], p.shape[0] * HALF), vmem(1))(p)


def wide(x):
    high, low = split(x)
    return jnp.concatenate([high, low], axis=1)


def three(table_high, table_low, both):
    y = jnp.dot(table_high, both, preferred_element_type=f32)
    return y[:, :LANES] + (
        y[:, LANES:] + jnp.dot(table_low, both[:, :LANES], preferred_element_type=f32)
    )


def analyze_kernel(scale, x_ref, high_ref, low_ref, o_ref):
    both = wide(x_ref[...])
    tile = 256
    for part in range(high_ref.shape[0] // tile):
        rows = pl.ds(part * tile, tile)
        o_ref[rows, :] = three(high_ref[rows, :], low_ref[rows, :], both) * scale


def grid_kernel(s_ref, x_ref, local_ref, cot_ref, high_ref, low_ref, thigh_ref, tlow_ref,
                out_ref, err_ref, mode_ref, both_ref):
    modes = wide(s_ref[...])
    lons = x_ref.shape[0]
    tile = lons // 5
    for part in range(5):
        rows = pl.ds(part * tile, tile)
        hidden = local_ref[rows, :] + three(thigh_ref[rows, :], tlow_ref[rows, :], modes)
        gate = 1.0 / (1.0 + jnp.exp(-hidden))
        out_ref[rows, :] = x_ref[rows, :] + hidden * gate
        error = cot_ref[rows, :] * (gate * (1.0 + hidden * (1.0 - gate)))
        err_ref[rows, :] = error
        both_ref[rows, :] = wide(error)
    both = both_ref[...]
    tile = 256
    for part in range(high_ref.shape[0] // tile):
        rows = pl.ds(part * tile, tile)
        mode_ref[rows, :] = three(high_ref[rows, :], low_ref[rows, :], both)


def final_kernel(scale, s_ref, base_ref, thigh_ref, tlow_ref, o_ref):
    modes = wide(s_ref[...])
    tile = base_ref.shape[0] // 5
    for part in range(5):
        rows = pl.ds(part * tile, tile)
        o_ref[rows, :] = base_ref[rows, :] + scale * three(
            thigh_ref[rows, :], tlow_ref[rows, :], modes
        )


def filter_kernel(add, prev_ref, own_ref, next_ref, coef_ref, *refs):
    base_ref = refs[0] if add else None
    o_ref, sums_ref = refs[-2], refs[-1]
    lons = own_ref.shape[0]
    tile = lons // 18
    low = lower_lanes((tile, LANES))

    @pl.loop(0, 18)
    def _(part):
        rows = pl.ds(pl.multiple_of(part * tile, 8), tile)
        prev, own, after = prev_ref[rows, :], own_ref[rows, :], next_ref[rows, :]
        swapped = swap(own)
        sources = (
            prev,
            jnp.where(low, swap(prev), swapped),
            own,
            jnp.where(low, swapped, swap(after)),
            after,
        )
        out_rows = pl.ds(pl.multiple_of(part * tile + 8, 8), tile)
        for tap in range(KLON):
            total = sources[0] * coef_ref[pl.ds(tap, 1), :]
            for offset in range(1, SPAN):
                total = total + sources[offset] * coef_ref[pl.ds(offset * KLON + tap, 1), :]
            sums_ref[tap, out_rows, :] = total

    for tap in range(KLON):
        sums_ref[tap, pl.ds(0, 8), :] = sums_ref[tap, pl.ds(lons, 8), :]
        sums_ref[tap, pl.ds(lons + 8, 8), :] = sums_ref[tap, pl.ds(8, 8), :]
    for part in range(18):
        rows = pl.ds(part * tile, tile)
        total = base_ref[rows, :] if add else None
        for tap in range(KLON):
            value = sums_ref[tap, pl.ds(part * tile + 8 + tap - KLON // 2, tile), :]
            total = value if total is None else total + value
        o_ref[rows, :] = total


def local_filter(prev, own, after, coef, base=None):
    lons = own.shape[0]
    args = (prev, own, after, coef) + (() if base is None else (base,))
    return call(
        functools.partial(filter_kernel, base is not None),
        struct(lons, LANES),
        vmem(len(args)),
        [VMEM((KLON, lons + 16, LANES), f32)],
    )(*args)


def coupling_kernel(lat_total, first_ref, gain_ref, o_ref, step_ref, back_ref, leg_ref, scale_ref,
                    padded_ref, column_ref):
    degree_count, chans = gain_ref.shape
    depth = padded_ref.shape[0]
    own = LANES // lat_total
    first_row = float((POLAR - lat_total) // 2)
    lane = lax.broadcasted_iota(jnp.int32, (1, LANES), 1)
    order = lane % own + first_ref[0]
    colatitude = math.pi * ((lane // own).astype(f32) + first_row) / POLAR
    cosine, log_sine = jnp.cos(colatitude), jnp.log(jnp.sin(colatitude))
    k = lax.broadcasted_iota(jnp.int32, (M, LANES), 0)
    k_f = k.astype(f32)
    log_terms = jnp.log((2.0 * k_f + 1.0) / jnp.maximum(2.0 * k_f, 1.0))
    log_norm = -0.5 * math.log(4.0 * math.pi) + 0.5 * jnp.sum(
        jnp.where((k > 0) & (k <= order), log_terms, 0.0), axis=0, keepdims=True
    )
    norm_start = jnp.exp(log_norm)
    degree = lax.broadcasted_iota(jnp.int32, (degree_count, LANES), 0)
    degree_f, order_f = degree.astype(f32), order.astype(f32)
    step_ref[...] = jnp.where(
        degree > order,
        jnp.sqrt(
            jnp.maximum(4.0 * degree_f * degree_f - 1.0, 0.0)
            / jnp.maximum(degree_f * degree_f - order_f * order_f, 1.0)
        ),
        0.0,
    )
    lower = degree_f - 1.0
    back_ref[...] = jnp.sqrt(
        jnp.maximum(lower * lower - order_f * order_f, 0.0) / (4.0 * lower * lower - 1.0)
    )
    zeros = jnp.zeros((1, LANES), f32)

    def block(index, carry):
        previous, second, log_scale = carry
        first = pl.multiple_of(index * 8, 8)
        rows = pl.ds(first, 8)
        steps, backs = step_ref[rows, :], back_ref[rows, :]
        produced, scales = [], []
        for offset in range(8):
            current = jnp.where(
                first + offset == order,
                norm_start,
                steps[offset : offset + 1] * (cosine * previous - backs[offset : offset + 1] * second),
            )
            too_large = jnp.abs(current) > upper_bound
            current = jnp.where(too_large, current * lower_factor, current)
            previous = jnp.where(too_large, previous * lower_factor, previous)
            log_scale = jnp.where(too_large, log_scale + log_step, log_scale)
            produced.append(current)
            scales.append(log_scale)
            second, previous = previous, current
        leg_ref[rows, :] = jnp.concatenate(produced, axis=0)
        scale_ref[rows, :] = jnp.concatenate(scales, axis=0)
        return previous, second, log_scale

    lax.fori_loop(0, degree_count // 8, block, (zeros, zeros, order_f * log_sine))
    leg_ref[pl.ds(0, degree_count), :] = leg_ref[pl.ds(0, degree_count), :] * jnp.exp(scale_ref[...])
    rest = depth - degree_count
    leg_ref[pl.ds(degree_count, rest), :] = jnp.zeros((rest, LANES), f32)
    padded_ref[pl.ds(0, degree_count), :] = gain_ref[...]
    padded_ref[pl.ds(degree_count, rest), :] = jnp.zeros((rest, chans), f32)
    column_ref[...] = leg_ref[...].T

    high, low = split(padded_ref[...])
    row = lax.broadcasted_iota(jnp.int32, (LANES, LANES), 0)
    quad = 2.0 * math.pi * math.pi / POLAR * jnp.sin(
        math.pi * ((row // own).astype(f32) + first_row) / POLAR
    )
    weight = quad * jnp.where(row % own + first_ref[0] == 0, 1.0, 2.0)
    weight = jnp.concatenate([weight] * (chans // LANES), axis=1)

    @pl.loop(0, lat_total)
    def _(j):
        mine = column_ref[pl.ds(pl.multiple_of(j * own, own), own), :]
        both = column_ref[...] * jnp.concatenate([mine] * lat_total, axis=0)
        both_high, both_low = split(both)
        total = jnp.dot(both_high, high, preferred_element_type=f32) + (
            jnp.dot(both_high, low, preferred_element_type=f32)
            + jnp.dot(both_low, high, preferred_element_type=f32)
        )
        o_ref[j] = (total * weight).reshape(lat_total, own, chans)


def coupling(first_order, degree_gain, lat_total):
    degrees, chans = degree_gain.shape
    own = LANES // lat_total
    depth = (degrees + LANES - 1) // LANES * LANES
    return call(
        functools.partial(coupling_kernel, lat_total),
        struct(lat_total, lat_total, own, chans),
        [smem] + vmem(1),
        [
            VMEM((degrees, LANES), f32),
            VMEM((degrees, LANES), f32),
            VMEM((depth, LANES), f32),
            VMEM((degrees, LANES), f32),
            VMEM((depth, chans), f32),
            VMEM((LANES, depth), f32),
        ],
    )(first_order, degree_gain)


def gather_modes(r_ref, write, parts):
    for band in range(r_ref.shape[0] // parts):
        for group in range(parts // 2):
            lanes = pl.ds(group * LANES, LANES)
            first, second = r_ref[band * parts + 2 * group], r_ref[band * parts + 2 * group + 1]
            for row in range(2):
                write(2 * band + row, lanes, pair(first, second, row))


def scatter_modes(read, s_ref, parts):
    for band in range(s_ref.shape[0] // parts):
        for part in range(parts):
            lanes = pl.ds(part // 2 * LANES, LANES)
            s_ref[band * parts + part] = pair(
                read(2 * band, lanes), read(2 * band + 1, lanes), part % 2
            )


def forward_modes_kernel(parts, r_ref, coupling_ref, w_ref, x_ref, s_ref, y_ref, z_ref):
    def write(j, lanes, value):
        x_ref[j, :, lanes] = value

    gather_modes(r_ref, write, parts)
    lats, rows, chans = x_ref.shape
    own = rows // 2
    y_ref[...] = dot_split(
        x_ref[...].reshape(lats * rows, chans), w_ref[...], ((1,), (0,))
    ).reshape(lats, rows, chans)

    @pl.loop(0, lats)
    def _(j):
        totals = [jnp.zeros((own, chans), f32)] * 2
        for other in range(lats):
            factor = coupling_ref[j, other]
            for p in range(2):
                totals[p] = totals[p] + factor * y_ref[other, pl.ds(p * own, own), :]
        for p in range(2):
            z_ref[j, pl.ds(p * own, own), :] = totals[p]

    scatter_modes(lambda j, lanes: z_ref[j, :, lanes], s_ref, parts)


def backward_modes_kernel(parts, r_ref, coupling_ref, w_ref, x_ref, s_ref, gw_ref, e_ref, v_ref):
    def write(j, lanes, value):
        e_ref[j, :, lanes] = value

    gather_modes(r_ref, write, parts)
    lats, rows, chans = x_ref.shape
    own = rows // 2

    @pl.loop(0, lats)
    def _(j):
        totals = [jnp.zeros((own, chans), f32)] * 2
        for other in range(lats):
            factor = coupling_ref[other, j]
            for p in range(2):
                totals[p] = totals[p] + factor * e_ref[other, pl.ds(p * own, own), :]
        for p in range(2):
            v_ref[j, pl.ds(p * own, own), :] = totals[p]

    v = v_ref[...].reshape(lats * rows, chans)
    e_ref[...] = dot_split(v, w_ref[...], ((1,), (1,))).reshape(lats, rows, chans)
    scatter_modes(lambda j, lanes: e_ref[j, :, lanes], s_ref, parts)
    gw_ref[...] = dot_split(x_ref[...].reshape(lats * rows, chans), v, ((0,), (0,)))


def legendre_orders(colatitude, orders, log_norm, degree_count):
    cosine = jnp.cos(colatitude)[None, :]
    log_sine = jnp.log(jnp.sin(colatitude))[None, :]
    order_f = orders.astype(f32)[:, None]
    norm_start = jnp.exp(log_norm)[:, None] + jnp.zeros_like(cosine)
    zeros_state = jnp.zeros((orders.shape[0], colatitude.shape[0]), f32)

    def advance(carry, degree):
        previous, second, log_scale = carry
        degree_f = degree.astype(f32)
        step_factor = jnp.where(
            degree > orders[:, None],
            jnp.sqrt(
                jnp.maximum(4.0 * degree_f * degree_f - 1.0, 0.0)
                / jnp.maximum(degree_f * degree_f - order_f * order_f, 1.0)
            ),
            0.0,
        )
        lower_degree = degree_f - 1.0
        back_factor = jnp.sqrt(
            jnp.maximum(lower_degree * lower_degree - order_f * order_f, 0.0)
            / (4.0 * lower_degree * lower_degree - 1.0)
        )
        current = jnp.where(
            degree == orders[:, None],
            norm_start,
            step_factor * (cosine * previous - back_factor * second),
        )
        too_large = jnp.abs(current) > upper_bound
        current = jnp.where(too_large, current * lower_factor, current)
        previous = jnp.where(too_large, previous * lower_factor, previous)
        log_scale = jnp.where(too_large, log_scale + log_step, log_scale)
        return ((current, previous, log_scale), current * jnp.exp(log_scale))

    start_state = (zeros_state, zeros_state, order_f * log_sine)
    _, tables = lax.scan(advance, start_state, jnp.arange(degree_count, dtype=jnp.int32), unroll=8)
    return tables


def plain_gather(received, parts, own):
    bands = received.shape[0] // parts
    blocks = received.reshape(bands, parts, 2, own, 2, HALF)
    return blocks.transpose(0, 4, 2, 3, 1, 5).reshape(2 * bands, 2, own, parts * HALF)


def plain_scatter(modes, parts):
    lats, _, own, chans = modes.shape
    blocks = modes.reshape(lats // 2, 2, 2, own, parts, HALF)
    return blocks.transpose(0, 4, 2, 3, 1, 5).reshape(lats // 2 * parts, 2 * own, LANES)


def mode_stages(first_order, own, lat_total, parts, degree_gain, spec_weight):
    if own % 8 == 0 and own * lat_total == LANES:
        factors = coupling(first_order[None], degree_gain, lat_total)
        chans = spec_weight.shape[0]
        shape = (lat_total, 2 * own, chans)

        def forward(received):
            return call(
                functools.partial(forward_modes_kernel, parts),
                (struct(*shape), struct(*received.shape)),
                vmem(3),
                [VMEM(shape, f32), VMEM(shape, f32)],
            )(received, factors, spec_weight)

        def backward(received, spectrum):
            return call(
                functools.partial(backward_modes_kernel, parts),
                (struct(*received.shape), struct(chans, chans)),
                vmem(4),
                [VMEM(shape, f32), VMEM(shape, f32)],
            )(received, factors, spec_weight, spectrum)

        return forward, backward

    colatitude, quad_weight = grid_tables(lat_total)
    orders = first_order + jnp.arange(own, dtype=jnp.int32)
    log_norm = lax.dynamic_slice_in_dim(log_norms(M), first_order, own)
    legendre = legendre_orders(colatitude, orders, log_norm, degree_gain.shape[0])
    order_weight = jnp.where(orders == 0, 1.0, 2.0).astype(f32)[None, None, :, None]
    quad_column = quad_weight[:, None, None, None]
    dot = functools.partial(jnp.einsum, precision=highest)

    def forward(received):
        spectrum = plain_gather(received, parts, own)
        mixed = dot("jpmc,cd->jpmd", spectrum, spec_weight) * quad_column
        degree = dot("lmj,jpmd->lpmd", legendre, mixed) * degree_gain[:, None, None, :]
        synthesis = dot("lmj,lpmd->jpmd", legendre, degree) * order_weight
        return spectrum, plain_scatter(synthesis, parts)

    def backward(received, spectrum):
        error = plain_gather(received, parts, own) * order_weight
        gained = dot("lmj,jpmd->lpmd", legendre, error) * degree_gain[:, None, None, :]
        back = dot("lmj,lpmd->jpmd", legendre, gained) * quad_column
        sent = plain_scatter(dot("jpmd,cd->jpmc", back, spec_weight), parts)
        return sent, dot("jpmc,jpmd->cd", spectrum, back)

    return forward, backward


def swap_parts(x, axis):
    return lax.all_to_all(x, axis, split_axis=0, concat_axis=0, tiled=True)


def body(
    grid_field, filters, disco_weight, band_start, band_reach, spec_weight, degree_gain, cotangent
):
    band_rows, lon_local, chans = grid_field.shape
    bands, parts = lax.axis_size("lat"), lax.axis_size("chan")
    devices = bands * parts
    lat_total, lon_total = band_rows * bands, lon_local * parts
    own = M // devices
    assert band_rows == HMAX and chans == parts * HALF
    band, part = lax.axis_index("lat"), lax.axis_index("chan")
    both_axes = ("lat", "chan")
    high, low = wave_tables(lon_total, own)
    high_t, low_t = (jnp.asarray(np.ascontiguousarray(t.T)) for t in (high, low))
    high, low = jnp.asarray(high), jnp.asarray(low)
    up = [(i, i + 1) for i in range(bands - 1)]
    down = [(i + 1, i) for i in range(bands - 1)]

    def spread_lons(x):
        return swap_parts(pack(x, parts), "chan").reshape(lon_total, LANES)

    def return_lons(x):
        return unpack(swap_parts(x.reshape(parts, lon_local, LANES), "chan"))

    def exchange(modes):
        return swap_parts(modes.reshape(devices, 2 * own, LANES), both_axes)

    field = spread_lons(grid_field)
    cot = spread_lons(cotangent)

    mine = lax.dynamic_slice_in_dim(disco_weight, part * HALF, HALF, axis=1)
    coefficient = jnp.einsum("ikrt,kc->irtc", filters, mine, precision=highest)
    window = jnp.arange(WIN, dtype=jnp.int32)
    coefficient = jnp.where(
        (window[None, :] < band_reach[:, None])[:, :, None, None], coefficient, 0.0
    )
    offset = jnp.arange(-HMAX, HMAX + 1, dtype=jnp.int32)
    lands = offset[None, :, None] == band_start[:, None, None] + window[None, None, :]
    by_offset = jnp.sum(
        jnp.where(lands[:, :, :, None, None], coefficient[:, None], 0.0), axis=2
    )
    before = lax.ppermute(by_offset, "lat", up)
    after = lax.ppermute(by_offset, "lat", down)
    rows = jnp.concatenate([before, by_offset, after], axis=0)
    coef = by_offset.transpose(1, 2, 0, 3).reshape(SPAN * KLON, LANES)
    adjoint = jnp.stack(
        [
            jnp.stack([rows[HMAX + i + u, HMAX - u, ::-1] for i in range(band_rows)], axis=1)
            for u in range(-HMAX, HMAX + 1)
        ]
    ).reshape(SPAN * KLON, LANES)

    forward, backward = mode_stages(
        (band * parts + part) * own, own, lat_total, parts, degree_gain, spec_weight
    )

    modes = call(
        functools.partial(analyze_kernel, 1.0 / lon_total), struct(2 * M, LANES), vmem(3)
    )(field, high, low)
    spectrum, synthesis = forward(exchange(modes))
    local = local_filter(
        lax.ppermute(field, "lat", up), field, lax.ppermute(field, "lat", down), coef
    )
    output, error, error_modes = call(
        grid_kernel,
        (struct(lon_total, LANES), struct(lon_total, LANES), struct(2 * M, LANES)),
        vmem(8),
        [VMEM((lon_total, 2 * LANES), bf16)],
    )(exchange(synthesis).reshape(2 * M, LANES), field, local, cot, high, low, high_t, low_t)
    sent, weight_part = backward(exchange(error_modes), spectrum)
    base = local_filter(
        lax.ppermute(error, "lat", up), error, lax.ppermute(error, "lat", down), adjoint, cot
    )
    gradient = call(
        functools.partial(final_kernel, 1.0 / lon_total), struct(lon_total, LANES), vmem(4)
    )(exchange(sent).reshape(2 * M, LANES), base, high_t, low_t)
    grad_input = return_lons(gradient)
    output = return_lons(output)
    shares = swap_parts(weight_part.reshape(devices, chans // devices, chans), both_axes)
    share = jnp.sum(shares, axis=0)
    grad_weight = swap_parts(
        jnp.broadcast_to(share[None], shares.shape), both_axes
    ).reshape(chans, chans)
    return (output, grad_input, grad_weight)


def solution(mesh):
    in_specs = (
        P("lat", "chan", None),
        P("lat", None, None, None),
        P(),
        P("lat"),
        P("lat"),
        P(),
        P(),
        P("lat", "chan", None),
    )
    out_specs = (P("lat", "chan", None), P("lat", "chan", None), P())
    return jax.shard_map(body, mesh=mesh, in_specs=in_specs, out_specs=out_specs, check_vma=False)
```

time: 746 us -> 192 us (0.26); the launches traced: 734 us -> 191 us
  loops' own time: 241 us -> 0 us
  local copies, waits for them, and re-layouts: 149 us -> 11.2 us
  waiting for transfers between devices: 186 us -> 60.3 us
  matrix products: 55.7 us -> 0.23 us
  other arithmetic: 52.7 us -> 0.4 us
  blocking collectives: 0 us -> 50.6 us
  Pallas kernels: 0 us -> 30.1 us
  between operations: 14.9 us -> 1.11 us
    another operation x1 -> x0, loops' own time: 241 us -> none  [legendre_orders(): _, tables = lax.scan(advance_block, start_state, block_firsts)]
    psum x1 -> x0, waiting for transfers between devices: 125 us -> none  [body(): grad_weight = lax.psum(weight_part, ('lat', 'chan'))]
    dot_general x13 -> x1, matrix products: 55.7 us -> 0.23 us  [body(): coefficient = jnp.einsum('ikrt,kc->irtc', filters, mine, precision=highest)]
    another operation x371 -> x7, local copies, waits for them, and re-layouts: 53.5 us -> 0.03 us  [body(): jnp.stack([rows[HMAX + i + u, HMAX - u, ::-1] for i in range(band_rows)],...]
    all_to_all x0 -> x3, blocking collectives: none -> 50.6 us  [swap_parts(): return lax.all_to_all(x, axis, split_axis=0, concat_axis=0, tiled=True)]
    all_to_all x4 -> x7, waiting for transfers between devices: 12.1 us -> 60.3 us  [swap_parts(): return lax.all_to_all(x, axis, split_axis=0, concat_axis=0, tiled=True)]
    scatter-add x5 -> x0, local copies, waits for them, and re-layouts: 45.9 us -> none  [body(): contrib.at[:, :, tap_index:tap_index + lon_local, :]]
    all_gather x4 -> x0, waiting for transfers between devices: 45.6 us -> none  [the longest x2 31.1 us: analyze(): piece = lax.all_gather(field, 'chan', axis=1, tiled=True)]
  transfers between devices with their start and end apart: 17 -> 13, of which waited for: 9 -> 7; matrix products, arithmetic and copies ran while one was open for 31% -> 1% of each run, Pallas kernels for 0% -> 11%
where the time goes in v1:
time: 192 us; the launch traced here: 191 us
  waiting for transfers between devices  60.3 us (31%)
  blocking collectives  50.6 us (26%)
  starting transfers between devices  36.7 us (19%)
  Pallas kernels  30.1 us (16%)
  local copies, waits for them, and re-layouts  11.2 us (6%)
    all_to_all x7, waiting for transfers between devices, swap_parts(): return lax.all_to_all(x, axis, split_axis=0, concat_axis=0, tiled=True)  60.3 us
    all_to_all x3, blocking collectives, swap_parts(): return lax.all_to_all(x, axis, split_axis=0, concat_axis=0, tiled=True)  50.6 us
    all_to_all x7, starting transfers between devices, swap_parts(): return lax.all_to_all(x, axis, split_axis=0, concat_axis=0, tiled=True)  22.8 us
    unnamed x43, local copies, waits for them, and re-layouts  10.3 us
    pallas_call x1, Pallas kernels, coupling(): call(functools.partial(coupling_kernel, lat_total), struct(lat_total, lat...  8.04 us
    pallas_call x2, Pallas kernels, local_filter(): call(functools.partial(filter_kernel, base is not None), struct(lons, LAN...  7.58 us
    pallas_call x1, Pallas kernels, body(): call(grid_kernel, (struct(lon_total, LANES), struct(lon_total, LANES), st...  4.43 us
    ppermute x1, starting transfers between devices, body(): lax.ppermute(field, 'lat', up)  3.93 us
  transfers between devices with their start and end apart: 13, of which 7 were waited for; matrix products, arithmetic and copies ran while one was open for 1% of the time, Pallas kernels for 11%

profile of v1, /device:TPU:0, one launch (start us, length us, event | category | flops | bytes accessed | tf_op | source)
XLA Modules:
  0.0 190.7 jit_solution(10141382126306354471)
XLA Ops:
  2.2 25.2 %all_to_all.50 = f32[4,360,128]{2,1,0:T(8,128)S(1)} all-to-all(f32[4,360,128]{2,1,0:T(8,128)S(1)} %shard_map.139), channel_id=1, replica_groups=mesh['lat'=8,'chan'=4] {'chan'}, dimensions={0} | all-to-all | bytes 1474560 | tf_op jit(solution)/shard_map/all_to_all | solution.py:499
  30.4 3.7 %all-to-all-start.1 = ((f32[32,16,128]{2,1,0:T(8,128)}), f32[32,16,128]{2,1,0:T(8,128)S(1)}, u32[]{:S(2)}, u32[]{:S(2)}) async-start(f32[32,16,128]{2,1,0:T(8,128)} %bitcast.1), calls=%async_computation.1 | async-start | bytes 524288 | tf_op jit(solution)/shard_map/all_to_all | solution.py:499
  36.4 8.0 %all-to-all-done.1.r_ref = f32[32,16,128]{2,1,0:T(8,128)S(1)} async-done(((f32[32,16,128]{2,1,0:T(8,128)}), f32[32,16,128]{2,1,0:T(8,128)S(1)}, u32[]{:S(2)}, u32[]{:S(2)}) %all-to-all-start.1) | async-done | bytes 262176 | tf_op jit(solution)/shard_map/all_to_all | solution.py:499
  44.4 4.2 %all-to-all-start.3 = ((f32[4,360,128]{2,1,0:T(8,128)}), f32[4,360,128]{2,1,0:T(8,128)}, u32[]{:S(2)}, u32[]{:S(2)}) async-start(f32[4,360,128]{2,1,0:T(8,128)} %shard_map.144), calls=%async_computation.3 | async-start | bytes 1474560 | tf_op jit(solution)/shard_map/all_to_all | solution.py:499
  49.9 3.9 %collective-permute-start = (f32[1440,128]{1,0:T(8,128)S(1)}, f32[1440,128]{1,0:T(8,128)}, u32[]{:S(2)}, u32[]{:S(2)}) collective-permute-start(f32[1440,128]{1,0:T(8,128)S(1)} %bitcast.62), channel_id=1, source_target_pairs={{0,4},{4,8},{8,12},{12,16},{16,20},{20,24},{24,28},{1,5},{5,9},{9,... | collective-permute-start | bytes 2211848 | tf_op jit(solution)/shard_map/ppermute | solution.py:562
  55.1 8.0 %shard_map.141.coupling_ref = f32[16,16,8,256]{3,2,1,0:T(8,128)S(1)} custom-call(s32[1]{0:T(128)} %bitcast.2.first_ref, f32[360,256]{1,0:T(8,128)S(1)} %copy-done.14), custom_call_target="tpu_custom_call" | custom-call | tf_op jit(solution)/shard_map/pallas_call | solution.py:317
  65.7 2.9 %all-to-all-done.3 = f32[4,360,128]{2,1,0:T(8,128)} async-done(((f32[4,360,128]{2,1,0:T(8,128)}), f32[4,360,128]{2,1,0:T(8,128)}, u32[]{:S(2)}, u32[]{:S(2)}) %all-to-all-start.3) | async-done | bytes 737312 | tf_op jit(solution)/shard_map/all_to_all | solution.py:499
  68.5 2.6 %all-to-all-start.2 = ((f32[32,16,128]{2,1,0:T(8,128)}), f32[32,16,128]{2,1,0:T(8,128)S(1)}, u32[]{:S(2)}, u32[]{:S(2)}) async-start(f32[32,16,128]{2,1,0:T(8,128)} %copy-done.15), calls=%async_computation.2 | async-start | bytes 524288 | tf_op jit(solution)/shard_map/all_to_all | solution.py:499
  71.5 3.8 %shard_map.143.local_ref = f32[1440,128]{1,0:T(8,128)S(1)} custom-call(f32[1440,128]{1,0:T(8,128)} %collective-permute-done.prev_ref, f32[1440,128]{1,0:T(8,128)S(1)} %bitcast.63, f32[1440,128]{1,0:T(8,128)} %collective-permute-done.1.next_ref, f32[25,128]{1,0:T(8,128)S(1)} %reshape.94.coef_ref), custom_call_target="tpu_custom_call" | custom-call | tf_op jit(solution)/shard_map/pallas_call | solution.py:221
  76.2 5.2 %all-to-all-done.2 = f32[32,16,128]{2,1,0:T(8,128)S(1)} async-done(((f32[32,16,128]{2,1,0:T(8,128)}), f32[32,16,128]{2,1,0:T(8,128)S(1)}, u32[]{:S(2)}, u32[]{:S(2)}) %all-to-all-start.2) | async-done | bytes 262176 | tf_op jit(solution)/shard_map/all_to_all | solution.py:499
  83.8 4.4 %shard_map.145 = (f32[1440,128]{1,0:T(8,128)S(1)}, f32[1440,128]{1,0:T(8,128)S(1)}, f32[512,128]{1,0:T(8,128)S(1)}) custom-call(f32[512,128]{1,0:T(8,128)S(1)} %bitcast.66, f32[1440,128]{1,0:T(8,128)S(1)} %bitcast.64, f32[1440,128]{1,0:T(8,128)S(1)} %copy-done.7, f32[1440,128]{1,0:T(8,128)} %bitcast.8.cot_ref.refs_0_, ...), custom_call_target="tpu_custom_call" | custom-call | tf_op jit(solution)/shard_map/pallas_call | solution.py:564
  88.3 12.7 %all_to_all.51.r_ref = f32[32,16,128]{2,1,0:T(8,128)S(1)} all-to-all(f32[32,16,128]{2,1,0:T(8,128)S(1)} %bitcast.68), channel_id=1, replica_groups=mesh['lat'=8,'chan'=4] {'lat','chan'}, dimensions={0} | all-to-all | bytes 524288 | tf_op jit(solution)/shard_map/all_to_all | solution.py:499
  102.9 12.7 %all_to_all.52 = f32[32,8,256]{2,1,0:T(8,128)S(1)} all-to-all(f32[32,8,256]{2,1,0:T(8,128)S(1)} %bitcast.69), channel_id=1, replica_groups=mesh['lat'=8,'chan'=4] {'lat','chan'}, dimensions={0} | all-to-all | bytes 524288 | tf_op jit(solution)/shard_map/all_to_all | solution.py:499
  115.6 2.7 %all-to-all-start.6 = ((f32[32,16,128]{2,1,0:T(8,128)}), f32[32,16,128]{2,1,0:T(8,128)S(1)}, u32[]{:S(2)}, u32[]{:S(2)}) async-start(f32[32,16,128]{2,1,0:T(8,128)} %get-tuple-element.14), calls=%async_computation.6 | async-start | bytes 524288 | tf_op jit(solution)/shard_map/all_to_all | solution.py:499
  119.7 3.0 %collective-permute-start.4 = (f32[2,5,5,64]{3,0,2,1:T(2,128)S(1)}, f32[2,5,5,64]{3,0,2,1:T(2,128)S(1)}, u32[]{:S(2)}, u32[]{:S(2)}) collective-permute-start(f32[2,5,5,64]{3,0,2,1:T(2,128)S(1)} %select_reduce_fusion), channel_id=1, source_target_pairs={{0,4},{4,8},{8,12},{12,16},{16,20},{20,24},{24,28},{1,5},{5,9},{9,... | collective-permute-start | bytes 38408 | tf_op jit(solution)/shard_map/ppermute | solution.py:542
  122.7 5.8 %all-to-all-done.6 = f32[32,16,128]{2,1,0:T(8,128)S(1)} async-done(((f32[32,16,128]{2,1,0:T(8,128)}), f32[32,16,128]{2,1,0:T(8,128)S(1)}, u32[]{:S(2)}, u32[]{:S(2)}) %all-to-all-start.6) | async-done | bytes 262176 | tf_op jit(solution)/shard_map/all_to_all | solution.py:499
  128.6 3.5 %all-to-all-start.4 = ((f32[4,360,128]{2,1,0:T(8,128)}), f32[4,360,128]{2,1,0:T(8,128)S(1)}, u32[]{:S(2)}, u32[]{:S(2)}) async-start(f32[4,360,128]{2,1,0:T(8,128)} %bitcast.67), calls=%async_computation.4 | async-start | bytes 1474560 | tf_op jit(solution)/shard_map/all_to_all | solution.py:499
  133.5 3.1 %collective-permute-start.2 = (f32[1440,128]{1,0:T(8,128)S(1)}, f32[1440,128]{1,0:T(8,128)S(1)}, u32[]{:S(2)}, u32[]{:S(2)}) collective-permute-start(f32[1440,128]{1,0:T(8,128)S(1)} %copy-done.10), channel_id=1, source_target_pairs={{0,4},{4,8},{8,12},{12,16},{16,20},{20,24},{24,28},{1,5},{5,9},{9,... | collective-permute-start | bytes 2211848 | tf_op jit(solution)/shard_map/ppermute | solution.py:572
  136.6 15.3 %all-to-all-done.4.p_ref = f32[4,360,128]{2,1,0:T(8,128)S(1)} async-done(((f32[4,360,128]{2,1,0:T(8,128)}), f32[4,360,128]{2,1,0:T(8,128)S(1)}, u32[]{:S(2)}, u32[]{:S(2)}) %all-to-all-start.4) | async-done | bytes 737312 | tf_op jit(solution)/shard_map/all_to_all | solution.py:499
  152.7 2.6 %all-to-all-start.9 = ((f32[32,8,256]{2,1,0:T(8,128)}), f32[32,8,256]{2,1,0:T(8,128)S(1)}, u32[]{:S(2)}, u32[]{:S(2)}) async-start(f32[32,8,256]{2,1,0:T(8,128)} %broadcast_in_dim.55), calls=%async_computation.9 | async-start | bytes 524288 | tf_op jit(solution)/shard_map/all_to_all | solution.py:499
  155.5 3.8 %shard_map.148.base_ref = f32[1440,128]{1,0:T(8,128)S(1)} custom-call(f32[1440,128]{1,0:T(8,128)S(1)} %collective-permute-done.2.prev_ref, f32[1440,128]{1,0:T(8,128)S(1)} %copy-done.10, f32[1440,128]{1,0:T(8,128)S(1)} %collective-permute-done.3.next_ref, f32[25,128]{1,0:T(8,128)S(1)} %reshape.99.coef_ref, f32[1440,128]{1,0:T(8,128)} %bitcast.8.cot_ref.refs_0_), custom_call_target="tpu_custom_call" | custom-call | tf_op jit(solution)/shard_map/pallas_call | solution.py:221
  161.1 4.4 %all-to-all-done.9 = f32[32,8,256]{2,1,0:T(8,128)S(1)} async-done(((f32[32,8,256]{2,1,0:T(8,128)}), f32[32,8,256]{2,1,0:T(8,128)S(1)}, u32[]{:S(2)}, u32[]{:S(2)}) %all-to-all-start.9) | async-done | bytes 262176 | tf_op jit(solution)/shard_map/all_to_all | solution.py:499
  165.5 3.5 %all-to-all-start.7 = ((f32[4,360,128]{2,1,0:T(8,128)}), f32[4,360,128]{2,1,0:T(8,128)S(1)}, u32[]{:S(2)}, u32[]{:S(2)}) async-start(f32[4,360,128]{2,1,0:T(8,128)} %bitcast.27), calls=%async_computation.7 | async-start | bytes 1474560 | tf_op jit(solution)/shard_map/all_to_all | solution.py:499
  170.1 18.8 %all-to-all-done.7.p_ref = f32[4,360,128]{2,1,0:T(8,128)S(1)} async-done(((f32[4,360,128]{2,1,0:T(8,128)}), f32[4,360,128]{2,1,0:T(8,128)S(1)}, u32[]{:S(2)}, u32[]{:S(2)}) %all-to-all-start.7) | async-done | bytes 737312 | tf_op jit(solution)/shard_map/all_to_all | solution.py:499
  (86 shorter events, 25.8 us)
Async XLA Ops:
  0.6 53.2 %copy-start = (f32[2,4,3,5]{3,1,2,0:T(4,128)S(1)}, f32[2,4,3,5]{3,1,2,0:T(4,128)}, u32[]{:S(2)}) copy-start(f32[2,4,3,5]{3,1,2,0:T(4,128)} %param.13) | copy-start | bytes 1444
  0.6 26.7 %copy-start.1 = (bf16[512,1440]{1,0:T(8,128)(2,1)S(1)}, bf16[512,1440]{1,0:T(8,128)(2,1)}, u32[]{:S(2)}) copy-start(bf16[512,1440]{1,0:T(8,128)(2,1)} %constant.34.clone.low_ref) | copy-start | bytes 4423684
  30.4 13.9 %all-to-all-start.1 = ((f32[32,16,128]{2,1,0:T(8,128)}), f32[32,16,128]{2,1,0:T(8,128)S(1)}, u32[]{:S(2)}, u32[]{:S(2)}) async-start(f32[32,16,128]{2,1,0:T(8,128)} %bitcast.1), calls=%async_computation.1 | async-start | bytes 524288 | tf_op jit(solution)/shard_map/all_to_all | solution.py:499
  35.3 13.3 %copy-start.20 = (s32[2]{0:T(128)S(1)}, s32[2]{0:T(128)}, u32[]{:S(2)}) copy-start(s32[2]{0:T(128)} %param.16) | copy-start | bytes 28
  35.3 18.6 %copy-start.19 = (f32[4,256]{1,0:T(4,128)S(1)}, f32[4,256]{1,0:T(4,128)}, u32[]{:S(2)}) copy-start(f32[4,256]{1,0:T(4,128)} %param.14) | copy-start | bytes 12292
  44.4 24.2 %all-to-all-start.3 = ((f32[4,360,128]{2,1,0:T(8,128)}), f32[4,360,128]{2,1,0:T(8,128)}, u32[]{:S(2)}, u32[]{:S(2)}) async-start(f32[4,360,128]{2,1,0:T(8,128)} %shard_map.144), calls=%async_computation.3 | async-start | bytes 1474560 | tf_op jit(solution)/shard_map/all_to_all | solution.py:499
  48.5 14.6 %copy-start.8 = (f32[256,256]{1,0:T(8,128)S(1)}, f32[256,256]{1,0:T(8,128)}, u32[]{:S(2)}) copy-start(f32[256,256]{1,0:T(8,128)} %w_ref.3) | copy-start | bytes 786436
  48.7 22.8 %collective-permute-start.1 = (f32[1440,128]{1,0:T(8,128)S(1)}, f32[1440,128]{1,0:T(8,128)}, u32[]{:S(2)}, u32[]{:S(2)}) collective-permute-start(f32[1440,128]{1,0:T(8,128)S(1)} %bitcast.61), channel_id=1, source_target_pairs={{4,0},{8,4},{12,8},{16,12},{20,16},{24,20},{28,24},{5,1},{9,5},{13... | collective-permute-start | bytes 2211848 | tf_op jit(solution)/shard_map/ppermute | solution.py:562
  49.9 21.5 %collective-permute-start = (f32[1440,128]{1,0:T(8,128)S(1)}, f32[1440,128]{1,0:T(8,128)}, u32[]{:S(2)}, u32[]{:S(2)}) collective-permute-start(f32[1440,128]{1,0:T(8,128)S(1)} %bitcast.62), channel_id=1, source_target_pairs={{0,4},{4,8},{8,12},{12,16},{16,20},{20,24},{24,28},{1,5},{5,9},{9,... | collective-permute-start | bytes 2211848 | tf_op jit(solution)/shard_map/ppermute | solution.py:562
  63.2 8.0 %copy-start.18 = (s32[2]{0:T(128)S(1)}, s32[2]{0:T(128)}, u32[]{:S(2)}) copy-start(s32[2]{0:T(128)} %param.15) | copy-start | bytes 28
  68.5 12.8 %all-to-all-start.2 = ((f32[32,16,128]{2,1,0:T(8,128)}), f32[32,16,128]{2,1,0:T(8,128)S(1)}, u32[]{:S(2)}, u32[]{:S(2)}) async-start(f32[32,16,128]{2,1,0:T(8,128)} %copy-done.15), calls=%async_computation.2 | async-start | bytes 524288 | tf_op jit(solution)/shard_map/all_to_all | solution.py:499
  83.8 17.2 %copy-start.17 = (f32[16,16,256]{2,1,0:T(8,128)S(1)}, f32[16,16,256]{2,1,0:T(8,128)}, u32[]{:S(2)}) copy-start(f32[16,16,256]{2,1,0:T(8,128)} %copy-done.16) | copy-start | bytes 786436
  88.3 14.7 %copy-start.9 = (f32[1440,128]{1,0:T(8,128)}, f32[1440,128]{1,0:T(8,128)S(1)}, u32[]{:S(2)}) copy-start(f32[1440,128]{1,0:T(8,128)S(1)} %get-tuple-element.15.own_ref) | copy-start | bytes 2211844
  88.3 14.6 %copy-start.13 = (f32[1440,128]{1,0:T(8,128)}, f32[1440,128]{1,0:T(8,128)S(1)}, u32[]{:S(2)}) copy-start(f32[1440,128]{1,0:T(8,128)S(1)} %get-tuple-element.11) | copy-start | bytes 2211844
  102.9 29.3 %copy-start.10 = (f32[1440,128]{1,0:T(8,128)S(1)}, f32[1440,128]{1,0:T(8,128)}, u32[]{:S(2)}) copy-start(f32[1440,128]{1,0:T(8,128)} %copy-done.9) | copy-start | bytes 2211844
  115.6 12.9 %all-to-all-start.6 = ((f32[32,16,128]{2,1,0:T(8,128)}), f32[32,16,128]{2,1,0:T(8,128)S(1)}, u32[]{:S(2)}, u32[]{:S(2)}) async-start(f32[32,16,128]{2,1,0:T(8,128)} %get-tuple-element.14), calls=%async_computation.6 | async-start | bytes 524288 | tf_op jit(solution)/shard_map/all_to_all | solution.py:499
  118.4 13.7 %collective-permute-start.5 = (f32[2,5,5,64]{3,0,2,1:T(2,128)S(1)}, f32[2,5,5,64]{3,0,2,1:T(2,128)S(1)}, u32[]{:S(2)}, u32[]{:S(2)}) collective-permute-start(f32[2,5,5,64]{3,0,2,1:T(2,128)S(1)} %select_reduce_fusion), channel_id=1, source_target_pairs={{4,0},{8,4},{12,8},{16,12},{20,16},{24,20},{28,24},{5,1},{9,5},{13... | collective-permute-start | bytes 38408 | tf_op jit(solution)/shard_map/ppermute | solution.py:543
  119.7 12.5 %collective-permute-start.4 = (f32[2,5,5,64]{3,0,2,1:T(2,128)S(1)}, f32[2,5,5,64]{3,0,2,1:T(2,128)S(1)}, u32[]{:S(2)}, u32[]{:S(2)}) collective-permute-start(f32[2,5,5,64]{3,0,2,1:T(2,128)S(1)} %select_reduce_fusion), channel_id=1, source_target_pairs={{0,4},{4,8},{8,12},{12,16},{16,20},{20,24},{24,28},{1,5},{5,9},{9,... | collective-permute-start | bytes 38408 | tf_op jit(solution)/shard_map/ppermute | solution.py:542
  128.6 23.4 %all-to-all-start.4 = ((f32[4,360,128]{2,1,0:T(8,128)}), f32[4,360,128]{2,1,0:T(8,128)S(1)}, u32[]{:S(2)}, u32[]{:S(2)}) async-start(f32[4,360,128]{2,1,0:T(8,128)} %bitcast.67), calls=%async_computation.4 | async-start | bytes 1474560 | tf_op jit(solution)/shard_map/all_to_all | solution.py:499
  132.2 23.3 %collective-permute-start.3 = (f32[1440,128]{1,0:T(8,128)S(1)}, f32[1440,128]{1,0:T(8,128)S(1)}, u32[]{:S(2)}, u32[]{:S(2)}) collective-permute-start(f32[1440,128]{1,0:T(8,128)S(1)} %copy-done.10), channel_id=1, source_target_pairs={{4,0},{8,4},{12,8},{16,12},{20,16},{24,20},{28,24},{5,1},{9,5},{13... | collective-permute-start | bytes 2211848 | tf_op jit(solution)/shard_map/ppermute | solution.py:572
  133.5 22.0 %collective-permute-start.2 = (f32[1440,128]{1,0:T(8,128)S(1)}, f32[1440,128]{1,0:T(8,128)S(1)}, u32[]{:S(2)}, u32[]{:S(2)}) collective-permute-start(f32[1440,128]{1,0:T(8,128)S(1)} %copy-done.10), channel_id=1, source_target_pairs={{0,4},{4,8},{8,12},{12,16},{16,20},{20,24},{24,28},{1,5},{5,9},{9,... | collective-permute-start | bytes 2211848 | tf_op jit(solution)/shard_map/ppermute | solution.py:572
  152.7 12.8 %all-to-all-start.9 = ((f32[32,8,256]{2,1,0:T(8,128)}), f32[32,8,256]{2,1,0:T(8,128)S(1)}, u32[]{:S(2)}, u32[]{:S(2)}) async-start(f32[32,8,256]{2,1,0:T(8,128)} %broadcast_in_dim.55), calls=%async_computation.9 | async-start | bytes 524288 | tf_op jit(solution)/shard_map/all_to_all | solution.py:499
  155.5 3.8 %copy-start.5 = (bf16[1440,512]{1,0:T(8,128)(2,1)S(1)}, bf16[1440,512]{1,0:T(8,128)(2,1)}, u32[]{:S(2)}) copy-start(bf16[1440,512]{1,0:T(8,128)(2,1)} %constant.31.clone.thigh_ref) | copy-start | bytes 4423684
  165.5 23.4 %all-to-all-start.7 = ((f32[4,360,128]{2,1,0:T(8,128)}), f32[4,360,128]{2,1,0:T(8,128)S(1)}, u32[]{:S(2)}, u32[]{:S(2)}) async-start(f32[4,360,128]{2,1,0:T(8,128)} %bitcast.27), calls=%async_computation.7 | async-start | bytes 1474560 | tf_op jit(solution)/shard_map/all_to_all | solution.py:499
  (10 other events, 13.3 us)

commit v2 on v1

v2 whole, which is shorter than its diff:
```python
import functools
import math

import jax
import jax.numpy as jnp
import ml_dtypes
import numpy as np
from jax import lax
from jax.experimental import pallas as pl
from jax.experimental.pallas import tpu as pltpu
from jax.sharding import PartitionSpec as P

L = 360
M = 256
WIN = 3
HMAX = 2
KLON = 5
POLAR = 720
SPAN = 2 * HMAX + 1
TAPS = 32
EDGES = 16
LANES = 128
MIB = 2**20


highest = lax.Precision.HIGHEST
upper_bound = 2.0**32
lower_factor = 2.0 ** (-32)
log_step = 32.0 * math.log(2.0)

f32 = jnp.float32
bf16 = jnp.bfloat16
VMEM = pltpu.VMEM


@functools.lru_cache(maxsize=None)
def wave_tables(lon_total, own_count):
    orders = np.concatenate([np.arange(0, M, 2), np.arange(1, M, 2)]).reshape(-1, own_count)
    lons = np.arange(lon_total // 2)
    angle = (orders[:, :, None] * lons) % lon_total * (2.0 * np.pi / lon_total)
    table = np.stack([np.cos(angle), -np.sin(angle)], axis=1).reshape(2 * M, lon_total // 2)
    high = table.astype(ml_dtypes.bfloat16)
    low = (table - high.astype(np.float64)).astype(ml_dtypes.bfloat16)
    return high, low


def owned_orders(owner, devices):
    half = devices // 2
    return owner % half * (2 * (M // devices)) + owner // half


def grid_tables(lat_total):
    first_row = (POLAR - lat_total) // 2
    colatitude = math.pi * (jnp.arange(lat_total, dtype=f32) + float(first_row)) / POLAR
    quad_weight = 2.0 * math.pi * math.pi / POLAR * jnp.sin(colatitude)
    return (colatitude, quad_weight)


def log_norms(order_count):
    order_index = jnp.arange(order_count, dtype=f32)
    log_terms = jnp.where(
        order_index > 0.0,
        jnp.log((2.0 * order_index + 1.0) / jnp.maximum(2.0 * order_index, 1.0)),
        0.0,
    )
    return -0.5 * math.log(4.0 * math.pi) + 0.5 * jnp.cumsum(log_terms)


def split(x):
    high = x.astype(bf16)
    return high, (x - high.astype(f32)).astype(bf16)


def dot_split(a, b, dims):
    (ah, al), (bh, bl) = split(a), split(b)
    dot = lambda u, v: lax.dot_general(u, v, (dims, ((), ())), preferred_element_type=f32)
    return dot(ah, bh) + (dot(ah, bl) + dot(al, bh))


def cost(us):
    return pl.CostEstimate(flops=int(us * 1e9), bytes_accessed=int(us * 3e6), transcendentals=0)


def call(kernel, out_shape, in_specs, scratch=(), us=1.0, limit=16, out_spaces=None):
    run = pl.pallas_call(
        kernel,
        out_shape=out_shape,
        in_specs=[pl.BlockSpec(memory_space=space) for space, _ in in_specs],
        out_specs=jax.tree.map(
            lambda space: pl.BlockSpec(memory_space=space),
            out_spaces or jax.tree.map(lambda _: VMEM, out_shape),
        ),
        scratch_shapes=list(scratch),
        compiler_params=pltpu.CompilerParams(vmem_limit_bytes=limit * MIB),
        cost_estimate=cost(us),
    )
    keeps = [keep for _, keep in in_specs]
    return lambda *args: run(
        *[held(x) if keep else x for x, keep in zip(args, keeps, strict=True)]
    )


def held(x):
    return pltpu.with_memory_space_constraint(x, pltpu.HBM)


def vmem(count):
    return [(VMEM, False)] * count


def loaded(count):
    return [(VMEM, True)] * count


def hbm(count):
    return [(pltpu.HBM, True)] * count


smem = (pltpu.SMEM, False)


def struct(*shape, dtype=f32):
    return jax.ShapeDtypeStruct(shape, dtype)


def kept(*shape, dtype=f32):
    return pltpu.HBM(shape, dtype)


def own_half(part):
    return part % 2


def lane_half(x_ref, half):
    return x_ref.at[:, :, pl.ds(pl.multiple_of(half * LANES, LANES), LANES)]


def lon_half(x_ref, half):
    width = x_ref.shape[1] // 2
    return x_ref.at[:, pl.ds(pl.multiple_of(half * width, 8), width), :]


def pair_copies(half, own_hbm, other_hbms, target, sems):
    copies = [pltpu.make_async_copy(lane_half(own_hbm, half), lon_half(target, half), sems.at[0])]
    there = lon_half(target, 1 - half)
    for row, other_hbm in enumerate(other_hbms):
        copies.append(
            pltpu.make_async_copy(other_hbm, there.at[pl.ds(row, 1)], sems.at[1 + row])
        )
    for copy in copies:
        copy.start()
    return copies


def join_kernel(part_ref, own_ref, *refs):
    o_ref = refs[-1]
    half = own_half(part_ref[0])
    mine, theirs = (
        pl.ds(pl.multiple_of(place * LANES, LANES), LANES) for place in (half, 1 - half)
    )
    o_ref[:, :, mine] = own_ref[...]
    for row, other_ref in enumerate(refs[:-1]):
        o_ref[pl.ds(row, other_ref.shape[0]), :, theirs] = other_ref[...]


def join(part, own, *others):
    rows, lons, _ = own.shape
    return call(
        join_kernel, kept(rows, lons, 2 * LANES), [smem] + vmem(1 + len(others))
    )(part, own, *others)


def side_by_side(x):
    return jnp.concatenate([x[0], x[1]], axis=1)


def three(table_high, table_low, high, low):
    dot = lambda u, v: jnp.dot(u, v, preferred_element_type=f32)
    return dot(table_high, high) + (dot(table_high, low) + dot(table_low, high))


def fetches(sources, targets, sems, pieces):
    copies = []
    for index, (source, target) in enumerate(zip(sources, targets, strict=True)):
        tile = source.shape[0] // pieces
        copies.append(
            [
                pltpu.make_async_copy(
                    source.at[pl.ds(piece * tile, tile)],
                    target.at[pl.ds(piece * tile, tile)],
                    sems.at[index, piece],
                )
                for piece in range(pieces)
            ]
        )
    for piece in range(pieces):
        for group in copies:
            group[piece].start()
    return lambda index, piece: copies[index][piece].wait()


def analyze_rows(x, sign, high_ref, low_ref, wait, store):
    high, low = split(x)
    tile = high_ref.shape[0] // 2
    for parity in range(2):
        rows = pl.ds(parity * tile, tile)
        wait(0, parity)
        wait(1, parity)
        value = three(high_ref[rows, :], low_ref[rows, :], high, low)
        store(rows, value * sign if parity else value)


def compose_rows(modes, sign, thigh_ref, tlow_ref, wait, store):
    count = modes.shape[0] // 2
    high, low = split(jnp.concatenate([modes[:count], modes[count:] * sign], axis=0))
    tile = thigh_ref.shape[0] // 3
    for piece in range(3):
        rows = pl.ds(piece * tile, tile)
        wait(0, piece)
        wait(1, piece)
        store(rows, three(thigh_ref[rows, :], tlow_ref[rows, :], high, low))


def turn_sign(part):
    return (1 - 2 * (part // 2)).astype(f32)


def analyze_kernel(scale, part_ref, own_hbm, other_ref, high_hbm, low_hbm, o_ref, field_hbm,
                   x_ref, high_ref, low_ref, pair_sem, sems, out_sem):
    part = part_ref[0]
    half = own_half(part)
    mine = pltpu.make_async_copy(lane_half(own_hbm, half), lon_half(x_ref, half), pair_sem)
    mine.start()
    wait = fetches((high_hbm, low_hbm), (high_ref, low_ref), sems, 2)
    lon_half(x_ref, 1 - half)[...] = other_ref[...]
    mine.wait()
    out = pltpu.make_async_copy(x_ref, field_hbm, out_sem)
    out.start()

    def store(rows, value):
        o_ref[rows, :] = value * scale

    analyze_rows(side_by_side(x_ref[...]), turn_sign(part), high_ref, low_ref, wait, store)
    out.wait()


def analyze(part, lon_total, own, other, high, low):
    rows, lons, _ = own.shape
    field = (rows, 2 * lons, LANES)
    return call(
        functools.partial(analyze_kernel, 1.0 / lon_total),
        (struct(2 * M, rows * LANES), kept(*field)),
        [smem] + hbm(1) + vmem(1) + hbm(2),
        [VMEM(field, f32), VMEM(high.shape, bf16), VMEM(high.shape, bf16)]
        + [pltpu.SemaphoreType.DMA, pltpu.SemaphoreType.DMA((2, 2)), pltpu.SemaphoreType.DMA],
        us=3.0,
        out_spaces=(VMEM, pltpu.HBM),
    )(part, own, other, high, low)


def grid_kernel(part_ref, s_ref, field_hbm, local_hbm, cot_hbm, first_hbm, second_hbm,
                high_hbm, low_hbm, thigh_hbm, tlow_hbm,
                mode_ref, own_hbm, send_first_hbm, send_second_hbm, err_hbm,
                x_ref, local_ref, cot_ref, spec_ref, out_ref, err_ref,
                high_ref, low_ref, thigh_ref, tlow_ref,
                back_sems, sems, cot_sems, other_sems, out_sems):
    part = part_ref[0]
    half, sign = own_half(part), turn_sign(part)
    wait_back = fetches((thigh_hbm, tlow_hbm), (thigh_ref, tlow_ref), back_sems, 3)
    others = [
        pltpu.make_async_copy(source, target, other_sems.at[index])
        for index, (source, target) in enumerate(((local_hbm, local_ref), (field_hbm, x_ref)))
    ]
    for copy in others:
        copy.start()
    others += pair_copies(half, cot_hbm, (first_hbm, second_hbm), cot_ref, cot_sems)
    wait = fetches((high_hbm, low_hbm), (high_ref, low_ref), sems, 2)

    def store_spec(rows, value):
        spec_ref[rows, :] = value

    modes = s_ref[...].reshape(thigh_ref.shape[1], s_ref.shape[2])
    compose_rows(modes, sign, thigh_ref, tlow_ref, wait_back, store_spec)
    for copy in others:
        copy.wait()
    tile = x_ref.shape[1] // 6
    for row in range(x_ref.shape[0]):
        for piece in range(6):
            lons = pl.ds(piece * tile, tile)
            hidden = local_ref[row, lons, :] + spec_ref[lons, pl.ds(row * LANES, LANES)]
            gate = 1.0 / (1.0 + jnp.exp(-hidden))
            out_ref[row, lons, :] = x_ref[row, lons, :] + hidden * gate
            err_ref[row, lons, :] = cot_ref[row, lons, :] * (gate * (1.0 + hidden * (1.0 - gate)))
    there = lon_half(out_ref, 1 - half)
    outs = [
        pltpu.make_async_copy(source, target, out_sems.at[index])
        for index, (source, target) in enumerate(
            (
                (err_ref, err_hbm),
                (lon_half(out_ref, half), own_hbm),
                (there.at[pl.ds(0, 1)], send_first_hbm),
                (there.at[pl.ds(1, 1)], send_second_hbm),
            )
        )
    ]
    for copy in outs:
        copy.start()

    def store(rows, value):
        mode_ref[rows, :] = value

    analyze_rows(side_by_side(err_ref[...]), sign, high_ref, low_ref, wait, store)
    for copy in outs:
        copy.wait()


def grid_stage(part, synthesis, field, local, cotangent, others, tables):
    rows, lons, _ = field.shape
    block = (rows, lons // 2, LANES)
    grid = VMEM(field.shape, f32)
    return call(
        grid_kernel,
        (
            struct(2 * M, rows * LANES),
            kept(*block),
            kept(1, *block[1:]),
            kept(1, *block[1:]),
            kept(*field.shape),
        ),
        [smem] + vmem(1) + hbm(9),
        [grid, grid, grid, VMEM((lons, rows * LANES), f32), grid, grid]
        + [VMEM(table.shape, bf16) for table in tables]
        + [pltpu.SemaphoreType.DMA((2, 3)), pltpu.SemaphoreType.DMA((2, 2))]
        + [pltpu.SemaphoreType.DMA((count,)) for count in (3, 2, 4)],
        us=4.0,
        limit=32,
        out_spaces=(VMEM,) + (pltpu.HBM,) * 4,
    )(part, synthesis, field, local, cotangent, *others, *tables)


def final_kernel(scale, rows_own, part_ref, s_ref, base_hbm, thigh_hbm, tlow_hbm,
                 send_ref, own_ref, share_ref, base_ref, thigh_ref, tlow_ref, sems, base_sem):
    part = part_ref[0]
    half = own_half(part)
    wait = fetches((thigh_hbm, tlow_hbm), (thigh_ref, tlow_ref), sems, 3)
    base_copy = pltpu.make_async_copy(base_hbm, base_ref, base_sem)
    base_copy.start()
    if rows_own < s_ref.shape[1]:
        share = jnp.sum(s_ref[:, pl.ds(rows_own, share_ref.shape[1]), :], axis=0)
        share_ref[...] = jnp.broadcast_to(share[None], share_ref.shape)
    modes = s_ref[:, pl.ds(0, rows_own), :].reshape(thigh_ref.shape[1], s_ref.shape[2])
    base_copy.wait()

    def store(lons, value):
        for row in range(base_ref.shape[0]):
            lanes = slice(row * LANES, (row + 1) * LANES)
            base_ref[row, lons, :] = base_ref[row, lons, :] + scale * value[:, lanes]

    compose_rows(modes, turn_sign(part), thigh_ref, tlow_ref, wait, store)
    own_ref[...] = lon_half(base_ref, half)[...]
    send_ref[...] = lon_half(base_ref, 1 - half)[...]


def final_stage(part, lon_total, rows_own, modes, base, high_t, low_t):
    rows, lons, _ = base.shape
    block = (rows, lons // 2, LANES)
    return call(
        functools.partial(final_kernel, 1.0 / lon_total, rows_own),
        (
            struct(*block),
            kept(*block),
            struct(modes.shape[0], max(modes.shape[1] - rows_own, 8), modes.shape[2]),
        ),
        [smem] + vmem(1) + hbm(3),
        [VMEM(base.shape, f32), VMEM(high_t.shape, bf16), VMEM(high_t.shape, bf16)]
        + [pltpu.SemaphoreType.DMA((2, 3)), pltpu.SemaphoreType.DMA],
        us=3.0,
    )(part, modes, base, high_t, low_t)


def filter_sums(prev_ref, own_ref, next_ref, edge_refs, coef_ref, finish, sums_ref):
    lons = own_ref.shape[1]
    tile = lons // 18
    sources = [(x_ref, row) for x_ref in (prev_ref, own_ref, next_ref) for row in range(2)]
    for row in range(2):
        def add(values, rows, row=row):
            for tap in range(KLON):
                total = values[0] * coef_ref[row, pl.ds(tap, 1), :]
                for offset in range(1, SPAN):
                    total = total + values[offset] * coef_ref[row, pl.ds(offset * KLON + tap, 1), :]
                sums_ref[tap, rows, :] = total

        near = sources[row : row + SPAN]
        edges = [(edge_ref, k) for edge_ref in edge_refs for k in range(2)][row : row + SPAN]
        add([edge_ref[k, pl.ds(8, 8), :] for edge_ref, k in edges], pl.ds(0, 8))
        add([edge_ref[k, pl.ds(0, 8), :] for edge_ref, k in edges], pl.ds(lons + 8, 8))

        @pl.loop(0, 18)
        def _(piece, near=near, add=add):
            start = pl.multiple_of(piece * tile, 8)
            values = [x_ref[k, pl.ds(start, tile), :] for x_ref, k in near]
            add(values, pl.ds(pl.multiple_of(start + 8, 8), tile))

        for piece in range(18):
            total = None
            for tap in range(KLON):
                value = sums_ref[tap, pl.ds(piece * tile + 8 + tap - KLON // 2, tile), :]
                total = value if total is None else total + value
            finish(row, pl.ds(piece * tile, tile), total)


def filter_kernel(prev_ref, own_ref, next_ref, lower_ref, middle_ref, upper_ref, o_ref, adjoint_ref,
                  sums_ref):
    def finish(row, lons, value):
        o_ref[row, lons, :] = value

    taps = pl.ds(EDGES, TAPS)
    coef_refs = [ref.at[:, taps] for ref in (lower_ref, middle_ref, upper_ref)]
    filter_sums(
        prev_ref, own_ref, next_ref, (lower_ref, middle_ref, upper_ref), coef_refs[1], finish, sums_ref
    )
    adjoint_ref[...] = jnp.zeros_like(adjoint_ref)
    sources = [(c_ref, row) for c_ref in coef_refs for row in range(2)]
    for row in range(2):
        for offset in range(SPAN):
            c_ref, k = sources[row + offset]
            for tap in range(KLON):
                mirrored = (SPAN - 1 - offset) * KLON + KLON - 1 - tap
                adjoint_ref[row, pl.ds(offset * KLON + tap, 1), :] = c_ref[k, pl.ds(mirrored, 1), :]


def adjoint_kernel(part_ref, prev_ref, own_ref, next_ref, lower_ref, middle_ref, upper_ref, coef_ref,
                   cot_hbm, first_hbm, second_hbm,
                   o_ref, sums_ref, cot_ref, cot_sems):
    copies = pair_copies(
        own_half(part_ref[0]), cot_hbm, (first_hbm, second_hbm), cot_ref, cot_sems
    )
    for copy in copies:
        copy.wait()

    def finish(row, lons, value):
        o_ref[row, lons, :] = cot_ref[row, lons, :] + value

    filter_sums(prev_ref, own_ref, next_ref, (lower_ref, middle_ref, upper_ref), coef_ref, finish, sums_ref)


def local_filter(prev, own, behind, *edges):
    return call(
        filter_kernel,
        (kept(*own.shape), kept(own.shape[0], TAPS, LANES)),
        loaded(3) + vmem(3),
        [VMEM((KLON, own.shape[1] + 16, LANES), f32)],
        us=4.0,
    )(prev, own, behind, *edges)


def adjoint_filter(part, prev, own, behind, lower, middle, upper, coef, cotangent, others):
    return call(
        adjoint_kernel,
        kept(*own.shape),
        [smem] + loaded(3) + vmem(4) + hbm(3),
        [VMEM((KLON, own.shape[1] + 16, LANES), f32), VMEM(own.shape, f32)]
        + [pltpu.SemaphoreType.DMA((3,))],
        us=4.0,
    )(part, prev, own, behind, lower, middle, upper, coef, cotangent, *others)


def coupling_kernel(lat_total, first_ref, gain_ref, o_hbm, step_ref, back_ref, start_ref, leg_ref,
                    scale_ref, padded_ref, column_ref, o_ref, out_sems):
    degree_count, chans = gain_ref.shape
    depth = padded_ref.shape[0]
    own = LANES // lat_total
    first_row = float((POLAR - lat_total) // 2)
    lane = lax.broadcasted_iota(jnp.int32, (1, LANES), 1)
    order = 2 * (lane % own) + first_ref[0]
    colatitude = math.pi * ((lane // own).astype(f32) + first_row) / POLAR
    cosine, log_sine = jnp.cos(colatitude), jnp.log(jnp.sin(colatitude))
    k = lax.broadcasted_iota(jnp.int32, (M, LANES), 0)
    k_f = k.astype(f32)
    log_terms = jnp.log((2.0 * k_f + 1.0) / jnp.maximum(2.0 * k_f, 1.0))
    log_norm = -0.5 * math.log(4.0 * math.pi) + 0.5 * jnp.sum(
        jnp.where((k > 0) & (k <= order), log_terms, 0.0), axis=0, keepdims=True
    )
    norm_start = jnp.exp(log_norm)
    degree = lax.broadcasted_iota(jnp.int32, (degree_count, LANES), 0)
    degree_f, order_f = degree.astype(f32), order.astype(f32)
    step = jnp.where(
        degree > order,
        jnp.sqrt(
            jnp.maximum(4.0 * degree_f * degree_f - 1.0, 0.0)
            / jnp.maximum(degree_f * degree_f - order_f * order_f, 1.0)
        ),
        0.0,
    )
    lower = degree_f - 1.0
    back = jnp.sqrt(
        jnp.maximum(lower * lower - order_f * order_f, 0.0) / (4.0 * lower * lower - 1.0)
    )
    step_ref[...] = step * cosine
    back_ref[...] = step * back
    start_ref[...] = jnp.where(degree == order, norm_start, 0.0)
    zeros = jnp.zeros((1, LANES), f32)

    def block(index, carry):
        previous, second, log_scale = carry
        first = pl.multiple_of(index * 8, 8)
        scale_ref[pl.ds(first, 8), :] = jnp.broadcast_to(log_scale, (8, LANES))
        for offset in range(8):
            row = pl.ds(first + offset, 1)
            rest = start_ref[row, :] - back_ref[row, :] * second
            current = step_ref[row, :] * previous + rest
            leg_ref[row, :] = current
            second, previous = previous, current
        too_large = jnp.abs(previous) > upper_bound
        second = jnp.where(too_large, second * lower_factor, second)
        previous = jnp.where(too_large, previous * lower_factor, previous)
        return previous, second, jnp.where(too_large, log_scale + log_step, log_scale)

    lax.fori_loop(0, degree_count // 8, block, (zeros, zeros, order_f * log_sine))
    leg_ref[pl.ds(0, degree_count), :] = leg_ref[pl.ds(0, degree_count), :] * jnp.exp(scale_ref[...])
    rest = depth - degree_count
    leg_ref[pl.ds(degree_count, rest), :] = jnp.zeros((rest, LANES), f32)
    padded_ref[pl.ds(0, degree_count), :] = gain_ref[...]
    padded_ref[pl.ds(degree_count, rest), :] = jnp.zeros((rest, chans), f32)
    column_ref[...] = leg_ref[...].T

    high, low = split(padded_ref[...])
    row = lax.broadcasted_iota(jnp.int32, (LANES, LANES), 0)
    quad = 2.0 * math.pi * math.pi / POLAR * jnp.sin(
        math.pi * ((row // own).astype(f32) + first_row) / POLAR
    )
    weight = quad * jnp.where(row % own + first_ref[0] == 0, 1.0, 2.0)
    weight = jnp.concatenate([weight] * (chans // LANES), axis=1)
    group = lat_total // out_sems.shape[0]
    copies = []
    for piece in range(out_sems.shape[0]):
        both = jnp.concatenate(
            [
                column_ref[...]
                * jnp.concatenate([column_ref[pl.ds(j * own, own), :]] * lat_total, axis=0)
                for j in range(piece * group, (piece + 1) * group)
            ],
            axis=0,
        )
        total = three(*split(both), high, low)
        for j in range(group):
            o_ref[piece * group + j] = (total[j * LANES : (j + 1) * LANES] * weight).reshape(
                lat_total, own, chans
            )
        block_of = pl.ds(piece * group, group)
        copies.append(
            pltpu.make_async_copy(o_ref.at[block_of], o_hbm.at[block_of], out_sems.at[piece])
        )
        copies[-1].start()
    for copy in copies:
        copy.wait()


def coupling(first_order, degree_gain, lat_total):
    degrees, chans = degree_gain.shape
    own = LANES // lat_total
    depth = (degrees + LANES - 1) // LANES * LANES
    table = (lat_total, lat_total, own, chans)
    rows = VMEM((degrees, LANES), f32)
    return call(
        functools.partial(coupling_kernel, lat_total),
        kept(*table),
        [smem] + loaded(1),
        [rows, rows, rows, VMEM((depth, LANES), f32), rows]
        + [VMEM((depth, chans), f32), VMEM((LANES, depth), f32), VMEM(table, f32)]
        + [pltpu.SemaphoreType.DMA((4,))],
        us=6.0,
        out_spaces=pltpu.HBM,
    )(first_order, degree_gain)


def gather_modes(r_ref, write, parts):
    for band in range(r_ref.shape[0] // parts):
        for half in range(2):
            both = r_ref[band * parts + half]
            for other in range(half + 2, parts, 2):
                both = both + r_ref[band * parts + other]
            for row in range(2):
                lanes = slice(row * LANES, (row + 1) * LANES)
                write(2 * band + row, pl.ds(half * LANES, LANES), both[:, lanes])


def scatter_modes(read, s_ref, parts, rows):
    for band in range(s_ref.shape[0] // parts):
        for part in range(parts):
            for row in range(2):
                lanes = pl.ds(row * LANES, LANES)
                value = read(2 * band + row, pl.ds(part % 2 * LANES, LANES))
                s_ref[band * parts + part, pl.ds(0, rows), lanes] = value


def forward_modes_kernel(parts, r_ref, coupling_hbm, w_hbm, x_ref, s_ref, y_ref, z_ref,
                         coupling_ref, w_ref, sems):
    wait_w = fetches((w_hbm,), (w_ref,), sems.at[pl.ds(0, 1)], 2)
    wait = fetches((coupling_hbm,), (coupling_ref,), sems.at[pl.ds(1, 1)], 8)

    def write(j, lanes, value):
        x_ref[j, :, lanes] = value

    gather_modes(r_ref, write, parts)
    lats, rows, chans = x_ref.shape
    own = rows // 2
    for piece in range(2):
        wait_w(0, piece)
    y_ref[...] = dot_split(
        x_ref[...].reshape(lats * rows, chans), w_ref[...], ((1,), (0,))
    ).reshape(lats, rows, chans)
    for piece in range(8):
        wait(0, piece)

        @pl.loop(piece * (lats // 8), (piece + 1) * (lats // 8))
        def _(j):
            totals = [jnp.zeros((own, chans), f32)] * 2
            for other in range(lats):
                factor = coupling_ref[j, other]
                for p in range(2):
                    totals[p] = totals[p] + factor * y_ref[other, pl.ds(p * own, own), :]
            for p in range(2):
                z_ref[j, pl.ds(p * own, own), :] = totals[p]

    scatter_modes(lambda j, lanes: z_ref[j, :, lanes], s_ref, parts, rows)


def backward_modes_kernel(parts, r_ref, coupling_hbm, w_hbm, x_hbm, s_ref, e_ref, v_ref,
                          coupling_ref, w_ref, x_ref, sems):
    wait = fetches((coupling_hbm,), (coupling_ref,), sems.at[pl.ds(0, 1)], 8)
    wait_rest = fetches((w_hbm, x_hbm), (w_ref, x_ref), sems.at[pl.ds(1, 2)], 2)

    def write(j, lanes, value):
        e_ref[j, :, lanes] = value

    gather_modes(r_ref, write, parts)
    lats, rows, chans = x_ref.shape
    own = rows // 2
    for piece in range(8):
        wait(0, piece)

    @pl.loop(0, lats)
    def _(j):
        totals = [jnp.zeros((own, chans), f32)] * 2
        for other in range(lats):
            factor = coupling_ref[other, j]
            for p in range(2):
                totals[p] = totals[p] + factor * e_ref[other, pl.ds(p * own, own), :]
        for p in range(2):
            v_ref[j, pl.ds(p * own, own), :] = totals[p]

    for piece in range(2):
        for index in range(2):
            wait_rest(index, piece)
    v = v_ref[...].reshape(lats * rows, chans)
    e_ref[...] = dot_split(v, w_ref[...], ((1,), (1,))).reshape(lats, rows, chans)
    scatter_modes(lambda j, lanes: e_ref[j, :, lanes], s_ref, parts, rows)
    weight_part = dot_split(x_ref[...].reshape(lats * rows, chans), v, ((0,), (0,)))
    share = chans // s_ref.shape[0]
    s_ref[:, pl.ds(rows, share), :] = weight_part.reshape(s_ref.shape[0], share, chans)


def legendre_orders(colatitude, orders, log_norm, degree_count):
    cosine = jnp.cos(colatitude)[None, :]
    log_sine = jnp.log(jnp.sin(colatitude))[None, :]
    order_f = orders.astype(f32)[:, None]
    norm_start = jnp.exp(log_norm)[:, None] + jnp.zeros_like(cosine)
    zeros_state = jnp.zeros((orders.shape[0], colatitude.shape[0]), f32)

    def advance(carry, degree):
        previous, second, log_scale = carry
        degree_f = degree.astype(f32)
        step_factor = jnp.where(
            degree > orders[:, None],
            jnp.sqrt(
                jnp.maximum(4.0 * degree_f * degree_f - 1.0, 0.0)
                / jnp.maximum(degree_f * degree_f - order_f * order_f, 1.0)
            ),
            0.0,
        )
        lower_degree = degree_f - 1.0
        back_factor = jnp.sqrt(
            jnp.maximum(lower_degree * lower_degree - order_f * order_f, 0.0)
            / (4.0 * lower_degree * lower_degree - 1.0)
        )
        current = jnp.where(
            degree == orders[:, None],
            norm_start,
            step_factor * (cosine * previous - back_factor * second),
        )
        too_large = jnp.abs(current) > upper_bound
        current = jnp.where(too_large, current * lower_factor, current)
        previous = jnp.where(too_large, previous * lower_factor, previous)
        log_scale = jnp.where(too_large, log_scale + log_step, log_scale)
        return ((current, previous, log_scale), current * jnp.exp(log_scale))

    start_state = (zeros_state, zeros_state, order_f * log_sine)
    _, tables = lax.scan(advance, start_state, jnp.arange(degree_count, dtype=jnp.int32), unroll=8)
    return tables


def plain_gather(received, parts, own):
    bands = received.shape[0] // parts
    blocks = received.reshape(bands, parts // 2, 2, 2, own, 2, LANES).sum(axis=1)
    return blocks.transpose(0, 4, 2, 3, 1, 5).reshape(2 * bands, 2, own, 2 * LANES)


def plain_scatter(modes, parts):
    lats, _, own, _ = modes.shape
    bands = lats // 2
    blocks = modes.reshape(bands, 2, 2, own, 2, LANES).transpose(0, 4, 2, 3, 1, 5)
    blocks = jnp.broadcast_to(blocks[:, None], (bands, parts // 2) + blocks.shape[1:])
    return blocks.reshape(bands * parts, 2 * own, 2 * LANES)


def mode_factors(first_order, own, lat_total, degree_gain):
    if own % 8 == 0 and own * lat_total == LANES and degree_gain.shape[0] % 8 == 0:
        return coupling(first_order[None], degree_gain, lat_total)
    orders = first_order + 2 * jnp.arange(own, dtype=jnp.int32)
    log_norm = jnp.take(log_norms(M), orders)
    return legendre_orders(grid_tables(lat_total)[0], orders, log_norm, degree_gain.shape[0])


def mode_stages(first_order, own, parts, factors, degree_gain, spec_weight):
    if factors.ndim == 4:
        chans = spec_weight.shape[0]
        shape = (factors.shape[0], 2 * own, chans)

        def forward(received):
            return call(
                functools.partial(forward_modes_kernel, parts),
                (kept(*shape), struct(*received.shape)),
                vmem(1) + hbm(2),
                [VMEM(shape, f32), VMEM(shape, f32), VMEM(factors.shape, f32)]
                + [VMEM(spec_weight.shape, f32), pltpu.SemaphoreType.DMA((2, 8))],
                us=2.0,
            )(received, factors, spec_weight)

        def backward(received, spectrum):
            return call(
                functools.partial(backward_modes_kernel, parts),
                struct(received.shape[0], 2 * own + chans // received.shape[0], chans),
                vmem(1) + hbm(3),
                [VMEM(shape, f32), VMEM(shape, f32), VMEM(factors.shape, f32)]
                + [VMEM(spec_weight.shape, f32), VMEM(shape, f32), pltpu.SemaphoreType.DMA((3, 8))],
                us=2.0,
            )(received, factors, spec_weight, spectrum)

        return forward, backward

    legendre, lat_total = factors, factors.shape[2]
    quad_weight = grid_tables(lat_total)[1]
    orders = first_order + 2 * jnp.arange(own, dtype=jnp.int32)
    order_weight = jnp.where(orders == 0, 1.0, 2.0).astype(f32)[None, None, :, None]
    quad_column = quad_weight[:, None, None, None]
    dot = functools.partial(jnp.einsum, precision=highest)

    def forward(received):
        spectrum = plain_gather(received, parts, own)
        mixed = dot("jpmc,cd->jpmd", spectrum, spec_weight) * quad_column
        degree = dot("lmj,jpmd->lpmd", legendre, mixed) * degree_gain[:, None, None, :]
        synthesis = dot("lmj,lpmd->jpmd", legendre, degree) * order_weight
        return spectrum, plain_scatter(synthesis, parts)

    def backward(received, spectrum):
        error = plain_gather(received, parts, own) * order_weight
        gained = dot("lmj,jpmd->lpmd", legendre, error) * degree_gain[:, None, None, :]
        back = dot("lmj,lpmd->jpmd", legendre, gained) * quad_column
        sent = plain_scatter(dot("jpmd,cd->jpmc", back, spec_weight), parts)
        weight_part = dot("jpmc,jpmd->cd", spectrum, back)
        shares = weight_part.reshape(sent.shape[0], -1, weight_part.shape[1])
        return jnp.concatenate([sent, shares], axis=1)

    return forward, backward


def filter_coefficients(filters, disco_weight, band_start, band_reach):
    coefficient = jnp.einsum("ikrt,kc->irtc", filters, disco_weight, precision=highest)
    window = jnp.arange(WIN, dtype=jnp.int32)
    coefficient = jnp.where(
        (window[None, :] < band_reach[:, None])[:, :, None, None], coefficient, 0.0
    )
    offset = jnp.arange(-HMAX, HMAX + 1, dtype=jnp.int32)
    lands = offset[None, :, None] == band_start[:, None, None] + window[None, None, :]
    by_offset = jnp.sum(
        jnp.where(lands[:, :, :, None, None], coefficient[:, None], 0.0), axis=2
    )
    coef = by_offset.reshape(filters.shape[0], SPAN * KLON, LANES)
    return jnp.pad(coef, ((0, 0), (0, TAPS - SPAN * KLON), (0, 0)))


def swap_parts(x, axis):
    return lax.all_to_all(x, axis, split_axis=0, concat_axis=0, tiled=True)


def after(first, *later):
    return lax.optimization_barrier((first, *later))


def body(
    grid_field, filters, disco_weight, band_start, band_reach, spec_weight, degree_gain, cotangent
):
    band_rows, lon_local, chans = grid_field.shape
    bands, parts = lax.axis_size("lat"), lax.axis_size("chan")
    devices = bands * parts
    lat_total, lon_total = band_rows * bands, lon_local * parts
    own, share = M // devices, chans // devices
    assert band_rows == HMAX and chans == 2 * LANES and parts == 4
    band, part = lax.axis_index("lat"), lax.axis_index("chan")
    me, half, part_index = band * parts + part, part % 2, part[None]
    both_axes = ("lat", "chan")
    high, low = wave_tables(lon_total, own)
    high_t, low_t = (jnp.asarray(np.ascontiguousarray(t.T)) for t in (high, low))
    high, low = jnp.asarray(high), jnp.asarray(low)
    up = [(i, i + 1) for i in range(bands - 1)]
    down = [(i + 1, i) for i in range(bands - 1)]

    def halo(x):
        return lax.ppermute(x, "lat", up), x, lax.ppermute(x, "lat", down)

    def part_swap(x, distance):
        return lax.ppermute(x, "chan", [(i, i ^ distance) for i in range(parts)])

    def half_of(x, which):
        return lax.dynamic_slice_in_dim(x, which * LANES, LANES, axis=2)

    def edges(x):
        return part_swap(jnp.concatenate([x[:, :8], x[:, -8:]], axis=1), 2)

    def exchange(modes):
        return swap_parts(modes.reshape(devices, -1, modes.shape[-1]), both_axes)

    outgoing, cotangent, degree_gain, disco_weight, band_start = after(
        half_of(grid_field, 1 - half), cotangent, degree_gain, disco_weight, band_start
    )
    field_other = part_swap(outgoing, 1)
    first_order = owned_orders(me, devices)
    factors = mode_factors(first_order, own, lat_total, degree_gain)
    cot_out = half_of(cotangent, 1 - half)
    field_other, factors, cot_out = after(field_other, factors, cot_out)
    modes, field = analyze(part_index, lon_total, grid_field, field_other, high, low)

    modes, field_sent, cot_out, disco_weight, band_start = after(
        modes, field, cot_out, disco_weight, band_start
    )
    mine = lax.dynamic_slice_in_dim(disco_weight, half * LANES, LANES, axis=1)
    coef = filter_coefficients(filters, mine, band_start, band_reach)
    rows = halo(field_sent)
    cot_others = [part_swap(cot_out[row : row + 1], 1) for row in range(band_rows)]
    received, edge, cot_others[0] = after(exchange(modes), edges(field_sent), cot_others[0])
    forward, backward = mode_stages(first_order, own, parts, factors, degree_gain, spec_weight)
    spectrum, synthesis = forward(received)

    local, adjoint = local_filter(*rows, *halo(jnp.concatenate([edge, coef], axis=1)))
    error_modes, out_own, *out_sends, error = grid_stage(
        part_index, exchange(synthesis), field, local, cotangent, cot_others,
        (high, low, high_t, low_t),
    )

    out_others = [part_swap(x, 1) for x in out_sends]
    rows = list(halo(error))
    received, edge, out_others[0], rows[0] = after(
        exchange(error_modes), edges(error), out_others[0], rows[0]
    )
    sent = backward(received, spectrum)
    base = adjoint_filter(part_index, *rows, *halo(edge), adjoint, cotangent, cot_others)
    received = exchange(sent)
    if own % 8 == 0:
        grad_send, grad_own, shares = final_stage(
            part_index, lon_total, 2 * own, received, base, high_t, low_t
        )
    else:
        grad_send, grad_own, _ = final_stage(
            part_index, lon_total, 2 * own, received[:, : 2 * own], base, high_t, low_t
        )
        shares = jnp.sum(received[:, 2 * own :], axis=0, keepdims=True)
        shares = jnp.broadcast_to(shares, (devices,) + shares.shape[1:])
    grad_send, *out_others = after(grad_send, *out_others)
    output, shares = after(join(part_index, out_own, *out_others), shares)
    grad_input = join(part_index, grad_own, part_swap(grad_send, 1))
    grad_weight = swap_parts(shares, both_axes).reshape(chans, chans)
    return (output, grad_input, grad_weight)


def solution(mesh):
    in_specs = (
        P("lat", "chan", None),
        P("lat", None, None, None),
        P(),
        P("lat"),
        P("lat"),
        P(),
        P(),
        P("lat", "chan", None),
    )
    out_specs = (P("lat", "chan", None), P("lat", "chan", None), P())
    return jax.shard_map(body, mesh=mesh, in_specs=in_specs, out_specs=out_specs, check_vma=False)
```

time: 192 us -> 151 us (0.79)
  blocking collectives: 50.6 us -> 0 us
  starting transfers between devices: 36.7 us -> 63.9 us
  waiting for transfers between devices: 60.3 us -> 43.8 us
  local copies, waits for them, and re-layouts: 11.2 us -> 4.96 us
  Pallas kernels: 30.1 us -> 36.2 us
    all_to_all x7 -> x5, waiting for transfers between devices: 60.3 us -> 6.1 us  [swap_parts(): return lax.all_to_all(x, axis, split_axis=0, concat_axis=0, tiled=True)]
    all_to_all x3 -> x0, blocking collectives: 50.6 us -> none  [swap_parts(): return lax.all_to_all(x, axis, split_axis=0, concat_axis=0, tiled=True)]
    ppermute x6 -> x16, waiting for transfers between devices: 0.02 us -> 37.7 us  [the longest x8 35.6 us: part_swap(): return lax.ppermute(x, 'chan', [(i, i ^ distance) for i in range(parts)])]
    ppermute x6 -> x16, starting transfers between devices: 13.9 us -> 31.5 us  [the longest x8 16.8 us: part_swap(): return lax.ppermute(x, 'chan', [(i, i ^ distance) for i in range(parts)])]
    all_to_all x7 -> x5, starting transfers between devices: 22.8 us -> 32.4 us  [swap_parts(): return lax.all_to_all(x, axis, split_axis=0, concat_axis=0, tiled=True)]
    unnamed x43 -> x31, local copies, waits for them, and re-layouts: 10.3 us -> 1.46 us
    pallas_call x12 -> x10, Pallas kernels: 30.1 us -> 36.2 us  [call(): run(*[held(x) if keep else x for x, keep in zip(args, keeps, strict=True)])]
    dynamic_slice x0 -> x2, local copies, waits for them, and re-layouts: none -> 2.03 us  [half_of(): return lax.dynamic_slice_in_dim(x, which * LANES, LANES, axis=2)]
  transfers between devices with their start and end apart: 13 -> 21, of which waited for: 7 -> 10; matrix products, arithmetic and copies ran while one was open for 1% -> 2% of each run, Pallas kernels for 11% -> 15%
where the time goes in v2:
time: 151 us; the launch traced here: 150 us
  starting transfers between devices  63.9 us (42%)
  waiting for transfers between devices  43.8 us (29%)
  Pallas kernels  36.2 us (24%)
  local copies, waits for them, and re-layouts  4.96 us (3%)
    pallas_call x10, Pallas kernels, call(): run(*[held(x) if keep else x for x, keep in zip(args, keeps, strict=True)])  36.2 us
    ppermute x8, waiting for transfers between devices, part_swap(): return lax.ppermute(x, 'chan', [(i, i ^ distance) for i in range(parts)])  35.6 us
    all_to_all x5, starting transfers between devices, swap_parts(): return lax.all_to_all(x, axis, split_axis=0, concat_axis=0, tiled=True)  32.4 us
    ppermute x8, starting transfers between devices, part_swap(): return lax.ppermute(x, 'chan', [(i, i ^ distance) for i in range(parts)])  16.8 us
    ppermute x8, starting transfers between devices, halo(): return (lax.ppermute(x, 'lat', up), x, lax.ppermute(x, 'lat', down))  14.7 us
    all_to_all x5, waiting for transfers between devices, swap_parts(): return lax.all_to_all(x, axis, split_axis=0, concat_axis=0, tiled=True)  6.1 us
  transfers between devices with their start and end apart: 21, of which 10 were waited for; matrix products, arithmetic and copies ran while one was open for 2% of the time, Pallas kernels for 15%

profile of v2, /device:TPU:0, one launch (start us, length us, event | category | flops | bytes accessed | tf_op | source)
XLA Modules:
  0.0 150.4 jit_solution(7192053442367778065)
XLA Ops:
  1.7 3.1 %collective-permute-start = (f32[2,360,128]{2,1,0:T(8,128)S(1)}, f32[2,360,128]{2,1,0:T(8,128)S(1)}, u32[]{:S(2)}, u32[]{:S(2)}) collective-permute-start(f32[2,360,128]{2,1,0:T(8,128)S(1)} %constant_dynamic-slice_fusion.1), channel_id=1, source_target_pairs={{0,1},{1,0},{2,3},{3,2},{4,5},{5,4},{6,7},{7,6},{8,9},{9,8},{10,11... | collective-permute-start | bytes 1105928 | tf_op jit(solution)/shard_map/ppermute | solution.py:823
  5.8 5.3 %shard_map.139.coupling_hbm = f32[16,16,8,256]{3,2,1,0:T(8,128)} custom-call(s32[1]{0:T(128)} %bitcast.1.first_ref, f32[360,256]{1,0:T(8,128)} %gain_ref), custom_call_target="tpu_custom_call" | custom-call | flops 6000000000 | bytes 18000000 | tf_op jit(solution)/shard_map/pallas_call | solution.py:98
  11.1 2.2 %collective-permute-done.other_ref = f32[2,360,128]{2,1,0:T(8,128)S(1)} collective-permute-done((f32[2,360,128]{2,1,0:T(8,128)S(1)}, f32[2,360,128]{2,1,0:T(8,128)S(1)}, u32[]{:S(2)}, u32[]{:S(2)}) %collective-permute-start) | collective-permute-done | bytes 368672 | tf_op jit(solution)/shard_map/ppermute | solution.py:823
  13.4 3.6 %shard_map.140 = (f32[512,256]{1,0:T(8,128)}, f32[2,720,128]{2,1,0:T(8,128)}) custom-call(s32[1]{0:T(128)} %bitcast.part_ref, f32[2,360,256]{2,1,0:T(8,128)} %own_hbm.1, f32[2,360,128]{2,1,0:T(8,128)S(1)} %collective-permute-done.other_ref, bf16[512,720]{1,0:T(8,128)(2,1)} %constant.66.clone.high_hbm, bf16[512,720]{1,0:T(8,128)(2,1)} %constant.67.clone.low_hbm), custom_call_target="tpu_custom_call" | custom-call | flops 3000000000 | bytes 9000000 | tf_op jit(solution)/shard_map/pallas_call | solution.py:98
  17.0 6.0 %all-to-all-start = ((f32[32,16,256]{2,1,0:T(8,128)}), f32[32,16,256]{2,1,0:T(8,128)S(1)}, u32[]{:S(2)}, u32[]{:S(2)}) async-start(f32[32,16,256]{2,1,0:T(8,128)} %bitcast.2), calls=%async_computation | async-start | bytes 1048576 | tf_op jit(solution)/shard_map/all_to_all | solution.py:794
  27.3 2.6 %collective-permute-start.1 = (f32[2,16,128]{2,1,0:T(8,128)S(1)}, f32[2,16,128]{2,1,0:T(8,128)S(1)}, u32[]{:S(2)}, u32[]{:S(2)}) collective-permute-start(f32[2,16,128]{2,1,0:T(8,128)S(1)} %pad_maximum_fusion), channel_id=1, source_target_pairs={{0,2},{1,3},{2,0},{3,1},{4,6},{5,7},{6,4},{7,5},{8,10},{9,11},{10,... | collective-permute-start | bytes 49160 | tf_op jit(solution)/shard_map/ppermute | solution.py:823
  31.7 7.0 %collective-permute-done.1 = f32[2,16,128]{2,1,0:T(8,128)S(1)} collective-permute-done((f32[2,16,128]{2,1,0:T(8,128)S(1)}, f32[2,16,128]{2,1,0:T(8,128)S(1)}, u32[]{:S(2)}, u32[]{:S(2)}) %collective-permute-start.1) | collective-permute-done | bytes 16416 | tf_op jit(solution)/shard_map/ppermute | solution.py:823
  39.5 2.8 %shard_map.141 = (f32[16,16,256]{2,1,0:T(8,128)}, f32[32,16,256]{2,1,0:T(8,128)}) custom-call(f32[32,16,256]{2,1,0:T(8,128)S(1)} %all-to-all-done.r_ref, f32[16,16,8,256]{3,2,1,0:T(8,128)} %shard_map.139.coupling_hbm, f32[256,256]{1,0:T(8,128)} %w_hbm.3), custom_call_target="tpu_custom_call" | custom-call | flops 2000000000 | bytes 6000000 | tf_op jit(solution)/shard_map/pallas_call | solution.py:98
  42.3 4.3 %all-to-all-start.1 = ((f32[32,16,256]{2,1,0:T(8,128)}), f32[32,16,256]{2,1,0:T(8,128)S(1)}, u32[]{:S(2)}, u32[]{:S(2)}) async-start(f32[32,16,256]{2,1,0:T(8,128)} %get-tuple-element.56), calls=%async_computation.1 | async-start | bytes 1048576 | tf_op jit(solution)/shard_map/all_to_all | solution.py:794
  53.3 4.0 %shard_map.142 = (f32[2,720,128]{2,1,0:T(8,128)}, f32[2,32,128]{2,1,0:T(8,128)}) custom-call(f32[2,720,128]{2,1,0:T(8,128)} %copy-done.6, f32[2,720,128]{2,1,0:T(8,128)} %get-tuple-element.52.own_ref.field_hbm, f32[2,720,128]{2,1,0:T(8,128)} %copy-done.7, f32[2,48,128]{2,1,0:T(8,128)S(1)} %collective-permute-done.5.lower_ref, ...), custom_call_target="tpu_custom_call" | custom-call | flops 4000000000 | bytes 12000000 | tf_op jit(solution)/shard_map/pallas_call | solution.py:98
  57.3 4.0 %collective-permute-done.7.second_hbm = f32[1,360,128]{2,1,0:T(8,128)S(1)} collective-permute-done((f32[1,360,128]{2,1,0:T(8,128)S(1)}, f32[1,360,128]{2,1,0:T(8,128)S(1)}, u32[]{:S(2)}, u32[]{:S(2)}) %collective-permute-start.7) | collective-permute-done | bytes 184352 | tf_op jit(solution)/shard_map/ppermute | solution.py:823
  62.0 5.4 %shard_map.143 = (f32[512,256]{1,0:T(8,128)}, f32[2,360,128]{2,1,0:T(8,128)}, f32[1,360,128]{2,1,0:T(8,128)}, f32[1,360,128]{2,1,0:T(8,128)}, f32[2,720,128]{2,1,0:T(8,128)}) custom-call(s32[1]{0:T(128)} %bitcast.part_ref, f32[32,16,256]{2,1,0:T(8,128)S(1)} %all-to-all-done.1.s_ref, f32[2,720,128]{2,1,0:T(8,128)} %get-tuple-element.52.own_ref.field_hbm, ...), custom_call_target="tpu_custom_call" | custom-call | flops 4000000000 | bytes 12000000 | tf_op jit(solution)/shard_map/pallas_call | solution.py:98
  67.4 5.4 %all-to-all-start.2 = ((f32[32,16,256]{2,1,0:T(8,128)}), f32[32,16,256]{2,1,0:T(8,128)S(1)}, u32[]{:S(2)}, u32[]{:S(2)}) async-start(f32[32,16,256]{2,1,0:T(8,128)} %bitcast.7), calls=%async_computation.2 | async-start | bytes 1048576 | tf_op jit(solution)/shard_map/all_to_all | solution.py:794
  72.8 2.2 %collective-permute-start.10 = (f32[2,720,128]{2,1,0:T(8,128)}, f32[2,720,128]{2,1,0:T(8,128)S(1)}, u32[]{:S(2)}, u32[]{:S(2)}) collective-permute-start(f32[2,720,128]{2,1,0:T(8,128)} %get-tuple-element.64.own_ref), channel_id=1, source_target_pairs={{0,4},{4,8},{8,12},{12,16},{16,20},{20,24},{24,28},{1,5},{5,9},{9,... | collective-permute-start | bytes 2211848 | tf_op jit(solution)/shard_map/ppermute | solution.py:820
  77.4 2.4 %collective-permute-start.8 = (f32[2,16,128]{2,1,0:T(8,128)S(1)}, f32[2,16,128]{2,1,0:T(8,128)S(1)}, u32[]{:S(2)}, u32[]{:S(2)}) collective-permute-start(f32[2,16,128]{2,1,0:T(8,128)S(1)} %pad_maximum_fusion.1), channel_id=1, source_target_pairs={{0,2},{1,3},{2,0},{3,1},{4,6},{5,7},{6,4},{7,5},{8,10},{9,11},{10,... | collective-permute-start | bytes 49160 | tf_op jit(solution)/shard_map/ppermute | solution.py:823
  79.8 8.3 %collective-permute-done.8.middle_ref = f32[2,16,128]{2,1,0:T(8,128)S(1)} collective-permute-done((f32[2,16,128]{2,1,0:T(8,128)S(1)}, f32[2,16,128]{2,1,0:T(8,128)S(1)}, u32[]{:S(2)}, u32[]{:S(2)}) %collective-permute-start.8) | collective-permute-done | bytes 16416 | tf_op jit(solution)/shard_map/ppermute | solution.py:823
  88.4 3.8 %shard_map.144 = f32[32,24,256]{2,1,0:T(8,128)} custom-call(f32[32,16,256]{2,1,0:T(8,128)S(1)} %all-to-all-done.2.r_ref, f32[16,16,8,256]{3,2,1,0:T(8,128)} %shard_map.139.coupling_hbm, f32[256,256]{1,0:T(8,128)} %w_hbm.3, f32[16,16,256]{2,1,0:T(8,128)} %get-tuple-element.67.x_hbm), custom_call_target="tpu_custom_call" | custom-call | flops 2000000000 | bytes 6000000 | tf_op jit(solution)/shard_map/pallas_call | solution.py:98
  92.2 5.7 %all-to-all-start.3 = ((f32[32,24,256]{2,1,0:T(8,128)}), f32[32,24,256]{2,1,0:T(8,128)S(1)}, u32[]{:S(2)}, u32[]{:S(2)}) async-start(f32[32,24,256]{2,1,0:T(8,128)} %shard_map.144), calls=%async_computation.3 | async-start | bytes 1572864 | tf_op jit(solution)/shard_map/all_to_all | solution.py:794
  99.3 3.0 %collective-permute-start.12 = (f32[2,16,128]{2,1,0:T(8,128)S(1)}, f32[2,16,128]{2,1,0:T(8,128)S(1)}, u32[]{:S(2)}, u32[]{:S(2)}) collective-permute-start(f32[2,16,128]{2,1,0:T(8,128)S(1)} %collective-permute-done.8.middle_ref), channel_id=1, source_target_pairs={{0,4},{4,8},{8,12},{12,16},{16,20},{20,24},{24,28},{1,5},{5,9},{9,... | collective-permute-start | bytes 49160 | tf_op jit(solution)/shard_map/ppermute | solution.py:820
  106.4 5.1 %shard_map.145.base_hbm = f32[2,720,128]{2,1,0:T(8,128)} custom-call(s32[1]{0:T(128)} %bitcast.part_ref, f32[2,720,128]{2,1,0:T(8,128)} %copy-done.8, f32[2,720,128]{2,1,0:T(8,128)} %get-tuple-element.64.own_ref, f32[2,720,128]{2,1,0:T(8,128)} %copy-done.9, f32[2,16,128]{2,1,0:T(8,128)S(1)} %collective-permute-done.12.lower_ref, ...), custom_call_target="tpu_custom_call" | custom-call | flops 4000000000 | bytes 12000000 | tf_op jit(solution)/shard_map/pallas_call | solution.py:98
  111.5 6.1 %all-to-all-done.3.s_ref = f32[32,24,256]{2,1,0:T(8,128)S(1)} async-done(((f32[32,24,256]{2,1,0:T(8,128)}), f32[32,24,256]{2,1,0:T(8,128)S(1)}, u32[]{:S(2)}, u32[]{:S(2)}) %all-to-all-start.3) | async-done | bytes 786464 | tf_op jit(solution)/shard_map/all_to_all | solution.py:794
  117.6 4.1 %shard_map.146 = (f32[2,360,128]{2,1,0:T(8,128)S(1)}, f32[2,360,128]{2,1,0:T(8,128)}, f32[32,8,256]{2,1,0:T(8,128)}) custom-call(s32[1]{0:T(128)} %bitcast.part_ref, f32[32,24,256]{2,1,0:T(8,128)S(1)} %all-to-all-done.3.s_ref, f32[2,720,128]{2,1,0:T(8,128)} %shard_map.145.base_hbm, bf16[720,512]{1,0:T(8,128)(2,1)} %constant.64.clone.thigh_hbm, ...), custom_call_target="tpu_custom_call" | custom-call | flops 3000000000 | bytes 9000000 | tf_op jit(solution)/shard_map/pallas_call | solution.py:98
  122.8 11.0 %all-to-all-start.4 = ((f32[32,8,256]{2,1,0:T(8,128)}), f32[32,8,256]{2,1,0:T(8,128)S(1)}, u32[]{:S(2)}, u32[]{:S(2)}) async-start(f32[32,8,256]{2,1,0:T(8,128)} %get-tuple-element.80), calls=%async_computation.4 | async-start | bytes 524288 | tf_op jit(solution)/shard_map/all_to_all | solution.py:794
  135.6 13.1 %collective-permute-done.15.refs_0_ = f32[2,360,128]{2,1,0:T(8,128)S(1)} collective-permute-done((f32[2,360,128]{2,1,0:T(8,128)S(1)}, f32[2,360,128]{2,1,0:T(8,128)S(1)}, u32[]{:S(2)}, u32[]{:S(2)}) %collective-permute-start.15) | collective-permute-done | bytes 368672 | tf_op jit(solution)/shard_map/ppermute | solution.py:823
  (75 shorter events, 28.8 us)
Async XLA Ops:
  0.6 30.9 %copy-start = (f32[2,4,3,5]{3,1,2,0:T(4,128)S(1)}, f32[2,4,3,5]{3,1,2,0:T(4,128)}, u32[]{:S(2)}) copy-start(f32[2,4,3,5]{3,1,2,0:T(4,128)} %param.13) | copy-start | bytes 1444
  1.7 11.7 %collective-permute-start = (f32[2,360,128]{2,1,0:T(8,128)S(1)}, f32[2,360,128]{2,1,0:T(8,128)S(1)}, u32[]{:S(2)}, u32[]{:S(2)}) collective-permute-start(f32[2,360,128]{2,1,0:T(8,128)S(1)} %constant_dynamic-slice_fusion.1), channel_id=1, source_target_pairs={{0,1},{1,0},{2,3},{3,2},{4,5},{5,4},{6,7},{7,6},{8,9},{9,8},{10,11... | collective-permute-start | bytes 1105928 | tf_op jit(solution)/shard_map/ppermute | solution.py:823
  13.4 18.1 %copy-start.13 = (f32[4,256]{1,0:T(4,128)S(1)}, f32[4,256]{1,0:T(4,128)}, u32[]{:S(2)}) copy-start(f32[4,256]{1,0:T(4,128)} %param.14) | copy-start | bytes 12292
  17.0 22.5 %all-to-all-start = ((f32[32,16,256]{2,1,0:T(8,128)}), f32[32,16,256]{2,1,0:T(8,128)S(1)}, u32[]{:S(2)}, u32[]{:S(2)}) async-start(f32[32,16,256]{2,1,0:T(8,128)} %bitcast.2), calls=%async_computation | async-start | bytes 1048576 | tf_op jit(solution)/shard_map/all_to_all | solution.py:794
  23.1 29.0 %collective-permute-start.3 = (f32[2,720,128]{2,1,0:T(8,128)}, f32[2,720,128]{2,1,0:T(8,128)S(1)}, u32[]{:S(2)}, u32[]{:S(2)}) collective-permute-start(f32[2,720,128]{2,1,0:T(8,128)} %get-tuple-element.52.own_ref.field_hbm), channel_id=1, source_target_pairs={{0,4},{4,8},{8,12},{12,16},{16,20},{20,24},{24,28},{1,5},{5,9},{9,... | collective-permute-start | bytes 2211848 | tf_op jit(solution)/shard_map/ppermute | solution.py:820
  25.3 26.8 %collective-permute-start.4 = (f32[2,720,128]{2,1,0:T(8,128)}, f32[2,720,128]{2,1,0:T(8,128)S(1)}, u32[]{:S(2)}, u32[]{:S(2)}) collective-permute-start(f32[2,720,128]{2,1,0:T(8,128)} %get-tuple-element.52.own_ref.field_hbm), channel_id=1, source_target_pairs={{4,0},{8,4},{12,8},{16,12},{20,16},{24,20},{28,24},{5,1},{9,5},{13... | collective-permute-start | bytes 2211848 | tf_op jit(solution)/shard_map/ppermute | solution.py:820
  27.3 11.4 %collective-permute-start.1 = (f32[2,16,128]{2,1,0:T(8,128)S(1)}, f32[2,16,128]{2,1,0:T(8,128)S(1)}, u32[]{:S(2)}, u32[]{:S(2)}) collective-permute-start(f32[2,16,128]{2,1,0:T(8,128)S(1)} %pad_maximum_fusion), channel_id=1, source_target_pairs={{0,2},{1,3},{2,0},{3,1},{4,6},{5,7},{6,4},{7,5},{8,10},{9,11},{10,... | collective-permute-start | bytes 49160 | tf_op jit(solution)/shard_map/ppermute | solution.py:823
  29.9 9.6 %collective-permute-start.2 = (f32[1,360,128]{2,1,0:T(8,128)S(1)}, f32[1,360,128]{2,1,0:T(8,128)S(1)}, u32[]{:S(2)}, u32[]{:S(2)}) collective-permute-start(f32[1,360,128]{2,1,0:T(8,128)S(1)} %get-tuple-element.86), channel_id=1, source_target_pairs={{0,1},{1,0},{2,3},{3,2},{4,5},{5,4},{6,7},{7,6},{8,9},{9,8},{10,11... | collective-permute-start | bytes 552968 | tf_op jit(solution)/shard_map/ppermute | solution.py:823
  42.3 18.9 %all-to-all-start.1 = ((f32[32,16,256]{2,1,0:T(8,128)}), f32[32,16,256]{2,1,0:T(8,128)S(1)}, u32[]{:S(2)}, u32[]{:S(2)}) async-start(f32[32,16,256]{2,1,0:T(8,128)} %get-tuple-element.56), calls=%async_computation.1 | async-start | bytes 1048576 | tf_op jit(solution)/shard_map/all_to_all | solution.py:794
  46.9 5.2 %collective-permute-start.5 = (f32[2,48,128]{2,1,0:T(8,128)S(1)}, f32[2,48,128]{2,1,0:T(8,128)S(1)}, u32[]{:S(2)}, u32[]{:S(2)}) collective-permute-start(f32[2,48,128]{2,1,0:T(8,128)S(1)} %select_maximum_fusion.middle_ref), channel_id=1, source_target_pairs={{0,4},{4,8},{8,12},{12,16},{16,20},{20,24},{24,28},{1,5},{5,9},{9,... | collective-permute-start | bytes 147464 | tf_op jit(solution)/shard_map/ppermute | solution.py:820
  49.0 4.3 %collective-permute-start.6 = (f32[2,48,128]{2,1,0:T(8,128)S(1)}, f32[2,48,128]{2,1,0:T(8,128)S(1)}, u32[]{:S(2)}, u32[]{:S(2)}) collective-permute-start(f32[2,48,128]{2,1,0:T(8,128)S(1)} %select_maximum_fusion.middle_ref), channel_id=1, source_target_pairs={{4,0},{8,4},{12,8},{16,12},{20,16},{24,20},{28,24},{5,1},{9,5},{13... | collective-permute-start | bytes 147464 | tf_op jit(solution)/shard_map/ppermute | solution.py:820
  50.3 10.9 %collective-permute-start.7 = (f32[1,360,128]{2,1,0:T(8,128)S(1)}, f32[1,360,128]{2,1,0:T(8,128)S(1)}, u32[]{:S(2)}, u32[]{:S(2)}) collective-permute-start(f32[1,360,128]{2,1,0:T(8,128)S(1)} %get-tuple-element.85), channel_id=1, source_target_pairs={{0,1},{1,0},{2,3},{3,2},{4,5},{5,4},{6,7},{7,6},{8,9},{9,8},{10,11... | collective-permute-start | bytes 552968 | tf_op jit(solution)/shard_map/ppermute | solution.py:823
  67.4 21.0 %all-to-all-start.2 = ((f32[32,16,256]{2,1,0:T(8,128)}), f32[32,16,256]{2,1,0:T(8,128)S(1)}, u32[]{:S(2)}, u32[]{:S(2)}) async-start(f32[32,16,256]{2,1,0:T(8,128)} %bitcast.7), calls=%async_computation.2 | async-start | bytes 1048576 | tf_op jit(solution)/shard_map/all_to_all | solution.py:794
  72.8 15.6 %collective-permute-start.10 = (f32[2,720,128]{2,1,0:T(8,128)}, f32[2,720,128]{2,1,0:T(8,128)S(1)}, u32[]{:S(2)}, u32[]{:S(2)}) collective-permute-start(f32[2,720,128]{2,1,0:T(8,128)} %get-tuple-element.64.own_ref), channel_id=1, source_target_pairs={{0,4},{4,8},{8,12},{12,16},{16,20},{20,24},{24,28},{1,5},{5,9},{9,... | collective-permute-start | bytes 2211848 | tf_op jit(solution)/shard_map/ppermute | solution.py:820
  75.0 13.4 %collective-permute-start.9 = (f32[1,360,128]{2,1,0:T(8,128)}, f32[1,360,128]{2,1,0:T(8,128)S(1)}, u32[]{:S(2)}, u32[]{:S(2)}) collective-permute-start(f32[1,360,128]{2,1,0:T(8,128)} %get-tuple-element.65), channel_id=1, source_target_pairs={{0,1},{1,0},{2,3},{3,2},{4,5},{5,4},{6,7},{7,6},{8,9},{9,8},{10,11... | collective-permute-start | bytes 552968 | tf_op jit(solution)/shard_map/ppermute | solution.py:823
  77.4 10.7 %collective-permute-start.8 = (f32[2,16,128]{2,1,0:T(8,128)S(1)}, f32[2,16,128]{2,1,0:T(8,128)S(1)}, u32[]{:S(2)}, u32[]{:S(2)}) collective-permute-start(f32[2,16,128]{2,1,0:T(8,128)S(1)} %pad_maximum_fusion.1), channel_id=1, source_target_pairs={{0,2},{1,3},{2,0},{3,1},{4,6},{5,7},{6,4},{7,5},{8,10},{9,11},{10,... | collective-permute-start | bytes 49160 | tf_op jit(solution)/shard_map/ppermute | solution.py:823
  92.2 25.4 %all-to-all-start.3 = ((f32[32,24,256]{2,1,0:T(8,128)}), f32[32,24,256]{2,1,0:T(8,128)S(1)}, u32[]{:S(2)}, u32[]{:S(2)}) async-start(f32[32,24,256]{2,1,0:T(8,128)} %shard_map.144), calls=%async_computation.3 | async-start | bytes 1572864 | tf_op jit(solution)/shard_map/all_to_all | solution.py:794
  98.0 7.5 %collective-permute-start.11 = (f32[2,720,128]{2,1,0:T(8,128)S(1)}, f32[2,720,128]{2,1,0:T(8,128)S(1)}, u32[]{:S(2)}, u32[]{:S(2)}) collective-permute-start(f32[2,720,128]{2,1,0:T(8,128)S(1)} %copy-done.5), channel_id=1, source_target_pairs={{4,0},{8,4},{12,8},{16,12},{20,16},{24,20},{28,24},{5,1},{9,5},{13... | collective-permute-start | bytes 2211848 | tf_op jit(solution)/shard_map/ppermute | solution.py:820
  99.3 6.2 %collective-permute-start.12 = (f32[2,16,128]{2,1,0:T(8,128)S(1)}, f32[2,16,128]{2,1,0:T(8,128)S(1)}, u32[]{:S(2)}, u32[]{:S(2)}) collective-permute-start(f32[2,16,128]{2,1,0:T(8,128)S(1)} %collective-permute-done.8.middle_ref), channel_id=1, source_target_pairs={{0,4},{4,8},{8,12},{12,16},{16,20},{20,24},{24,28},{1,5},{5,9},{9,... | collective-permute-start | bytes 49160 | tf_op jit(solution)/shard_map/ppermute | solution.py:820
  102.3 4.1 %collective-permute-start.13 = (f32[2,16,128]{2,1,0:T(8,128)S(1)}, f32[2,16,128]{2,1,0:T(8,128)S(1)}, u32[]{:S(2)}, u32[]{:S(2)}) collective-permute-start(f32[2,16,128]{2,1,0:T(8,128)S(1)} %collective-permute-done.8.middle_ref), channel_id=1, source_target_pairs={{4,0},{8,4},{12,8},{16,12},{20,16},{24,20},{28,24},{5,1},{9,5},{13... | collective-permute-start | bytes 49160 | tf_op jit(solution)/shard_map/ppermute | solution.py:820
  103.6 18.1 %collective-permute-start.14 = (f32[1,360,128]{2,1,0:T(8,128)S(1)}, f32[1,360,128]{2,1,0:T(8,128)S(1)}, u32[]{:S(2)}, u32[]{:S(2)}) collective-permute-start(f32[1,360,128]{2,1,0:T(8,128)S(1)} %copy-done.12), channel_id=1, source_target_pairs={{0,1},{1,0},{2,3},{3,2},{4,5},{5,4},{6,7},{7,6},{8,9},{9,8},{10,11... | collective-permute-start | bytes 552968 | tf_op jit(solution)/shard_map/ppermute | solution.py:823
  121.8 27.0 %copy-start.2 = (f32[2,360,128]{2,1,0:T(8,128)S(1)}, f32[2,360,128]{2,1,0:T(8,128)}, u32[]{:S(2)}) copy-start(f32[2,360,128]{2,1,0:T(8,128)} %get-tuple-element.78.own_ref) | copy-start | bytes 1105924
  122.8 27.0 %all-to-all-start.4 = ((f32[32,8,256]{2,1,0:T(8,128)}), f32[32,8,256]{2,1,0:T(8,128)S(1)}, u32[]{:S(2)}, u32[]{:S(2)}) async-start(f32[32,8,256]{2,1,0:T(8,128)} %get-tuple-element.80), calls=%async_computation.4 | async-start | bytes 524288 | tf_op jit(solution)/shard_map/all_to_all | solution.py:794
  133.7 15.0 %collective-permute-start.15 = (f32[2,360,128]{2,1,0:T(8,128)S(1)}, f32[2,360,128]{2,1,0:T(8,128)S(1)}, u32[]{:S(2)}, u32[]{:S(2)}) collective-permute-start(f32[2,360,128]{2,1,0:T(8,128)S(1)} %get-tuple-element.79), channel_id=1, source_target_pairs={{0,1},{1,0},{2,3},{3,2},{4,5},{5,4},{6,7},{7,6},{8,9},{9,8},{10,11... | collective-permute-start | bytes 1105928 | tf_op jit(solution)/shard_map/ppermute | solution.py:823
  (12 other events, 88.5 us)

commit v3 on v2

--- a/solution.py
+++ b/solution.py
@@ -44,6 +44,12 @@
     return high, low
 
 
+def half_tables(table, depth):
+    rows, lons = table.shape
+    blocks = table.reshape(rows, 2, lons // 2).transpose(1, 0, 2)
+    return np.pad(blocks, ((0, 0), (0, 0), (0, depth - lons // 2)))
+
+
 def owned_orders(owner, devices):
     half = devices // 2
     return owner % half * (2 * (M // devices)) + owner // half
@@ -81,7 +87,7 @@
     return pl.CostEstimate(flops=int(us * 1e9), bytes_accessed=int(us * 3e6), transcendentals=0)
 
 
-def call(kernel, out_shape, in_specs, scratch=(), us=1.0, limit=16, out_spaces=None):
+def call(kernel, out_shape, in_specs, scratch=(), us=1.0, limit=16, out_spaces=None, aliases=None):
     run = pl.pallas_call(
         kernel,
         out_shape=out_shape,
@@ -91,6 +97,7 @@
             out_spaces or jax.tree.map(lambda _: VMEM, out_shape),
         ),
         scratch_shapes=list(scratch),
+        input_output_aliases=aliases or {},
         compiler_params=pltpu.CompilerParams(vmem_limit_bytes=limit * MIB),
         cost_estimate=cost(us),
     )
@@ -338,50 +345,88 @@
     )(part, synthesis, field, local, cotangent, *others, *tables)
 
 
-def final_kernel(scale, rows_own, part_ref, s_ref, base_hbm, thigh_hbm, tlow_hbm,
-                 send_ref, own_ref, share_ref, base_ref, thigh_ref, tlow_ref, sems, base_sem):
+def final_kernel(scale, rows_own, theirs, part_ref, s_ref, base_hbm, thigh_hbm, tlow_hbm,
+                 *refs):
+    o_ref, base_ref, thigh_ref, tlow_ref, sems, base_sem = refs[-6:]
+    out_hbm = refs[0]
     part = part_ref[0]
-    half = own_half(part)
-    wait = fetches((thigh_hbm, tlow_hbm), (thigh_ref, tlow_ref), sems, 3)
-    base_copy = pltpu.make_async_copy(base_hbm, base_ref, base_sem)
+    half = 1 - own_half(part) if theirs else own_half(part)
+    wait = fetches((thigh_hbm.at[half], tlow_hbm.at[half]), (thigh_ref, tlow_ref), sems, 3)
+    base_copy = pltpu.make_async_copy(lon_half(base_hbm, half), base_ref, base_sem)
     base_copy.start()
-    if rows_own < s_ref.shape[1]:
-        share = jnp.sum(s_ref[:, pl.ds(rows_own, share_ref.shape[1]), :], axis=0)
-        share_ref[...] = jnp.broadcast_to(share[None], share_ref.shape)
     modes = s_ref[:, pl.ds(0, rows_own), :].reshape(thigh_ref.shape[1], s_ref.shape[2])
-    base_copy.wait()
+    total = o_ref.shape[1]
 
     def store(lons, value):
+        count = min(lons.size, total - lons.start)
         for row in range(base_ref.shape[0]):
             lanes = slice(row * LANES, (row + 1) * LANES)
-            base_ref[row, lons, :] = base_ref[row, lons, :] + scale * value[:, lanes]
+            o_ref[row, pl.ds(lons.start, count), :] = scale * value[:count, lanes]
 
     compose_rows(modes, turn_sign(part), thigh_ref, tlow_ref, wait, store)
-    own_ref[...] = lon_half(base_ref, half)[...]
-    send_ref[...] = lon_half(base_ref, 1 - half)[...]
-
-
-def final_stage(part, lon_total, rows_own, modes, base, high_t, low_t):
+    base_copy.wait()
+    o_ref[...] = o_ref[...] + base_ref[...]
+    if not theirs:
+        out = pltpu.make_async_copy(o_ref, lane_half(out_hbm, half), base_sem)
+        out.start()
+        out.wait()
+
+
+def final_stage(part, lon_total, rows_own, modes, base, high_t, low_t, theirs):
     rows, lons, _ = base.shape
     block = (rows, lons // 2, LANES)
+    table = high_t.shape[1:]
     return call(
-        functools.partial(final_kernel, 1.0 / lon_total, rows_own),
-        (
-            struct(*block),
-            kept(*block),
-            struct(modes.shape[0], max(modes.shape[1] - rows_own, 8), modes.shape[2]),
-        ),
+        functools.partial(final_kernel, 1.0 / lon_total, rows_own, theirs),
+        struct(*block) if theirs else kept(rows, lons // 2, 2 * LANES),
         [smem] + vmem(1) + hbm(3),
-        [VMEM(base.shape, f32), VMEM(high_t.shape, bf16), VMEM(high_t.shape, bf16)]
+        [VMEM(block, f32)] * (1 if theirs else 2)
+        + [VMEM(table, bf16), VMEM(table, bf16)]
         + [pltpu.SemaphoreType.DMA((2, 3)), pltpu.SemaphoreType.DMA],
-        us=3.0,
+        us=2.0,
+        out_spaces=VMEM if theirs else pltpu.HBM,
     )(part, modes, base, high_t, low_t)
 
 
-def filter_sums(prev_ref, own_ref, next_ref, edge_refs, coef_ref, finish, sums_ref):
-    lons = own_ref.shape[1]
+def close_kernel(part_ref, held_hbm, other_ref, weight_ref, o_hbm, weight_hbm, sems):
+    del held_hbm
+    copies = (
+        pltpu.make_async_copy(other_ref, lane_half(o_hbm, 1 - own_half(part_ref[0])), sems.at[0]),
+        pltpu.make_async_copy(weight_ref, weight_hbm, sems.at[1]),
+    )
+    for copy in copies:
+        copy.start()
+    for copy in copies:
+        copy.wait()
+
+
+def close(part, held_half, other, weight):
+    return call(
+        close_kernel,
+        (kept(*held_half.shape), kept(*weight.shape)),
+        [smem] + hbm(1) + vmem(2),
+        [pltpu.SemaphoreType.DMA((2,))],
+        out_spaces=(pltpu.HBM, pltpu.HBM),
+        aliases={1: 0},
+    )(part, held_half, other, weight)
+
+
+def shares_kernel(first, r_ref, o_ref):
+    share = jnp.sum(r_ref[:, pl.ds(first, o_ref.shape[1]), :], axis=0)
+    o_ref[...] = jnp.broadcast_to(share[None], o_ref.shape)
+
+
+def spread_shares(received, first):
+    devices, rows, chans = received.shape
+    return call(
+        functools.partial(shares_kernel, first), struct(devices, rows - first, chans), vmem(1)
+    )(received)
+
+
+def filter_sums(refs, edge_refs, coef_ref, finish, sums_ref):
+    lons = refs[0].shape[1]
     tile = lons // 18
-    sources = [(x_ref, row) for x_ref in (prev_ref, own_ref, next_ref) for row in range(2)]
+    sources = [(x_ref, row) for x_ref in refs for row in range(x_ref.shape[0])]
     for row in range(2):
         def add(values, rows, row=row):
             for tap in range(KLON):
@@ -417,7 +462,7 @@
     taps = pl.ds(EDGES, TAPS)
     coef_refs = [ref.at[:, taps] for ref in (lower_ref, middle_ref, upper_ref)]
     filter_sums(
-        prev_ref, own_ref, next_ref, (lower_ref, middle_ref, upper_ref), coef_refs[1], finish, sums_ref
+        (prev_ref, own_ref, next_ref), (lower_ref, middle_ref, upper_ref), coef_refs[1], finish, sums_ref
     )
     adjoint_ref[...] = jnp.zeros_like(adjoint_ref)
     sources = [(c_ref, row) for c_ref in coef_refs for row in range(2)]
@@ -429,7 +474,7 @@
                 adjoint_ref[row, pl.ds(offset * KLON + tap, 1), :] = c_ref[k, pl.ds(mirrored, 1), :]
 
 
-def adjoint_kernel(part_ref, prev_ref, own_ref, next_ref, lower_ref, middle_ref, upper_ref, coef_ref,
+def adjoint_kernel(part_ref, first_ref, second_ref, own_ref, next_ref, lower_ref, middle_ref, upper_ref, coef_ref,
                    cot_hbm, first_hbm, second_hbm,
                    o_ref, sums_ref, cot_ref, cot_sems):
     copies = pair_copies(
@@ -441,7 +486,8 @@
     def finish(row, lons, value):
         o_ref[row, lons, :] = cot_ref[row, lons, :] + value
 
-    filter_sums(prev_ref, own_ref, next_ref, (lower_ref, middle_ref, upper_ref), coef_ref, finish, sums_ref)
+    edge_refs = (lower_ref, middle_ref, upper_ref)
+    filter_sums((first_ref, second_ref, own_ref, next_ref), edge_refs, coef_ref, finish, sums_ref)
 
 
 def local_filter(prev, own, behind, *edges):
@@ -454,15 +500,15 @@
     )(prev, own, behind, *edges)
 
 
-def adjoint_filter(part, prev, own, behind, lower, middle, upper, coef, cotangent, others):
+def adjoint_filter(part, first, second, own, behind, lower, middle, upper, coef, cotangent, others):
     return call(
         adjoint_kernel,
         kept(*own.shape),
-        [smem] + loaded(3) + vmem(4) + hbm(3),
+        [smem] + loaded(4) + vmem(4) + hbm(3),
         [VMEM((KLON, own.shape[1] + 16, LANES), f32), VMEM(own.shape, f32)]
         + [pltpu.SemaphoreType.DMA((3,))],
         us=4.0,
-    )(part, prev, own, behind, lower, middle, upper, coef, cotangent, *others)
+    )(part, first, second, own, behind, lower, middle, upper, coef, cotangent, *others)
 
 
 def coupling_kernel(lat_total, first_ref, gain_ref, o_hbm, step_ref, back_ref, start_ref, leg_ref,
@@ -626,8 +672,8 @@
     scatter_modes(lambda j, lanes: z_ref[j, :, lanes], s_ref, parts, rows)
 
 
-def backward_modes_kernel(parts, r_ref, coupling_hbm, w_hbm, x_hbm, s_ref, e_ref, v_ref,
-                          coupling_ref, w_ref, x_ref, sems):
+def backward_modes_kernel(parts, r_ref, coupling_hbm, w_hbm, x_hbm, s_hbm, s_ref, e_ref, v_ref,
+                          coupling_ref, w_ref, x_ref, sems, out_sems):
     wait = fetches((coupling_hbm,), (coupling_ref,), sems.at[pl.ds(0, 1)], 8)
     wait_rest = fetches((w_hbm, x_hbm), (w_ref, x_ref), sems.at[pl.ds(1, 2)], 2)
 
@@ -656,9 +702,19 @@
     v = v_ref[...].reshape(lats * rows, chans)
     e_ref[...] = dot_split(v, w_ref[...], ((1,), (1,))).reshape(lats, rows, chans)
     scatter_modes(lambda j, lanes: e_ref[j, :, lanes], s_ref, parts, rows)
+    sent = pltpu.make_async_copy(
+        s_ref.at[:, pl.ds(0, rows), :], s_hbm.at[:, pl.ds(0, rows), :], out_sems.at[0]
+    )
+    sent.start()
     weight_part = dot_split(x_ref[...].reshape(lats * rows, chans), v, ((0,), (0,)))
     share = chans // s_ref.shape[0]
     s_ref[:, pl.ds(rows, share), :] = weight_part.reshape(s_ref.shape[0], share, chans)
+    shares = pltpu.make_async_copy(
+        s_ref.at[:, pl.ds(rows, share), :], s_hbm.at[:, pl.ds(rows, share), :], out_sems.at[1]
+    )
+    shares.start()
+    sent.wait()
+    shares.wait()
 
 
 def legendre_orders(colatitude, orders, log_norm, degree_count):
@@ -738,13 +794,16 @@
             )(received, factors, spec_weight)
 
         def backward(received, spectrum):
+            sent = (received.shape[0], 2 * own + chans // received.shape[0], chans)
             return call(
                 functools.partial(backward_modes_kernel, parts),
-                struct(received.shape[0], 2 * own + chans // received.shape[0], chans),
+                kept(*sent),
                 vmem(1) + hbm(3),
-                [VMEM(shape, f32), VMEM(shape, f32), VMEM(factors.shape, f32)]
-                + [VMEM(spec_weight.shape, f32), VMEM(shape, f32), pltpu.SemaphoreType.DMA((3, 8))],
+                [VMEM(sent, f32), VMEM(shape, f32), VMEM(shape, f32), VMEM(factors.shape, f32)]
+                + [VMEM(spec_weight.shape, f32), VMEM(shape, f32)]
+                + [pltpu.SemaphoreType.DMA((3, 8)), pltpu.SemaphoreType.DMA((2,))],
                 us=2.0,
+                out_spaces=pltpu.HBM,
             )(received, factors, spec_weight, spectrum)
 
         return forward, backward
@@ -811,6 +870,11 @@
     me, half, part_index = band * parts + part, part % 2, part[None]
     both_axes = ("lat", "chan")
     high, low = wave_tables(lon_total, own)
+    depth = (lon_local + LANES - 1) // LANES * LANES
+    apart_t = [
+        jnp.asarray(np.ascontiguousarray(half_tables(table, depth).transpose(0, 2, 1)))
+        for table in (high, low)
+    ]
     high_t, low_t = (jnp.asarray(np.ascontiguousarray(t.T)) for t in (high, low))
     high, low = jnp.asarray(high), jnp.asarray(low)
     up = [(i, i + 1) for i in range(bands - 1)]
@@ -841,16 +905,17 @@
     field_other, factors, cot_out = after(field_other, factors, cot_out)
     modes, field = analyze(part_index, lon_total, grid_field, field_other, high, low)
 
-    modes, field_sent, cot_out, disco_weight, band_start = after(
-        modes, field, cot_out, disco_weight, band_start
+    cot_others = [part_swap(cot_out[:1], 1)]
+    modes, field_sent, cot_others[0], cot_out, disco_weight, band_start = after(
+        modes, field, cot_others[0], cot_out, disco_weight, band_start
     )
     mine = lax.dynamic_slice_in_dim(disco_weight, half * LANES, LANES, axis=1)
     coef = filter_coefficients(filters, mine, band_start, band_reach)
     rows = halo(field_sent)
-    cot_others = [part_swap(cot_out[row : row + 1], 1) for row in range(band_rows)]
-    received, edge, cot_others[0] = after(exchange(modes), edges(field_sent), cot_others[0])
+    cot_others.append(part_swap(cot_out[1:], 1))
     forward, backward = mode_stages(first_order, own, parts, factors, degree_gain, spec_weight)
-    spectrum, synthesis = forward(received)
+    spectrum, synthesis = forward(exchange(modes))
+    synthesis, edge, cot_others[1] = after(synthesis, edges(field_sent), cot_others[1])
 
     local, adjoint = local_filter(*rows, *halo(jnp.concatenate([edge, coef], axis=1)))
     error_modes, out_own, *out_sends, error = grid_stage(
@@ -859,27 +924,28 @@
     )
 
     out_others = [part_swap(x, 1) for x in out_sends]
-    rows = list(halo(error))
-    received, edge, out_others[0], rows[0] = after(
-        exchange(error_modes), edges(error), out_others[0], rows[0]
-    )
-    sent = backward(received, spectrum)
+    rows = [lax.ppermute(error[row : row + 1], "lat", up) for row in range(band_rows)]
+    rows += [error, lax.ppermute(error, "lat", down)]
+    sent = backward(exchange(error_modes), spectrum)
+    sent, edge, out_others[0], rows[0], rows[3] = after(
+        sent, edges(error), out_others[0], rows[0], rows[3]
+    )
     base = adjoint_filter(part_index, *rows, *halo(edge), adjoint, cotangent, cot_others)
     received = exchange(sent)
-    if own % 8 == 0:
-        grad_send, grad_own, shares = final_stage(
-            part_index, lon_total, 2 * own, received, base, high_t, low_t
-        )
+    if own % 8 == 0 and share % 8 == 0:
+        shares = spread_shares(received, 2 * own)
     else:
-        grad_send, grad_own, _ = final_stage(
-            part_index, lon_total, 2 * own, received[:, : 2 * own], base, high_t, low_t
-        )
         shares = jnp.sum(received[:, 2 * own :], axis=0, keepdims=True)
         shares = jnp.broadcast_to(shares, (devices,) + shares.shape[1:])
+        received = received[:, : 2 * own]
+    grad_weight = swap_parts(shares, both_axes).reshape(chans, chans)
+    grad_send, grad_own = (
+        final_stage(part_index, lon_total, 2 * own, received, base, *apart_t, theirs)
+        for theirs in (True, False)
+    )
     grad_send, *out_others = after(grad_send, *out_others)
-    output, shares = after(join(part_index, out_own, *out_others), shares)
-    grad_input = join(part_index, grad_own, part_swap(grad_send, 1))
-    grad_weight = swap_parts(shares, both_axes).reshape(chans, chans)
+    output = join(part_index, out_own, *out_others)
+    grad_input, grad_weight = close(part_index, grad_own, part_swap(grad_send, 1), grad_weight)
     return (output, grad_input, grad_weight)
 
 

time: 151 us -> 138 us (0.914)
  waiting for transfers between devices: 43.8 us -> 29.4 us
    ppermute x8, waiting for transfers between devices: 35.6 us -> 10.1 us  [part_swap(): return lax.ppermute(x, 'chan', [(i, i ^ distance) for i in range(parts)])]
    all_to_all x5, waiting for transfers between devices: 6.1 us -> 18.5 us  [swap_parts(): return lax.all_to_all(x, axis, split_axis=0, concat_axis=0, tiled=True)]
    all_to_all x5, starting transfers between devices: 32.4 us -> 25.3 us  [swap_parts(): return lax.all_to_all(x, axis, split_axis=0, concat_axis=0, tiled=True)]
    ppermute x0 -> x3, starting transfers between devices: none -> 6.52 us  [the longest x2 5.23 us: body(): lax.ppermute(error[row:row + 1], 'lat', up)]
    pallas_call x10 -> x12, Pallas kernels: 36.2 us -> 37.5 us  [call(): run(*[held(x) if keep else x for x, keep in zip(args, keeps, strict=True)])]
    ppermute x8 -> x6, starting transfers between devices: 14.7 us -> 14.1 us  [halo(): return (lax.ppermute(x, 'lat', up), x, lax.ppermute(x, 'lat', down))]
  transfers between devices with their start and end apart: 21 -> 22, of which waited for: 10 -> 9; matrix products, arithmetic and copies ran while one was open for 2% -> 3% of each run, Pallas kernels for 15% -> 23%
where the time goes in v3:
time: 138 us; the launch traced here: 137 us
  starting transfers between devices  62.7 us (45%)
  Pallas kernels  37.5 us (27%)
  waiting for transfers between devices  29.4 us (21%)
  local copies, waits for them, and re-layouts  5.68 us (4%)
    pallas_call x12, Pallas kernels, call(): run(*[held(x) if keep else x for x, keep in zip(args, keeps, strict=True)])  37.5 us
    all_to_all x5, starting transfers between devices, swap_parts(): return lax.all_to_all(x, axis, split_axis=0, concat_axis=0, tiled=True)  25.3 us
    all_to_all x5, waiting for transfers between devices, swap_parts(): return lax.all_to_all(x, axis, split_axis=0, concat_axis=0, tiled=True)  18.5 us
    ppermute x8, starting transfers between devices, part_swap(): return lax.ppermute(x, 'chan', [(i, i ^ distance) for i in range(parts)])  16.7 us
    ppermute x6, starting transfers between devices, halo(): return (lax.ppermute(x, 'lat', up), x, lax.ppermute(x, 'lat', down))  14.1 us
    ppermute x8, waiting for transfers between devices, part_swap(): return lax.ppermute(x, 'chan', [(i, i ^ distance) for i in range(parts)])  10.1 us
    ppermute x2, starting transfers between devices, body(): lax.ppermute(error[row:row + 1], 'lat', up)  5.23 us
  transfers between devices with their start and end apart: 22, of which 9 were waited for; matrix products, arithmetic and copies ran while one was open for 3% of the time, Pallas kernels for 23%

profile of v3, /device:TPU:0, one launch (start us, length us, event | category | flops | bytes accessed | tf_op | source)
XLA Modules:
  0.0 137.0 jit_solution(15942151881935035760)
XLA Ops:
  1.7 3.1 %collective-permute-start = (f32[2,360,128]{2,1,0:T(8,128)S(1)}, f32[2,360,128]{2,1,0:T(8,128)S(1)}, u32[]{:S(2)}, u32[]{:S(2)}) collective-permute-start(f32[2,360,128]{2,1,0:T(8,128)S(1)} %constant_dynamic-slice_fusion.1), channel_id=1, source_target_pairs={{0,1},{1,0},{2,3},{3,2},{4,5},{5,4},{6,7},{7,6},{8,9},{9,8},{10,11... | collective-permute-start | bytes 1105928 | tf_op jit(solution)/shard_map/ppermute | solution.py:887
  5.8 5.3 %shard_map.157.coupling_hbm = f32[16,16,8,256]{3,2,1,0:T(8,128)} custom-call(s32[1]{0:T(128)} %bitcast.1.first_ref, f32[360,256]{1,0:T(8,128)} %gain_ref), custom_call_target="tpu_custom_call" | custom-call | flops 6000000000 | bytes 18000000 | tf_op jit(solution)/shard_map/pallas_call | solution.py:105
  15.2 3.6 %shard_map.158 = (f32[512,256]{1,0:T(8,128)}, f32[2,720,128]{2,1,0:T(8,128)}) custom-call(s32[1]{0:T(128)} %bitcast.part_ref, f32[2,360,256]{2,1,0:T(8,128)} %own_hbm.1, f32[2,360,128]{2,1,0:T(8,128)S(1)} %collective-permute-done.other_ref, bf16[512,720]{1,0:T(8,128)(2,1)} %constant.72.clone.high_hbm, bf16[512,720]{1,0:T(8,128)(2,1)} %constant.73.clone.low_hbm), custom_call_target="tpu_custom_call" | custom-call | flops 3000000000 | bytes 9000000 | tf_op jit(solution)/shard_map/pallas_call | solution.py:105
  19.3 5.7 %all-to-all-start = ((f32[32,16,256]{2,1,0:T(8,128)}), f32[32,16,256]{2,1,0:T(8,128)S(1)}, u32[]{:S(2)}, u32[]{:S(2)}) async-start(f32[32,16,256]{2,1,0:T(8,128)} %bitcast.2), calls=%async_computation | async-start | bytes 1048576 | tf_op jit(solution)/shard_map/all_to_all | solution.py:853
  26.4 3.1 %collective-permute-start.4 = (f32[2,720,128]{2,1,0:T(8,128)}, f32[2,720,128]{2,1,0:T(8,128)S(1)}, u32[]{:S(2)}, u32[]{:S(2)}) collective-permute-start(f32[2,720,128]{2,1,0:T(8,128)} %get-tuple-element.53.own_ref.field_hbm), channel_id=1, source_target_pairs={{0,4},{4,8},{8,12},{12,16},{16,20},{20,24},{24,28},{1,5},{5,9},{9,... | collective-permute-start | bytes 2211848 | tf_op jit(solution)/shard_map/ppermute | solution.py:884
  34.8 4.9 %all-to-all-done.r_ref = f32[32,16,256]{2,1,0:T(8,128)S(1)} async-done(((f32[32,16,256]{2,1,0:T(8,128)}), f32[32,16,256]{2,1,0:T(8,128)S(1)}, u32[]{:S(2)}, u32[]{:S(2)}) %all-to-all-start) | async-done | bytes 524320 | tf_op jit(solution)/shard_map/all_to_all | solution.py:853
  39.7 2.9 %shard_map.159 = (f32[16,16,256]{2,1,0:T(8,128)}, f32[32,16,256]{2,1,0:T(8,128)}) custom-call(f32[32,16,256]{2,1,0:T(8,128)S(1)} %all-to-all-done.r_ref, f32[16,16,8,256]{3,2,1,0:T(8,128)} %shard_map.157.coupling_hbm, f32[256,256]{1,0:T(8,128)} %w_hbm.3), custom_call_target="tpu_custom_call" | custom-call | flops 2000000000 | bytes 6000000 | tf_op jit(solution)/shard_map/pallas_call | solution.py:105
  42.7 4.2 %all-to-all-start.1 = ((f32[32,16,256]{2,1,0:T(8,128)}), f32[32,16,256]{2,1,0:T(8,128)S(1)}, u32[]{:S(2)}, u32[]{:S(2)}) async-start(f32[32,16,256]{2,1,0:T(8,128)} %get-tuple-element.55), calls=%async_computation.1 | async-start | bytes 1048576 | tf_op jit(solution)/shard_map/all_to_all | solution.py:853
  48.4 3.0 %collective-permute-start.6 = (f32[2,48,128]{2,1,0:T(8,128)S(1)}, f32[2,48,128]{2,1,0:T(8,128)S(1)}, u32[]{:S(2)}, u32[]{:S(2)}) collective-permute-start(f32[2,48,128]{2,1,0:T(8,128)S(1)} %select_maximum_fusion.middle_ref), channel_id=1, source_target_pairs={{0,4},{4,8},{8,12},{12,16},{16,20},{20,24},{24,28},{1,5},{5,9},{9,... | collective-permute-start | bytes 147464 | tf_op jit(solution)/shard_map/ppermute | solution.py:884
  52.6 3.9 %shard_map.160 = (f32[2,720,128]{2,1,0:T(8,128)}, f32[2,32,128]{2,1,0:T(8,128)}) custom-call(f32[2,720,128]{2,1,0:T(8,128)} %copy-done.6, f32[2,720,128]{2,1,0:T(8,128)} %get-tuple-element.53.own_ref.field_hbm, f32[2,720,128]{2,1,0:T(8,128)} %copy-done.5, f32[2,48,128]{2,1,0:T(8,128)S(1)} %collective-permute-done.6.lower_ref, ...), custom_call_target="tpu_custom_call" | custom-call | flops 4000000000 | bytes 12000000 | tf_op jit(solution)/shard_map/pallas_call | solution.py:105
  56.5 4.7 %all-to-all-done.1.s_ref = f32[32,16,256]{2,1,0:T(8,128)S(1)} async-done(((f32[32,16,256]{2,1,0:T(8,128)}), f32[32,16,256]{2,1,0:T(8,128)S(1)}, u32[]{:S(2)}, u32[]{:S(2)}) %all-to-all-start.1) | async-done | bytes 524320 | tf_op jit(solution)/shard_map/all_to_all | solution.py:853
  61.2 5.4 %shard_map.161 = (f32[512,256]{1,0:T(8,128)}, f32[2,360,128]{2,1,0:T(8,128)}, f32[1,360,128]{2,1,0:T(8,128)}, f32[1,360,128]{2,1,0:T(8,128)}, f32[2,720,128]{2,1,0:T(8,128)}) custom-call(s32[1]{0:T(128)} %bitcast.part_ref, f32[32,16,256]{2,1,0:T(8,128)S(1)} %all-to-all-done.1.s_ref, f32[2,720,128]{2,1,0:T(8,128)} %get-tuple-element.53.own_ref.field_hbm, ...), custom_call_target="tpu_custom_call" | custom-call | flops 4000000000 | bytes 12000000 | tf_op jit(solution)/shard_map/pallas_call | solution.py:105
  66.7 4.2 %all-to-all-start.2 = ((f32[32,16,256]{2,1,0:T(8,128)}), f32[32,16,256]{2,1,0:T(8,128)S(1)}, u32[]{:S(2)}, u32[]{:S(2)}) async-start(f32[32,16,256]{2,1,0:T(8,128)} %bitcast.7), calls=%async_computation.2 | async-start | bytes 1048576 | tf_op jit(solution)/shard_map/all_to_all | solution.py:853
  73.4 3.1 %collective-permute-start.10 = (f32[1,720,128]{2,1,0:T(8,128)S(1)}, f32[1,720,128]{2,1,0:T(8,128)S(1)}, u32[]{:S(2)}, u32[]{:S(2)}) collective-permute-start(f32[1,720,128]{2,1,0:T(8,128)S(1)} %get-tuple-element.80), channel_id=1, source_target_pairs={{0,4},{4,8},{8,12},{12,16},{16,20},{20,24},{24,28},{1,5},{5,9},{9,... | collective-permute-start | bytes 1105928 | tf_op jit(solution)/shard_map/ppermute | solution.py:927
  77.2 2.7 %collective-permute-start.8 = (f32[2,16,128]{2,1,0:T(8,128)S(1)}, f32[2,16,128]{2,1,0:T(8,128)S(1)}, u32[]{:S(2)}, u32[]{:S(2)}) collective-permute-start(f32[2,16,128]{2,1,0:T(8,128)S(1)} %pad_maximum_fusion.1), channel_id=1, source_target_pairs={{0,2},{1,3},{2,0},{3,1},{4,6},{5,7},{6,4},{7,5},{8,10},{9,11},{10,... | collective-permute-start | bytes 49160 | tf_op jit(solution)/shard_map/ppermute | solution.py:887
  81.3 4.3 %all-to-all-done.2.r_ref = f32[32,16,256]{2,1,0:T(8,128)S(1)} async-done(((f32[32,16,256]{2,1,0:T(8,128)}), f32[32,16,256]{2,1,0:T(8,128)S(1)}, u32[]{:S(2)}, u32[]{:S(2)}) %all-to-all-start.2) | async-done | bytes 524320 | tf_op jit(solution)/shard_map/all_to_all | solution.py:853
  85.7 3.7 %shard_map.162 = f32[32,24,256]{2,1,0:T(8,128)} custom-call(f32[32,16,256]{2,1,0:T(8,128)S(1)} %all-to-all-done.2.r_ref, f32[16,16,8,256]{3,2,1,0:T(8,128)} %shard_map.157.coupling_hbm, f32[256,256]{1,0:T(8,128)} %w_hbm.3, f32[16,16,256]{2,1,0:T(8,128)} %get-tuple-element.64.x_hbm), custom_call_target="tpu_custom_call" | custom-call | flops 2000000000 | bytes 6000000 | tf_op jit(solution)/shard_map/pallas_call | solution.py:105
  89.4 6.2 %all-to-all-start.3 = ((f32[32,24,256]{2,1,0:T(8,128)}), f32[32,24,256]{2,1,0:T(8,128)S(1)}, u32[]{:S(2)}, u32[]{:S(2)}) async-start(f32[32,24,256]{2,1,0:T(8,128)} %shard_map.162), calls=%async_computation.3 | async-start | bytes 1572864 | tf_op jit(solution)/shard_map/all_to_all | solution.py:853
  99.1 4.1 %collective-permute-start.13 = (f32[2,16,128]{2,1,0:T(8,128)S(1)}, f32[2,16,128]{2,1,0:T(8,128)S(1)}, u32[]{:S(2)}, u32[]{:S(2)}) collective-permute-start(f32[2,16,128]{2,1,0:T(8,128)S(1)} %collective-permute-done.8.middle_ref), channel_id=1, source_target_pairs={{0,4},{4,8},{8,12},{12,16},{16,20},{20,24},{24,28},{1,5},{5,9},{9,... | collective-permute-start | bytes 49160 | tf_op jit(solution)/shard_map/ppermute | solution.py:884
  105.5 5.2 %shard_map.163.base_hbm = f32[2,720,128]{2,1,0:T(8,128)} custom-call(s32[1]{0:T(128)} %bitcast.part_ref, f32[1,720,128]{2,1,0:T(8,128)} %copy-done.7, f32[1,720,128]{2,1,0:T(8,128)} %copy-done.8, f32[2,720,128]{2,1,0:T(8,128)} %get-tuple-element.65.own_ref, f32[2,720,128]{2,1,0:T(8,128)} %copy-done.4, f32[2,16,128]{2,1,0:T(8,128)S(1)} %collective-permute-done.13.lower_ref, ...), custom_call_target="tpu_custom_call" | custom-call | flops 4000000000 | bytes 12000000 | tf_op jit(solution)/shard_map/pallas_call | solution.py:105
  110.7 4.5 %all-to-all-done.3.s_ref.r_ref = f32[32,24,256]{2,1,0:T(8,128)S(1)} async-done(((f32[32,24,256]{2,1,0:T(8,128)}), f32[32,24,256]{2,1,0:T(8,128)S(1)}, u32[]{:S(2)}, u32[]{:S(2)}) %all-to-all-start.3) | async-done | bytes 786464 | tf_op jit(solution)/shard_map/all_to_all | solution.py:853
  116.0 5.0 %all-to-all-start.4 = ((f32[32,8,256]{2,1,0:T(8,128)}), f32[32,8,256]{2,1,0:T(8,128)S(1)}, u32[]{:S(2)}, u32[]{:S(2)}) async-start(f32[32,8,256]{2,1,0:T(8,128)} %shard_map.167), calls=%async_computation.4 | async-start | bytes 524288 | tf_op jit(solution)/shard_map/all_to_all | solution.py:853
  126.0 2.8 %shard_map.166.held_hbm = f32[2,360,256]{2,1,0:T(8,128)} custom-call(s32[1]{0:T(128)} %bitcast.part_ref, f32[32,24,256]{2,1,0:T(8,128)S(1)} %all-to-all-done.3.s_ref.r_ref, f32[2,720,128]{2,1,0:T(8,128)} %shard_map.163.base_hbm, bf16[2,384,512]{2,1,0:T(8,128)(2,1)} %constant.68.clone.thigh_hbm, bf16[2,384,512]{2,1,0:T(8,128)(2,1)} %constant.69.clone.tlow_hbm), custom_call_target="tpu_custom_call" | custom-call | flops 2000000000 | bytes 6000000 | tf_op jit(solution)/shard_map/pallas_call | solution.py:105
  128.8 7.3 %collective-permute-done.16.other_ref = f32[2,360,128]{2,1,0:T(8,128)S(1)} collective-permute-done((f32[2,360,128]{2,1,0:T(8,128)S(1)}, f32[2,360,128]{2,1,0:T(8,128)S(1)}, u32[]{:S(2)}, u32[]{:S(2)}) %collective-permute-start.16) | collective-permute-done | bytes 368672 | tf_op jit(solution)/shard_map/ppermute | solution.py:887
  (80 shorter events, 32.8 us)
Async XLA Ops:
  0.6 28.9 %copy-start = (f32[2,4,3,5]{3,1,2,0:T(4,128)S(1)}, f32[2,4,3,5]{3,1,2,0:T(4,128)}, u32[]{:S(2)}) copy-start(f32[2,4,3,5]{3,1,2,0:T(4,128)} %param.15) | copy-start | bytes 1444
  1.7 11.7 %collective-permute-start = (f32[2,360,128]{2,1,0:T(8,128)S(1)}, f32[2,360,128]{2,1,0:T(8,128)S(1)}, u32[]{:S(2)}, u32[]{:S(2)}) collective-permute-start(f32[2,360,128]{2,1,0:T(8,128)S(1)} %constant_dynamic-slice_fusion.1), channel_id=1, source_target_pairs={{0,1},{1,0},{2,3},{3,2},{4,5},{5,4},{6,7},{7,6},{8,9},{9,8},{10,11... | collective-permute-start | bytes 1105928 | tf_op jit(solution)/shard_map/ppermute | solution.py:887
  13.4 5.9 %collective-permute-start.1 = (f32[1,360,128]{2,1,0:T(8,128)S(1)}, f32[1,360,128]{2,1,0:T(8,128)S(1)}, u32[]{:S(2)}, u32[]{:S(2)}) collective-permute-start(f32[1,360,128]{2,1,0:T(8,128)S(1)} %slice.24), channel_id=1, source_target_pairs={{0,1},{1,0},{2,3},{3,2},{4,5},{5,4},{6,7},{7,6},{8,9},{9,8},{10,11... | collective-permute-start | bytes 552968 | tf_op jit(solution)/shard_map/ppermute | solution.py:887
  19.3 23.3 %copy-start.9 = (f32[1,360,128]{2,1,0:T(8,128)}, f32[1,360,128]{2,1,0:T(8,128)S(1)}, u32[]{:S(2)}) copy-start(f32[1,360,128]{2,1,0:T(8,128)S(1)} %collective-permute-done.1.first_hbm) | copy-start | bytes 552964
  19.3 20.4 %all-to-all-start = ((f32[32,16,256]{2,1,0:T(8,128)}), f32[32,16,256]{2,1,0:T(8,128)S(1)}, u32[]{:S(2)}, u32[]{:S(2)}) async-start(f32[32,16,256]{2,1,0:T(8,128)} %bitcast.2), calls=%async_computation | async-start | bytes 1048576 | tf_op jit(solution)/shard_map/all_to_all | solution.py:853
  25.1 26.3 %collective-permute-start.5 = (f32[2,720,128]{2,1,0:T(8,128)}, f32[2,720,128]{2,1,0:T(8,128)S(1)}, u32[]{:S(2)}, u32[]{:S(2)}) collective-permute-start(f32[2,720,128]{2,1,0:T(8,128)} %get-tuple-element.53.own_ref.field_hbm), channel_id=1, source_target_pairs={{4,0},{8,4},{12,8},{16,12},{20,16},{24,20},{28,24},{5,1},{9,5},{13... | collective-permute-start | bytes 2211848 | tf_op jit(solution)/shard_map/ppermute | solution.py:884
  26.4 25.1 %collective-permute-start.4 = (f32[2,720,128]{2,1,0:T(8,128)}, f32[2,720,128]{2,1,0:T(8,128)S(1)}, u32[]{:S(2)}, u32[]{:S(2)}) collective-permute-start(f32[2,720,128]{2,1,0:T(8,128)} %get-tuple-element.53.own_ref.field_hbm), channel_id=1, source_target_pairs={{0,4},{4,8},{8,12},{12,16},{16,20},{20,24},{24,28},{1,5},{5,9},{9,... | collective-permute-start | bytes 2211848 | tf_op jit(solution)/shard_map/ppermute | solution.py:884
  30.5 12.1 %collective-permute-start.2 = (f32[2,16,128]{2,1,0:T(8,128)S(1)}, f32[2,16,128]{2,1,0:T(8,128)S(1)}, u32[]{:S(2)}, u32[]{:S(2)}) collective-permute-start(f32[2,16,128]{2,1,0:T(8,128)S(1)} %pad_maximum_fusion), channel_id=1, source_target_pairs={{0,2},{1,3},{2,0},{3,1},{4,6},{5,7},{6,4},{7,5},{8,10},{9,11},{10,... | collective-permute-start | bytes 49160 | tf_op jit(solution)/shard_map/ppermute | solution.py:887
  33.2 9.5 %collective-permute-start.3 = (f32[1,360,128]{2,1,0:T(8,128)S(1)}, f32[1,360,128]{2,1,0:T(8,128)S(1)}, u32[]{:S(2)}, u32[]{:S(2)}) collective-permute-start(f32[1,360,128]{2,1,0:T(8,128)S(1)} %slice.27), channel_id=1, source_target_pairs={{0,1},{1,0},{2,3},{3,2},{4,5},{5,4},{6,7},{7,6},{8,9},{9,8},{10,11... | collective-permute-start | bytes 552968 | tf_op jit(solution)/shard_map/ppermute | solution.py:887
  42.7 18.6 %all-to-all-start.1 = ((f32[32,16,256]{2,1,0:T(8,128)}), f32[32,16,256]{2,1,0:T(8,128)S(1)}, u32[]{:S(2)}, u32[]{:S(2)}) async-start(f32[32,16,256]{2,1,0:T(8,128)} %get-tuple-element.55), calls=%async_computation.1 | async-start | bytes 1048576 | tf_op jit(solution)/shard_map/all_to_all | solution.py:853
  47.1 4.4 %collective-permute-start.7 = (f32[2,48,128]{2,1,0:T(8,128)S(1)}, f32[2,48,128]{2,1,0:T(8,128)S(1)}, u32[]{:S(2)}, u32[]{:S(2)}) collective-permute-start(f32[2,48,128]{2,1,0:T(8,128)S(1)} %select_maximum_fusion.middle_ref), channel_id=1, source_target_pairs={{4,0},{8,4},{12,8},{16,12},{20,16},{24,20},{28,24},{5,1},{9,5},{13... | collective-permute-start | bytes 147464 | tf_op jit(solution)/shard_map/ppermute | solution.py:884
  48.4 3.9 %collective-permute-start.6 = (f32[2,48,128]{2,1,0:T(8,128)S(1)}, f32[2,48,128]{2,1,0:T(8,128)S(1)}, u32[]{:S(2)}, u32[]{:S(2)}) collective-permute-start(f32[2,48,128]{2,1,0:T(8,128)S(1)} %select_maximum_fusion.middle_ref), channel_id=1, source_target_pairs={{0,4},{4,8},{8,12},{12,16},{16,20},{20,24},{24,28},{1,5},{5,9},{9,... | collective-permute-start | bytes 147464 | tf_op jit(solution)/shard_map/ppermute | solution.py:884
  66.7 19.0 %all-to-all-start.2 = ((f32[32,16,256]{2,1,0:T(8,128)}), f32[32,16,256]{2,1,0:T(8,128)S(1)}, u32[]{:S(2)}, u32[]{:S(2)}) async-start(f32[32,16,256]{2,1,0:T(8,128)} %bitcast.7), calls=%async_computation.2 | async-start | bytes 1048576 | tf_op jit(solution)/shard_map/all_to_all | solution.py:853
  70.9 18.5 %collective-permute-start.11 = (f32[2,720,128]{2,1,0:T(8,128)}, f32[2,720,128]{2,1,0:T(8,128)S(1)}, u32[]{:S(2)}, u32[]{:S(2)}) collective-permute-start(f32[2,720,128]{2,1,0:T(8,128)} %get-tuple-element.65.own_ref), channel_id=1, source_target_pairs={{4,0},{8,4},{12,8},{16,12},{20,16},{24,20},{28,24},{5,1},{9,5},{13... | collective-permute-start | bytes 2211848 | tf_op jit(solution)/shard_map/ppermute | solution.py:928
  73.4 16.0 %collective-permute-start.10 = (f32[1,720,128]{2,1,0:T(8,128)S(1)}, f32[1,720,128]{2,1,0:T(8,128)S(1)}, u32[]{:S(2)}, u32[]{:S(2)}) collective-permute-start(f32[1,720,128]{2,1,0:T(8,128)S(1)} %get-tuple-element.80), channel_id=1, source_target_pairs={{0,4},{4,8},{8,12},{12,16},{16,20},{20,24},{24,28},{1,5},{5,9},{9,... | collective-permute-start | bytes 1105928 | tf_op jit(solution)/shard_map/ppermute | solution.py:927
  77.2 12.2 %collective-permute-start.8 = (f32[2,16,128]{2,1,0:T(8,128)S(1)}, f32[2,16,128]{2,1,0:T(8,128)S(1)}, u32[]{:S(2)}, u32[]{:S(2)}) collective-permute-start(f32[2,16,128]{2,1,0:T(8,128)S(1)} %pad_maximum_fusion.1), channel_id=1, source_target_pairs={{0,2},{1,3},{2,0},{3,1},{4,6},{5,7},{6,4},{7,5},{8,10},{9,11},{10,... | collective-permute-start | bytes 49160 | tf_op jit(solution)/shard_map/ppermute | solution.py:887
  79.8 9.5 %collective-permute-start.9 = (f32[1,360,128]{2,1,0:T(8,128)S(1)}, f32[1,360,128]{2,1,0:T(8,128)S(1)}, u32[]{:S(2)}, u32[]{:S(2)}) collective-permute-start(f32[1,360,128]{2,1,0:T(8,128)S(1)} %copy-done.12), channel_id=1, source_target_pairs={{0,1},{1,0},{2,3},{3,2},{4,5},{5,4},{6,7},{7,6},{8,9},{9,8},{10,11... | collective-permute-start | bytes 552968 | tf_op jit(solution)/shard_map/ppermute | solution.py:887
  89.4 25.8 %all-to-all-start.3 = ((f32[32,24,256]{2,1,0:T(8,128)}), f32[32,24,256]{2,1,0:T(8,128)S(1)}, u32[]{:S(2)}, u32[]{:S(2)}) async-start(f32[32,24,256]{2,1,0:T(8,128)} %shard_map.162), calls=%async_computation.3 | async-start | bytes 1572864 | tf_op jit(solution)/shard_map/all_to_all | solution.py:853
  95.6 9.2 %collective-permute-start.12 = (f32[1,720,128]{2,1,0:T(8,128)S(1)}, f32[1,720,128]{2,1,0:T(8,128)S(1)}, u32[]{:S(2)}, u32[]{:S(2)}) collective-permute-start(f32[1,720,128]{2,1,0:T(8,128)S(1)} %get-tuple-element.79), channel_id=1, source_target_pairs={{0,4},{4,8},{8,12},{12,16},{16,20},{20,24},{24,28},{1,5},{5,9},{9,... | collective-permute-start | bytes 1105928 | tf_op jit(solution)/shard_map/ppermute | solution.py:927
  97.8 7.0 %collective-permute-start.14 = (f32[2,16,128]{2,1,0:T(8,128)S(1)}, f32[2,16,128]{2,1,0:T(8,128)S(1)}, u32[]{:S(2)}, u32[]{:S(2)}) collective-permute-start(f32[2,16,128]{2,1,0:T(8,128)S(1)} %collective-permute-done.8.middle_ref), channel_id=1, source_target_pairs={{4,0},{8,4},{12,8},{16,12},{20,16},{24,20},{28,24},{5,1},{9,5},{13... | collective-permute-start | bytes 49160 | tf_op jit(solution)/shard_map/ppermute | solution.py:884
  99.1 5.7 %collective-permute-start.13 = (f32[2,16,128]{2,1,0:T(8,128)S(1)}, f32[2,16,128]{2,1,0:T(8,128)S(1)}, u32[]{:S(2)}, u32[]{:S(2)}) collective-permute-start(f32[2,16,128]{2,1,0:T(8,128)S(1)} %collective-permute-done.8.middle_ref), channel_id=1, source_target_pairs={{0,4},{4,8},{8,12},{12,16},{16,20},{20,24},{24,28},{1,5},{5,9},{9,... | collective-permute-start | bytes 49160 | tf_op jit(solution)/shard_map/ppermute | solution.py:884
  103.3 19.9 %collective-permute-start.15 = (f32[1,360,128]{2,1,0:T(8,128)S(1)}, f32[1,360,128]{2,1,0:T(8,128)S(1)}, u32[]{:S(2)}, u32[]{:S(2)}) collective-permute-start(f32[1,360,128]{2,1,0:T(8,128)S(1)} %copy-done.11), channel_id=1, source_target_pairs={{0,1},{1,0},{2,3},{3,2},{4,5},{5,4},{6,7},{7,6},{8,9},{9,8},{10,11... | collective-permute-start | bytes 552968 | tf_op jit(solution)/shard_map/ppermute | solution.py:887
  116.0 20.1 %all-to-all-start.4 = ((f32[32,8,256]{2,1,0:T(8,128)}), f32[32,8,256]{2,1,0:T(8,128)S(1)}, u32[]{:S(2)}, u32[]{:S(2)}) async-start(f32[32,8,256]{2,1,0:T(8,128)} %shard_map.167), calls=%async_computation.4 | async-start | bytes 524288 | tf_op jit(solution)/shard_map/all_to_all | solution.py:853
  123.2 12.9 %collective-permute-start.16 = (f32[2,360,128]{2,1,0:T(8,128)S(1)}, f32[2,360,128]{2,1,0:T(8,128)S(1)}, u32[]{:S(2)}, u32[]{:S(2)}) collective-permute-start(f32[2,360,128]{2,1,0:T(8,128)S(1)} %shard_map.164), channel_id=1, source_target_pairs={{0,1},{1,0},{2,3},{3,2},{4,5},{5,4},{6,7},{7,6},{8,9},{9,8},{10,11... | collective-permute-start | bytes 1105928 | tf_op jit(solution)/shard_map/ppermute | solution.py:887
  (13 other events, 139.9 us)

commit v4 on v3

--- a/solution.py
+++ b/solution.py
@@ -208,20 +208,19 @@
 
 def analyze_rows(x, sign, high_ref, low_ref, wait, store):
     high, low = split(x)
-    tile = high_ref.shape[0] // 2
-    for parity in range(2):
-        rows = pl.ds(parity * tile, tile)
-        wait(0, parity)
-        wait(1, parity)
-        value = three(high_ref[rows, :], low_ref[rows, :], high, low)
-        store(rows, value * sign if parity else value)
-
-
-def compose_rows(modes, sign, thigh_ref, tlow_ref, wait, store):
+    wait(0, 0)
+    wait(1, 0)
+    value = three(high_ref[...], low_ref[...], high, low)
+    count = value.shape[0] // 2
+    store(pl.ds(0, count), value[:count])
+    store(pl.ds(count, count), value[count:] * sign)
+
+
+def compose_rows(modes, sign, thigh_ref, tlow_ref, wait, store, pieces):
     count = modes.shape[0] // 2
     high, low = split(jnp.concatenate([modes[:count], modes[count:] * sign], axis=0))
-    tile = thigh_ref.shape[0] // 3
-    for piece in range(3):
+    tile = thigh_ref.shape[0] // pieces
+    for piece in range(pieces):
         rows = pl.ds(piece * tile, tile)
         wait(0, piece)
         wait(1, piece)
@@ -238,7 +237,7 @@
     half = own_half(part)
     mine = pltpu.make_async_copy(lane_half(own_hbm, half), lon_half(x_ref, half), pair_sem)
     mine.start()
-    wait = fetches((high_hbm, low_hbm), (high_ref, low_ref), sems, 2)
+    wait = fetches((high_hbm, low_hbm), (high_ref, low_ref), sems, 1)
     lon_half(x_ref, 1 - half)[...] = other_ref[...]
     mine.wait()
     out = pltpu.make_async_copy(x_ref, field_hbm, out_sem)
@@ -259,7 +258,7 @@
         (struct(2 * M, rows * LANES), kept(*field)),
         [smem] + hbm(1) + vmem(1) + hbm(2),
         [VMEM(field, f32), VMEM(high.shape, bf16), VMEM(high.shape, bf16)]
-        + [pltpu.SemaphoreType.DMA, pltpu.SemaphoreType.DMA((2, 2)), pltpu.SemaphoreType.DMA],
+        + [pltpu.SemaphoreType.DMA, pltpu.SemaphoreType.DMA((2, 1)), pltpu.SemaphoreType.DMA],
         us=3.0,
         out_spaces=(VMEM, pltpu.HBM),
     )(part, own, other, high, low)
@@ -281,13 +280,13 @@
     for copy in others:
         copy.start()
     others += pair_copies(half, cot_hbm, (first_hbm, second_hbm), cot_ref, cot_sems)
-    wait = fetches((high_hbm, low_hbm), (high_ref, low_ref), sems, 2)
+    wait = fetches((high_hbm, low_hbm), (high_ref, low_ref), sems, 1)
 
     def store_spec(rows, value):
         spec_ref[rows, :] = value
 
     modes = s_ref[...].reshape(thigh_ref.shape[1], s_ref.shape[2])
-    compose_rows(modes, sign, thigh_ref, tlow_ref, wait_back, store_spec)
+    compose_rows(modes, sign, thigh_ref, tlow_ref, wait_back, store_spec, 3)
     for copy in others:
         copy.wait()
     tile = x_ref.shape[1] // 6
@@ -337,7 +336,7 @@
         [smem] + vmem(1) + hbm(9),
         [grid, grid, grid, VMEM((lons, rows * LANES), f32), grid, grid]
         + [VMEM(table.shape, bf16) for table in tables]
-        + [pltpu.SemaphoreType.DMA((2, 3)), pltpu.SemaphoreType.DMA((2, 2))]
+        + [pltpu.SemaphoreType.DMA((2, 3)), pltpu.SemaphoreType.DMA((2, 1))]
         + [pltpu.SemaphoreType.DMA((count,)) for count in (3, 2, 4)],
         us=4.0,
         limit=32,
@@ -351,7 +350,7 @@
     out_hbm = refs[0]
     part = part_ref[0]
     half = 1 - own_half(part) if theirs else own_half(part)
-    wait = fetches((thigh_hbm.at[half], tlow_hbm.at[half]), (thigh_ref, tlow_ref), sems, 3)
+    wait = fetches((thigh_hbm.at[half], tlow_hbm.at[half]), (thigh_ref, tlow_ref), sems, 1)
     base_copy = pltpu.make_async_copy(lon_half(base_hbm, half), base_ref, base_sem)
     base_copy.start()
     modes = s_ref[:, pl.ds(0, rows_own), :].reshape(thigh_ref.shape[1], s_ref.shape[2])
@@ -363,7 +362,7 @@
             lanes = slice(row * LANES, (row + 1) * LANES)
             o_ref[row, pl.ds(lons.start, count), :] = scale * value[:count, lanes]
 
-    compose_rows(modes, turn_sign(part), thigh_ref, tlow_ref, wait, store)
+    compose_rows(modes, turn_sign(part), thigh_ref, tlow_ref, wait, store, 1)
     base_copy.wait()
     o_ref[...] = o_ref[...] + base_ref[...]
     if not theirs:
@@ -382,33 +381,29 @@
         [smem] + vmem(1) + hbm(3),
         [VMEM(block, f32)] * (1 if theirs else 2)
         + [VMEM(table, bf16), VMEM(table, bf16)]
-        + [pltpu.SemaphoreType.DMA((2, 3)), pltpu.SemaphoreType.DMA],
+        + [pltpu.SemaphoreType.DMA((2, 1)), pltpu.SemaphoreType.DMA],
         us=2.0,
         out_spaces=VMEM if theirs else pltpu.HBM,
     )(part, modes, base, high_t, low_t)
 
 
-def close_kernel(part_ref, held_hbm, other_ref, weight_ref, o_hbm, weight_hbm, sems):
+def close_kernel(part_ref, held_hbm, other_ref, o_hbm, sem):
     del held_hbm
-    copies = (
-        pltpu.make_async_copy(other_ref, lane_half(o_hbm, 1 - own_half(part_ref[0])), sems.at[0]),
-        pltpu.make_async_copy(weight_ref, weight_hbm, sems.at[1]),
-    )
-    for copy in copies:
-        copy.start()
-    for copy in copies:
-        copy.wait()
-
-
-def close(part, held_half, other, weight):
+    copy = pltpu.make_async_copy(other_ref, lane_half(o_hbm, 1 - own_half(part_ref[0])), sem)
+    copy.start()
+    copy.wait()
+
+
+def close(part, held_half, other):
     return call(
         close_kernel,
-        (kept(*held_half.shape), kept(*weight.shape)),
-        [smem] + hbm(1) + vmem(2),
-        [pltpu.SemaphoreType.DMA((2,))],
-        out_spaces=(pltpu.HBM, pltpu.HBM),
+        kept(*held_half.shape),
+        [smem] + hbm(1) + vmem(1),
+        [pltpu.SemaphoreType.DMA],
+        us=8.0,
+        out_spaces=pltpu.HBM,
         aliases={1: 0},
-    )(part, held_half, other, weight)
+    )(part, held_half, other)
 
 
 def shares_kernel(first, r_ref, o_ref):
@@ -905,17 +900,16 @@
     field_other, factors, cot_out = after(field_other, factors, cot_out)
     modes, field = analyze(part_index, lon_total, grid_field, field_other, high, low)
 
-    cot_others = [part_swap(cot_out[:1], 1)]
-    modes, field_sent, cot_others[0], cot_out, disco_weight, band_start = after(
-        modes, field, cot_others[0], cot_out, disco_weight, band_start
+    modes, field_sent, cot_out, disco_weight, band_start = after(
+        modes, field, cot_out, disco_weight, band_start
     )
     mine = lax.dynamic_slice_in_dim(disco_weight, half * LANES, LANES, axis=1)
     coef = filter_coefficients(filters, mine, band_start, band_reach)
     rows = halo(field_sent)
-    cot_others.append(part_swap(cot_out[1:], 1))
+    cot_others = [part_swap(cot_out[row : row + 1], 1) for row in range(band_rows)]
     forward, backward = mode_stages(first_order, own, parts, factors, degree_gain, spec_weight)
     spectrum, synthesis = forward(exchange(modes))
-    synthesis, edge, cot_others[1] = after(synthesis, edges(field_sent), cot_others[1])
+    synthesis, edge, cot_others[0] = after(synthesis, edges(field_sent), cot_others[0])
 
     local, adjoint = local_filter(*rows, *halo(jnp.concatenate([edge, coef], axis=1)))
     error_modes, out_own, *out_sends, error = grid_stage(
@@ -932,20 +926,19 @@
     )
     base = adjoint_filter(part_index, *rows, *halo(edge), adjoint, cotangent, cot_others)
     received = exchange(sent)
+    modes = received if own % 8 == 0 else received[:, : 2 * own]
+    grad_send = final_stage(part_index, lon_total, 2 * own, modes, base, *apart_t, True)
+    grad_send, received, *out_others = after(grad_send, received, *out_others)
+    grad_other = part_swap(grad_send, 1)
     if own % 8 == 0 and share % 8 == 0:
         shares = spread_shares(received, 2 * own)
     else:
         shares = jnp.sum(received[:, 2 * own :], axis=0, keepdims=True)
         shares = jnp.broadcast_to(shares, (devices,) + shares.shape[1:])
-        received = received[:, : 2 * own]
     grad_weight = swap_parts(shares, both_axes).reshape(chans, chans)
-    grad_send, grad_own = (
-        final_stage(part_index, lon_total, 2 * own, received, base, *apart_t, theirs)
-        for theirs in (True, False)
-    )
-    grad_send, *out_others = after(grad_send, *out_others)
+    grad_own = final_stage(part_index, lon_total, 2 * own, modes, base, *apart_t, False)
     output = join(part_index, out_own, *out_others)
-    grad_input, grad_weight = close(part_index, grad_own, part_swap(grad_send, 1), grad_weight)
+    grad_input, grad_weight = after(close(part_index, grad_own, grad_other), grad_weight)
     return (output, grad_input, grad_weight)
 
 

time: 138 us -> 135 us (0.978)
  waiting for transfers between devices: 29.4 us -> 26.4 us
  local copies, waits for them, and re-layouts: 5.68 us -> 7.86 us
  Pallas kernels: 37.5 us -> 35.7 us
    all_to_all x5, waiting for transfers between devices: 18.5 us -> 15.9 us  [swap_parts(): return lax.all_to_all(x, axis, split_axis=0, concat_axis=0, tiled=True)]
    unnamed x30 -> x31, local copies, waits for them, and re-layouts: 1.02 us -> 3.2 us
    pallas_call x12, Pallas kernels: 37.5 us -> 35.7 us  [call(): run(*[held(x) if keep else x for x, keep in zip(args, keeps, strict=True)])]
    all_to_all x5, starting transfers between devices: 25.3 us -> 23.9 us  [swap_parts(): return lax.all_to_all(x, axis, split_axis=0, concat_axis=0, tiled=True)]
  transfers between devices with their start and end apart: 22 -> 22, of which waited for: 9 -> 8; matrix products, arithmetic and copies ran while one was open for 3% -> 3% of each run, Pallas kernels for 23% -> 21%
where the time goes in v4:
time: 135 us; the launch traced here: 134 us
  starting transfers between devices  62.4 us (46%)
  Pallas kernels  35.7 us (26%)
  waiting for transfers between devices  26.4 us (20%)
  local copies, waits for them, and re-layouts  7.86 us (6%)
    pallas_call x12, Pallas kernels, call(): run(*[held(x) if keep else x for x, keep in zip(args, keeps, strict=True)])  35.7 us
    all_to_all x5, starting transfers between devices, swap_parts(): return lax.all_to_all(x, axis, split_axis=0, concat_axis=0, tiled=True)  23.9 us
    ppermute x8, starting transfers between devices, part_swap(): return lax.ppermute(x, 'chan', [(i, i ^ distance) for i in range(parts)])  17.9 us
    all_to_all x5, waiting for transfers between devices, swap_parts(): return lax.all_to_all(x, axis, split_axis=0, concat_axis=0, tiled=True)  15.9 us
    ppermute x6, starting transfers between devices, halo(): return (lax.ppermute(x, 'lat', up), x, lax.ppermute(x, 'lat', down))  14.1 us
    ppermute x8, waiting for transfers between devices, part_swap(): return lax.ppermute(x, 'chan', [(i, i ^ distance) for i in range(parts)])  10.5 us
    ppermute x2, starting transfers between devices, body(): lax.ppermute(error[row:row + 1], 'lat', up)  5.23 us
    unnamed x31, local copies, waits for them, and re-layouts  3.2 us
  transfers between devices with their start and end apart: 22, of which 8 were waited for; matrix products, arithmetic and copies ran while one was open for 3% of the time, Pallas kernels for 21%

profile of v4, /device:TPU:0, one launch (start us, length us, event | category | flops | bytes accessed | tf_op | source)
XLA Modules:
  0.0 134.0 jit_solution(10985024936042283032)
XLA Ops:
  1.7 3.1 %collective-permute-start = (f32[2,360,128]{2,1,0:T(8,128)S(1)}, f32[2,360,128]{2,1,0:T(8,128)S(1)}, u32[]{:S(2)}, u32[]{:S(2)}) collective-permute-start(f32[2,360,128]{2,1,0:T(8,128)S(1)} %constant_dynamic-slice_fusion.1), channel_id=1, source_target_pairs={{0,1},{1,0},{2,3},{3,2},{4,5},{5,4},{6,7},{7,6},{8,9},{9,8},{10,11... | collective-permute-start | bytes 1105928 | tf_op jit(solution)/shard_map/ppermute | solution.py:882
  5.8 5.3 %shard_map.157.coupling_hbm = f32[16,16,8,256]{3,2,1,0:T(8,128)} custom-call(s32[1]{0:T(128)} %bitcast.1.first_ref, f32[360,256]{1,0:T(8,128)} %gain_ref), custom_call_target="tpu_custom_call" | custom-call | flops 6000000000 | bytes 18000000 | tf_op jit(solution)/shard_map/pallas_call | solution.py:105
  13.4 3.1 %shard_map.158 = (f32[512,256]{1,0:T(8,128)}, f32[2,720,128]{2,1,0:T(8,128)}) custom-call(s32[1]{0:T(128)} %bitcast.part_ref, f32[2,360,256]{2,1,0:T(8,128)} %own_hbm.1, f32[2,360,128]{2,1,0:T(8,128)S(1)} %collective-permute-done.other_ref, bf16[512,720]{1,0:T(8,128)(2,1)} %constant.72.clone.high_hbm, bf16[512,720]{1,0:T(8,128)(2,1)} %constant.73.clone.low_hbm), custom_call_target="tpu_custom_call" | custom-call | flops 3000000000 | bytes 9000000 | tf_op jit(solution)/shard_map/pallas_call | solution.py:105
  16.5 6.0 %all-to-all-start = ((f32[32,16,256]{2,1,0:T(8,128)}), f32[32,16,256]{2,1,0:T(8,128)S(1)}, u32[]{:S(2)}, u32[]{:S(2)}) async-start(f32[32,16,256]{2,1,0:T(8,128)} %bitcast.2), calls=%async_computation | async-start | bytes 1048576 | tf_op jit(solution)/shard_map/all_to_all | solution.py:848
  23.9 3.1 %collective-permute-start.3 = (f32[2,720,128]{2,1,0:T(8,128)}, f32[2,720,128]{2,1,0:T(8,128)S(1)}, u32[]{:S(2)}, u32[]{:S(2)}) collective-permute-start(f32[2,720,128]{2,1,0:T(8,128)} %get-tuple-element.53.own_ref.field_hbm), channel_id=1, source_target_pairs={{0,4},{4,8},{8,12},{12,16},{16,20},{20,24},{24,28},{1,5},{5,9},{9,... | collective-permute-start | bytes 2211848 | tf_op jit(solution)/shard_map/ppermute | solution.py:879
  32.2 4.9 %all-to-all-done.r_ref = f32[32,16,256]{2,1,0:T(8,128)S(1)} async-done(((f32[32,16,256]{2,1,0:T(8,128)}), f32[32,16,256]{2,1,0:T(8,128)S(1)}, u32[]{:S(2)}, u32[]{:S(2)}) %all-to-all-start) | async-done | bytes 524320 | tf_op jit(solution)/shard_map/all_to_all | solution.py:848
  37.2 2.9 %shard_map.159 = (f32[16,16,256]{2,1,0:T(8,128)}, f32[32,16,256]{2,1,0:T(8,128)}) custom-call(f32[32,16,256]{2,1,0:T(8,128)S(1)} %all-to-all-done.r_ref, f32[16,16,8,256]{3,2,1,0:T(8,128)} %shard_map.157.coupling_hbm, f32[256,256]{1,0:T(8,128)} %w_hbm.3), custom_call_target="tpu_custom_call" | custom-call | flops 2000000000 | bytes 6000000 | tf_op jit(solution)/shard_map/pallas_call | solution.py:105
  40.2 4.2 %all-to-all-start.1 = ((f32[32,16,256]{2,1,0:T(8,128)}), f32[32,16,256]{2,1,0:T(8,128)S(1)}, u32[]{:S(2)}, u32[]{:S(2)}) async-start(f32[32,16,256]{2,1,0:T(8,128)} %get-tuple-element.55), calls=%async_computation.1 | async-start | bytes 1048576 | tf_op jit(solution)/shard_map/all_to_all | solution.py:848
  45.9 3.0 %collective-permute-start.5 = (f32[2,48,128]{2,1,0:T(8,128)S(1)}, f32[2,48,128]{2,1,0:T(8,128)S(1)}, u32[]{:S(2)}, u32[]{:S(2)}) collective-permute-start(f32[2,48,128]{2,1,0:T(8,128)S(1)} %select_maximum_fusion.middle_ref), channel_id=1, source_target_pairs={{0,4},{4,8},{8,12},{12,16},{16,20},{20,24},{24,28},{1,5},{5,9},{9,... | collective-permute-start | bytes 147464 | tf_op jit(solution)/shard_map/ppermute | solution.py:879
  51.9 3.9 %shard_map.160 = (f32[2,720,128]{2,1,0:T(8,128)}, f32[2,32,128]{2,1,0:T(8,128)}) custom-call(f32[2,720,128]{2,1,0:T(8,128)} %copy-done.5, f32[2,720,128]{2,1,0:T(8,128)} %get-tuple-element.53.own_ref.field_hbm, f32[2,720,128]{2,1,0:T(8,128)} %copy-done.4, f32[2,48,128]{2,1,0:T(8,128)S(1)} %collective-permute-done.5.lower_ref, ...), custom_call_target="tpu_custom_call" | custom-call | flops 4000000000 | bytes 12000000 | tf_op jit(solution)/shard_map/pallas_call | solution.py:105
  55.8 3.7 %collective-permute-done.7.second_hbm = f32[1,360,128]{2,1,0:T(8,128)S(1)} collective-permute-done((f32[1,360,128]{2,1,0:T(8,128)S(1)}, f32[1,360,128]{2,1,0:T(8,128)S(1)}, u32[]{:S(2)}, u32[]{:S(2)}) %collective-permute-start.7) | collective-permute-done | bytes 184352 | tf_op jit(solution)/shard_map/ppermute | solution.py:882
  60.2 5.1 %shard_map.161 = (f32[512,256]{1,0:T(8,128)}, f32[2,360,128]{2,1,0:T(8,128)}, f32[1,360,128]{2,1,0:T(8,128)}, f32[1,360,128]{2,1,0:T(8,128)}, f32[2,720,128]{2,1,0:T(8,128)}) custom-call(s32[1]{0:T(128)} %bitcast.part_ref, f32[32,16,256]{2,1,0:T(8,128)S(1)} %all-to-all-done.1.s_ref, f32[2,720,128]{2,1,0:T(8,128)} %get-tuple-element.53.own_ref.field_hbm, ...), custom_call_target="tpu_custom_call" | custom-call | flops 4000000000 | bytes 12000000 | tf_op jit(solution)/shard_map/pallas_call | solution.py:105
  65.4 4.7 %all-to-all-start.2 = ((f32[32,16,256]{2,1,0:T(8,128)}), f32[32,16,256]{2,1,0:T(8,128)S(1)}, u32[]{:S(2)}, u32[]{:S(2)}) async-start(f32[32,16,256]{2,1,0:T(8,128)} %bitcast.7), calls=%async_computation.2 | async-start | bytes 1048576 | tf_op jit(solution)/shard_map/all_to_all | solution.py:848
  72.5 3.1 %collective-permute-start.10 = (f32[1,720,128]{2,1,0:T(8,128)S(1)}, f32[1,720,128]{2,1,0:T(8,128)S(1)}, u32[]{:S(2)}, u32[]{:S(2)}) collective-permute-start(f32[1,720,128]{2,1,0:T(8,128)S(1)} %get-tuple-element.80), channel_id=1, source_target_pairs={{0,4},{4,8},{8,12},{12,16},{16,20},{20,24},{24,28},{1,5},{5,9},{9,... | collective-permute-start | bytes 1105928 | tf_op jit(solution)/shard_map/ppermute | solution.py:921
  76.3 2.7 %collective-permute-start.8 = (f32[2,16,128]{2,1,0:T(8,128)S(1)}, f32[2,16,128]{2,1,0:T(8,128)S(1)}, u32[]{:S(2)}, u32[]{:S(2)}) collective-permute-start(f32[2,16,128]{2,1,0:T(8,128)S(1)} %pad_maximum_fusion.1), channel_id=1, source_target_pairs={{0,2},{1,3},{2,0},{3,1},{4,6},{5,7},{6,4},{7,5},{8,10},{9,11},{10,... | collective-permute-start | bytes 49160 | tf_op jit(solution)/shard_map/ppermute | solution.py:882
  80.4 4.3 %all-to-all-done.2.r_ref = f32[32,16,256]{2,1,0:T(8,128)S(1)} async-done(((f32[32,16,256]{2,1,0:T(8,128)}), f32[32,16,256]{2,1,0:T(8,128)S(1)}, u32[]{:S(2)}, u32[]{:S(2)}) %all-to-all-start.2) | async-done | bytes 524320 | tf_op jit(solution)/shard_map/all_to_all | solution.py:848
  84.8 3.7 %shard_map.162 = f32[32,24,256]{2,1,0:T(8,128)} custom-call(f32[32,16,256]{2,1,0:T(8,128)S(1)} %all-to-all-done.2.r_ref, f32[16,16,8,256]{3,2,1,0:T(8,128)} %shard_map.157.coupling_hbm, f32[256,256]{1,0:T(8,128)} %w_hbm.3, f32[16,16,256]{2,1,0:T(8,128)} %get-tuple-element.63.x_hbm), custom_call_target="tpu_custom_call" | custom-call | flops 2000000000 | bytes 6000000 | tf_op jit(solution)/shard_map/pallas_call | solution.py:105
  88.5 6.2 %all-to-all-start.3 = ((f32[32,24,256]{2,1,0:T(8,128)}), f32[32,24,256]{2,1,0:T(8,128)S(1)}, u32[]{:S(2)}, u32[]{:S(2)}) async-start(f32[32,24,256]{2,1,0:T(8,128)} %shard_map.162), calls=%async_computation.3 | async-start | bytes 1572864 | tf_op jit(solution)/shard_map/all_to_all | solution.py:848
  98.2 4.1 %collective-permute-start.13 = (f32[2,16,128]{2,1,0:T(8,128)S(1)}, f32[2,16,128]{2,1,0:T(8,128)S(1)}, u32[]{:S(2)}, u32[]{:S(2)}) collective-permute-start(f32[2,16,128]{2,1,0:T(8,128)S(1)} %collective-permute-done.8.middle_ref), channel_id=1, source_target_pairs={{0,4},{4,8},{8,12},{12,16},{16,20},{20,24},{24,28},{1,5},{5,9},{9,... | collective-permute-start | bytes 49160 | tf_op jit(solution)/shard_map/ppermute | solution.py:879
  104.7 5.2 %shard_map.163.base_hbm = f32[2,720,128]{2,1,0:T(8,128)} custom-call(s32[1]{0:T(128)} %bitcast.part_ref, f32[1,720,128]{2,1,0:T(8,128)} %copy-done.7, f32[1,720,128]{2,1,0:T(8,128)} %copy-done.8, f32[2,720,128]{2,1,0:T(8,128)} %get-tuple-element.64.own_ref, f32[2,720,128]{2,1,0:T(8,128)} %copy-done.6, f32[2,16,128]{2,1,0:T(8,128)S(1)} %collective-permute-done.13.lower_ref, ...), custom_call_target="tpu_custom_call" | custom-call | flops 4000000000 | bytes 12000000 | tf_op jit(solution)/shard_map/pallas_call | solution.py:105
  109.8 4.5 %all-to-all-done.3.s_ref.r_ref = f32[32,24,256]{2,1,0:T(8,128)S(1)} async-done(((f32[32,24,256]{2,1,0:T(8,128)}), f32[32,24,256]{2,1,0:T(8,128)S(1)}, u32[]{:S(2)}, u32[]{:S(2)}) %all-to-all-start.3) | async-done | bytes 786464 | tf_op jit(solution)/shard_map/all_to_all | solution.py:848
  116.0 3.0 %collective-permute-start.16 = (f32[2,360,128]{2,1,0:T(8,128)S(1)}, f32[2,360,128]{2,1,0:T(8,128)S(1)}, u32[]{:S(2)}, u32[]{:S(2)}) collective-permute-start(f32[2,360,128]{2,1,0:T(8,128)S(1)} %shard_map.164), channel_id=1, source_target_pairs={{0,1},{1,0},{2,3},{3,2},{4,5},{5,4},{6,7},{7,6},{8,9},{9,8},{10,11... | collective-permute-start | bytes 1105928 | tf_op jit(solution)/shard_map/ppermute | solution.py:882
  119.8 2.8 %all-to-all-start.4 = ((f32[32,8,256]{2,1,0:T(8,128)}), f32[32,8,256]{2,1,0:T(8,128)S(1)}, u32[]{:S(2)}, u32[]{:S(2)}) async-start(f32[32,8,256]{2,1,0:T(8,128)} %shard_map.168), calls=%async_computation.4 | async-start | bytes 524288 | tf_op jit(solution)/shard_map/all_to_all | solution.py:848
  126.0 4.4 %collective-permute-done.16.other_ref = f32[2,360,128]{2,1,0:T(8,128)S(1)} collective-permute-done((f32[2,360,128]{2,1,0:T(8,128)S(1)}, f32[2,360,128]{2,1,0:T(8,128)S(1)}, u32[]{:S(2)}, u32[]{:S(2)}) %collective-permute-start.16) | collective-permute-done | bytes 368672 | tf_op jit(solution)/shard_map/ppermute | solution.py:882
  (80 shorter events, 35.9 us)
Async XLA Ops:
  0.6 26.3 %copy-start = (f32[2,4,3,5]{3,1,2,0:T(4,128)S(1)}, f32[2,4,3,5]{3,1,2,0:T(4,128)}, u32[]{:S(2)}) copy-start(f32[2,4,3,5]{3,1,2,0:T(4,128)} %param.15) | copy-start | bytes 1444
  1.7 11.7 %collective-permute-start = (f32[2,360,128]{2,1,0:T(8,128)S(1)}, f32[2,360,128]{2,1,0:T(8,128)S(1)}, u32[]{:S(2)}, u32[]{:S(2)}) collective-permute-start(f32[2,360,128]{2,1,0:T(8,128)S(1)} %constant_dynamic-slice_fusion.1), channel_id=1, source_target_pairs={{0,1},{1,0},{2,3},{3,2},{4,5},{5,4},{6,7},{7,6},{8,9},{9,8},{10,11... | collective-permute-start | bytes 1105928 | tf_op jit(solution)/shard_map/ppermute | solution.py:882
  16.5 20.7 %all-to-all-start = ((f32[32,16,256]{2,1,0:T(8,128)}), f32[32,16,256]{2,1,0:T(8,128)S(1)}, u32[]{:S(2)}, u32[]{:S(2)}) async-start(f32[32,16,256]{2,1,0:T(8,128)} %bitcast.2), calls=%async_computation | async-start | bytes 1048576 | tf_op jit(solution)/shard_map/all_to_all | solution.py:848
  22.6 28.2 %collective-permute-start.4 = (f32[2,720,128]{2,1,0:T(8,128)}, f32[2,720,128]{2,1,0:T(8,128)S(1)}, u32[]{:S(2)}, u32[]{:S(2)}) collective-permute-start(f32[2,720,128]{2,1,0:T(8,128)} %get-tuple-element.53.own_ref.field_hbm), channel_id=1, source_target_pairs={{4,0},{8,4},{12,8},{16,12},{20,16},{24,20},{28,24},{5,1},{9,5},{13... | collective-permute-start | bytes 2211848 | tf_op jit(solution)/shard_map/ppermute | solution.py:879
  23.9 26.9 %collective-permute-start.3 = (f32[2,720,128]{2,1,0:T(8,128)}, f32[2,720,128]{2,1,0:T(8,128)S(1)}, u32[]{:S(2)}, u32[]{:S(2)}) collective-permute-start(f32[2,720,128]{2,1,0:T(8,128)} %get-tuple-element.53.own_ref.field_hbm), channel_id=1, source_target_pairs={{0,4},{4,8},{8,12},{12,16},{16,20},{20,24},{24,28},{1,5},{5,9},{9,... | collective-permute-start | bytes 2211848 | tf_op jit(solution)/shard_map/ppermute | solution.py:879
  28.0 12.1 %collective-permute-start.1 = (f32[2,16,128]{2,1,0:T(8,128)S(1)}, f32[2,16,128]{2,1,0:T(8,128)S(1)}, u32[]{:S(2)}, u32[]{:S(2)}) collective-permute-start(f32[2,16,128]{2,1,0:T(8,128)S(1)} %pad_maximum_fusion), channel_id=1, source_target_pairs={{0,2},{1,3},{2,0},{3,1},{4,6},{5,7},{6,4},{7,5},{8,10},{9,11},{10,... | collective-permute-start | bytes 49160 | tf_op jit(solution)/shard_map/ppermute | solution.py:882
  30.7 9.5 %collective-permute-start.2 = (f32[1,360,128]{2,1,0:T(8,128)S(1)}, f32[1,360,128]{2,1,0:T(8,128)S(1)}, u32[]{:S(2)}, u32[]{:S(2)}) collective-permute-start(f32[1,360,128]{2,1,0:T(8,128)S(1)} %get-tuple-element.86), channel_id=1, source_target_pairs={{0,1},{1,0},{2,3},{3,2},{4,5},{5,4},{6,7},{7,6},{8,9},{9,8},{10,11... | collective-permute-start | bytes 552968 | tf_op jit(solution)/shard_map/ppermute | solution.py:882
  40.2 19.4 %all-to-all-start.1 = ((f32[32,16,256]{2,1,0:T(8,128)}), f32[32,16,256]{2,1,0:T(8,128)S(1)}, u32[]{:S(2)}, u32[]{:S(2)}) async-start(f32[32,16,256]{2,1,0:T(8,128)} %get-tuple-element.55), calls=%async_computation.1 | async-start | bytes 1048576 | tf_op jit(solution)/shard_map/all_to_all | solution.py:848
  44.6 6.2 %collective-permute-start.6 = (f32[2,48,128]{2,1,0:T(8,128)S(1)}, f32[2,48,128]{2,1,0:T(8,128)S(1)}, u32[]{:S(2)}, u32[]{:S(2)}) collective-permute-start(f32[2,48,128]{2,1,0:T(8,128)S(1)} %select_maximum_fusion.middle_ref), channel_id=1, source_target_pairs={{4,0},{8,4},{12,8},{16,12},{20,16},{24,20},{28,24},{5,1},{9,5},{13... | collective-permute-start | bytes 147464 | tf_op jit(solution)/shard_map/ppermute | solution.py:879
  45.9 4.9 %collective-permute-start.5 = (f32[2,48,128]{2,1,0:T(8,128)S(1)}, f32[2,48,128]{2,1,0:T(8,128)S(1)}, u32[]{:S(2)}, u32[]{:S(2)}) collective-permute-start(f32[2,48,128]{2,1,0:T(8,128)S(1)} %select_maximum_fusion.middle_ref), channel_id=1, source_target_pairs={{0,4},{4,8},{8,12},{12,16},{16,20},{20,24},{24,28},{1,5},{5,9},{9,... | collective-permute-start | bytes 147464 | tf_op jit(solution)/shard_map/ppermute | solution.py:879
  48.9 10.6 %collective-permute-start.7 = (f32[1,360,128]{2,1,0:T(8,128)S(1)}, f32[1,360,128]{2,1,0:T(8,128)S(1)}, u32[]{:S(2)}, u32[]{:S(2)}) collective-permute-start(f32[1,360,128]{2,1,0:T(8,128)S(1)} %get-tuple-element.85), channel_id=1, source_target_pairs={{0,1},{1,0},{2,3},{3,2},{4,5},{5,4},{6,7},{7,6},{8,9},{9,8},{10,11... | collective-permute-start | bytes 552968 | tf_op jit(solution)/shard_map/ppermute | solution.py:882
  65.4 19.4 %all-to-all-start.2 = ((f32[32,16,256]{2,1,0:T(8,128)}), f32[32,16,256]{2,1,0:T(8,128)S(1)}, u32[]{:S(2)}, u32[]{:S(2)}) async-start(f32[32,16,256]{2,1,0:T(8,128)} %bitcast.7), calls=%async_computation.2 | async-start | bytes 1048576 | tf_op jit(solution)/shard_map/all_to_all | solution.py:848
  70.0 18.5 %collective-permute-start.11 = (f32[2,720,128]{2,1,0:T(8,128)}, f32[2,720,128]{2,1,0:T(8,128)S(1)}, u32[]{:S(2)}, u32[]{:S(2)}) collective-permute-start(f32[2,720,128]{2,1,0:T(8,128)} %get-tuple-element.64.own_ref), channel_id=1, source_target_pairs={{4,0},{8,4},{12,8},{16,12},{20,16},{24,20},{28,24},{5,1},{9,5},{13... | collective-permute-start | bytes 2211848 | tf_op jit(solution)/shard_map/ppermute | solution.py:922
  72.5 16.0 %collective-permute-start.10 = (f32[1,720,128]{2,1,0:T(8,128)S(1)}, f32[1,720,128]{2,1,0:T(8,128)S(1)}, u32[]{:S(2)}, u32[]{:S(2)}) collective-permute-start(f32[1,720,128]{2,1,0:T(8,128)S(1)} %get-tuple-element.80), channel_id=1, source_target_pairs={{0,4},{4,8},{8,12},{12,16},{16,20},{20,24},{24,28},{1,5},{5,9},{9,... | collective-permute-start | bytes 1105928 | tf_op jit(solution)/shard_map/ppermute | solution.py:921
  76.3 12.2 %collective-permute-start.8 = (f32[2,16,128]{2,1,0:T(8,128)S(1)}, f32[2,16,128]{2,1,0:T(8,128)S(1)}, u32[]{:S(2)}, u32[]{:S(2)}) collective-permute-start(f32[2,16,128]{2,1,0:T(8,128)S(1)} %pad_maximum_fusion.1), channel_id=1, source_target_pairs={{0,2},{1,3},{2,0},{3,1},{4,6},{5,7},{6,4},{7,5},{8,10},{9,11},{10,... | collective-permute-start | bytes 49160 | tf_op jit(solution)/shard_map/ppermute | solution.py:882
  78.9 9.5 %collective-permute-start.9 = (f32[1,360,128]{2,1,0:T(8,128)S(1)}, f32[1,360,128]{2,1,0:T(8,128)S(1)}, u32[]{:S(2)}, u32[]{:S(2)}) collective-permute-start(f32[1,360,128]{2,1,0:T(8,128)S(1)} %copy-done.12), channel_id=1, source_target_pairs={{0,1},{1,0},{2,3},{3,2},{4,5},{5,4},{6,7},{7,6},{8,9},{9,8},{10,11... | collective-permute-start | bytes 552968 | tf_op jit(solution)/shard_map/ppermute | solution.py:882
  84.8 19.9 %copy-start.2 = (f32[2,32,128]{2,1,0:T(8,128)S(1)}, f32[2,32,128]{2,1,0:T(8,128)}, u32[]{:S(2)}) copy-start(f32[2,32,128]{2,1,0:T(8,128)} %get-tuple-element.70.coef_ref) | copy-start | bytes 98308
  88.5 25.8 %all-to-all-start.3 = ((f32[32,24,256]{2,1,0:T(8,128)}), f32[32,24,256]{2,1,0:T(8,128)S(1)}, u32[]{:S(2)}, u32[]{:S(2)}) async-start(f32[32,24,256]{2,1,0:T(8,128)} %shard_map.162), calls=%async_computation.3 | async-start | bytes 1572864 | tf_op jit(solution)/shard_map/all_to_all | solution.py:848
  94.7 9.2 %collective-permute-start.12 = (f32[1,720,128]{2,1,0:T(8,128)S(1)}, f32[1,720,128]{2,1,0:T(8,128)S(1)}, u32[]{:S(2)}, u32[]{:S(2)}) collective-permute-start(f32[1,720,128]{2,1,0:T(8,128)S(1)} %get-tuple-element.79), channel_id=1, source_target_pairs={{0,4},{4,8},{8,12},{12,16},{16,20},{20,24},{24,28},{1,5},{5,9},{9,... | collective-permute-start | bytes 1105928 | tf_op jit(solution)/shard_map/ppermute | solution.py:921
  96.9 7.0 %collective-permute-start.14 = (f32[2,16,128]{2,1,0:T(8,128)S(1)}, f32[2,16,128]{2,1,0:T(8,128)S(1)}, u32[]{:S(2)}, u32[]{:S(2)}) collective-permute-start(f32[2,16,128]{2,1,0:T(8,128)S(1)} %collective-permute-done.8.middle_ref), channel_id=1, source_target_pairs={{4,0},{8,4},{12,8},{16,12},{20,16},{24,20},{28,24},{5,1},{9,5},{13... | collective-permute-start | bytes 49160 | tf_op jit(solution)/shard_map/ppermute | solution.py:879
  98.2 5.7 %collective-permute-start.13 = (f32[2,16,128]{2,1,0:T(8,128)S(1)}, f32[2,16,128]{2,1,0:T(8,128)S(1)}, u32[]{:S(2)}, u32[]{:S(2)}) collective-permute-start(f32[2,16,128]{2,1,0:T(8,128)S(1)} %collective-permute-done.8.middle_ref), channel_id=1, source_target_pairs={{0,4},{4,8},{8,12},{12,16},{16,20},{20,24},{24,28},{1,5},{5,9},{9,... | collective-permute-start | bytes 49160 | tf_op jit(solution)/shard_map/ppermute | solution.py:879
  102.4 13.6 %collective-permute-start.15 = (f32[1,360,128]{2,1,0:T(8,128)S(1)}, f32[1,360,128]{2,1,0:T(8,128)S(1)}, u32[]{:S(2)}, u32[]{:S(2)}) collective-permute-start(f32[1,360,128]{2,1,0:T(8,128)S(1)} %copy-done.11), channel_id=1, source_target_pairs={{0,1},{1,0},{2,3},{3,2},{4,5},{5,4},{6,7},{7,6},{8,9},{9,8},{10,11... | collective-permute-start | bytes 552968 | tf_op jit(solution)/shard_map/ppermute | solution.py:882
  116.0 14.4 %collective-permute-start.16 = (f32[2,360,128]{2,1,0:T(8,128)S(1)}, f32[2,360,128]{2,1,0:T(8,128)S(1)}, u32[]{:S(2)}, u32[]{:S(2)}) collective-permute-start(f32[2,360,128]{2,1,0:T(8,128)S(1)} %shard_map.164), channel_id=1, source_target_pairs={{0,1},{1,0},{2,3},{3,2},{4,5},{5,4},{6,7},{7,6},{8,9},{9,8},{10,11... | collective-permute-start | bytes 1105928 | tf_op jit(solution)/shard_map/ppermute | solution.py:882
  119.8 13.6 %all-to-all-start.4 = ((f32[32,8,256]{2,1,0:T(8,128)}), f32[32,8,256]{2,1,0:T(8,128)S(1)}, u32[]{:S(2)}, u32[]{:S(2)}) async-start(f32[32,8,256]{2,1,0:T(8,128)} %shard_map.168), calls=%async_computation.4 | async-start | bytes 524288 | tf_op jit(solution)/shard_map/all_to_all | solution.py:848
  (13 other events, 124.2 us)

commit v5 on v4

--- a/solution.py
+++ b/solution.py
@@ -103,31 +103,39 @@
     )
     keeps = [keep for _, keep in in_specs]
     return lambda *args: run(
-        *[held(x) if keep else x for x, keep in zip(args, keeps, strict=True)]
-    )
-
-
-def held(x):
-    return pltpu.with_memory_space_constraint(x, pltpu.HBM)
+        *[held(x, keep) if keep else x for x, keep in zip(args, keeps, strict=True)]
+    )
+
+
+def held(x, space):
+    return pltpu.with_memory_space_constraint(x, space)
 
 
 def vmem(count):
-    return [(VMEM, False)] * count
+    return [(VMEM, None)] * count
+
+
+def resident(count):
+    return [(VMEM, VMEM)] * count
 
 
 def loaded(count):
-    return [(VMEM, True)] * count
+    return [(VMEM, pltpu.HBM)] * count
 
 
 def hbm(count):
-    return [(pltpu.HBM, True)] * count
-
-
-smem = (pltpu.SMEM, False)
+    return [(pltpu.HBM, pltpu.HBM)] * count
+
+
+smem = (pltpu.SMEM, None)
 
 
 def struct(*shape, dtype=f32):
     return jax.ShapeDtypeStruct(shape, dtype)
+
+
+def near(*shape, dtype=f32):
+    return pltpu.VMEM(shape, dtype)
 
 
 def kept(*shape, dtype=f32):
@@ -206,6 +214,35 @@
     return lambda index, piece: copies[index][piece].wait()
 
 
+def bring_kernel(views, part_ref, *refs):
+    sources, targets, sems = refs[: len(views)], refs[len(views) : -1], refs[-1]
+    copies = [
+        pltpu.make_async_copy(view(source, part_ref[0]), target, sems.at[index])
+        for index, (view, source, target) in enumerate(zip(views, sources, targets, strict=True))
+    ]
+    for copy in copies:
+        copy.start()
+    for copy in copies:
+        copy.wait()
+
+
+def bring(part, sources, view=None):
+    views = [view or (lambda ref, part: ref)] * len(sources)
+    shapes = [x.shape[1:] if view else x.shape for x in sources]
+    return call(
+        functools.partial(bring_kernel, views),
+        [near(*shape, dtype=x.dtype) for shape, x in zip(shapes, sources, strict=True)],
+        [smem] + hbm(len(sources)),
+        [pltpu.SemaphoreType.DMA((len(sources),))],
+        us=2.0,
+        limit=8,
+    )(part, *sources)
+
+
+def there_already(index, piece):
+    del index, piece
+
+
 def analyze_rows(x, sign, high_ref, low_ref, wait, store):
     high, low = split(x)
     wait(0, 0)
@@ -231,13 +268,12 @@
     return (1 - 2 * (part // 2)).astype(f32)
 
 
-def analyze_kernel(scale, part_ref, own_hbm, other_ref, high_hbm, low_hbm, o_ref, field_hbm,
-                   x_ref, high_ref, low_ref, pair_sem, sems, out_sem):
+def analyze_kernel(scale, part_ref, own_hbm, other_ref, high_ref, low_ref, o_ref, field_hbm,
+                   x_ref, pair_sem, out_sem):
     part = part_ref[0]
     half = own_half(part)
     mine = pltpu.make_async_copy(lane_half(own_hbm, half), lon_half(x_ref, half), pair_sem)
     mine.start()
-    wait = fetches((high_hbm, low_hbm), (high_ref, low_ref), sems, 1)
     lon_half(x_ref, 1 - half)[...] = other_ref[...]
     mine.wait()
     out = pltpu.make_async_copy(x_ref, field_hbm, out_sem)
@@ -246,7 +282,7 @@
     def store(rows, value):
         o_ref[rows, :] = value * scale
 
-    analyze_rows(side_by_side(x_ref[...]), turn_sign(part), high_ref, low_ref, wait, store)
+    analyze_rows(side_by_side(x_ref[...]), turn_sign(part), high_ref, low_ref, there_already, store)
     out.wait()
 
 
@@ -256,9 +292,8 @@
     return call(
         functools.partial(analyze_kernel, 1.0 / lon_total),
         (struct(2 * M, rows * LANES), kept(*field)),
-        [smem] + hbm(1) + vmem(1) + hbm(2),
-        [VMEM(field, f32), VMEM(high.shape, bf16), VMEM(high.shape, bf16)]
-        + [pltpu.SemaphoreType.DMA, pltpu.SemaphoreType.DMA((2, 1)), pltpu.SemaphoreType.DMA],
+        [smem] + hbm(1) + vmem(1) + resident(2),
+        [VMEM(field, f32), pltpu.SemaphoreType.DMA, pltpu.SemaphoreType.DMA],
         us=3.0,
         out_spaces=(VMEM, pltpu.HBM),
     )(part, own, other, high, low)
@@ -344,13 +379,18 @@
     )(part, synthesis, field, local, cotangent, *others, *tables)
 
 
-def final_kernel(scale, rows_own, theirs, part_ref, s_ref, base_hbm, thigh_hbm, tlow_hbm,
-                 *refs):
-    o_ref, base_ref, thigh_ref, tlow_ref, sems, base_sem = refs[-6:]
-    out_hbm = refs[0]
+def final_kernel(scale, rows_own, theirs, part_ref, s_ref, base_hbm, *refs):
     part = part_ref[0]
     half = 1 - own_half(part) if theirs else own_half(part)
-    wait = fetches((thigh_hbm.at[half], tlow_hbm.at[half]), (thigh_ref, tlow_ref), sems, 1)
+    if theirs:
+        thigh_ref, tlow_ref, o_ref, *shares_ref, base_ref, base_sem = refs
+        wait = there_already
+        if shares_ref:
+            share = jnp.sum(s_ref[:, pl.ds(rows_own, shares_ref[0].shape[1]), :], axis=0)
+            shares_ref[0][...] = jnp.broadcast_to(share[None], shares_ref[0].shape)
+    else:
+        thigh_hbm, tlow_hbm, out_hbm, o_ref, base_ref, thigh_ref, tlow_ref, sems, base_sem = refs
+        wait = fetches((thigh_hbm.at[half], tlow_hbm.at[half]), (thigh_ref, tlow_ref), sems, 1)
     base_copy = pltpu.make_async_copy(lon_half(base_hbm, half), base_ref, base_sem)
     base_copy.start()
     modes = s_ref[:, pl.ds(0, rows_own), :].reshape(thigh_ref.shape[1], s_ref.shape[2])
@@ -374,16 +414,22 @@
 def final_stage(part, lon_total, rows_own, modes, base, high_t, low_t, theirs):
     rows, lons, _ = base.shape
     block = (rows, lons // 2, LANES)
-    table = high_t.shape[1:]
+    scratch = [VMEM(block, f32)]
+    out_shape = [struct(*block)]
+    share = modes.shape[1] - rows_own
+    if share:
+        out_shape.append(struct(modes.shape[0], share, modes.shape[2]))
+    if not theirs:
+        out_shape = kept(rows, lons // 2, 2 * LANES)
+        table = VMEM(high_t.shape[1:], bf16)
+        scratch = [VMEM(block, f32)] * 2 + [table, table, pltpu.SemaphoreType.DMA((2, 1))]
     return call(
         functools.partial(final_kernel, 1.0 / lon_total, rows_own, theirs),
-        struct(*block) if theirs else kept(rows, lons // 2, 2 * LANES),
-        [smem] + vmem(1) + hbm(3),
-        [VMEM(block, f32)] * (1 if theirs else 2)
-        + [VMEM(table, bf16), VMEM(table, bf16)]
-        + [pltpu.SemaphoreType.DMA((2, 1)), pltpu.SemaphoreType.DMA],
+        out_shape,
+        [smem] + vmem(1) + hbm(1) + (resident(2) if theirs else hbm(2)),
+        scratch + [pltpu.SemaphoreType.DMA],
         us=2.0,
-        out_spaces=VMEM if theirs else pltpu.HBM,
+        out_spaces=None if theirs else pltpu.HBM,
     )(part, modes, base, high_t, low_t)
 
 
@@ -404,18 +450,6 @@
         out_spaces=pltpu.HBM,
         aliases={1: 0},
     )(part, held_half, other)
-
-
-def shares_kernel(first, r_ref, o_ref):
-    share = jnp.sum(r_ref[:, pl.ds(first, o_ref.shape[1]), :], axis=0)
-    o_ref[...] = jnp.broadcast_to(share[None], o_ref.shape)
-
-
-def spread_shares(received, first):
-    devices, rows, chans = received.shape
-    return call(
-        functools.partial(shares_kernel, first), struct(devices, rows - first, chans), vmem(1)
-    )(received)
 
 
 def filter_sums(refs, edge_refs, coef_ref, finish, sums_ref):
@@ -890,15 +924,16 @@
     def exchange(modes):
         return swap_parts(modes.reshape(devices, -1, modes.shape[-1]), both_axes)
 
-    outgoing, cotangent, degree_gain, disco_weight, band_start = after(
-        half_of(grid_field, 1 - half), cotangent, degree_gain, disco_weight, band_start
+    outgoing, cotangent, degree_gain, disco_weight, band_start, tied = after(
+        half_of(grid_field, 1 - half), cotangent, degree_gain, disco_weight, band_start, part_index
     )
     field_other = part_swap(outgoing, 1)
     first_order = owned_orders(me, devices)
     factors = mode_factors(first_order, own, lat_total, degree_gain)
     cot_out = half_of(cotangent, 1 - half)
     field_other, factors, cot_out = after(field_other, factors, cot_out)
-    modes, field = analyze(part_index, lon_total, grid_field, field_other, high, low)
+    tables = bring(tied, [high, low])
+    modes, field = analyze(part_index, lon_total, grid_field, field_other, *tables)
 
     modes, field_sent, cot_out, disco_weight, band_start = after(
         modes, field, cot_out, disco_weight, band_start
@@ -921,20 +956,20 @@
     rows = [lax.ppermute(error[row : row + 1], "lat", up) for row in range(band_rows)]
     rows += [error, lax.ppermute(error, "lat", down)]
     sent = backward(exchange(error_modes), spectrum)
-    sent, edge, out_others[0], rows[0], rows[3] = after(
-        sent, edges(error), out_others[0], rows[0], rows[3]
+    sent, edge, out_others[0], rows[0], rows[3], tied = after(
+        sent, edges(error), out_others[0], rows[0], rows[3], part_index
     )
     base = adjoint_filter(part_index, *rows, *halo(edge), adjoint, cotangent, cot_others)
     received = exchange(sent)
     modes = received if own % 8 == 0 else received[:, : 2 * own]
-    grad_send = final_stage(part_index, lon_total, 2 * own, modes, base, *apart_t, True)
-    grad_send, received, *out_others = after(grad_send, received, *out_others)
-    grad_other = part_swap(grad_send, 1)
-    if own % 8 == 0 and share % 8 == 0:
-        shares = spread_shares(received, 2 * own)
+    tables = bring(tied, apart_t, lambda ref, part: ref.at[1 - own_half(part)])
+    grad_send, *shares = final_stage(part_index, lon_total, 2 * own, modes, base, *tables, True)
+    if shares:
+        grad_send, shares, *out_others = after(grad_send, shares[0], *out_others)
     else:
         shares = jnp.sum(received[:, 2 * own :], axis=0, keepdims=True)
         shares = jnp.broadcast_to(shares, (devices,) + shares.shape[1:])
+    grad_other = part_swap(grad_send, 1)
     grad_weight = swap_parts(shares, both_axes).reshape(chans, chans)
     grad_own = final_stage(part_index, lon_total, 2 * own, modes, base, *apart_t, False)
     output = join(part_index, out_own, *out_others)

time: 135 us -> 135 us (level)
  Pallas kernels: 35.7 us -> 37.2 us
    pallas_call x12 -> x13, Pallas kernels: 35.7 us -> 37.2 us  [call(): run(*[held(x, keep) if keep else x for x, keep in zip(args, keeps, strict...]
  transfers between devices with their start and end apart: 22 -> 22, of which waited for: 8 -> 8; matrix products, arithmetic and copies ran while one was open for 3% -> 2% of each run, Pallas kernels for 21% -> 22%
where the time goes in v5:
time: 135 us; the launch traced here: 134 us
  starting transfers between devices  62.1 us (46%)
  Pallas kernels  37.2 us (28%)
  waiting for transfers between devices  26 us (19%)
  local copies, waits for them, and re-layouts  6.9 us (5%)
    pallas_call x13, Pallas kernels, call(): run(*[held(x, keep) if keep else x for x, keep in zip(args, keeps, strict...  37.2 us
    all_to_all x5, starting transfers between devices, swap_parts(): return lax.all_to_all(x, axis, split_axis=0, concat_axis=0, tiled=True)  23.8 us
    ppermute x8, starting transfers between devices, part_swap(): return lax.ppermute(x, 'chan', [(i, i ^ distance) for i in range(parts)])  18.1 us
    all_to_all x5, waiting for transfers between devices, swap_parts(): return lax.all_to_all(x, axis, split_axis=0, concat_axis=0, tiled=True)  15 us
    ppermute x6, starting transfers between devices, halo(): return (lax.ppermute(x, 'lat', up), x, lax.ppermute(x, 'lat', down))  13.6 us
    ppermute x8, waiting for transfers between devices, part_swap(): return lax.ppermute(x, 'chan', [(i, i ^ distance) for i in range(parts)])  11 us
    ppermute x2, starting transfers between devices, body(): lax.ppermute(error[row:row + 1], 'lat', up)  5.23 us
    unnamed x31, local copies, waits for them, and re-layouts  3.22 us
  transfers between devices with their start and end apart: 22, of which 8 were waited for; matrix products, arithmetic and copies ran while one was open for 2% of the time, Pallas kernels for 22%

profile of v5, /device:TPU:0, one launch (start us, length us, event | category | flops | bytes accessed | tf_op | source)
XLA Modules:
  0.0 133.8 jit_solution(2394616885040070634)
XLA Ops:
  1.7 3.1 %collective-permute-start = (f32[2,360,128]{2,1,0:T(8,128)S(1)}, f32[2,360,128]{2,1,0:T(8,128)S(1)}, u32[]{:S(2)}, u32[]{:S(2)}) collective-permute-start(f32[2,360,128]{2,1,0:T(8,128)S(1)} %constant_dynamic-slice_fusion.1), channel_id=1, source_target_pairs={{0,1},{1,0},{2,3},{3,2},{4,5},{5,4},{6,7},{7,6},{8,9},{9,8},{10,11... | collective-permute-start | bytes 1105928 | tf_op jit(solution)/shard_map/ppermute | solution.py:916
  4.8 5.4 %shard_map.157.coupling_hbm = f32[16,16,8,256]{3,2,1,0:T(8,128)} custom-call(s32[1]{0:T(128)} %bitcast.1.first_ref, f32[360,256]{1,0:T(8,128)} %gain_ref), custom_call_target="tpu_custom_call" | custom-call | flops 6000000000 | bytes 18000000 | tf_op jit(solution)/shard_map/pallas_call | solution.py:105
  13.4 2.7 %shard_map.159 = (f32[512,256]{1,0:T(8,128)}, f32[2,720,128]{2,1,0:T(8,128)}) custom-call(s32[1]{0:T(128)} %bitcast.part_ref, f32[2,360,256]{2,1,0:T(8,128)} %own_hbm.1, f32[2,360,128]{2,1,0:T(8,128)S(1)} %collective-permute-done.other_ref, bf16[512,720]{1,0:T(8,128)(2,1)S(1)} %get-tuple-element.54.high_ref, bf16[512,720]{1,0:T(8,128)(2,1)S(1)} %get-tuple-element.55.low_ref), custom_call_target="tpu_custom_call" | custom-call | flops 3000000000 | bytes 9000000 | tf_op jit(solution)/shard_map/pallas_call | solution.py:105
  16.1 6.0 %all-to-all-start = ((f32[32,16,256]{2,1,0:T(8,128)}), f32[32,16,256]{2,1,0:T(8,128)S(1)}, u32[]{:S(2)}, u32[]{:S(2)}) async-start(f32[32,16,256]{2,1,0:T(8,128)} %bitcast.2), calls=%async_computation | async-start | bytes 1048576 | tf_op jit(solution)/shard_map/all_to_all | solution.py:882
  23.5 3.1 %collective-permute-start.3 = (f32[2,720,128]{2,1,0:T(8,128)}, f32[2,720,128]{2,1,0:T(8,128)S(1)}, u32[]{:S(2)}, u32[]{:S(2)}) collective-permute-start(f32[2,720,128]{2,1,0:T(8,128)} %get-tuple-element.64.own_ref.field_hbm), channel_id=1, source_target_pairs={{0,4},{4,8},{8,12},{12,16},{16,20},{20,24},{24,28},{1,5},{5,9},{9,... | collective-permute-start | bytes 2211848 | tf_op jit(solution)/shard_map/ppermute | solution.py:913
  27.5 2.7 %collective-permute-start.1 = (f32[2,16,128]{2,1,0:T(8,128)S(1)}, f32[2,16,128]{2,1,0:T(8,128)S(1)}, u32[]{:S(2)}, u32[]{:S(2)}) collective-permute-start(f32[2,16,128]{2,1,0:T(8,128)S(1)} %pad_maximum_fusion), channel_id=1, source_target_pairs={{0,2},{1,3},{2,0},{3,1},{4,6},{5,7},{6,4},{7,5},{8,10},{9,11},{10,... | collective-permute-start | bytes 49160 | tf_op jit(solution)/shard_map/ppermute | solution.py:916
  31.8 4.9 %all-to-all-done.r_ref = f32[32,16,256]{2,1,0:T(8,128)S(1)} async-done(((f32[32,16,256]{2,1,0:T(8,128)}), f32[32,16,256]{2,1,0:T(8,128)S(1)}, u32[]{:S(2)}, u32[]{:S(2)}) %all-to-all-start) | async-done | bytes 524320 | tf_op jit(solution)/shard_map/all_to_all | solution.py:882
  36.7 2.9 %shard_map.160 = (f32[16,16,256]{2,1,0:T(8,128)}, f32[32,16,256]{2,1,0:T(8,128)}) custom-call(f32[32,16,256]{2,1,0:T(8,128)S(1)} %all-to-all-done.r_ref, f32[16,16,8,256]{3,2,1,0:T(8,128)} %shard_map.157.coupling_hbm, f32[256,256]{1,0:T(8,128)} %w_hbm.3), custom_call_target="tpu_custom_call" | custom-call | flops 2000000000 | bytes 6000000 | tf_op jit(solution)/shard_map/pallas_call | solution.py:105
  39.7 4.2 %all-to-all-start.1 = ((f32[32,16,256]{2,1,0:T(8,128)}), f32[32,16,256]{2,1,0:T(8,128)S(1)}, u32[]{:S(2)}, u32[]{:S(2)}) async-start(f32[32,16,256]{2,1,0:T(8,128)} %get-tuple-element.66), calls=%async_computation.1 | async-start | bytes 1048576 | tf_op jit(solution)/shard_map/all_to_all | solution.py:882
  45.5 3.0 %collective-permute-start.5 = (f32[2,48,128]{2,1,0:T(8,128)S(1)}, f32[2,48,128]{2,1,0:T(8,128)S(1)}, u32[]{:S(2)}, u32[]{:S(2)}) collective-permute-start(f32[2,48,128]{2,1,0:T(8,128)S(1)} %select_maximum_fusion.middle_ref), channel_id=1, source_target_pairs={{0,4},{4,8},{8,12},{12,16},{16,20},{20,24},{24,28},{1,5},{5,9},{9,... | collective-permute-start | bytes 147464 | tf_op jit(solution)/shard_map/ppermute | solution.py:913
  51.5 3.9 %shard_map.161 = (f32[2,720,128]{2,1,0:T(8,128)}, f32[2,32,128]{2,1,0:T(8,128)}) custom-call(f32[2,720,128]{2,1,0:T(8,128)} %copy-done.7, f32[2,720,128]{2,1,0:T(8,128)} %get-tuple-element.64.own_ref.field_hbm, f32[2,720,128]{2,1,0:T(8,128)} %copy-done.5, f32[2,48,128]{2,1,0:T(8,128)S(1)} %collective-permute-done.5.lower_ref, ...), custom_call_target="tpu_custom_call" | custom-call | flops 4000000000 | bytes 12000000 | tf_op jit(solution)/shard_map/pallas_call | solution.py:105
  55.4 3.8 %collective-permute-done.7.second_hbm = f32[1,360,128]{2,1,0:T(8,128)S(1)} collective-permute-done((f32[1,360,128]{2,1,0:T(8,128)S(1)}, f32[1,360,128]{2,1,0:T(8,128)S(1)}, u32[]{:S(2)}, u32[]{:S(2)}) %collective-permute-start.7) | collective-permute-done | bytes 184352 | tf_op jit(solution)/shard_map/ppermute | solution.py:916
  59.8 5.1 %shard_map.162 = (f32[512,256]{1,0:T(8,128)}, f32[2,360,128]{2,1,0:T(8,128)}, f32[1,360,128]{2,1,0:T(8,128)}, f32[1,360,128]{2,1,0:T(8,128)}, f32[2,720,128]{2,1,0:T(8,128)}) custom-call(s32[1]{0:T(128)} %bitcast.part_ref, f32[32,16,256]{2,1,0:T(8,128)S(1)} %all-to-all-done.1.s_ref, f32[2,720,128]{2,1,0:T(8,128)} %get-tuple-element.64.own_ref.field_hbm, ...), custom_call_target="tpu_custom_call" | custom-call | flops 4000000000 | bytes 12000000 | tf_op jit(solution)/shard_map/pallas_call | solution.py:105
  64.9 4.7 %all-to-all-start.2 = ((f32[32,16,256]{2,1,0:T(8,128)}), f32[32,16,256]{2,1,0:T(8,128)S(1)}, u32[]{:S(2)}, u32[]{:S(2)}) async-start(f32[32,16,256]{2,1,0:T(8,128)} %bitcast.7), calls=%async_computation.2 | async-start | bytes 1048576 | tf_op jit(solution)/shard_map/all_to_all | solution.py:882
  72.0 3.1 %collective-permute-start.10 = (f32[1,720,128]{2,1,0:T(8,128)S(1)}, f32[1,720,128]{2,1,0:T(8,128)S(1)}, u32[]{:S(2)}, u32[]{:S(2)}) collective-permute-start(f32[1,720,128]{2,1,0:T(8,128)S(1)} %get-tuple-element.96), channel_id=1, source_target_pairs={{0,4},{4,8},{8,12},{12,16},{16,20},{20,24},{24,28},{1,5},{5,9},{9,... | collective-permute-start | bytes 1105928 | tf_op jit(solution)/shard_map/ppermute | solution.py:956
  80.0 4.3 %all-to-all-done.2.r_ref = f32[32,16,256]{2,1,0:T(8,128)S(1)} async-done(((f32[32,16,256]{2,1,0:T(8,128)}), f32[32,16,256]{2,1,0:T(8,128)S(1)}, u32[]{:S(2)}, u32[]{:S(2)}) %all-to-all-start.2) | async-done | bytes 524320 | tf_op jit(solution)/shard_map/all_to_all | solution.py:882
  84.3 3.6 %shard_map.163 = f32[32,24,256]{2,1,0:T(8,128)} custom-call(f32[32,16,256]{2,1,0:T(8,128)S(1)} %all-to-all-done.2.r_ref, f32[16,16,8,256]{3,2,1,0:T(8,128)} %shard_map.157.coupling_hbm, f32[256,256]{1,0:T(8,128)} %w_hbm.3, f32[16,16,256]{2,1,0:T(8,128)} %get-tuple-element.74.x_hbm), custom_call_target="tpu_custom_call" | custom-call | flops 2000000000 | bytes 6000000 | tf_op jit(solution)/shard_map/pallas_call | solution.py:105
  88.0 6.3 %all-to-all-start.3 = ((f32[32,24,256]{2,1,0:T(8,128)}), f32[32,24,256]{2,1,0:T(8,128)S(1)}, u32[]{:S(2)}, u32[]{:S(2)}) async-start(f32[32,24,256]{2,1,0:T(8,128)} %shard_map.163), calls=%async_computation.3 | async-start | bytes 1572864 | tf_op jit(solution)/shard_map/all_to_all | solution.py:882
  99.5 3.7 %collective-permute-start.13 = (f32[2,16,128]{2,1,0:T(8,128)S(1)}, f32[2,16,128]{2,1,0:T(8,128)S(1)}, u32[]{:S(2)}, u32[]{:S(2)}) collective-permute-start(f32[2,16,128]{2,1,0:T(8,128)S(1)} %collective-permute-done.8.middle_ref), channel_id=1, source_target_pairs={{0,4},{4,8},{8,12},{12,16},{16,20},{20,24},{24,28},{1,5},{5,9},{9,... | collective-permute-start | bytes 49160 | tf_op jit(solution)/shard_map/ppermute | solution.py:913
  105.1 5.2 %shard_map.164.base_hbm = f32[2,720,128]{2,1,0:T(8,128)} custom-call(s32[1]{0:T(128)} %bitcast.part_ref, f32[1,720,128]{2,1,0:T(8,128)} %copy-done.8, f32[1,720,128]{2,1,0:T(8,128)} %copy-done.9, f32[2,720,128]{2,1,0:T(8,128)} %get-tuple-element.75.own_ref, f32[2,720,128]{2,1,0:T(8,128)} %copy-done.6, f32[2,16,128]{2,1,0:T(8,128)S(1)} %collective-permute-done.13.lower_ref, ...), custom_call_target="tpu_custom_call" | custom-call | flops 4000000000 | bytes 12000000 | tf_op jit(solution)/shard_map/pallas_call | solution.py:105
  110.3 3.6 %all-to-all-done.3.s_ref = f32[32,24,256]{2,1,0:T(8,128)S(1)} async-done(((f32[32,24,256]{2,1,0:T(8,128)}), f32[32,24,256]{2,1,0:T(8,128)S(1)}, u32[]{:S(2)}, u32[]{:S(2)}) %all-to-all-start.3) | async-done | bytes 786464 | tf_op jit(solution)/shard_map/all_to_all | solution.py:882
  115.8 3.0 %collective-permute-start.16 = (f32[2,360,128]{2,1,0:T(8,128)S(1)}, f32[2,360,128]{2,1,0:T(8,128)S(1)}, u32[]{:S(2)}, u32[]{:S(2)}) collective-permute-start(f32[2,360,128]{2,1,0:T(8,128)S(1)} %get-tuple-element.91), channel_id=1, source_target_pairs={{0,1},{1,0},{2,3},{3,2},{4,5},{5,4},{6,7},{7,6},{8,9},{9,8},{10,11... | collective-permute-start | bytes 1105928 | tf_op jit(solution)/shard_map/ppermute | solution.py:916
  118.7 2.7 %all-to-all-start.4 = ((f32[32,8,256]{2,1,0:T(8,128)}), f32[32,8,256]{2,1,0:T(8,128)S(1)}, u32[]{:S(2)}, u32[]{:S(2)}) async-start(f32[32,8,256]{2,1,0:T(8,128)} %get-tuple-element.92), calls=%async_computation.4 | async-start | bytes 524288 | tf_op jit(solution)/shard_map/all_to_all | solution.py:882
  124.8 5.3 %collective-permute-done.16.other_ref = f32[2,360,128]{2,1,0:T(8,128)S(1)} collective-permute-done((f32[2,360,128]{2,1,0:T(8,128)S(1)}, f32[2,360,128]{2,1,0:T(8,128)S(1)}, u32[]{:S(2)}, u32[]{:S(2)}) %collective-permute-start.16) | collective-permute-done | bytes 368672 | tf_op jit(solution)/shard_map/ppermute | solution.py:916
  (81 shorter events, 36.6 us)
Async XLA Ops:
  0.6 25.9 %copy-start = (f32[2,4,3,5]{3,1,2,0:T(4,128)S(1)}, f32[2,4,3,5]{3,1,2,0:T(4,128)}, u32[]{:S(2)}) copy-start(f32[2,4,3,5]{3,1,2,0:T(4,128)} %param.15) | copy-start | bytes 1444
  1.7 11.7 %collective-permute-start = (f32[2,360,128]{2,1,0:T(8,128)S(1)}, f32[2,360,128]{2,1,0:T(8,128)S(1)}, u32[]{:S(2)}, u32[]{:S(2)}) collective-permute-start(f32[2,360,128]{2,1,0:T(8,128)S(1)} %constant_dynamic-slice_fusion.1), channel_id=1, source_target_pairs={{0,1},{1,0},{2,3},{3,2},{4,5},{5,4},{6,7},{7,6},{8,9},{9,8},{10,11... | collective-permute-start | bytes 1105928 | tf_op jit(solution)/shard_map/ppermute | solution.py:916
  16.1 20.7 %all-to-all-start = ((f32[32,16,256]{2,1,0:T(8,128)}), f32[32,16,256]{2,1,0:T(8,128)S(1)}, u32[]{:S(2)}, u32[]{:S(2)}) async-start(f32[32,16,256]{2,1,0:T(8,128)} %bitcast.2), calls=%async_computation | async-start | bytes 1048576 | tf_op jit(solution)/shard_map/all_to_all | solution.py:882
  22.2 28.2 %collective-permute-start.4 = (f32[2,720,128]{2,1,0:T(8,128)}, f32[2,720,128]{2,1,0:T(8,128)S(1)}, u32[]{:S(2)}, u32[]{:S(2)}) collective-permute-start(f32[2,720,128]{2,1,0:T(8,128)} %get-tuple-element.64.own_ref.field_hbm), channel_id=1, source_target_pairs={{4,0},{8,4},{12,8},{16,12},{20,16},{24,20},{28,24},{5,1},{9,5},{13... | collective-permute-start | bytes 2211848 | tf_op jit(solution)/shard_map/ppermute | solution.py:913
  23.5 26.9 %collective-permute-start.3 = (f32[2,720,128]{2,1,0:T(8,128)}, f32[2,720,128]{2,1,0:T(8,128)S(1)}, u32[]{:S(2)}, u32[]{:S(2)}) collective-permute-start(f32[2,720,128]{2,1,0:T(8,128)} %get-tuple-element.64.own_ref.field_hbm), channel_id=1, source_target_pairs={{0,4},{4,8},{8,12},{12,16},{16,20},{20,24},{24,28},{1,5},{5,9},{9,... | collective-permute-start | bytes 2211848 | tf_op jit(solution)/shard_map/ppermute | solution.py:913
  27.5 12.1 %collective-permute-start.1 = (f32[2,16,128]{2,1,0:T(8,128)S(1)}, f32[2,16,128]{2,1,0:T(8,128)S(1)}, u32[]{:S(2)}, u32[]{:S(2)}) collective-permute-start(f32[2,16,128]{2,1,0:T(8,128)S(1)} %pad_maximum_fusion), channel_id=1, source_target_pairs={{0,2},{1,3},{2,0},{3,1},{4,6},{5,7},{6,4},{7,5},{8,10},{9,11},{10,... | collective-permute-start | bytes 49160 | tf_op jit(solution)/shard_map/ppermute | solution.py:916
  30.2 9.5 %collective-permute-start.2 = (f32[1,360,128]{2,1,0:T(8,128)S(1)}, f32[1,360,128]{2,1,0:T(8,128)S(1)}, u32[]{:S(2)}, u32[]{:S(2)}) collective-permute-start(f32[1,360,128]{2,1,0:T(8,128)S(1)} %get-tuple-element.102), channel_id=1, source_target_pairs={{0,1},{1,0},{2,3},{3,2},{4,5},{5,4},{6,7},{7,6},{8,9},{9,8},{10,11... | collective-permute-start | bytes 552968 | tf_op jit(solution)/shard_map/ppermute | solution.py:916
  39.7 19.4 %all-to-all-start.1 = ((f32[32,16,256]{2,1,0:T(8,128)}), f32[32,16,256]{2,1,0:T(8,128)S(1)}, u32[]{:S(2)}, u32[]{:S(2)}) async-start(f32[32,16,256]{2,1,0:T(8,128)} %get-tuple-element.66), calls=%async_computation.1 | async-start | bytes 1048576 | tf_op jit(solution)/shard_map/all_to_all | solution.py:882
  44.2 6.2 %collective-permute-start.6 = (f32[2,48,128]{2,1,0:T(8,128)S(1)}, f32[2,48,128]{2,1,0:T(8,128)S(1)}, u32[]{:S(2)}, u32[]{:S(2)}) collective-permute-start(f32[2,48,128]{2,1,0:T(8,128)S(1)} %select_maximum_fusion.middle_ref), channel_id=1, source_target_pairs={{4,0},{8,4},{12,8},{16,12},{20,16},{24,20},{28,24},{5,1},{9,5},{13... | collective-permute-start | bytes 147464 | tf_op jit(solution)/shard_map/ppermute | solution.py:913
  45.5 4.9 %collective-permute-start.5 = (f32[2,48,128]{2,1,0:T(8,128)S(1)}, f32[2,48,128]{2,1,0:T(8,128)S(1)}, u32[]{:S(2)}, u32[]{:S(2)}) collective-permute-start(f32[2,48,128]{2,1,0:T(8,128)S(1)} %select_maximum_fusion.middle_ref), channel_id=1, source_target_pairs={{0,4},{4,8},{8,12},{12,16},{16,20},{20,24},{24,28},{1,5},{5,9},{9,... | collective-permute-start | bytes 147464 | tf_op jit(solution)/shard_map/ppermute | solution.py:913
  48.5 10.6 %collective-permute-start.7 = (f32[1,360,128]{2,1,0:T(8,128)S(1)}, f32[1,360,128]{2,1,0:T(8,128)S(1)}, u32[]{:S(2)}, u32[]{:S(2)}) collective-permute-start(f32[1,360,128]{2,1,0:T(8,128)S(1)} %get-tuple-element.101), channel_id=1, source_target_pairs={{0,1},{1,0},{2,3},{3,2},{4,5},{5,4},{6,7},{7,6},{8,9},{9,8},{10,11... | collective-permute-start | bytes 552968 | tf_op jit(solution)/shard_map/ppermute | solution.py:916
  64.9 19.4 %all-to-all-start.2 = ((f32[32,16,256]{2,1,0:T(8,128)}), f32[32,16,256]{2,1,0:T(8,128)S(1)}, u32[]{:S(2)}, u32[]{:S(2)}) async-start(f32[32,16,256]{2,1,0:T(8,128)} %bitcast.7), calls=%async_computation.2 | async-start | bytes 1048576 | tf_op jit(solution)/shard_map/all_to_all | solution.py:882
  69.6 18.4 %collective-permute-start.11 = (f32[2,720,128]{2,1,0:T(8,128)}, f32[2,720,128]{2,1,0:T(8,128)S(1)}, u32[]{:S(2)}, u32[]{:S(2)}) collective-permute-start(f32[2,720,128]{2,1,0:T(8,128)} %get-tuple-element.75.own_ref), channel_id=1, source_target_pairs={{4,0},{8,4},{12,8},{16,12},{20,16},{24,20},{28,24},{5,1},{9,5},{13... | collective-permute-start | bytes 2211848 | tf_op jit(solution)/shard_map/ppermute | solution.py:957
  72.0 15.9 %collective-permute-start.10 = (f32[1,720,128]{2,1,0:T(8,128)S(1)}, f32[1,720,128]{2,1,0:T(8,128)S(1)}, u32[]{:S(2)}, u32[]{:S(2)}) collective-permute-start(f32[1,720,128]{2,1,0:T(8,128)S(1)} %get-tuple-element.96), channel_id=1, source_target_pairs={{0,4},{4,8},{8,12},{12,16},{16,20},{20,24},{24,28},{1,5},{5,9},{9,... | collective-permute-start | bytes 1105928 | tf_op jit(solution)/shard_map/ppermute | solution.py:956
  75.8 12.1 %collective-permute-start.8 = (f32[2,16,128]{2,1,0:T(8,128)S(1)}, f32[2,16,128]{2,1,0:T(8,128)S(1)}, u32[]{:S(2)}, u32[]{:S(2)}) collective-permute-start(f32[2,16,128]{2,1,0:T(8,128)S(1)} %pad_maximum_fusion.1), channel_id=1, source_target_pairs={{0,2},{1,3},{2,0},{3,1},{4,6},{5,7},{6,4},{7,5},{8,10},{9,11},{10,... | collective-permute-start | bytes 49160 | tf_op jit(solution)/shard_map/ppermute | solution.py:916
  78.5 9.4 %collective-permute-start.9 = (f32[1,360,128]{2,1,0:T(8,128)S(1)}, f32[1,360,128]{2,1,0:T(8,128)S(1)}, u32[]{:S(2)}, u32[]{:S(2)}) collective-permute-start(f32[1,360,128]{2,1,0:T(8,128)S(1)} %copy-done.12), channel_id=1, source_target_pairs={{0,1},{1,0},{2,3},{3,2},{4,5},{5,4},{6,7},{7,6},{8,9},{9,8},{10,11... | collective-permute-start | bytes 552968 | tf_op jit(solution)/shard_map/ppermute | solution.py:916
  88.0 16.4 %copy-start.6 = (f32[2,720,128]{2,1,0:T(8,128)}, f32[2,720,128]{2,1,0:T(8,128)S(1)}, u32[]{:S(2)}) copy-start(f32[2,720,128]{2,1,0:T(8,128)S(1)} %collective-permute-done.11.next_ref) | copy-start | bytes 2211844
  88.0 25.9 %all-to-all-start.3 = ((f32[32,24,256]{2,1,0:T(8,128)}), f32[32,24,256]{2,1,0:T(8,128)S(1)}, u32[]{:S(2)}, u32[]{:S(2)}) async-start(f32[32,24,256]{2,1,0:T(8,128)} %shard_map.163), calls=%async_computation.3 | async-start | bytes 1572864 | tf_op jit(solution)/shard_map/all_to_all | solution.py:882
  94.3 10.1 %collective-permute-start.12 = (f32[1,720,128]{2,1,0:T(8,128)S(1)}, f32[1,720,128]{2,1,0:T(8,128)S(1)}, u32[]{:S(2)}, u32[]{:S(2)}) collective-permute-start(f32[1,720,128]{2,1,0:T(8,128)S(1)} %get-tuple-element.95), channel_id=1, source_target_pairs={{0,4},{4,8},{8,12},{12,16},{16,20},{20,24},{24,28},{1,5},{5,9},{9,... | collective-permute-start | bytes 1105928 | tf_op jit(solution)/shard_map/ppermute | solution.py:956
  96.5 19.2 %collective-permute-start.15 = (f32[1,360,128]{2,1,0:T(8,128)}, f32[1,360,128]{2,1,0:T(8,128)S(1)}, u32[]{:S(2)}, u32[]{:S(2)}) collective-permute-start(f32[1,360,128]{2,1,0:T(8,128)} %get-tuple-element.88), channel_id=1, source_target_pairs={{0,1},{1,0},{2,3},{3,2},{4,5},{5,4},{6,7},{7,6},{8,9},{9,8},{10,11... | collective-permute-start | bytes 552968 | tf_op jit(solution)/shard_map/ppermute | solution.py:916
  98.2 6.2 %collective-permute-start.14 = (f32[2,16,128]{2,1,0:T(8,128)S(1)}, f32[2,16,128]{2,1,0:T(8,128)S(1)}, u32[]{:S(2)}, u32[]{:S(2)}) collective-permute-start(f32[2,16,128]{2,1,0:T(8,128)S(1)} %collective-permute-done.8.middle_ref), channel_id=1, source_target_pairs={{4,0},{8,4},{12,8},{16,12},{20,16},{24,20},{28,24},{5,1},{9,5},{13... | collective-permute-start | bytes 49160 | tf_op jit(solution)/shard_map/ppermute | solution.py:913
  99.5 4.9 %collective-permute-start.13 = (f32[2,16,128]{2,1,0:T(8,128)S(1)}, f32[2,16,128]{2,1,0:T(8,128)S(1)}, u32[]{:S(2)}, u32[]{:S(2)}) collective-permute-start(f32[2,16,128]{2,1,0:T(8,128)S(1)} %collective-permute-done.8.middle_ref), channel_id=1, source_target_pairs={{0,4},{4,8},{8,12},{12,16},{16,20},{20,24},{24,28},{1,5},{5,9},{9,... | collective-permute-start | bytes 49160 | tf_op jit(solution)/shard_map/ppermute | solution.py:913
  115.8 14.4 %collective-permute-start.16 = (f32[2,360,128]{2,1,0:T(8,128)S(1)}, f32[2,360,128]{2,1,0:T(8,128)S(1)}, u32[]{:S(2)}, u32[]{:S(2)}) collective-permute-start(f32[2,360,128]{2,1,0:T(8,128)S(1)} %get-tuple-element.91), channel_id=1, source_target_pairs={{0,1},{1,0},{2,3},{3,2},{4,5},{5,4},{6,7},{7,6},{8,9},{9,8},{10,11... | collective-permute-start | bytes 1105928 | tf_op jit(solution)/shard_map/ppermute | solution.py:916
  118.7 14.3 %all-to-all-start.4 = ((f32[32,8,256]{2,1,0:T(8,128)}), f32[32,8,256]{2,1,0:T(8,128)S(1)}, u32[]{:S(2)}, u32[]{:S(2)}) async-start(f32[32,8,256]{2,1,0:T(8,128)} %get-tuple-element.92), calls=%async_computation.4 | async-start | bytes 524288 | tf_op jit(solution)/shard_map/all_to_all | solution.py:882
  (13 other events, 101.4 us)

commit v6 on v5

--- a/solution.py
+++ b/solution.py
@@ -167,22 +167,22 @@
     return copies
 
 
-def join_kernel(part_ref, own_ref, *refs):
+def join_kernel(part_ref, field_ref, own_ref, *refs):
     o_ref = refs[-1]
     half = own_half(part_ref[0])
     mine, theirs = (
         pl.ds(pl.multiple_of(place * LANES, LANES), LANES) for place in (half, 1 - half)
     )
-    o_ref[:, :, mine] = own_ref[...]
+    o_ref[:, :, mine] = field_ref[:, :, mine] + own_ref[...]
     for row, other_ref in enumerate(refs[:-1]):
-        o_ref[pl.ds(row, other_ref.shape[0]), :, theirs] = other_ref[...]
-
-
-def join(part, own, *others):
-    rows, lons, _ = own.shape
+        this = pl.ds(row, 1)
+        o_ref[this, :, theirs] = field_ref[this, :, theirs] + other_ref[...]
+
+
+def join(part, field, own, *others):
     return call(
-        join_kernel, kept(rows, lons, 2 * LANES), [smem] + vmem(1 + len(others))
-    )(part, own, *others)
+        join_kernel, kept(*field.shape), [smem] + loaded(2) + vmem(len(others))
+    )(part, field, own, *others)
 
 
 def side_by_side(x):
@@ -226,7 +226,7 @@
         copy.wait()
 
 
-def bring(part, sources, view=None):
+def bring(part, sources, view=None, us=2.0):
     views = [view or (lambda ref, part: ref)] * len(sources)
     shapes = [x.shape[1:] if view else x.shape for x in sources]
     return call(
@@ -234,7 +234,7 @@
         [near(*shape, dtype=x.dtype) for shape, x in zip(shapes, sources, strict=True)],
         [smem] + hbm(len(sources)),
         [pltpu.SemaphoreType.DMA((len(sources),))],
-        us=2.0,
+        us=us,
         limit=8,
     )(part, *sources)
 
@@ -299,38 +299,38 @@
     )(part, own, other, high, low)
 
 
-def grid_kernel(part_ref, s_ref, field_hbm, local_hbm, cot_hbm, first_hbm, second_hbm,
-                high_hbm, low_hbm, thigh_hbm, tlow_hbm,
+def grid_kernel(part_ref, s_ref, first_ref, second_ref, thigh_ref, tlow_ref, local_hbm, cot_hbm,
+                high_hbm, low_hbm,
                 mode_ref, own_hbm, send_first_hbm, send_second_hbm, err_hbm,
-                x_ref, local_ref, cot_ref, spec_ref, out_ref, err_ref,
-                high_ref, low_ref, thigh_ref, tlow_ref,
-                back_sems, sems, cot_sems, other_sems, out_sems):
+                local_ref, cot_ref, spec_ref, out_ref, err_ref,
+                high_ref, low_ref, sems, other_sems, out_sems):
     part = part_ref[0]
     half, sign = own_half(part), turn_sign(part)
-    wait_back = fetches((thigh_hbm, tlow_hbm), (thigh_ref, tlow_ref), back_sems, 3)
     others = [
-        pltpu.make_async_copy(source, target, other_sems.at[index])
-        for index, (source, target) in enumerate(((local_hbm, local_ref), (field_hbm, x_ref)))
+        pltpu.make_async_copy(local_hbm, local_ref, other_sems.at[0]),
+        pltpu.make_async_copy(lane_half(cot_hbm, half), lon_half(cot_ref, half), other_sems.at[1]),
     ]
     for copy in others:
         copy.start()
-    others += pair_copies(half, cot_hbm, (first_hbm, second_hbm), cot_ref, cot_sems)
     wait = fetches((high_hbm, low_hbm), (high_ref, low_ref), sems, 1)
+    there = lon_half(cot_ref, 1 - half)
+    for row, other_ref in enumerate((first_ref, second_ref)):
+        there[pl.ds(row, 1)] = other_ref[...]
 
     def store_spec(rows, value):
         spec_ref[rows, :] = value
 
     modes = s_ref[...].reshape(thigh_ref.shape[1], s_ref.shape[2])
-    compose_rows(modes, sign, thigh_ref, tlow_ref, wait_back, store_spec, 3)
+    compose_rows(modes, sign, thigh_ref, tlow_ref, there_already, store_spec, 1)
     for copy in others:
         copy.wait()
-    tile = x_ref.shape[1] // 6
-    for row in range(x_ref.shape[0]):
+    tile = cot_ref.shape[1] // 6
+    for row in range(cot_ref.shape[0]):
         for piece in range(6):
             lons = pl.ds(piece * tile, tile)
             hidden = local_ref[row, lons, :] + spec_ref[lons, pl.ds(row * LANES, LANES)]
             gate = 1.0 / (1.0 + jnp.exp(-hidden))
-            out_ref[row, lons, :] = x_ref[row, lons, :] + hidden * gate
+            out_ref[row, lons, :] = hidden * gate
             err_ref[row, lons, :] = cot_ref[row, lons, :] * (gate * (1.0 + hidden * (1.0 - gate)))
     there = lon_half(out_ref, 1 - half)
     outs = [
@@ -355,10 +355,10 @@
         copy.wait()
 
 
-def grid_stage(part, synthesis, field, local, cotangent, others, tables):
-    rows, lons, _ = field.shape
+def grid_stage(part, synthesis, local, cotangent, others, tables):
+    rows, lons, _ = local.shape
     block = (rows, lons // 2, LANES)
-    grid = VMEM(field.shape, f32)
+    grid = VMEM(local.shape, f32)
     return call(
         grid_kernel,
         (
@@ -366,17 +366,17 @@
             kept(*block),
             kept(1, *block[1:]),
             kept(1, *block[1:]),
-            kept(*field.shape),
+            kept(*local.shape),
         ),
-        [smem] + vmem(1) + hbm(9),
-        [grid, grid, grid, VMEM((lons, rows * LANES), f32), grid, grid]
-        + [VMEM(table.shape, bf16) for table in tables]
-        + [pltpu.SemaphoreType.DMA((2, 3)), pltpu.SemaphoreType.DMA((2, 1))]
-        + [pltpu.SemaphoreType.DMA((count,)) for count in (3, 2, 4)],
+        [smem] + vmem(3) + resident(2) + hbm(4),
+        [grid, grid, VMEM((lons, rows * LANES), f32), grid, grid]
+        + [VMEM(table.shape, bf16) for table in tables[:2]]
+        + [pltpu.SemaphoreType.DMA((2, 1))]
+        + [pltpu.SemaphoreType.DMA((count,)) for count in (2, 4)],
         us=4.0,
         limit=32,
         out_spaces=(VMEM,) + (pltpu.HBM,) * 4,
-    )(part, synthesis, field, local, cotangent, *others, *tables)
+    )(part, synthesis, *others, *tables[2:], local, cotangent, *tables[:2])
 
 
 def final_kernel(scale, rows_own, theirs, part_ref, s_ref, base_hbm, *refs):
@@ -947,9 +947,10 @@
     synthesis, edge, cot_others[0] = after(synthesis, edges(field_sent), cot_others[0])
 
     local, adjoint = local_filter(*rows, *halo(jnp.concatenate([edge, coef], axis=1)))
+    local, tied = after(local, part_index)
     error_modes, out_own, *out_sends, error = grid_stage(
-        part_index, exchange(synthesis), field, local, cotangent, cot_others,
-        (high, low, high_t, low_t),
+        part_index, exchange(synthesis), local, cotangent, cot_others,
+        (high, low, *bring(tied, [high_t, low_t], us=0.1)),
     )
 
     out_others = [part_swap(x, 1) for x in out_sends]
@@ -972,7 +973,7 @@
     grad_other = part_swap(grad_send, 1)
     grad_weight = swap_parts(shares, both_axes).reshape(chans, chans)
     grad_own = final_stage(part_index, lon_total, 2 * own, modes, base, *apart_t, False)
-    output = join(part_index, out_own, *out_others)
+    output = join(part_index, grid_field, out_own, *out_others)
     grad_input, grad_weight = after(close(part_index, grad_own, grad_other), grad_weight)
     return (output, grad_input, grad_weight)
 

time: 135 us -> 134 us (level)
  waiting for transfers between devices: 26 us -> 23.4 us
  Pallas kernels: 37.2 us -> 39.2 us
    ppermute x8, waiting for transfers between devices: 11 us -> 8.37 us  [part_swap(): return lax.ppermute(x, 'chan', [(i, i ^ distance) for i in range(parts)])]
    pallas_call x13 -> x14, Pallas kernels: 37.2 us -> 39.2 us  [call(): run(*[held(x, keep) if keep else x for x, keep in zip(args, keeps, strict...]
    unnamed x31 -> x29, local copies, waits for them, and re-layouts: 3.22 us -> 2.56 us
  transfers between devices with their start and end apart: 22 -> 22, of which waited for: 8 -> 8; matrix products, arithmetic and copies ran while one was open for 2% -> 2% of each run, Pallas kernels for 22% -> 24%
where the time goes in v6:
time: 134 us; the launch traced here: 133 us
  starting transfers between devices  62.1 us (46%)
  Pallas kernels  39.2 us (29%)
  waiting for transfers between devices  23.4 us (17%)
  local copies, waits for them, and re-layouts  6.23 us (5%)
    pallas_call x14, Pallas kernels, call(): run(*[held(x, keep) if keep else x for x, keep in zip(args, keeps, strict...  39.2 us
    all_to_all x5, starting transfers between devices, swap_parts(): return lax.all_to_all(x, axis, split_axis=0, concat_axis=0, tiled=True)  23.9 us
    ppermute x8, starting transfers between devices, part_swap(): return lax.ppermute(x, 'chan', [(i, i ^ distance) for i in range(parts)])  18.1 us
    all_to_all x5, waiting for transfers between devices, swap_parts(): return lax.all_to_all(x, axis, split_axis=0, concat_axis=0, tiled=True)  15 us
    ppermute x6, starting transfers between devices, halo(): return (lax.ppermute(x, 'lat', up), x, lax.ppermute(x, 'lat', down))  13.6 us
    ppermute x8, waiting for transfers between devices, part_swap(): return lax.ppermute(x, 'chan', [(i, i ^ distance) for i in range(parts)])  8.37 us
    ppermute x2, starting transfers between devices, body(): lax.ppermute(error[row:row + 1], 'lat', up)  5.23 us
  transfers between devices with their start and end apart: 22, of which 8 were waited for; matrix products, arithmetic and copies ran while one was open for 2% of the time, Pallas kernels for 24%

profile of v6, /device:TPU:0, one launch (start us, length us, event | category | flops | bytes accessed | tf_op | source)
XLA Modules:
  0.0 132.6 jit_solution(15413036563745047693)
XLA Ops:
  1.7 3.1 %collective-permute-start = (f32[2,360,128]{2,1,0:T(8,128)S(1)}, f32[2,360,128]{2,1,0:T(8,128)S(1)}, u32[]{:S(2)}, u32[]{:S(2)}) collective-permute-start(f32[2,360,128]{2,1,0:T(8,128)S(1)} %constant_dynamic-slice_fusion.1), channel_id=1, source_target_pairs={{0,1},{1,0},{2,3},{3,2},{4,5},{5,4},{6,7},{7,6},{8,9},{9,8},{10,11... | collective-permute-start | bytes 1105928 | tf_op jit(solution)/shard_map/ppermute | solution.py:916
  4.8 5.4 %shard_map.157.coupling_hbm = f32[16,16,8,256]{3,2,1,0:T(8,128)} custom-call(s32[1]{0:T(128)} %bitcast.1.first_ref, f32[360,256]{1,0:T(8,128)} %gain_ref), custom_call_target="tpu_custom_call" | custom-call | flops 6000000000 | bytes 18000000 | tf_op jit(solution)/shard_map/pallas_call | solution.py:105
  13.4 2.7 %shard_map.159 = (f32[512,256]{1,0:T(8,128)}, f32[2,720,128]{2,1,0:T(8,128)}) custom-call(s32[1]{0:T(128)} %bitcast.part_ref, f32[2,360,256]{2,1,0:T(8,128)} %field_ref.1, f32[2,360,128]{2,1,0:T(8,128)S(1)} %collective-permute-done.other_ref, bf16[512,720]{1,0:T(8,128)(2,1)S(1)} %get-tuple-element.58.high_ref, bf16[512,720]{1,0:T(8,128)(2,1)S(1)} %get-tuple-element.59.low_ref), custom_call_target="tpu_custom_call" | custom-call | flops 3000000000 | bytes 9000000 | tf_op jit(solution)/shard_map/pallas_call | solution.py:105
  16.1 6.0 %all-to-all-start = ((f32[32,16,256]{2,1,0:T(8,128)}), f32[32,16,256]{2,1,0:T(8,128)S(1)}, u32[]{:S(2)}, u32[]{:S(2)}) async-start(f32[32,16,256]{2,1,0:T(8,128)} %bitcast.2), calls=%async_computation | async-start | bytes 1048576 | tf_op jit(solution)/shard_map/all_to_all | solution.py:882
  23.5 3.1 %collective-permute-start.4 = (f32[2,720,128]{2,1,0:T(8,128)}, f32[2,720,128]{2,1,0:T(8,128)S(1)}, u32[]{:S(2)}, u32[]{:S(2)}) collective-permute-start(f32[2,720,128]{2,1,0:T(8,128)} %get-tuple-element.68.own_ref), channel_id=1, source_target_pairs={{0,4},{4,8},{8,12},{12,16},{16,20},{20,24},{24,28},{1,5},{5,9},{9,... | collective-permute-start | bytes 2211848 | tf_op jit(solution)/shard_map/ppermute | solution.py:913
  27.5 2.7 %collective-permute-start.1 = (f32[2,16,128]{2,1,0:T(8,128)S(1)}, f32[2,16,128]{2,1,0:T(8,128)S(1)}, u32[]{:S(2)}, u32[]{:S(2)}) collective-permute-start(f32[2,16,128]{2,1,0:T(8,128)S(1)} %pad_maximum_fusion), channel_id=1, source_target_pairs={{0,2},{1,3},{2,0},{3,1},{4,6},{5,7},{6,4},{7,5},{8,10},{9,11},{10,... | collective-permute-start | bytes 49160 | tf_op jit(solution)/shard_map/ppermute | solution.py:916
  31.8 4.9 %all-to-all-done.r_ref = f32[32,16,256]{2,1,0:T(8,128)S(1)} async-done(((f32[32,16,256]{2,1,0:T(8,128)}), f32[32,16,256]{2,1,0:T(8,128)S(1)}, u32[]{:S(2)}, u32[]{:S(2)}) %all-to-all-start) | async-done | bytes 524320 | tf_op jit(solution)/shard_map/all_to_all | solution.py:882
  36.7 2.9 %shard_map.160 = (f32[16,16,256]{2,1,0:T(8,128)}, f32[32,16,256]{2,1,0:T(8,128)}) custom-call(f32[32,16,256]{2,1,0:T(8,128)S(1)} %all-to-all-done.r_ref, f32[16,16,8,256]{3,2,1,0:T(8,128)} %shard_map.157.coupling_hbm, f32[256,256]{1,0:T(8,128)} %w_hbm.3), custom_call_target="tpu_custom_call" | custom-call | flops 2000000000 | bytes 6000000 | tf_op jit(solution)/shard_map/pallas_call | solution.py:105
  39.7 4.2 %all-to-all-start.1 = ((f32[32,16,256]{2,1,0:T(8,128)}), f32[32,16,256]{2,1,0:T(8,128)S(1)}, u32[]{:S(2)}, u32[]{:S(2)}) async-start(f32[32,16,256]{2,1,0:T(8,128)} %get-tuple-element.70), calls=%async_computation.1 | async-start | bytes 1048576 | tf_op jit(solution)/shard_map/all_to_all | solution.py:882
  45.5 3.0 %collective-permute-start.6 = (f32[2,48,128]{2,1,0:T(8,128)S(1)}, f32[2,48,128]{2,1,0:T(8,128)S(1)}, u32[]{:S(2)}, u32[]{:S(2)}) collective-permute-start(f32[2,48,128]{2,1,0:T(8,128)S(1)} %select_maximum_fusion.middle_ref), channel_id=1, source_target_pairs={{0,4},{4,8},{8,12},{12,16},{16,20},{20,24},{24,28},{1,5},{5,9},{9,... | collective-permute-start | bytes 147464 | tf_op jit(solution)/shard_map/ppermute | solution.py:913
  51.4 3.9 %shard_map.161 = (f32[2,720,128]{2,1,0:T(8,128)}, f32[2,32,128]{2,1,0:T(8,128)}) custom-call(f32[2,720,128]{2,1,0:T(8,128)} %copy-done.7, f32[2,720,128]{2,1,0:T(8,128)} %get-tuple-element.68.own_ref, f32[2,720,128]{2,1,0:T(8,128)} %copy-done.6, f32[2,48,128]{2,1,0:T(8,128)S(1)} %collective-permute-done.6.lower_ref, ...), custom_call_target="tpu_custom_call" | custom-call | flops 4000000000 | bytes 12000000 | tf_op jit(solution)/shard_map/pallas_call | solution.py:105
  59.1 4.5 %shard_map.163 = (f32[512,256]{1,0:T(8,128)}, f32[2,360,128]{2,1,0:T(8,128)}, f32[1,360,128]{2,1,0:T(8,128)}, f32[1,360,128]{2,1,0:T(8,128)}, f32[2,720,128]{2,1,0:T(8,128)}) custom-call(s32[1]{0:T(128)} %bitcast.part_ref, f32[32,16,256]{2,1,0:T(8,128)S(1)} %all-to-all-done.1.s_ref, f32[1,360,128]{2,1,0:T(8,128)S(1)} %collective-permute-done.2.first_ref.first_hbm, ...), custom_call_target="tpu_custom_call" | custom-call | flops 4000000000 | bytes 12000000 | tf_op jit(solution)/shard_map/pallas_call | solution.py:105
  63.7 4.7 %all-to-all-start.2 = ((f32[32,16,256]{2,1,0:T(8,128)}), f32[32,16,256]{2,1,0:T(8,128)S(1)}, u32[]{:S(2)}, u32[]{:S(2)}) async-start(f32[32,16,256]{2,1,0:T(8,128)} %bitcast.7), calls=%async_computation.2 | async-start | bytes 1048576 | tf_op jit(solution)/shard_map/all_to_all | solution.py:882
  70.9 3.1 %collective-permute-start.10 = (f32[1,720,128]{2,1,0:T(8,128)S(1)}, f32[1,720,128]{2,1,0:T(8,128)S(1)}, u32[]{:S(2)}, u32[]{:S(2)}) collective-permute-start(f32[1,720,128]{2,1,0:T(8,128)S(1)} %get-tuple-element.104), channel_id=1, source_target_pairs={{0,4},{4,8},{8,12},{12,16},{16,20},{20,24},{24,28},{1,5},{5,9},{9,... | collective-permute-start | bytes 1105928 | tf_op jit(solution)/shard_map/ppermute | solution.py:957
  74.7 2.7 %collective-permute-start.8 = (f32[2,16,128]{2,1,0:T(8,128)S(1)}, f32[2,16,128]{2,1,0:T(8,128)S(1)}, u32[]{:S(2)}, u32[]{:S(2)}) collective-permute-start(f32[2,16,128]{2,1,0:T(8,128)S(1)} %pad_maximum_fusion.1), channel_id=1, source_target_pairs={{0,2},{1,3},{2,0},{3,1},{4,6},{5,7},{6,4},{7,5},{8,10},{9,11},{10,... | collective-permute-start | bytes 49160 | tf_op jit(solution)/shard_map/ppermute | solution.py:916
  78.9 4.3 %all-to-all-done.2.r_ref = f32[32,16,256]{2,1,0:T(8,128)S(1)} async-done(((f32[32,16,256]{2,1,0:T(8,128)}), f32[32,16,256]{2,1,0:T(8,128)S(1)}, u32[]{:S(2)}, u32[]{:S(2)}) %all-to-all-start.2) | async-done | bytes 524320 | tf_op jit(solution)/shard_map/all_to_all | solution.py:882
  83.2 3.7 %shard_map.164 = f32[32,24,256]{2,1,0:T(8,128)} custom-call(f32[32,16,256]{2,1,0:T(8,128)S(1)} %all-to-all-done.2.r_ref, f32[16,16,8,256]{3,2,1,0:T(8,128)} %shard_map.157.coupling_hbm, f32[256,256]{1,0:T(8,128)} %w_hbm.3, f32[16,16,256]{2,1,0:T(8,128)} %get-tuple-element.82.x_hbm), custom_call_target="tpu_custom_call" | custom-call | flops 2000000000 | bytes 6000000 | tf_op jit(solution)/shard_map/pallas_call | solution.py:105
  86.9 6.2 %all-to-all-start.3 = ((f32[32,24,256]{2,1,0:T(8,128)}), f32[32,24,256]{2,1,0:T(8,128)S(1)}, u32[]{:S(2)}, u32[]{:S(2)}) async-start(f32[32,24,256]{2,1,0:T(8,128)} %shard_map.164), calls=%async_computation.3 | async-start | bytes 1572864 | tf_op jit(solution)/shard_map/all_to_all | solution.py:882
  98.4 3.7 %collective-permute-start.13 = (f32[2,16,128]{2,1,0:T(8,128)S(1)}, f32[2,16,128]{2,1,0:T(8,128)S(1)}, u32[]{:S(2)}, u32[]{:S(2)}) collective-permute-start(f32[2,16,128]{2,1,0:T(8,128)S(1)} %collective-permute-done.8.middle_ref), channel_id=1, source_target_pairs={{0,4},{4,8},{8,12},{12,16},{16,20},{20,24},{24,28},{1,5},{5,9},{9,... | collective-permute-start | bytes 49160 | tf_op jit(solution)/shard_map/ppermute | solution.py:913
  104.0 5.2 %shard_map.165.base_hbm = f32[2,720,128]{2,1,0:T(8,128)} custom-call(s32[1]{0:T(128)} %bitcast.part_ref, f32[1,720,128]{2,1,0:T(8,128)} %copy-done.9, f32[1,720,128]{2,1,0:T(8,128)} %copy-done.10, f32[2,720,128]{2,1,0:T(8,128)} %get-tuple-element.83.own_ref, f32[2,720,128]{2,1,0:T(8,128)} %copy-done.8, f32[2,16,128]{2,1,0:T(8,128)S(1)} %collective-permute-done.13.lower_ref, ...), custom_call_target="tpu_custom_call" | custom-call | flops 4000000000 | bytes 12000000 | tf_op jit(solution)/shard_map/pallas_call | solution.py:105
  109.1 3.6 %all-to-all-done.3.s_ref = f32[32,24,256]{2,1,0:T(8,128)S(1)} async-done(((f32[32,24,256]{2,1,0:T(8,128)}), f32[32,24,256]{2,1,0:T(8,128)S(1)}, u32[]{:S(2)}, u32[]{:S(2)}) %all-to-all-start.3) | async-done | bytes 786464 | tf_op jit(solution)/shard_map/all_to_all | solution.py:882
  114.6 3.0 %collective-permute-start.16 = (f32[2,360,128]{2,1,0:T(8,128)S(1)}, f32[2,360,128]{2,1,0:T(8,128)S(1)}, u32[]{:S(2)}, u32[]{:S(2)}) collective-permute-start(f32[2,360,128]{2,1,0:T(8,128)S(1)} %get-tuple-element.99), channel_id=1, source_target_pairs={{0,1},{1,0},{2,3},{3,2},{4,5},{5,4},{6,7},{7,6},{8,9},{9,8},{10,11... | collective-permute-start | bytes 1105928 | tf_op jit(solution)/shard_map/ppermute | solution.py:916
  117.5 2.7 %all-to-all-start.4 = ((f32[32,8,256]{2,1,0:T(8,128)}), f32[32,8,256]{2,1,0:T(8,128)S(1)}, u32[]{:S(2)}, u32[]{:S(2)}) async-start(f32[32,8,256]{2,1,0:T(8,128)} %get-tuple-element.100), calls=%async_computation.4 | async-start | bytes 524288 | tf_op jit(solution)/shard_map/all_to_all | solution.py:882
  124.8 4.1 %collective-permute-done.16.other_ref = f32[2,360,128]{2,1,0:T(8,128)S(1)} collective-permute-done((f32[2,360,128]{2,1,0:T(8,128)S(1)}, f32[2,360,128]{2,1,0:T(8,128)S(1)}, u32[]{:S(2)}, u32[]{:S(2)}) %collective-permute-start.16) | collective-permute-done | bytes 368672 | tf_op jit(solution)/shard_map/ppermute | solution.py:916
  (80 shorter events, 38.2 us)
Async XLA Ops:
  0.6 25.9 %copy-start = (f32[2,4,3,5]{3,1,2,0:T(4,128)S(1)}, f32[2,4,3,5]{3,1,2,0:T(4,128)}, u32[]{:S(2)}) copy-start(f32[2,4,3,5]{3,1,2,0:T(4,128)} %param.15) | copy-start | bytes 1444
  1.7 11.7 %collective-permute-start = (f32[2,360,128]{2,1,0:T(8,128)S(1)}, f32[2,360,128]{2,1,0:T(8,128)S(1)}, u32[]{:S(2)}, u32[]{:S(2)}) collective-permute-start(f32[2,360,128]{2,1,0:T(8,128)S(1)} %constant_dynamic-slice_fusion.1), channel_id=1, source_target_pairs={{0,1},{1,0},{2,3},{3,2},{4,5},{5,4},{6,7},{7,6},{8,9},{9,8},{10,11... | collective-permute-start | bytes 1105928 | tf_op jit(solution)/shard_map/ppermute | solution.py:916
  16.1 20.7 %all-to-all-start = ((f32[32,16,256]{2,1,0:T(8,128)}), f32[32,16,256]{2,1,0:T(8,128)S(1)}, u32[]{:S(2)}, u32[]{:S(2)}) async-start(f32[32,16,256]{2,1,0:T(8,128)} %bitcast.2), calls=%async_computation | async-start | bytes 1048576 | tf_op jit(solution)/shard_map/all_to_all | solution.py:882
  22.2 28.2 %collective-permute-start.5 = (f32[2,720,128]{2,1,0:T(8,128)}, f32[2,720,128]{2,1,0:T(8,128)S(1)}, u32[]{:S(2)}, u32[]{:S(2)}) collective-permute-start(f32[2,720,128]{2,1,0:T(8,128)} %get-tuple-element.68.own_ref), channel_id=1, source_target_pairs={{4,0},{8,4},{12,8},{16,12},{20,16},{24,20},{28,24},{5,1},{9,5},{13... | collective-permute-start | bytes 2211848 | tf_op jit(solution)/shard_map/ppermute | solution.py:913
  23.5 26.9 %collective-permute-start.4 = (f32[2,720,128]{2,1,0:T(8,128)}, f32[2,720,128]{2,1,0:T(8,128)S(1)}, u32[]{:S(2)}, u32[]{:S(2)}) collective-permute-start(f32[2,720,128]{2,1,0:T(8,128)} %get-tuple-element.68.own_ref), channel_id=1, source_target_pairs={{0,4},{4,8},{8,12},{12,16},{16,20},{20,24},{24,28},{1,5},{5,9},{9,... | collective-permute-start | bytes 2211848 | tf_op jit(solution)/shard_map/ppermute | solution.py:913
  27.5 12.1 %collective-permute-start.1 = (f32[2,16,128]{2,1,0:T(8,128)S(1)}, f32[2,16,128]{2,1,0:T(8,128)S(1)}, u32[]{:S(2)}, u32[]{:S(2)}) collective-permute-start(f32[2,16,128]{2,1,0:T(8,128)S(1)} %pad_maximum_fusion), channel_id=1, source_target_pairs={{0,2},{1,3},{2,0},{3,1},{4,6},{5,7},{6,4},{7,5},{8,10},{9,11},{10,... | collective-permute-start | bytes 49160 | tf_op jit(solution)/shard_map/ppermute | solution.py:916
  30.2 9.5 %collective-permute-start.2 = (f32[1,360,128]{2,1,0:T(8,128)S(1)}, f32[1,360,128]{2,1,0:T(8,128)S(1)}, u32[]{:S(2)}, u32[]{:S(2)}) collective-permute-start(f32[1,360,128]{2,1,0:T(8,128)S(1)} %get-tuple-element.110), channel_id=1, source_target_pairs={{0,1},{1,0},{2,3},{3,2},{4,5},{5,4},{6,7},{7,6},{8,9},{9,8},{10,11... | collective-permute-start | bytes 552968 | tf_op jit(solution)/shard_map/ppermute | solution.py:916
  39.7 19.4 %copy-start.1 = (f32[1,360,128]{2,1,0:T(8,128)}, f32[1,360,128]{2,1,0:T(8,128)S(1)}, u32[]{:S(2)}) copy-start(f32[1,360,128]{2,1,0:T(8,128)S(1)} %collective-permute-done.2.first_ref.first_hbm) | copy-start | bytes 552964
  39.7 19.4 %all-to-all-start.1 = ((f32[32,16,256]{2,1,0:T(8,128)}), f32[32,16,256]{2,1,0:T(8,128)S(1)}, u32[]{:S(2)}, u32[]{:S(2)}) async-start(f32[32,16,256]{2,1,0:T(8,128)} %get-tuple-element.70), calls=%async_computation.1 | async-start | bytes 1048576 | tf_op jit(solution)/shard_map/all_to_all | solution.py:882
  44.2 6.2 %collective-permute-start.7 = (f32[2,48,128]{2,1,0:T(8,128)S(1)}, f32[2,48,128]{2,1,0:T(8,128)S(1)}, u32[]{:S(2)}, u32[]{:S(2)}) collective-permute-start(f32[2,48,128]{2,1,0:T(8,128)S(1)} %select_maximum_fusion.middle_ref), channel_id=1, source_target_pairs={{4,0},{8,4},{12,8},{16,12},{20,16},{24,20},{28,24},{5,1},{9,5},{13... | collective-permute-start | bytes 147464 | tf_op jit(solution)/shard_map/ppermute | solution.py:913
  45.5 4.9 %collective-permute-start.6 = (f32[2,48,128]{2,1,0:T(8,128)S(1)}, f32[2,48,128]{2,1,0:T(8,128)S(1)}, u32[]{:S(2)}, u32[]{:S(2)}) collective-permute-start(f32[2,48,128]{2,1,0:T(8,128)S(1)} %select_maximum_fusion.middle_ref), channel_id=1, source_target_pairs={{0,4},{4,8},{8,12},{12,16},{16,20},{20,24},{24,28},{1,5},{5,9},{9,... | collective-permute-start | bytes 147464 | tf_op jit(solution)/shard_map/ppermute | solution.py:913
  48.5 10.6 %collective-permute-start.3 = (f32[1,360,128]{2,1,0:T(8,128)S(1)}, f32[1,360,128]{2,1,0:T(8,128)S(1)}, u32[]{:S(2)}, u32[]{:S(2)}) collective-permute-start(f32[1,360,128]{2,1,0:T(8,128)S(1)} %get-tuple-element.109), channel_id=1, source_target_pairs={{0,1},{1,0},{2,3},{3,2},{4,5},{5,4},{6,7},{7,6},{8,9},{9,8},{10,11... | collective-permute-start | bytes 552968 | tf_op jit(solution)/shard_map/ppermute | solution.py:916
  63.7 19.5 %all-to-all-start.2 = ((f32[32,16,256]{2,1,0:T(8,128)}), f32[32,16,256]{2,1,0:T(8,128)S(1)}, u32[]{:S(2)}, u32[]{:S(2)}) async-start(f32[32,16,256]{2,1,0:T(8,128)} %bitcast.7), calls=%async_computation.2 | async-start | bytes 1048576 | tf_op jit(solution)/shard_map/all_to_all | solution.py:882
  68.4 18.5 %collective-permute-start.11 = (f32[2,720,128]{2,1,0:T(8,128)}, f32[2,720,128]{2,1,0:T(8,128)S(1)}, u32[]{:S(2)}, u32[]{:S(2)}) collective-permute-start(f32[2,720,128]{2,1,0:T(8,128)} %get-tuple-element.83.own_ref), channel_id=1, source_target_pairs={{4,0},{8,4},{12,8},{16,12},{20,16},{24,20},{28,24},{5,1},{9,5},{13... | collective-permute-start | bytes 2211848 | tf_op jit(solution)/shard_map/ppermute | solution.py:958
  70.9 16.0 %collective-permute-start.10 = (f32[1,720,128]{2,1,0:T(8,128)S(1)}, f32[1,720,128]{2,1,0:T(8,128)S(1)}, u32[]{:S(2)}, u32[]{:S(2)}) collective-permute-start(f32[1,720,128]{2,1,0:T(8,128)S(1)} %get-tuple-element.104), channel_id=1, source_target_pairs={{0,4},{4,8},{8,12},{12,16},{16,20},{20,24},{24,28},{1,5},{5,9},{9,... | collective-permute-start | bytes 1105928 | tf_op jit(solution)/shard_map/ppermute | solution.py:957
  74.7 12.2 %collective-permute-start.8 = (f32[2,16,128]{2,1,0:T(8,128)S(1)}, f32[2,16,128]{2,1,0:T(8,128)S(1)}, u32[]{:S(2)}, u32[]{:S(2)}) collective-permute-start(f32[2,16,128]{2,1,0:T(8,128)S(1)} %pad_maximum_fusion.1), channel_id=1, source_target_pairs={{0,2},{1,3},{2,0},{3,1},{4,6},{5,7},{6,4},{7,5},{8,10},{9,11},{10,... | collective-permute-start | bytes 49160 | tf_op jit(solution)/shard_map/ppermute | solution.py:916
  77.3 9.5 %collective-permute-start.9 = (f32[1,360,128]{2,1,0:T(8,128)S(1)}, f32[1,360,128]{2,1,0:T(8,128)S(1)}, u32[]{:S(2)}, u32[]{:S(2)}) collective-permute-start(f32[1,360,128]{2,1,0:T(8,128)S(1)} %copy-done.11), channel_id=1, source_target_pairs={{0,1},{1,0},{2,3},{3,2},{4,5},{5,4},{6,7},{7,6},{8,9},{9,8},{10,11... | collective-permute-start | bytes 552968 | tf_op jit(solution)/shard_map/ppermute | solution.py:916
  86.9 25.8 %all-to-all-start.3 = ((f32[32,24,256]{2,1,0:T(8,128)}), f32[32,24,256]{2,1,0:T(8,128)S(1)}, u32[]{:S(2)}, u32[]{:S(2)}) async-start(f32[32,24,256]{2,1,0:T(8,128)} %shard_map.164), calls=%async_computation.3 | async-start | bytes 1572864 | tf_op jit(solution)/shard_map/all_to_all | solution.py:882
  93.1 10.1 %collective-permute-start.12 = (f32[1,720,128]{2,1,0:T(8,128)S(1)}, f32[1,720,128]{2,1,0:T(8,128)S(1)}, u32[]{:S(2)}, u32[]{:S(2)}) collective-permute-start(f32[1,720,128]{2,1,0:T(8,128)S(1)} %get-tuple-element.103), channel_id=1, source_target_pairs={{0,4},{4,8},{8,12},{12,16},{16,20},{20,24},{24,28},{1,5},{5,9},{9,... | collective-permute-start | bytes 1105928 | tf_op jit(solution)/shard_map/ppermute | solution.py:957
  95.3 19.2 %collective-permute-start.15 = (f32[1,360,128]{2,1,0:T(8,128)}, f32[1,360,128]{2,1,0:T(8,128)S(1)}, u32[]{:S(2)}, u32[]{:S(2)}) collective-permute-start(f32[1,360,128]{2,1,0:T(8,128)} %get-tuple-element.96), channel_id=1, source_target_pairs={{0,1},{1,0},{2,3},{3,2},{4,5},{5,4},{6,7},{7,6},{8,9},{9,8},{10,11... | collective-permute-start | bytes 552968 | tf_op jit(solution)/shard_map/ppermute | solution.py:916
  97.1 6.2 %collective-permute-start.14 = (f32[2,16,128]{2,1,0:T(8,128)S(1)}, f32[2,16,128]{2,1,0:T(8,128)S(1)}, u32[]{:S(2)}, u32[]{:S(2)}) collective-permute-start(f32[2,16,128]{2,1,0:T(8,128)S(1)} %collective-permute-done.8.middle_ref), channel_id=1, source_target_pairs={{4,0},{8,4},{12,8},{16,12},{20,16},{24,20},{28,24},{5,1},{9,5},{13... | collective-permute-start | bytes 49160 | tf_op jit(solution)/shard_map/ppermute | solution.py:913
  98.4 4.9 %collective-permute-start.13 = (f32[2,16,128]{2,1,0:T(8,128)S(1)}, f32[2,16,128]{2,1,0:T(8,128)S(1)}, u32[]{:S(2)}, u32[]{:S(2)}) collective-permute-start(f32[2,16,128]{2,1,0:T(8,128)S(1)} %collective-permute-done.8.middle_ref), channel_id=1, source_target_pairs={{0,4},{4,8},{8,12},{12,16},{16,20},{20,24},{24,28},{1,5},{5,9},{9,... | collective-permute-start | bytes 49160 | tf_op jit(solution)/shard_map/ppermute | solution.py:913
  114.6 14.4 %collective-permute-start.16 = (f32[2,360,128]{2,1,0:T(8,128)S(1)}, f32[2,360,128]{2,1,0:T(8,128)S(1)}, u32[]{:S(2)}, u32[]{:S(2)}) collective-permute-start(f32[2,360,128]{2,1,0:T(8,128)S(1)} %get-tuple-element.99), channel_id=1, source_target_pairs={{0,1},{1,0},{2,3},{3,2},{4,5},{5,4},{6,7},{7,6},{8,9},{9,8},{10,11... | collective-permute-start | bytes 1105928 | tf_op jit(solution)/shard_map/ppermute | solution.py:916
  117.5 14.3 %all-to-all-start.4 = ((f32[32,8,256]{2,1,0:T(8,128)}), f32[32,8,256]{2,1,0:T(8,128)S(1)}, u32[]{:S(2)}, u32[]{:S(2)}) async-start(f32[32,8,256]{2,1,0:T(8,128)} %get-tuple-element.100), calls=%async_computation.4 | async-start | bytes 524288 | tf_op jit(solution)/shard_map/all_to_all | solution.py:882
  (12 other events, 98.4 us)

commit v7 on v6

--- a/solution.py
+++ b/solution.py
@@ -669,10 +669,9 @@
                 s_ref[band * parts + part, pl.ds(0, rows), lanes] = value
 
 
-def forward_modes_kernel(parts, r_ref, coupling_hbm, w_hbm, x_ref, s_ref, y_ref, z_ref,
-                         coupling_ref, w_ref, sems):
-    wait_w = fetches((w_hbm,), (w_ref,), sems.at[pl.ds(0, 1)], 2)
-    wait = fetches((coupling_hbm,), (coupling_ref,), sems.at[pl.ds(1, 1)], 8)
+def forward_modes_kernel(parts, r_ref, w_ref, coupling_hbm, x_ref, s_ref, y_ref, z_ref,
+                         coupling_ref, sems):
+    wait = fetches((coupling_hbm,), (coupling_ref,), sems, 8)
 
     def write(j, lanes, value):
         x_ref[j, :, lanes] = value
@@ -680,8 +679,6 @@
     gather_modes(r_ref, write, parts)
     lats, rows, chans = x_ref.shape
     own = rows // 2
-    for piece in range(2):
-        wait_w(0, piece)
     y_ref[...] = dot_split(
         x_ref[...].reshape(lats * rows, chans), w_ref[...], ((1,), (0,))
     ).reshape(lats, rows, chans)
@@ -812,15 +809,16 @@
         chans = spec_weight.shape[0]
         shape = (factors.shape[0], 2 * own, chans)
 
-        def forward(received):
+        def forward(received, tied):
+            (weight,) = bring(tied, [spec_weight], us=0.1)
             return call(
                 functools.partial(forward_modes_kernel, parts),
                 (kept(*shape), struct(*received.shape)),
-                vmem(1) + hbm(2),
+                vmem(1) + resident(1) + hbm(1),
                 [VMEM(shape, f32), VMEM(shape, f32), VMEM(factors.shape, f32)]
-                + [VMEM(spec_weight.shape, f32), pltpu.SemaphoreType.DMA((2, 8))],
+                + [pltpu.SemaphoreType.DMA((1, 8))],
                 us=2.0,
-            )(received, factors, spec_weight)
+            )(received, weight, factors)
 
         def backward(received, spectrum):
             sent = (received.shape[0], 2 * own + chans // received.shape[0], chans)
@@ -844,7 +842,8 @@
     quad_column = quad_weight[:, None, None, None]
     dot = functools.partial(jnp.einsum, precision=highest)
 
-    def forward(received):
+    def forward(received, tied):
+        del tied
         spectrum = plain_gather(received, parts, own)
         mixed = dot("jpmc,cd->jpmd", spectrum, spec_weight) * quad_column
         degree = dot("lmj,jpmd->lpmd", legendre, mixed) * degree_gain[:, None, None, :]
@@ -935,15 +934,15 @@
     tables = bring(tied, [high, low])
     modes, field = analyze(part_index, lon_total, grid_field, field_other, *tables)
 
-    modes, field_sent, cot_out, disco_weight, band_start = after(
-        modes, field, cot_out, disco_weight, band_start
+    modes, field_sent, cot_out, disco_weight, band_start, tied = after(
+        modes, field, cot_out, disco_weight, band_start, part_index
     )
     mine = lax.dynamic_slice_in_dim(disco_weight, half * LANES, LANES, axis=1)
     coef = filter_coefficients(filters, mine, band_start, band_reach)
     rows = halo(field_sent)
     cot_others = [part_swap(cot_out[row : row + 1], 1) for row in range(band_rows)]
     forward, backward = mode_stages(first_order, own, parts, factors, degree_gain, spec_weight)
-    spectrum, synthesis = forward(exchange(modes))
+    spectrum, synthesis = forward(exchange(modes), tied)
     synthesis, edge, cot_others[0] = after(synthesis, edges(field_sent), cot_others[0])
 
     local, adjoint = local_filter(*rows, *halo(jnp.concatenate([edge, coef], axis=1)))

time: 134 us -> 134 us (level)
    pallas_call x14 -> x15, Pallas kernels: 39.2 us -> 39.9 us  [call(): run(*[held(x, keep) if keep else x for x, keep in zip(args, keeps, strict...]
  transfers between devices with their start and end apart: 22 -> 22, of which waited for: 8 -> 8; matrix products, arithmetic and copies ran while one was open for 2% -> 2% of each run, Pallas kernels for 24% -> 25%
where the time goes in v7:
time: 134 us; the launch traced here: 132 us
  starting transfers between devices  61.8 us (46%)
  Pallas kernels  39.9 us (30%)
  waiting for transfers between devices  22.7 us (17%)
  local copies, waits for them, and re-layouts  6.23 us (5%)
    pallas_call x15, Pallas kernels, call(): run(*[held(x, keep) if keep else x for x, keep in zip(args, keeps, strict...  39.9 us
    all_to_all x5, starting transfers between devices, swap_parts(): return lax.all_to_all(x, axis, split_axis=0, concat_axis=0, tiled=True)  23.6 us
    ppermute x8, starting transfers between devices, part_swap(): return lax.ppermute(x, 'chan', [(i, i ^ distance) for i in range(parts)])  18.1 us
    all_to_all x5, waiting for transfers between devices, swap_parts(): return lax.all_to_all(x, axis, split_axis=0, concat_axis=0, tiled=True)  14 us
    ppermute x6, starting transfers between devices, halo(): return (lax.ppermute(x, 'lat', up), x, lax.ppermute(x, 'lat', down))  13.6 us
    ppermute x8, waiting for transfers between devices, part_swap(): return lax.ppermute(x, 'chan', [(i, i ^ distance) for i in range(parts)])  8.64 us
    ppermute x2, starting transfers between devices, body(): lax.ppermute(error[row:row + 1], 'lat', up)  5.23 us
  transfers between devices with their start and end apart: 22, of which 8 were waited for; matrix products, arithmetic and copies ran while one was open for 2% of the time, Pallas kernels for 25%

profile of v7, /device:TPU:0, one launch (start us, length us, event | category | flops | bytes accessed | tf_op | source)
XLA Modules:
  0.0 132.3 jit_solution(6148364551989101748)
XLA Ops:
  1.7 3.1 %collective-permute-start = (f32[2,360,128]{2,1,0:T(8,128)S(1)}, f32[2,360,128]{2,1,0:T(8,128)S(1)}, u32[]{:S(2)}, u32[]{:S(2)}) collective-permute-start(f32[2,360,128]{2,1,0:T(8,128)S(1)} %constant_dynamic-slice_fusion.1), channel_id=1, source_target_pairs={{0,1},{1,0},{2,3},{3,2},{4,5},{5,4},{6,7},{7,6},{8,9},{9,8},{10,11... | collective-permute-start | bytes 1105928 | tf_op jit(solution)/shard_map/ppermute | solution.py:915
  4.8 5.4 %shard_map.157.coupling_hbm = f32[16,16,8,256]{3,2,1,0:T(8,128)} custom-call(s32[1]{0:T(128)} %bitcast.1.first_ref, f32[360,256]{1,0:T(8,128)} %gain_ref), custom_call_target="tpu_custom_call" | custom-call | flops 6000000000 | bytes 18000000 | tf_op jit(solution)/shard_map/pallas_call | solution.py:105
  13.4 2.7 %shard_map.159 = (f32[512,256]{1,0:T(8,128)}, f32[2,720,128]{2,1,0:T(8,128)}) custom-call(s32[1]{0:T(128)} %bitcast.part_ref, f32[2,360,256]{2,1,0:T(8,128)} %field_ref.1, f32[2,360,128]{2,1,0:T(8,128)S(1)} %collective-permute-done.other_ref, bf16[512,720]{1,0:T(8,128)(2,1)S(1)} %get-tuple-element.59.high_ref, bf16[512,720]{1,0:T(8,128)(2,1)S(1)} %get-tuple-element.60.low_ref), custom_call_target="tpu_custom_call" | custom-call | flops 3000000000 | bytes 9000000 | tf_op jit(solution)/shard_map/pallas_call | solution.py:105
  16.1 6.0 %all-to-all-start = ((f32[32,16,256]{2,1,0:T(8,128)}), f32[32,16,256]{2,1,0:T(8,128)S(1)}, u32[]{:S(2)}, u32[]{:S(2)}) async-start(f32[32,16,256]{2,1,0:T(8,128)} %bitcast.2), calls=%async_computation | async-start | bytes 1048576 | tf_op jit(solution)/shard_map/all_to_all | solution.py:881
  23.5 3.1 %collective-permute-start.4 = (f32[2,720,128]{2,1,0:T(8,128)}, f32[2,720,128]{2,1,0:T(8,128)S(1)}, u32[]{:S(2)}, u32[]{:S(2)}) collective-permute-start(f32[2,720,128]{2,1,0:T(8,128)} %get-tuple-element.70.own_ref), channel_id=1, source_target_pairs={{0,4},{4,8},{8,12},{12,16},{16,20},{20,24},{24,28},{1,5},{5,9},{9,... | collective-permute-start | bytes 2211848 | tf_op jit(solution)/shard_map/ppermute | solution.py:912
  27.5 2.7 %collective-permute-start.1 = (f32[2,16,128]{2,1,0:T(8,128)S(1)}, f32[2,16,128]{2,1,0:T(8,128)S(1)}, u32[]{:S(2)}, u32[]{:S(2)}) collective-permute-start(f32[2,16,128]{2,1,0:T(8,128)S(1)} %pad_maximum_fusion), channel_id=1, source_target_pairs={{0,2},{1,3},{2,0},{3,1},{4,6},{5,7},{6,4},{7,5},{8,10},{9,11},{10,... | collective-permute-start | bytes 49160 | tf_op jit(solution)/shard_map/ppermute | solution.py:915
  32.8 3.9 %all-to-all-done.r_ref = f32[32,16,256]{2,1,0:T(8,128)S(1)} async-done(((f32[32,16,256]{2,1,0:T(8,128)}), f32[32,16,256]{2,1,0:T(8,128)S(1)}, u32[]{:S(2)}, u32[]{:S(2)}) %all-to-all-start) | async-done | bytes 524320 | tf_op jit(solution)/shard_map/all_to_all | solution.py:881
  36.7 2.6 %shard_map.161 = (f32[16,16,256]{2,1,0:T(8,128)}, f32[32,16,256]{2,1,0:T(8,128)}) custom-call(f32[32,16,256]{2,1,0:T(8,128)S(1)} %all-to-all-done.r_ref, f32[256,256]{1,0:T(8,128)S(1)} %shard_map.160.w_ref, f32[16,16,8,256]{3,2,1,0:T(8,128)} %shard_map.157.coupling_hbm), custom_call_target="tpu_custom_call" | custom-call | flops 2000000000 | bytes 6000000 | tf_op jit(solution)/shard_map/pallas_call | solution.py:105
  39.7 3.9 %all-to-all-start.1 = ((f32[32,16,256]{2,1,0:T(8,128)}), f32[32,16,256]{2,1,0:T(8,128)S(1)}, u32[]{:S(2)}, u32[]{:S(2)}) async-start(f32[32,16,256]{2,1,0:T(8,128)} %get-tuple-element.72), calls=%async_computation.1 | async-start | bytes 1048576 | tf_op jit(solution)/shard_map/all_to_all | solution.py:881
  45.2 3.0 %collective-permute-start.6 = (f32[2,48,128]{2,1,0:T(8,128)S(1)}, f32[2,48,128]{2,1,0:T(8,128)S(1)}, u32[]{:S(2)}, u32[]{:S(2)}) collective-permute-start(f32[2,48,128]{2,1,0:T(8,128)S(1)} %select_maximum_fusion.middle_ref), channel_id=1, source_target_pairs={{0,4},{4,8},{8,12},{12,16},{16,20},{20,24},{24,28},{1,5},{5,9},{9,... | collective-permute-start | bytes 147464 | tf_op jit(solution)/shard_map/ppermute | solution.py:912
  51.2 3.9 %shard_map.162 = (f32[2,720,128]{2,1,0:T(8,128)}, f32[2,32,128]{2,1,0:T(8,128)}) custom-call(f32[2,720,128]{2,1,0:T(8,128)} %copy-done.7, f32[2,720,128]{2,1,0:T(8,128)} %get-tuple-element.70.own_ref, f32[2,720,128]{2,1,0:T(8,128)} %copy-done.6, f32[2,48,128]{2,1,0:T(8,128)S(1)} %collective-permute-done.6.lower_ref, ...), custom_call_target="tpu_custom_call" | custom-call | flops 4000000000 | bytes 12000000 | tf_op jit(solution)/shard_map/pallas_call | solution.py:105
  58.9 4.5 %shard_map.164 = (f32[512,256]{1,0:T(8,128)}, f32[2,360,128]{2,1,0:T(8,128)}, f32[1,360,128]{2,1,0:T(8,128)}, f32[1,360,128]{2,1,0:T(8,128)}, f32[2,720,128]{2,1,0:T(8,128)}) custom-call(s32[1]{0:T(128)} %bitcast.part_ref, f32[32,16,256]{2,1,0:T(8,128)S(1)} %all-to-all-done.1.s_ref, f32[1,360,128]{2,1,0:T(8,128)S(1)} %collective-permute-done.2.first_ref.first_hbm, ...), custom_call_target="tpu_custom_call" | custom-call | flops 4000000000 | bytes 12000000 | tf_op jit(solution)/shard_map/pallas_call | solution.py:105
  63.4 4.7 %all-to-all-start.2 = ((f32[32,16,256]{2,1,0:T(8,128)}), f32[32,16,256]{2,1,0:T(8,128)S(1)}, u32[]{:S(2)}, u32[]{:S(2)}) async-start(f32[32,16,256]{2,1,0:T(8,128)} %bitcast.7), calls=%async_computation.2 | async-start | bytes 1048576 | tf_op jit(solution)/shard_map/all_to_all | solution.py:881
  70.6 3.1 %collective-permute-start.10 = (f32[1,720,128]{2,1,0:T(8,128)S(1)}, f32[1,720,128]{2,1,0:T(8,128)S(1)}, u32[]{:S(2)}, u32[]{:S(2)}) collective-permute-start(f32[1,720,128]{2,1,0:T(8,128)S(1)} %get-tuple-element.106), channel_id=1, source_target_pairs={{0,4},{4,8},{8,12},{12,16},{16,20},{20,24},{24,28},{1,5},{5,9},{9,... | collective-permute-start | bytes 1105928 | tf_op jit(solution)/shard_map/ppermute | solution.py:956
  74.4 2.7 %collective-permute-start.8 = (f32[2,16,128]{2,1,0:T(8,128)S(1)}, f32[2,16,128]{2,1,0:T(8,128)S(1)}, u32[]{:S(2)}, u32[]{:S(2)}) collective-permute-start(f32[2,16,128]{2,1,0:T(8,128)S(1)} %pad_maximum_fusion.1), channel_id=1, source_target_pairs={{0,2},{1,3},{2,0},{3,1},{4,6},{5,7},{6,4},{7,5},{8,10},{9,11},{10,... | collective-permute-start | bytes 49160 | tf_op jit(solution)/shard_map/ppermute | solution.py:915
  78.6 4.3 %all-to-all-done.2.r_ref = f32[32,16,256]{2,1,0:T(8,128)S(1)} async-done(((f32[32,16,256]{2,1,0:T(8,128)}), f32[32,16,256]{2,1,0:T(8,128)S(1)}, u32[]{:S(2)}, u32[]{:S(2)}) %all-to-all-start.2) | async-done | bytes 524320 | tf_op jit(solution)/shard_map/all_to_all | solution.py:881
  82.9 3.7 %shard_map.165 = f32[32,24,256]{2,1,0:T(8,128)} custom-call(f32[32,16,256]{2,1,0:T(8,128)S(1)} %all-to-all-done.2.r_ref, f32[16,16,8,256]{3,2,1,0:T(8,128)} %shard_map.157.coupling_hbm, f32[256,256]{1,0:T(8,128)} %w_hbm.1, f32[16,16,256]{2,1,0:T(8,128)} %get-tuple-element.84.x_hbm), custom_call_target="tpu_custom_call" | custom-call | flops 2000000000 | bytes 6000000 | tf_op jit(solution)/shard_map/pallas_call | solution.py:105
  86.6 6.2 %all-to-all-start.3 = ((f32[32,24,256]{2,1,0:T(8,128)}), f32[32,24,256]{2,1,0:T(8,128)S(1)}, u32[]{:S(2)}, u32[]{:S(2)}) async-start(f32[32,24,256]{2,1,0:T(8,128)} %shard_map.165), calls=%async_computation.3 | async-start | bytes 1572864 | tf_op jit(solution)/shard_map/all_to_all | solution.py:881
  98.1 3.7 %collective-permute-start.13 = (f32[2,16,128]{2,1,0:T(8,128)S(1)}, f32[2,16,128]{2,1,0:T(8,128)S(1)}, u32[]{:S(2)}, u32[]{:S(2)}) collective-permute-start(f32[2,16,128]{2,1,0:T(8,128)S(1)} %collective-permute-done.8.middle_ref), channel_id=1, source_target_pairs={{0,4},{4,8},{8,12},{12,16},{16,20},{20,24},{24,28},{1,5},{5,9},{9,... | collective-permute-start | bytes 49160 | tf_op jit(solution)/shard_map/ppermute | solution.py:912
  103.7 5.2 %shard_map.166.base_hbm = f32[2,720,128]{2,1,0:T(8,128)} custom-call(s32[1]{0:T(128)} %bitcast.part_ref, f32[1,720,128]{2,1,0:T(8,128)} %copy-done.9, f32[1,720,128]{2,1,0:T(8,128)} %copy-done.10, f32[2,720,128]{2,1,0:T(8,128)} %get-tuple-element.85.own_ref, f32[2,720,128]{2,1,0:T(8,128)} %copy-done.8, f32[2,16,128]{2,1,0:T(8,128)S(1)} %collective-permute-done.13.lower_ref, ...), custom_call_target="tpu_custom_call" | custom-call | flops 4000000000 | bytes 12000000 | tf_op jit(solution)/shard_map/pallas_call | solution.py:105
  108.8 3.6 %all-to-all-done.3.s_ref = f32[32,24,256]{2,1,0:T(8,128)S(1)} async-done(((f32[32,24,256]{2,1,0:T(8,128)}), f32[32,24,256]{2,1,0:T(8,128)S(1)}, u32[]{:S(2)}, u32[]{:S(2)}) %all-to-all-start.3) | async-done | bytes 786464 | tf_op jit(solution)/shard_map/all_to_all | solution.py:881
  114.3 3.0 %collective-permute-start.16 = (f32[2,360,128]{2,1,0:T(8,128)S(1)}, f32[2,360,128]{2,1,0:T(8,128)S(1)}, u32[]{:S(2)}, u32[]{:S(2)}) collective-permute-start(f32[2,360,128]{2,1,0:T(8,128)S(1)} %get-tuple-element.101), channel_id=1, source_target_pairs={{0,1},{1,0},{2,3},{3,2},{4,5},{5,4},{6,7},{7,6},{8,9},{9,8},{10,11... | collective-permute-start | bytes 1105928 | tf_op jit(solution)/shard_map/ppermute | solution.py:915
  117.2 2.7 %all-to-all-start.4 = ((f32[32,8,256]{2,1,0:T(8,128)}), f32[32,8,256]{2,1,0:T(8,128)S(1)}, u32[]{:S(2)}, u32[]{:S(2)}) async-start(f32[32,8,256]{2,1,0:T(8,128)} %get-tuple-element.102), calls=%async_computation.4 | async-start | bytes 524288 | tf_op jit(solution)/shard_map/all_to_all | solution.py:881
  124.6 4.1 %collective-permute-done.16.other_ref = f32[2,360,128]{2,1,0:T(8,128)S(1)} collective-permute-done((f32[2,360,128]{2,1,0:T(8,128)S(1)}, f32[2,360,128]{2,1,0:T(8,128)S(1)}, u32[]{:S(2)}, u32[]{:S(2)}) %collective-permute-start.16) | collective-permute-done | bytes 368672 | tf_op jit(solution)/shard_map/ppermute | solution.py:915
  (81 shorter events, 39.4 us)
Async XLA Ops:
  0.6 25.9 %copy-start = (f32[2,4,3,5]{3,1,2,0:T(4,128)S(1)}, f32[2,4,3,5]{3,1,2,0:T(4,128)}, u32[]{:S(2)}) copy-start(f32[2,4,3,5]{3,1,2,0:T(4,128)} %param.15) | copy-start | bytes 1444
  1.7 11.7 %collective-permute-start = (f32[2,360,128]{2,1,0:T(8,128)S(1)}, f32[2,360,128]{2,1,0:T(8,128)S(1)}, u32[]{:S(2)}, u32[]{:S(2)}) collective-permute-start(f32[2,360,128]{2,1,0:T(8,128)S(1)} %constant_dynamic-slice_fusion.1), channel_id=1, source_target_pairs={{0,1},{1,0},{2,3},{3,2},{4,5},{5,4},{6,7},{7,6},{8,9},{9,8},{10,11... | collective-permute-start | bytes 1105928 | tf_op jit(solution)/shard_map/ppermute | solution.py:915
  16.1 20.7 %all-to-all-start = ((f32[32,16,256]{2,1,0:T(8,128)}), f32[32,16,256]{2,1,0:T(8,128)S(1)}, u32[]{:S(2)}, u32[]{:S(2)}) async-start(f32[32,16,256]{2,1,0:T(8,128)} %bitcast.2), calls=%async_computation | async-start | bytes 1048576 | tf_op jit(solution)/shard_map/all_to_all | solution.py:881
  22.2 27.9 %collective-permute-start.5 = (f32[2,720,128]{2,1,0:T(8,128)}, f32[2,720,128]{2,1,0:T(8,128)S(1)}, u32[]{:S(2)}, u32[]{:S(2)}) collective-permute-start(f32[2,720,128]{2,1,0:T(8,128)} %get-tuple-element.70.own_ref), channel_id=1, source_target_pairs={{4,0},{8,4},{12,8},{16,12},{20,16},{24,20},{28,24},{5,1},{9,5},{13... | collective-permute-start | bytes 2211848 | tf_op jit(solution)/shard_map/ppermute | solution.py:912
  23.5 26.6 %collective-permute-start.4 = (f32[2,720,128]{2,1,0:T(8,128)}, f32[2,720,128]{2,1,0:T(8,128)S(1)}, u32[]{:S(2)}, u32[]{:S(2)}) collective-permute-start(f32[2,720,128]{2,1,0:T(8,128)} %get-tuple-element.70.own_ref), channel_id=1, source_target_pairs={{0,4},{4,8},{8,12},{12,16},{16,20},{20,24},{24,28},{1,5},{5,9},{9,... | collective-permute-start | bytes 2211848 | tf_op jit(solution)/shard_map/ppermute | solution.py:912
  27.5 11.8 %collective-permute-start.1 = (f32[2,16,128]{2,1,0:T(8,128)S(1)}, f32[2,16,128]{2,1,0:T(8,128)S(1)}, u32[]{:S(2)}, u32[]{:S(2)}) collective-permute-start(f32[2,16,128]{2,1,0:T(8,128)S(1)} %pad_maximum_fusion), channel_id=1, source_target_pairs={{0,2},{1,3},{2,0},{3,1},{4,6},{5,7},{6,4},{7,5},{8,10},{9,11},{10,... | collective-permute-start | bytes 49160 | tf_op jit(solution)/shard_map/ppermute | solution.py:915
  30.2 9.5 %collective-permute-start.2 = (f32[1,360,128]{2,1,0:T(8,128)S(1)}, f32[1,360,128]{2,1,0:T(8,128)S(1)}, u32[]{:S(2)}, u32[]{:S(2)}) collective-permute-start(f32[1,360,128]{2,1,0:T(8,128)S(1)} %get-tuple-element.112), channel_id=1, source_target_pairs={{0,1},{1,0},{2,3},{3,2},{4,5},{5,4},{6,7},{7,6},{8,9},{9,8},{10,11... | collective-permute-start | bytes 552968 | tf_op jit(solution)/shard_map/ppermute | solution.py:915
  39.7 19.1 %copy-start.1 = (f32[1,360,128]{2,1,0:T(8,128)}, f32[1,360,128]{2,1,0:T(8,128)S(1)}, u32[]{:S(2)}) copy-start(f32[1,360,128]{2,1,0:T(8,128)S(1)} %collective-permute-done.2.first_ref.first_hbm) | copy-start | bytes 552964
  39.7 19.1 %all-to-all-start.1 = ((f32[32,16,256]{2,1,0:T(8,128)}), f32[32,16,256]{2,1,0:T(8,128)S(1)}, u32[]{:S(2)}, u32[]{:S(2)}) async-start(f32[32,16,256]{2,1,0:T(8,128)} %get-tuple-element.72), calls=%async_computation.1 | async-start | bytes 1048576 | tf_op jit(solution)/shard_map/all_to_all | solution.py:881
  43.9 6.2 %collective-permute-start.7 = (f32[2,48,128]{2,1,0:T(8,128)S(1)}, f32[2,48,128]{2,1,0:T(8,128)S(1)}, u32[]{:S(2)}, u32[]{:S(2)}) collective-permute-start(f32[2,48,128]{2,1,0:T(8,128)S(1)} %select_maximum_fusion.middle_ref), channel_id=1, source_target_pairs={{4,0},{8,4},{12,8},{16,12},{20,16},{24,20},{28,24},{5,1},{9,5},{13... | collective-permute-start | bytes 147464 | tf_op jit(solution)/shard_map/ppermute | solution.py:912
  45.2 4.9 %collective-permute-start.6 = (f32[2,48,128]{2,1,0:T(8,128)S(1)}, f32[2,48,128]{2,1,0:T(8,128)S(1)}, u32[]{:S(2)}, u32[]{:S(2)}) collective-permute-start(f32[2,48,128]{2,1,0:T(8,128)S(1)} %select_maximum_fusion.middle_ref), channel_id=1, source_target_pairs={{0,4},{4,8},{8,12},{12,16},{16,20},{20,24},{24,28},{1,5},{5,9},{9,... | collective-permute-start | bytes 147464 | tf_op jit(solution)/shard_map/ppermute | solution.py:912
  48.2 10.6 %collective-permute-start.3 = (f32[1,360,128]{2,1,0:T(8,128)S(1)}, f32[1,360,128]{2,1,0:T(8,128)S(1)}, u32[]{:S(2)}, u32[]{:S(2)}) collective-permute-start(f32[1,360,128]{2,1,0:T(8,128)S(1)} %get-tuple-element.111), channel_id=1, source_target_pairs={{0,1},{1,0},{2,3},{3,2},{4,5},{5,4},{6,7},{7,6},{8,9},{9,8},{10,11... | collective-permute-start | bytes 552968 | tf_op jit(solution)/shard_map/ppermute | solution.py:915
  63.4 19.5 %all-to-all-start.2 = ((f32[32,16,256]{2,1,0:T(8,128)}), f32[32,16,256]{2,1,0:T(8,128)S(1)}, u32[]{:S(2)}, u32[]{:S(2)}) async-start(f32[32,16,256]{2,1,0:T(8,128)} %bitcast.7), calls=%async_computation.2 | async-start | bytes 1048576 | tf_op jit(solution)/shard_map/all_to_all | solution.py:881
  68.1 18.5 %collective-permute-start.11 = (f32[2,720,128]{2,1,0:T(8,128)}, f32[2,720,128]{2,1,0:T(8,128)S(1)}, u32[]{:S(2)}, u32[]{:S(2)}) collective-permute-start(f32[2,720,128]{2,1,0:T(8,128)} %get-tuple-element.85.own_ref), channel_id=1, source_target_pairs={{4,0},{8,4},{12,8},{16,12},{20,16},{24,20},{28,24},{5,1},{9,5},{13... | collective-permute-start | bytes 2211848 | tf_op jit(solution)/shard_map/ppermute | solution.py:957
  70.6 16.0 %collective-permute-start.10 = (f32[1,720,128]{2,1,0:T(8,128)S(1)}, f32[1,720,128]{2,1,0:T(8,128)S(1)}, u32[]{:S(2)}, u32[]{:S(2)}) collective-permute-start(f32[1,720,128]{2,1,0:T(8,128)S(1)} %get-tuple-element.106), channel_id=1, source_target_pairs={{0,4},{4,8},{8,12},{12,16},{16,20},{20,24},{24,28},{1,5},{5,9},{9,... | collective-permute-start | bytes 1105928 | tf_op jit(solution)/shard_map/ppermute | solution.py:956
  74.4 12.2 %collective-permute-start.8 = (f32[2,16,128]{2,1,0:T(8,128)S(1)}, f32[2,16,128]{2,1,0:T(8,128)S(1)}, u32[]{:S(2)}, u32[]{:S(2)}) collective-permute-start(f32[2,16,128]{2,1,0:T(8,128)S(1)} %pad_maximum_fusion.1), channel_id=1, source_target_pairs={{0,2},{1,3},{2,0},{3,1},{4,6},{5,7},{6,4},{7,5},{8,10},{9,11},{10,... | collective-permute-start | bytes 49160 | tf_op jit(solution)/shard_map/ppermute | solution.py:915
  77.0 9.5 %collective-permute-start.9 = (f32[1,360,128]{2,1,0:T(8,128)S(1)}, f32[1,360,128]{2,1,0:T(8,128)S(1)}, u32[]{:S(2)}, u32[]{:S(2)}) collective-permute-start(f32[1,360,128]{2,1,0:T(8,128)S(1)} %copy-done.11), channel_id=1, source_target_pairs={{0,1},{1,0},{2,3},{3,2},{4,5},{5,4},{6,7},{7,6},{8,9},{9,8},{10,11... | collective-permute-start | bytes 552968 | tf_op jit(solution)/shard_map/ppermute | solution.py:915
  86.6 25.8 %all-to-all-start.3 = ((f32[32,24,256]{2,1,0:T(8,128)}), f32[32,24,256]{2,1,0:T(8,128)S(1)}, u32[]{:S(2)}, u32[]{:S(2)}) async-start(f32[32,24,256]{2,1,0:T(8,128)} %shard_map.165), calls=%async_computation.3 | async-start | bytes 1572864 | tf_op jit(solution)/shard_map/all_to_all | solution.py:881
  92.8 10.1 %collective-permute-start.12 = (f32[1,720,128]{2,1,0:T(8,128)S(1)}, f32[1,720,128]{2,1,0:T(8,128)S(1)}, u32[]{:S(2)}, u32[]{:S(2)}) collective-permute-start(f32[1,720,128]{2,1,0:T(8,128)S(1)} %get-tuple-element.105), channel_id=1, source_target_pairs={{0,4},{4,8},{8,12},{12,16},{16,20},{20,24},{24,28},{1,5},{5,9},{9,... | collective-permute-start | bytes 1105928 | tf_op jit(solution)/shard_map/ppermute | solution.py:956
  95.0 19.2 %collective-permute-start.15 = (f32[1,360,128]{2,1,0:T(8,128)}, f32[1,360,128]{2,1,0:T(8,128)S(1)}, u32[]{:S(2)}, u32[]{:S(2)}) collective-permute-start(f32[1,360,128]{2,1,0:T(8,128)} %get-tuple-element.98), channel_id=1, source_target_pairs={{0,1},{1,0},{2,3},{3,2},{4,5},{5,4},{6,7},{7,6},{8,9},{9,8},{10,11... | collective-permute-start | bytes 552968 | tf_op jit(solution)/shard_map/ppermute | solution.py:915
  96.8 6.2 %collective-permute-start.14 = (f32[2,16,128]{2,1,0:T(8,128)S(1)}, f32[2,16,128]{2,1,0:T(8,128)S(1)}, u32[]{:S(2)}, u32[]{:S(2)}) collective-permute-start(f32[2,16,128]{2,1,0:T(8,128)S(1)} %collective-permute-done.8.middle_ref), channel_id=1, source_target_pairs={{4,0},{8,4},{12,8},{16,12},{20,16},{24,20},{28,24},{5,1},{9,5},{13... | collective-permute-start | bytes 49160 | tf_op jit(solution)/shard_map/ppermute | solution.py:912
  98.1 4.9 %collective-permute-start.13 = (f32[2,16,128]{2,1,0:T(8,128)S(1)}, f32[2,16,128]{2,1,0:T(8,128)S(1)}, u32[]{:S(2)}, u32[]{:S(2)}) collective-permute-start(f32[2,16,128]{2,1,0:T(8,128)S(1)} %collective-permute-done.8.middle_ref), channel_id=1, source_target_pairs={{0,4},{4,8},{8,12},{12,16},{16,20},{20,24},{24,28},{1,5},{5,9},{9,... | collective-permute-start | bytes 49160 | tf_op jit(solution)/shard_map/ppermute | solution.py:912
  114.3 14.4 %collective-permute-start.16 = (f32[2,360,128]{2,1,0:T(8,128)S(1)}, f32[2,360,128]{2,1,0:T(8,128)S(1)}, u32[]{:S(2)}, u32[]{:S(2)}) collective-permute-start(f32[2,360,128]{2,1,0:T(8,128)S(1)} %get-tuple-element.101), channel_id=1, source_target_pairs={{0,1},{1,0},{2,3},{3,2},{4,5},{5,4},{6,7},{7,6},{8,9},{9,8},{10,11... | collective-permute-start | bytes 1105928 | tf_op jit(solution)/shard_map/ppermute | solution.py:915
  117.2 14.3 %all-to-all-start.4 = ((f32[32,8,256]{2,1,0:T(8,128)}), f32[32,8,256]{2,1,0:T(8,128)S(1)}, u32[]{:S(2)}, u32[]{:S(2)}) async-start(f32[32,8,256]{2,1,0:T(8,128)} %get-tuple-element.102), calls=%async_computation.4 | async-start | bytes 524288 | tf_op jit(solution)/shard_map/all_to_all | solution.py:881
  (12 other events, 95.5 us)

commit v8 on v7

--- a/solution.py
+++ b/solution.py
@@ -226,9 +226,12 @@
         copy.wait()
 
 
-def bring(part, sources, view=None, us=2.0):
+def bring(part, sources, view=None, us=2.0, first=0):
     views = [view or (lambda ref, part: ref)] * len(sources)
     shapes = [x.shape[1:] if view else x.shape for x in sources]
+    if first:
+        views[0] = lambda ref, part: ref.at[pl.ds(0, first)]
+        shapes[0] = (first, *shapes[0][1:])
     return call(
         functools.partial(bring_kernel, views),
         [near(*shape, dtype=x.dtype) for shape, x in zip(shapes, sources, strict=True)],
@@ -299,16 +302,15 @@
     )(part, own, other, high, low)
 
 
-def grid_kernel(part_ref, s_ref, first_ref, second_ref, thigh_ref, tlow_ref, local_hbm, cot_hbm,
+def grid_kernel(part_ref, s_ref, first_ref, second_ref, thigh_ref, tlow_ref, local_ref, cot_hbm,
                 high_hbm, low_hbm,
                 mode_ref, own_hbm, send_first_hbm, send_second_hbm, err_hbm,
-                local_ref, cot_ref, spec_ref, out_ref, err_ref,
+                cot_ref, spec_ref, out_ref, err_ref,
                 high_ref, low_ref, sems, other_sems, out_sems):
     part = part_ref[0]
     half, sign = own_half(part), turn_sign(part)
     others = [
-        pltpu.make_async_copy(local_hbm, local_ref, other_sems.at[0]),
-        pltpu.make_async_copy(lane_half(cot_hbm, half), lon_half(cot_ref, half), other_sems.at[1]),
+        pltpu.make_async_copy(lane_half(cot_hbm, half), lon_half(cot_ref, half), other_sems.at[0]),
     ]
     for copy in others:
         copy.start()
@@ -368,11 +370,11 @@
             kept(1, *block[1:]),
             kept(*local.shape),
         ),
-        [smem] + vmem(3) + resident(2) + hbm(4),
-        [grid, grid, VMEM((lons, rows * LANES), f32), grid, grid]
+        [smem] + vmem(3) + resident(3) + hbm(3),
+        [grid, VMEM((lons, rows * LANES), f32), grid, grid]
         + [VMEM(table.shape, bf16) for table in tables[:2]]
         + [pltpu.SemaphoreType.DMA((2, 1))]
-        + [pltpu.SemaphoreType.DMA((count,)) for count in (2, 4)],
+        + [pltpu.SemaphoreType.DMA((count,)) for count in (1, 4)],
         us=4.0,
         limit=32,
         out_spaces=(VMEM,) + (pltpu.HBM,) * 4,
@@ -522,7 +524,7 @@
 def local_filter(prev, own, behind, *edges):
     return call(
         filter_kernel,
-        (kept(*own.shape), kept(own.shape[0], TAPS, LANES)),
+        (near(*own.shape), kept(own.shape[0], TAPS, LANES)),
         loaded(3) + vmem(3),
         [VMEM((KLON, own.shape[1] + 16, LANES), f32)],
         us=4.0,
@@ -698,10 +700,10 @@
     scatter_modes(lambda j, lanes: z_ref[j, :, lanes], s_ref, parts, rows)
 
 
-def backward_modes_kernel(parts, r_ref, coupling_hbm, w_hbm, x_hbm, s_hbm, s_ref, e_ref, v_ref,
-                          coupling_ref, w_ref, x_ref, sems, out_sems):
-    wait = fetches((coupling_hbm,), (coupling_ref,), sems.at[pl.ds(0, 1)], 8)
-    wait_rest = fetches((w_hbm, x_hbm), (w_ref, x_ref), sems.at[pl.ds(1, 2)], 2)
+def backward_modes_kernel(parts, r_ref, early_ref, w_ref, x_ref, coupling_hbm, s_hbm,
+                          s_ref, e_ref, v_ref, coupling_ref, sems, out_sems):
+    early = early_ref.shape[0]
+    wait = fetches((coupling_hbm.at[pl.ds(early, coupling_ref.shape[0])],), (coupling_ref,), sems, 4)
 
     def write(j, lanes, value):
         e_ref[j, :, lanes] = value
@@ -709,22 +711,19 @@
     gather_modes(r_ref, write, parts)
     lats, rows, chans = x_ref.shape
     own = rows // 2
-    for piece in range(8):
+    for piece in range(4):
         wait(0, piece)
 
     @pl.loop(0, lats)
     def _(j):
         totals = [jnp.zeros((own, chans), f32)] * 2
         for other in range(lats):
-            factor = coupling_ref[other, j]
+            factor = early_ref[other, j] if other < early else coupling_ref[other - early, j]
             for p in range(2):
                 totals[p] = totals[p] + factor * e_ref[other, pl.ds(p * own, own), :]
         for p in range(2):
             v_ref[j, pl.ds(p * own, own), :] = totals[p]
 
-    for piece in range(2):
-        for index in range(2):
-            wait_rest(index, piece)
     v = v_ref[...].reshape(lats * rows, chans)
     e_ref[...] = dot_split(v, w_ref[...], ((1,), (1,))).reshape(lats, rows, chans)
     scatter_modes(lambda j, lanes: e_ref[j, :, lanes], s_ref, parts, rows)
@@ -820,18 +819,24 @@
                 us=2.0,
             )(received, weight, factors)
 
-        def backward(received, spectrum):
+        def backward(received, spectrum, tied):
             sent = (received.shape[0], 2 * own + chans // received.shape[0], chans)
+            half = (factors.shape[0] // 2, *factors.shape[1:])
+            early, weight, spectrum = bring(
+                tied,
+                [factors, spec_weight, spectrum],
+                us=0.1,
+                first=half[0],
+            )
             return call(
                 functools.partial(backward_modes_kernel, parts),
                 kept(*sent),
-                vmem(1) + hbm(3),
-                [VMEM(sent, f32), VMEM(shape, f32), VMEM(shape, f32), VMEM(factors.shape, f32)]
-                + [VMEM(spec_weight.shape, f32), VMEM(shape, f32)]
-                + [pltpu.SemaphoreType.DMA((3, 8)), pltpu.SemaphoreType.DMA((2,))],
+                vmem(1) + resident(3) + hbm(1),
+                [VMEM(sent, f32), VMEM(shape, f32), VMEM(shape, f32), VMEM(half, f32)]
+                + [pltpu.SemaphoreType.DMA((1, 4)), pltpu.SemaphoreType.DMA((2,))],
                 us=2.0,
                 out_spaces=pltpu.HBM,
-            )(received, factors, spec_weight, spectrum)
+            )(received, early, weight, spectrum, factors)
 
         return forward, backward
 
@@ -850,7 +855,8 @@
         synthesis = dot("lmj,lpmd->jpmd", legendre, degree) * order_weight
         return spectrum, plain_scatter(synthesis, parts)
 
-    def backward(received, spectrum):
+    def backward(received, spectrum, tied):
+        del tied
         error = plain_gather(received, parts, own) * order_weight
         gained = dot("lmj,jpmd->lpmd", legendre, error) * degree_gain[:, None, None, :]
         back = dot("lmj,lpmd->jpmd", legendre, gained) * quad_column
@@ -955,7 +961,8 @@
     out_others = [part_swap(x, 1) for x in out_sends]
     rows = [lax.ppermute(error[row : row + 1], "lat", up) for row in range(band_rows)]
     rows += [error, lax.ppermute(error, "lat", down)]
-    sent = backward(exchange(error_modes), spectrum)
+    error_modes, tied = after(error_modes, part_index)
+    sent = backward(exchange(error_modes), spectrum, tied)
     sent, edge, out_others[0], rows[0], rows[3], tied = after(
         sent, edges(error), out_others[0], rows[0], rows[3], part_index
     )

time: 134 us -> 134 us (level)
  waiting for transfers between devices: 22.7 us -> 25.1 us
  local copies, waits for them, and re-layouts: 6.23 us -> 4.56 us
    ppermute x6, starting transfers between devices: 13.6 us -> 11.2 us  [halo(): return (lax.ppermute(x, 'lat', up), x, lax.ppermute(x, 'lat', down))]
    ppermute x6, waiting for transfers between devices: 0.02 us -> 1.8 us  [halo(): return (lax.ppermute(x, 'lat', up), x, lax.ppermute(x, 'lat', down))]
    unnamed x29 -> x23, local copies, waits for them, and re-layouts: 2.56 us -> 0.88 us
    all_to_all x5, starting transfers between devices: 23.6 us -> 25.2 us  [swap_parts(): return lax.all_to_all(x, axis, split_axis=0, concat_axis=0, tiled=True)]
    pallas_call x15 -> x16, Pallas kernels: 39.9 us -> 40.3 us  [call(): run(*[held(x, keep) if keep else x for x, keep in zip(args, keeps, strict...]
  transfers between devices with their start and end apart: 22 -> 22, of which waited for: 8 -> 10; matrix products, arithmetic and copies ran while one was open for 2% -> 2% of each run, Pallas kernels for 25% -> 25%
where the time goes in v8:
time: 134 us; the launch traced here: 132 us
  starting transfers between devices  60.8 us (45%)
  Pallas kernels  40.3 us (30%)
  waiting for transfers between devices  25.1 us (19%)
  local copies, waits for them, and re-layouts  4.56 us (3%)
    pallas_call x16, Pallas kernels, call(): run(*[held(x, keep) if keep else x for x, keep in zip(args, keeps, strict...  40.3 us
    all_to_all x5, starting transfers between devices, swap_parts(): return lax.all_to_all(x, axis, split_axis=0, concat_axis=0, tiled=True)  25.2 us
    ppermute x8, starting transfers between devices, part_swap(): return lax.ppermute(x, 'chan', [(i, i ^ distance) for i in range(parts)])  17.9 us
    all_to_all x5, waiting for transfers between devices, swap_parts(): return lax.all_to_all(x, axis, split_axis=0, concat_axis=0, tiled=True)  14.3 us
    ppermute x6, starting transfers between devices, halo(): return (lax.ppermute(x, 'lat', up), x, lax.ppermute(x, 'lat', down))  11.2 us
    ppermute x8, waiting for transfers between devices, part_swap(): return lax.ppermute(x, 'chan', [(i, i ^ distance) for i in range(parts)])  8.95 us
    ppermute x2, starting transfers between devices, body(): lax.ppermute(error[row:row + 1], 'lat', up)  5.23 us
  transfers between devices with their start and end apart: 22, of which 10 were waited for; matrix products, arithmetic and copies ran while one was open for 2% of the time, Pallas kernels for 25%

profile of v8, /device:TPU:0, one launch (start us, length us, event | category | flops | bytes accessed | tf_op | source)
XLA Modules:
  0.0 132.3 jit_solution(18211385702094395588)
XLA Ops:
  1.7 3.1 %collective-permute-start = (f32[2,360,128]{2,1,0:T(8,128)S(1)}, f32[2,360,128]{2,1,0:T(8,128)S(1)}, u32[]{:S(2)}, u32[]{:S(2)}) collective-permute-start(f32[2,360,128]{2,1,0:T(8,128)S(1)} %constant_dynamic-slice_fusion.1), channel_id=1, source_target_pairs={{0,1},{1,0},{2,3},{3,2},{4,5},{5,4},{6,7},{7,6},{8,9},{9,8},{10,11... | collective-permute-start | bytes 1105928 | tf_op jit(solution)/shard_map/ppermute | solution.py:921
  4.8 5.4 %shard_map.157.coupling_hbm.refs_0_ = f32[16,16,8,256]{3,2,1,0:T(8,128)} custom-call(s32[1]{0:T(128)} %bitcast.1.first_ref, f32[360,256]{1,0:T(8,128)} %gain_ref), custom_call_target="tpu_custom_call" | custom-call | flops 6000000000 | bytes 18000000 | tf_op jit(solution)/shard_map/pallas_call | solution.py:105
  13.4 2.7 %shard_map.159 = (f32[512,256]{1,0:T(8,128)}, f32[2,720,128]{2,1,0:T(8,128)}) custom-call(s32[1]{0:T(128)} %bitcast.part_ref, f32[2,360,256]{2,1,0:T(8,128)} %field_ref.1, f32[2,360,128]{2,1,0:T(8,128)S(1)} %collective-permute-done.other_ref, bf16[512,720]{1,0:T(8,128)(2,1)S(1)} %get-tuple-element.64.high_ref, bf16[512,720]{1,0:T(8,128)(2,1)S(1)} %get-tuple-element.65.low_ref), custom_call_target="tpu_custom_call" | custom-call | flops 3000000000 | bytes 9000000 | tf_op jit(solution)/shard_map/pallas_call | solution.py:105
  16.1 6.0 %all-to-all-start = ((f32[32,16,256]{2,1,0:T(8,128)}), f32[32,16,256]{2,1,0:T(8,128)S(1)}, u32[]{:S(2)}, u32[]{:S(2)}) async-start(f32[32,16,256]{2,1,0:T(8,128)} %bitcast.2), calls=%async_computation | async-start | bytes 1048576 | tf_op jit(solution)/shard_map/all_to_all | solution.py:887
  26.7 2.6 %collective-permute-start.1 = (f32[2,16,128]{2,1,0:T(8,128)S(1)}, f32[2,16,128]{2,1,0:T(8,128)S(1)}, u32[]{:S(2)}, u32[]{:S(2)}) collective-permute-start(f32[2,16,128]{2,1,0:T(8,128)S(1)} %pad_maximum_fusion), channel_id=1, source_target_pairs={{0,2},{1,3},{2,0},{3,1},{4,6},{5,7},{6,4},{7,5},{8,10},{9,11},{10,... | collective-permute-start | bytes 49160 | tf_op jit(solution)/shard_map/ppermute | solution.py:921
  31.8 4.9 %all-to-all-done.r_ref = f32[32,16,256]{2,1,0:T(8,128)S(1)} async-done(((f32[32,16,256]{2,1,0:T(8,128)}), f32[32,16,256]{2,1,0:T(8,128)S(1)}, u32[]{:S(2)}, u32[]{:S(2)}) %all-to-all-start) | async-done | bytes 524320 | tf_op jit(solution)/shard_map/all_to_all | solution.py:887
  36.7 2.6 %shard_map.161 = (f32[16,16,256]{2,1,0:T(8,128)}, f32[32,16,256]{2,1,0:T(8,128)}) custom-call(f32[32,16,256]{2,1,0:T(8,128)S(1)} %all-to-all-done.r_ref, f32[256,256]{1,0:T(8,128)S(1)} %shard_map.160.w_ref, f32[16,16,8,256]{3,2,1,0:T(8,128)} %shard_map.157.coupling_hbm.refs_0_), custom_call_target="tpu_custom_call" | custom-call | flops 2000000000 | bytes 6000000 | tf_op jit(solution)/shard_map/pallas_call | solution.py:105
  39.4 4.3 %all-to-all-start.1 = ((f32[32,16,256]{2,1,0:T(8,128)}), f32[32,16,256]{2,1,0:T(8,128)S(1)}, u32[]{:S(2)}, u32[]{:S(2)}) async-start(f32[32,16,256]{2,1,0:T(8,128)} %get-tuple-element.77), calls=%async_computation.1 | async-start | bytes 1048576 | tf_op jit(solution)/shard_map/all_to_all | solution.py:887
  50.3 3.6 %shard_map.162 = (f32[2,720,128]{2,1,0:T(8,128)S(1)}, f32[2,32,128]{2,1,0:T(8,128)}) custom-call(f32[2,720,128]{2,1,0:T(8,128)} %copy-done.6, f32[2,720,128]{2,1,0:T(8,128)} %get-tuple-element.75.own_ref, f32[2,720,128]{2,1,0:T(8,128)} %collective-permute-done.5.next_ref, f32[2,48,128]{2,1,0:T(8,128)S(1)} %collective-permute-done.6.lower_ref, ...), custom_call_target="tpu_custom_call" | custom-call | flops 4000000000 | bytes 12000000 | tf_op jit(solution)/shard_map/pallas_call | solution.py:105
  55.2 3.0 %collective-permute-done.3.second_ref.second_hbm = f32[1,360,128]{2,1,0:T(8,128)S(1)} collective-permute-done((f32[1,360,128]{2,1,0:T(8,128)S(1)}, f32[1,360,128]{2,1,0:T(8,128)S(1)}, u32[]{:S(2)}, u32[]{:S(2)}) %collective-permute-start.3) | collective-permute-done | bytes 184352 | tf_op jit(solution)/shard_map/ppermute | solution.py:921
  58.3 4.4 %shard_map.164 = (f32[512,256]{1,0:T(8,128)}, f32[2,360,128]{2,1,0:T(8,128)}, f32[1,360,128]{2,1,0:T(8,128)}, f32[1,360,128]{2,1,0:T(8,128)}, f32[2,720,128]{2,1,0:T(8,128)}) custom-call(s32[1]{0:T(128)} %bitcast.part_ref, f32[32,16,256]{2,1,0:T(8,128)S(1)} %all-to-all-done.1.s_ref, f32[1,360,128]{2,1,0:T(8,128)S(1)} %collective-permute-done.2.first_ref.first_hbm, ...), custom_call_target="tpu_custom_call" | custom-call | flops 4000000000 | bytes 12000000 | tf_op jit(solution)/shard_map/pallas_call | solution.py:105
  62.7 5.4 %all-to-all-start.2 = ((f32[32,16,256]{2,1,0:T(8,128)}), f32[32,16,256]{2,1,0:T(8,128)S(1)}, u32[]{:S(2)}, u32[]{:S(2)}) async-start(f32[32,16,256]{2,1,0:T(8,128)} %bitcast.7), calls=%async_computation.2 | async-start | bytes 1048576 | tf_op jit(solution)/shard_map/all_to_all | solution.py:887
  70.5 3.1 %collective-permute-start.10 = (f32[1,720,128]{2,1,0:T(8,128)S(1)}, f32[1,720,128]{2,1,0:T(8,128)S(1)}, u32[]{:S(2)}, u32[]{:S(2)}) collective-permute-start(f32[1,720,128]{2,1,0:T(8,128)S(1)} %get-tuple-element.116), channel_id=1, source_target_pairs={{0,4},{4,8},{8,12},{12,16},{16,20},{20,24},{24,28},{1,5},{5,9},{9,... | collective-permute-start | bytes 1105928 | tf_op jit(solution)/shard_map/ppermute | solution.py:962
  74.3 2.7 %collective-permute-start.8 = (f32[2,16,128]{2,1,0:T(8,128)S(1)}, f32[2,16,128]{2,1,0:T(8,128)S(1)}, u32[]{:S(2)}, u32[]{:S(2)}) collective-permute-start(f32[2,16,128]{2,1,0:T(8,128)S(1)} %pad_maximum_fusion.1), channel_id=1, source_target_pairs={{0,2},{1,3},{2,0},{3,1},{4,6},{5,7},{6,4},{7,5},{8,10},{9,11},{10,... | collective-permute-start | bytes 49160 | tf_op jit(solution)/shard_map/ppermute | solution.py:921
  79.9 2.9 %all-to-all-done.2.r_ref = f32[32,16,256]{2,1,0:T(8,128)S(1)} async-done(((f32[32,16,256]{2,1,0:T(8,128)}), f32[32,16,256]{2,1,0:T(8,128)S(1)}, u32[]{:S(2)}, u32[]{:S(2)}) %all-to-all-start.2) | async-done | bytes 524320 | tf_op jit(solution)/shard_map/all_to_all | solution.py:887
  82.8 3.1 %shard_map.166 = f32[32,24,256]{2,1,0:T(8,128)} custom-call(f32[32,16,256]{2,1,0:T(8,128)S(1)} %all-to-all-done.2.r_ref, f32[8,16,8,256]{3,2,1,0:T(8,128)S(1)} %get-tuple-element.92.early_ref, f32[256,256]{1,0:T(8,128)S(1)} %get-tuple-element.93.w_ref, f32[16,16,256]{2,1,0:T(8,128)S(1)} %get-tuple-element.94.x_ref, ...), custom_call_target="tpu_custom_call" | custom-call | flops 2000000000 | bytes 6000000 | tf_op jit(solution)/shard_map/pallas_call | solution.py:105
  86.1 6.8 %all-to-all-start.3 = ((f32[32,24,256]{2,1,0:T(8,128)}), f32[32,24,256]{2,1,0:T(8,128)S(1)}, u32[]{:S(2)}, u32[]{:S(2)}) async-start(f32[32,24,256]{2,1,0:T(8,128)} %shard_map.166), calls=%async_computation.3 | async-start | bytes 1572864 | tf_op jit(solution)/shard_map/all_to_all | solution.py:887
  96.8 3.0 %collective-permute-start.13 = (f32[2,16,128]{2,1,0:T(8,128)S(1)}, f32[2,16,128]{2,1,0:T(8,128)S(1)}, u32[]{:S(2)}, u32[]{:S(2)}) collective-permute-start(f32[2,16,128]{2,1,0:T(8,128)S(1)} %collective-permute-done.8.middle_ref), channel_id=1, source_target_pairs={{0,4},{4,8},{8,12},{12,16},{16,20},{20,24},{24,28},{1,5},{5,9},{9,... | collective-permute-start | bytes 49160 | tf_op jit(solution)/shard_map/ppermute | solution.py:918
  103.1 5.2 %shard_map.167.base_hbm = f32[2,720,128]{2,1,0:T(8,128)} custom-call(s32[1]{0:T(128)} %bitcast.part_ref, f32[1,720,128]{2,1,0:T(8,128)} %copy-done.7, f32[1,720,128]{2,1,0:T(8,128)} %copy-done.8, f32[2,720,128]{2,1,0:T(8,128)} %get-tuple-element.95.own_ref, f32[2,720,128]{2,1,0:T(8,128)} %collective-permute-done.11.next_ref, ...), custom_call_target="tpu_custom_call" | custom-call | flops 4000000000 | bytes 12000000 | tf_op jit(solution)/shard_map/pallas_call | solution.py:105
  108.2 4.3 %all-to-all-done.3.s_ref = f32[32,24,256]{2,1,0:T(8,128)S(1)} async-done(((f32[32,24,256]{2,1,0:T(8,128)}), f32[32,24,256]{2,1,0:T(8,128)S(1)}, u32[]{:S(2)}, u32[]{:S(2)}) %all-to-all-start.3) | async-done | bytes 786464 | tf_op jit(solution)/shard_map/all_to_all | solution.py:887
  114.3 3.0 %collective-permute-start.16 = (f32[2,360,128]{2,1,0:T(8,128)S(1)}, f32[2,360,128]{2,1,0:T(8,128)S(1)}, u32[]{:S(2)}, u32[]{:S(2)}) collective-permute-start(f32[2,360,128]{2,1,0:T(8,128)S(1)} %get-tuple-element.111), channel_id=1, source_target_pairs={{0,1},{1,0},{2,3},{3,2},{4,5},{5,4},{6,7},{7,6},{8,9},{9,8},{10,11... | collective-permute-start | bytes 1105928 | tf_op jit(solution)/shard_map/ppermute | solution.py:921
  117.3 2.7 %all-to-all-start.4 = ((f32[32,8,256]{2,1,0:T(8,128)}), f32[32,8,256]{2,1,0:T(8,128)S(1)}, u32[]{:S(2)}, u32[]{:S(2)}) async-start(f32[32,8,256]{2,1,0:T(8,128)} %get-tuple-element.112), calls=%async_computation.4 | async-start | bytes 524288 | tf_op jit(solution)/shard_map/all_to_all | solution.py:887
  122.2 2.4 %shard_map.171.held_hbm = f32[2,360,256]{2,1,0:T(8,128)} custom-call(s32[1]{0:T(128)} %bitcast.part_ref, f32[32,24,256]{2,1,0:T(8,128)S(1)} %all-to-all-done.3.s_ref, f32[2,720,128]{2,1,0:T(8,128)} %shard_map.167.base_hbm, bf16[2,384,512]{2,1,0:T(8,128)(2,1)} %constant.68.clone.refs_0_, bf16[2,384,512]{2,1,0:T(8,128)(2,1)} %constant.69.clone.refs_1_), custom_call_target="tpu_custom_call" | custom-call | flops 2000000000 | bytes 6000000 | tf_op jit(solution)/shard_map/pallas_call | solution.py:105
  124.6 4.1 %collective-permute-done.16.other_ref = f32[2,360,128]{2,1,0:T(8,128)S(1)} collective-permute-done((f32[2,360,128]{2,1,0:T(8,128)S(1)}, f32[2,360,128]{2,1,0:T(8,128)S(1)}, u32[]{:S(2)}, u32[]{:S(2)}) %collective-permute-start.16) | collective-permute-done | bytes 368672 | tf_op jit(solution)/shard_map/ppermute | solution.py:921
  (76 shorter events, 40.0 us)
Async XLA Ops:
  0.6 25.0 %copy-start = (f32[2,4,3,5]{3,1,2,0:T(4,128)S(1)}, f32[2,4,3,5]{3,1,2,0:T(4,128)}, u32[]{:S(2)}) copy-start(f32[2,4,3,5]{3,1,2,0:T(4,128)} %param.15) | copy-start | bytes 1444
  1.7 11.7 %collective-permute-start = (f32[2,360,128]{2,1,0:T(8,128)S(1)}, f32[2,360,128]{2,1,0:T(8,128)S(1)}, u32[]{:S(2)}, u32[]{:S(2)}) collective-permute-start(f32[2,360,128]{2,1,0:T(8,128)S(1)} %constant_dynamic-slice_fusion.1), channel_id=1, source_target_pairs={{0,1},{1,0},{2,3},{3,2},{4,5},{5,4},{6,7},{7,6},{8,9},{9,8},{10,11... | collective-permute-start | bytes 1105928 | tf_op jit(solution)/shard_map/ppermute | solution.py:921
  16.1 20.7 %all-to-all-start = ((f32[32,16,256]{2,1,0:T(8,128)}), f32[32,16,256]{2,1,0:T(8,128)S(1)}, u32[]{:S(2)}, u32[]{:S(2)}) async-start(f32[32,16,256]{2,1,0:T(8,128)} %bitcast.2), calls=%async_computation | async-start | bytes 1048576 | tf_op jit(solution)/shard_map/all_to_all | solution.py:887
  22.2 26.9 %collective-permute-start.4 = (f32[2,720,128]{2,1,0:T(8,128)}, f32[2,720,128]{2,1,0:T(8,128)S(1)}, u32[]{:S(2)}, u32[]{:S(2)}) collective-permute-start(f32[2,720,128]{2,1,0:T(8,128)} %get-tuple-element.75.own_ref), channel_id=1, source_target_pairs={{0,4},{4,8},{8,12},{12,16},{16,20},{20,24},{24,28},{1,5},{5,9},{9,... | collective-permute-start | bytes 2211848 | tf_op jit(solution)/shard_map/ppermute | solution.py:918
  24.4 24.7 %collective-permute-start.5 = (f32[2,720,128]{2,1,0:T(8,128)}, f32[2,720,128]{2,1,0:T(8,128)}, u32[]{:S(2)}, u32[]{:S(2)}) collective-permute-start(f32[2,720,128]{2,1,0:T(8,128)} %get-tuple-element.75.own_ref), channel_id=1, source_target_pairs={{4,0},{8,4},{12,8},{16,12},{20,16},{24,20},{28,24},{5,1},{9,5},{13... | collective-permute-start | bytes 2211848 | tf_op jit(solution)/shard_map/ppermute | solution.py:918
  26.7 12.7 %collective-permute-start.1 = (f32[2,16,128]{2,1,0:T(8,128)S(1)}, f32[2,16,128]{2,1,0:T(8,128)S(1)}, u32[]{:S(2)}, u32[]{:S(2)}) collective-permute-start(f32[2,16,128]{2,1,0:T(8,128)S(1)} %pad_maximum_fusion), channel_id=1, source_target_pairs={{0,2},{1,3},{2,0},{3,1},{4,6},{5,7},{6,4},{7,5},{8,10},{9,11},{10,... | collective-permute-start | bytes 49160 | tf_op jit(solution)/shard_map/ppermute | solution.py:921
  29.3 10.1 %collective-permute-start.2 = (f32[1,360,128]{2,1,0:T(8,128)S(1)}, f32[1,360,128]{2,1,0:T(8,128)S(1)}, u32[]{:S(2)}, u32[]{:S(2)}) collective-permute-start(f32[1,360,128]{2,1,0:T(8,128)S(1)} %get-tuple-element.122), channel_id=1, source_target_pairs={{0,1},{1,0},{2,3},{3,2},{4,5},{5,4},{6,7},{7,6},{8,9},{9,8},{10,11... | collective-permute-start | bytes 552968 | tf_op jit(solution)/shard_map/ppermute | solution.py:921
  39.3 18.9 %copy-start.1 = (f32[1,360,128]{2,1,0:T(8,128)}, f32[1,360,128]{2,1,0:T(8,128)S(1)}, u32[]{:S(2)}) copy-start(f32[1,360,128]{2,1,0:T(8,128)S(1)} %collective-permute-done.2.first_ref.first_hbm) | copy-start | bytes 552964
  39.4 18.9 %all-to-all-start.1 = ((f32[32,16,256]{2,1,0:T(8,128)}), f32[32,16,256]{2,1,0:T(8,128)S(1)}, u32[]{:S(2)}, u32[]{:S(2)}) async-start(f32[32,16,256]{2,1,0:T(8,128)} %get-tuple-element.77), calls=%async_computation.1 | async-start | bytes 1048576 | tf_op jit(solution)/shard_map/all_to_all | solution.py:887
  43.9 5.2 %collective-permute-start.6 = (f32[2,48,128]{2,1,0:T(8,128)S(1)}, f32[2,48,128]{2,1,0:T(8,128)S(1)}, u32[]{:S(2)}, u32[]{:S(2)}) collective-permute-start(f32[2,48,128]{2,1,0:T(8,128)S(1)} %select_maximum_fusion.middle_ref), channel_id=1, source_target_pairs={{0,4},{4,8},{8,12},{12,16},{16,20},{20,24},{24,28},{1,5},{5,9},{9,... | collective-permute-start | bytes 147464 | tf_op jit(solution)/shard_map/ppermute | solution.py:918
  46.0 4.3 %collective-permute-start.7 = (f32[2,48,128]{2,1,0:T(8,128)S(1)}, f32[2,48,128]{2,1,0:T(8,128)S(1)}, u32[]{:S(2)}, u32[]{:S(2)}) collective-permute-start(f32[2,48,128]{2,1,0:T(8,128)S(1)} %select_maximum_fusion.middle_ref), channel_id=1, source_target_pairs={{4,0},{8,4},{12,8},{16,12},{20,16},{24,20},{28,24},{5,1},{9,5},{13... | collective-permute-start | bytes 147464 | tf_op jit(solution)/shard_map/ppermute | solution.py:918
  47.3 10.9 %collective-permute-start.3 = (f32[1,360,128]{2,1,0:T(8,128)S(1)}, f32[1,360,128]{2,1,0:T(8,128)S(1)}, u32[]{:S(2)}, u32[]{:S(2)}) collective-permute-start(f32[1,360,128]{2,1,0:T(8,128)S(1)} %get-tuple-element.121), channel_id=1, source_target_pairs={{0,1},{1,0},{2,3},{3,2},{4,5},{5,4},{6,7},{7,6},{8,9},{9,8},{10,11... | collective-permute-start | bytes 552968 | tf_op jit(solution)/shard_map/ppermute | solution.py:921
  62.7 20.1 %all-to-all-start.2 = ((f32[32,16,256]{2,1,0:T(8,128)}), f32[32,16,256]{2,1,0:T(8,128)S(1)}, u32[]{:S(2)}, u32[]{:S(2)}) async-start(f32[32,16,256]{2,1,0:T(8,128)} %bitcast.7), calls=%async_computation.2 | async-start | bytes 1048576 | tf_op jit(solution)/shard_map/all_to_all | solution.py:887
  68.1 18.0 %collective-permute-start.11 = (f32[2,720,128]{2,1,0:T(8,128)}, f32[2,720,128]{2,1,0:T(8,128)}, u32[]{:S(2)}, u32[]{:S(2)}) collective-permute-start(f32[2,720,128]{2,1,0:T(8,128)} %get-tuple-element.95.own_ref), channel_id=1, source_target_pairs={{4,0},{8,4},{12,8},{16,12},{20,16},{24,20},{28,24},{5,1},{9,5},{13... | collective-permute-start | bytes 2211848 | tf_op jit(solution)/shard_map/ppermute | solution.py:963
  70.5 15.5 %collective-permute-start.10 = (f32[1,720,128]{2,1,0:T(8,128)S(1)}, f32[1,720,128]{2,1,0:T(8,128)S(1)}, u32[]{:S(2)}, u32[]{:S(2)}) collective-permute-start(f32[1,720,128]{2,1,0:T(8,128)S(1)} %get-tuple-element.116), channel_id=1, source_target_pairs={{0,4},{4,8},{8,12},{12,16},{16,20},{20,24},{24,28},{1,5},{5,9},{9,... | collective-permute-start | bytes 1105928 | tf_op jit(solution)/shard_map/ppermute | solution.py:962
  74.3 11.6 %collective-permute-start.8 = (f32[2,16,128]{2,1,0:T(8,128)S(1)}, f32[2,16,128]{2,1,0:T(8,128)S(1)}, u32[]{:S(2)}, u32[]{:S(2)}) collective-permute-start(f32[2,16,128]{2,1,0:T(8,128)S(1)} %pad_maximum_fusion.1), channel_id=1, source_target_pairs={{0,2},{1,3},{2,0},{3,1},{4,6},{5,7},{6,4},{7,5},{8,10},{9,11},{10,... | collective-permute-start | bytes 49160 | tf_op jit(solution)/shard_map/ppermute | solution.py:921
  77.0 9.0 %collective-permute-start.9 = (f32[1,360,128]{2,1,0:T(8,128)}, f32[1,360,128]{2,1,0:T(8,128)S(1)}, u32[]{:S(2)}, u32[]{:S(2)}) collective-permute-start(f32[1,360,128]{2,1,0:T(8,128)} %get-tuple-element.96), channel_id=1, source_target_pairs={{0,1},{1,0},{2,3},{3,2},{4,5},{5,4},{6,7},{7,6},{8,9},{9,8},{10,11... | collective-permute-start | bytes 552968 | tf_op jit(solution)/shard_map/ppermute | solution.py:921
  86.1 26.5 %all-to-all-start.3 = ((f32[32,24,256]{2,1,0:T(8,128)}), f32[32,24,256]{2,1,0:T(8,128)S(1)}, u32[]{:S(2)}, u32[]{:S(2)}) async-start(f32[32,24,256]{2,1,0:T(8,128)} %shard_map.166), calls=%async_computation.3 | async-start | bytes 1572864 | tf_op jit(solution)/shard_map/all_to_all | solution.py:887
  92.9 9.4 %collective-permute-start.12 = (f32[1,720,128]{2,1,0:T(8,128)S(1)}, f32[1,720,128]{2,1,0:T(8,128)S(1)}, u32[]{:S(2)}, u32[]{:S(2)}) collective-permute-start(f32[1,720,128]{2,1,0:T(8,128)S(1)} %get-tuple-element.115), channel_id=1, source_target_pairs={{0,4},{4,8},{8,12},{12,16},{16,20},{20,24},{24,28},{1,5},{5,9},{9,... | collective-permute-start | bytes 1105928 | tf_op jit(solution)/shard_map/ppermute | solution.py:962
  95.1 19.2 %collective-permute-start.15 = (f32[1,360,128]{2,1,0:T(8,128)}, f32[1,360,128]{2,1,0:T(8,128)S(1)}, u32[]{:S(2)}, u32[]{:S(2)}) collective-permute-start(f32[1,360,128]{2,1,0:T(8,128)} %get-tuple-element.108), channel_id=1, source_target_pairs={{0,1},{1,0},{2,3},{3,2},{4,5},{5,4},{6,7},{7,6},{8,9},{9,8},{10,11... | collective-permute-start | bytes 552968 | tf_op jit(solution)/shard_map/ppermute | solution.py:921
  96.8 5.5 %collective-permute-start.13 = (f32[2,16,128]{2,1,0:T(8,128)S(1)}, f32[2,16,128]{2,1,0:T(8,128)S(1)}, u32[]{:S(2)}, u32[]{:S(2)}) collective-permute-start(f32[2,16,128]{2,1,0:T(8,128)S(1)} %collective-permute-done.8.middle_ref), channel_id=1, source_target_pairs={{0,4},{4,8},{8,12},{12,16},{16,20},{20,24},{24,28},{1,5},{5,9},{9,... | collective-permute-start | bytes 49160 | tf_op jit(solution)/shard_map/ppermute | solution.py:918
  99.9 3.1 %collective-permute-start.14 = (f32[2,16,128]{2,1,0:T(8,128)S(1)}, f32[2,16,128]{2,1,0:T(8,128)S(1)}, u32[]{:S(2)}, u32[]{:S(2)}) collective-permute-start(f32[2,16,128]{2,1,0:T(8,128)S(1)} %collective-permute-done.8.middle_ref), channel_id=1, source_target_pairs={{4,0},{8,4},{12,8},{16,12},{20,16},{24,20},{28,24},{5,1},{9,5},{13... | collective-permute-start | bytes 49160 | tf_op jit(solution)/shard_map/ppermute | solution.py:918
  114.3 14.4 %collective-permute-start.16 = (f32[2,360,128]{2,1,0:T(8,128)S(1)}, f32[2,360,128]{2,1,0:T(8,128)S(1)}, u32[]{:S(2)}, u32[]{:S(2)}) collective-permute-start(f32[2,360,128]{2,1,0:T(8,128)S(1)} %get-tuple-element.111), channel_id=1, source_target_pairs={{0,1},{1,0},{2,3},{3,2},{4,5},{5,4},{6,7},{7,6},{8,9},{9,8},{10,11... | collective-permute-start | bytes 1105928 | tf_op jit(solution)/shard_map/ppermute | solution.py:921
  117.3 14.3 %all-to-all-start.4 = ((f32[32,8,256]{2,1,0:T(8,128)}), f32[32,8,256]{2,1,0:T(8,128)S(1)}, u32[]{:S(2)}, u32[]{:S(2)}) async-start(f32[32,8,256]{2,1,0:T(8,128)} %get-tuple-element.112), calls=%async_computation.4 | async-start | bytes 524288 | tf_op jit(solution)/shard_map/all_to_all | solution.py:887
  (9 other events, 69.0 us)

commit v9 on v7

--- a/solution.py
+++ b/solution.py
@@ -299,16 +299,15 @@
     )(part, own, other, high, low)
 
 
-def grid_kernel(part_ref, s_ref, first_ref, second_ref, thigh_ref, tlow_ref, local_hbm, cot_hbm,
+def grid_kernel(part_ref, s_ref, first_ref, second_ref, thigh_ref, tlow_ref, local_ref, cot_hbm,
                 high_hbm, low_hbm,
                 mode_ref, own_hbm, send_first_hbm, send_second_hbm, err_hbm,
-                local_ref, cot_ref, spec_ref, out_ref, err_ref,
+                cot_ref, spec_ref, out_ref, err_ref,
                 high_ref, low_ref, sems, other_sems, out_sems):
     part = part_ref[0]
     half, sign = own_half(part), turn_sign(part)
     others = [
-        pltpu.make_async_copy(local_hbm, local_ref, other_sems.at[0]),
-        pltpu.make_async_copy(lane_half(cot_hbm, half), lon_half(cot_ref, half), other_sems.at[1]),
+        pltpu.make_async_copy(lane_half(cot_hbm, half), lon_half(cot_ref, half), other_sems.at[0]),
     ]
     for copy in others:
         copy.start()
@@ -368,11 +367,11 @@
             kept(1, *block[1:]),
             kept(*local.shape),
         ),
-        [smem] + vmem(3) + resident(2) + hbm(4),
-        [grid, grid, VMEM((lons, rows * LANES), f32), grid, grid]
+        [smem] + vmem(3) + resident(3) + hbm(3),
+        [grid, VMEM((lons, rows * LANES), f32), grid, grid]
         + [VMEM(table.shape, bf16) for table in tables[:2]]
         + [pltpu.SemaphoreType.DMA((2, 1))]
-        + [pltpu.SemaphoreType.DMA((count,)) for count in (2, 4)],
+        + [pltpu.SemaphoreType.DMA((count,)) for count in (1, 4)],
         us=4.0,
         limit=32,
         out_spaces=(VMEM,) + (pltpu.HBM,) * 4,
@@ -522,7 +521,7 @@
 def local_filter(prev, own, behind, *edges):
     return call(
         filter_kernel,
-        (kept(*own.shape), kept(own.shape[0], TAPS, LANES)),
+        (near(*own.shape), kept(own.shape[0], TAPS, LANES)),
         loaded(3) + vmem(3),
         [VMEM((KLON, own.shape[1] + 16, LANES), f32)],
         us=4.0,

time: 134 us -> 133 us (level)
  transfers between devices with their start and end apart: 22 -> 22, of which waited for: 8 -> 8; matrix products, arithmetic and copies ran while one was open for 2% -> 2% of each run, Pallas kernels for 25% -> 24%
where the time goes in v9:
time: 133 us; the launch traced here: 132 us
  starting transfers between devices  61.8 us (46%)
  Pallas kernels  39.4 us (30%)
  waiting for transfers between devices  23.1 us (17%)
  local copies, waits for them, and re-layouts  6.24 us (5%)
    pallas_call x15, Pallas kernels, call(): run(*[held(x, keep) if keep else x for x, keep in zip(args, keeps, strict...  39.4 us
    all_to_all x5, starting transfers between devices, swap_parts(): return lax.all_to_all(x, axis, split_axis=0, concat_axis=0, tiled=True)  23.5 us
    ppermute x8, starting transfers between devices, part_swap(): return lax.ppermute(x, 'chan', [(i, i ^ distance) for i in range(parts)])  18.1 us
    all_to_all x5, waiting for transfers between devices, swap_parts(): return lax.all_to_all(x, axis, split_axis=0, concat_axis=0, tiled=True)  14 us
    ppermute x6, starting transfers between devices, halo(): return (lax.ppermute(x, 'lat', up), x, lax.ppermute(x, 'lat', down))  13.6 us
    ppermute x8, waiting for transfers between devices, part_swap(): return lax.ppermute(x, 'chan', [(i, i ^ distance) for i in range(parts)])  9 us
    ppermute x2, starting transfers between devices, body(): lax.ppermute(error[row:row + 1], 'lat', up)  5.23 us
  transfers between devices with their start and end apart: 22, of which 8 were waited for; matrix products, arithmetic and copies ran while one was open for 2% of the time, Pallas kernels for 24%

profile of v9, /device:TPU:0, one launch (start us, length us, event | category | flops | bytes accessed | tf_op | source)
XLA Modules:
  0.0 132.1 jit_solution(9912608742262445273)
XLA Ops:
  1.7 3.1 %collective-permute-start = (f32[2,360,128]{2,1,0:T(8,128)S(1)}, f32[2,360,128]{2,1,0:T(8,128)S(1)}, u32[]{:S(2)}, u32[]{:S(2)}) collective-permute-start(f32[2,360,128]{2,1,0:T(8,128)S(1)} %constant_dynamic-slice_fusion.1), channel_id=1, source_target_pairs={{0,1},{1,0},{2,3},{3,2},{4,5},{5,4},{6,7},{7,6},{8,9},{9,8},{10,11... | collective-permute-start | bytes 1105928 | tf_op jit(solution)/shard_map/ppermute | solution.py:914
  4.8 5.4 %shard_map.157.coupling_hbm = f32[16,16,8,256]{3,2,1,0:T(8,128)} custom-call(s32[1]{0:T(128)} %bitcast.1.first_ref, f32[360,256]{1,0:T(8,128)} %gain_ref), custom_call_target="tpu_custom_call" | custom-call | flops 6000000000 | bytes 18000000 | tf_op jit(solution)/shard_map/pallas_call | solution.py:105
  13.4 2.7 %shard_map.159 = (f32[512,256]{1,0:T(8,128)}, f32[2,720,128]{2,1,0:T(8,128)}) custom-call(s32[1]{0:T(128)} %bitcast.part_ref, f32[2,360,256]{2,1,0:T(8,128)} %field_ref.1, f32[2,360,128]{2,1,0:T(8,128)S(1)} %collective-permute-done.other_ref, bf16[512,720]{1,0:T(8,128)(2,1)S(1)} %get-tuple-element.59.high_ref, bf16[512,720]{1,0:T(8,128)(2,1)S(1)} %get-tuple-element.60.low_ref), custom_call_target="tpu_custom_call" | custom-call | flops 3000000000 | bytes 9000000 | tf_op jit(solution)/shard_map/pallas_call | solution.py:105
  16.1 6.0 %all-to-all-start = ((f32[32,16,256]{2,1,0:T(8,128)}), f32[32,16,256]{2,1,0:T(8,128)S(1)}, u32[]{:S(2)}, u32[]{:S(2)}) async-start(f32[32,16,256]{2,1,0:T(8,128)} %bitcast.2), calls=%async_computation | async-start | bytes 1048576 | tf_op jit(solution)/shard_map/all_to_all | solution.py:880
  23.5 3.1 %collective-permute-start.4 = (f32[2,720,128]{2,1,0:T(8,128)}, f32[2,720,128]{2,1,0:T(8,128)S(1)}, u32[]{:S(2)}, u32[]{:S(2)}) collective-permute-start(f32[2,720,128]{2,1,0:T(8,128)} %get-tuple-element.70.own_ref), channel_id=1, source_target_pairs={{0,4},{4,8},{8,12},{12,16},{16,20},{20,24},{24,28},{1,5},{5,9},{9,... | collective-permute-start | bytes 2211848 | tf_op jit(solution)/shard_map/ppermute | solution.py:911
  27.5 2.7 %collective-permute-start.1 = (f32[2,16,128]{2,1,0:T(8,128)S(1)}, f32[2,16,128]{2,1,0:T(8,128)S(1)}, u32[]{:S(2)}, u32[]{:S(2)}) collective-permute-start(f32[2,16,128]{2,1,0:T(8,128)S(1)} %pad_maximum_fusion), channel_id=1, source_target_pairs={{0,2},{1,3},{2,0},{3,1},{4,6},{5,7},{6,4},{7,5},{8,10},{9,11},{10,... | collective-permute-start | bytes 49160 | tf_op jit(solution)/shard_map/ppermute | solution.py:914
  32.8 3.9 %all-to-all-done.r_ref = f32[32,16,256]{2,1,0:T(8,128)S(1)} async-done(((f32[32,16,256]{2,1,0:T(8,128)}), f32[32,16,256]{2,1,0:T(8,128)S(1)}, u32[]{:S(2)}, u32[]{:S(2)}) %all-to-all-start) | async-done | bytes 524320 | tf_op jit(solution)/shard_map/all_to_all | solution.py:880
  39.7 3.9 %all-to-all-start.1 = ((f32[32,16,256]{2,1,0:T(8,128)}), f32[32,16,256]{2,1,0:T(8,128)S(1)}, u32[]{:S(2)}, u32[]{:S(2)}) async-start(f32[32,16,256]{2,1,0:T(8,128)} %get-tuple-element.72), calls=%async_computation.1 | async-start | bytes 1048576 | tf_op jit(solution)/shard_map/all_to_all | solution.py:880
  45.2 3.0 %collective-permute-start.6 = (f32[2,48,128]{2,1,0:T(8,128)S(1)}, f32[2,48,128]{2,1,0:T(8,128)S(1)}, u32[]{:S(2)}, u32[]{:S(2)}) collective-permute-start(f32[2,48,128]{2,1,0:T(8,128)S(1)} %select_maximum_fusion.middle_ref), channel_id=1, source_target_pairs={{0,4},{4,8},{8,12},{12,16},{16,20},{20,24},{24,28},{1,5},{5,9},{9,... | collective-permute-start | bytes 147464 | tf_op jit(solution)/shard_map/ppermute | solution.py:911
  51.2 3.6 %shard_map.162 = (f32[2,720,128]{2,1,0:T(8,128)S(1)}, f32[2,32,128]{2,1,0:T(8,128)}) custom-call(f32[2,720,128]{2,1,0:T(8,128)} %copy-done.7, f32[2,720,128]{2,1,0:T(8,128)} %get-tuple-element.70.own_ref, f32[2,720,128]{2,1,0:T(8,128)} %copy-done.6, f32[2,48,128]{2,1,0:T(8,128)S(1)} %collective-permute-done.6.lower_ref, ...), custom_call_target="tpu_custom_call" | custom-call | flops 4000000000 | bytes 12000000 | tf_op jit(solution)/shard_map/pallas_call | solution.py:105
  56.1 2.8 %collective-permute-done.3.second_ref.second_hbm = f32[1,360,128]{2,1,0:T(8,128)S(1)} collective-permute-done((f32[1,360,128]{2,1,0:T(8,128)S(1)}, f32[1,360,128]{2,1,0:T(8,128)S(1)}, u32[]{:S(2)}, u32[]{:S(2)}) %collective-permute-start.3) | collective-permute-done | bytes 184352 | tf_op jit(solution)/shard_map/ppermute | solution.py:914
  58.9 4.4 %shard_map.164 = (f32[512,256]{1,0:T(8,128)}, f32[2,360,128]{2,1,0:T(8,128)}, f32[1,360,128]{2,1,0:T(8,128)}, f32[1,360,128]{2,1,0:T(8,128)}, f32[2,720,128]{2,1,0:T(8,128)}) custom-call(s32[1]{0:T(128)} %bitcast.part_ref, f32[32,16,256]{2,1,0:T(8,128)S(1)} %all-to-all-done.1.s_ref, f32[1,360,128]{2,1,0:T(8,128)S(1)} %collective-permute-done.2.first_ref.first_hbm, ...), custom_call_target="tpu_custom_call" | custom-call | flops 4000000000 | bytes 12000000 | tf_op jit(solution)/shard_map/pallas_call | solution.py:105
  63.3 4.7 %all-to-all-start.2 = ((f32[32,16,256]{2,1,0:T(8,128)}), f32[32,16,256]{2,1,0:T(8,128)S(1)}, u32[]{:S(2)}, u32[]{:S(2)}) async-start(f32[32,16,256]{2,1,0:T(8,128)} %bitcast.7), calls=%async_computation.2 | async-start | bytes 1048576 | tf_op jit(solution)/shard_map/all_to_all | solution.py:880
  70.4 3.1 %collective-permute-start.10 = (f32[1,720,128]{2,1,0:T(8,128)S(1)}, f32[1,720,128]{2,1,0:T(8,128)S(1)}, u32[]{:S(2)}, u32[]{:S(2)}) collective-permute-start(f32[1,720,128]{2,1,0:T(8,128)S(1)} %get-tuple-element.106), channel_id=1, source_target_pairs={{0,4},{4,8},{8,12},{12,16},{16,20},{20,24},{24,28},{1,5},{5,9},{9,... | collective-permute-start | bytes 1105928 | tf_op jit(solution)/shard_map/ppermute | solution.py:955
  74.2 2.7 %collective-permute-start.8 = (f32[2,16,128]{2,1,0:T(8,128)S(1)}, f32[2,16,128]{2,1,0:T(8,128)S(1)}, u32[]{:S(2)}, u32[]{:S(2)}) collective-permute-start(f32[2,16,128]{2,1,0:T(8,128)S(1)} %pad_maximum_fusion.1), channel_id=1, source_target_pairs={{0,2},{1,3},{2,0},{3,1},{4,6},{5,7},{6,4},{7,5},{8,10},{9,11},{10,... | collective-permute-start | bytes 49160 | tf_op jit(solution)/shard_map/ppermute | solution.py:914
  78.4 4.3 %all-to-all-done.2.r_ref = f32[32,16,256]{2,1,0:T(8,128)S(1)} async-done(((f32[32,16,256]{2,1,0:T(8,128)}), f32[32,16,256]{2,1,0:T(8,128)S(1)}, u32[]{:S(2)}, u32[]{:S(2)}) %all-to-all-start.2) | async-done | bytes 524320 | tf_op jit(solution)/shard_map/all_to_all | solution.py:880
  82.7 3.6 %shard_map.165 = f32[32,24,256]{2,1,0:T(8,128)} custom-call(f32[32,16,256]{2,1,0:T(8,128)S(1)} %all-to-all-done.2.r_ref, f32[16,16,8,256]{3,2,1,0:T(8,128)} %shard_map.157.coupling_hbm, f32[256,256]{1,0:T(8,128)} %w_hbm.1, f32[16,16,256]{2,1,0:T(8,128)} %get-tuple-element.84.x_hbm), custom_call_target="tpu_custom_call" | custom-call | flops 2000000000 | bytes 6000000 | tf_op jit(solution)/shard_map/pallas_call | solution.py:105
  86.4 6.3 %all-to-all-start.3 = ((f32[32,24,256]{2,1,0:T(8,128)}), f32[32,24,256]{2,1,0:T(8,128)S(1)}, u32[]{:S(2)}, u32[]{:S(2)}) async-start(f32[32,24,256]{2,1,0:T(8,128)} %shard_map.165), calls=%async_computation.3 | async-start | bytes 1572864 | tf_op jit(solution)/shard_map/all_to_all | solution.py:880
  97.9 3.7 %collective-permute-start.13 = (f32[2,16,128]{2,1,0:T(8,128)S(1)}, f32[2,16,128]{2,1,0:T(8,128)S(1)}, u32[]{:S(2)}, u32[]{:S(2)}) collective-permute-start(f32[2,16,128]{2,1,0:T(8,128)S(1)} %collective-permute-done.8.middle_ref), channel_id=1, source_target_pairs={{0,4},{4,8},{8,12},{12,16},{16,20},{20,24},{24,28},{1,5},{5,9},{9,... | collective-permute-start | bytes 49160 | tf_op jit(solution)/shard_map/ppermute | solution.py:911
  103.5 5.1 %shard_map.166.base_hbm = f32[2,720,128]{2,1,0:T(8,128)} custom-call(s32[1]{0:T(128)} %bitcast.part_ref, f32[1,720,128]{2,1,0:T(8,128)} %copy-done.9, f32[1,720,128]{2,1,0:T(8,128)} %copy-done.10, f32[2,720,128]{2,1,0:T(8,128)} %get-tuple-element.85.own_ref, f32[2,720,128]{2,1,0:T(8,128)} %copy-done.8, f32[2,16,128]{2,1,0:T(8,128)S(1)} %collective-permute-done.13.lower_ref, ...), custom_call_target="tpu_custom_call" | custom-call | flops 4000000000 | bytes 12000000 | tf_op jit(solution)/shard_map/pallas_call | solution.py:105
  108.7 3.6 %all-to-all-done.3.s_ref = f32[32,24,256]{2,1,0:T(8,128)S(1)} async-done(((f32[32,24,256]{2,1,0:T(8,128)}), f32[32,24,256]{2,1,0:T(8,128)S(1)}, u32[]{:S(2)}, u32[]{:S(2)}) %all-to-all-start.3) | async-done | bytes 786464 | tf_op jit(solution)/shard_map/all_to_all | solution.py:880
  114.1 3.0 %collective-permute-start.16 = (f32[2,360,128]{2,1,0:T(8,128)S(1)}, f32[2,360,128]{2,1,0:T(8,128)S(1)}, u32[]{:S(2)}, u32[]{:S(2)}) collective-permute-start(f32[2,360,128]{2,1,0:T(8,128)S(1)} %get-tuple-element.101), channel_id=1, source_target_pairs={{0,1},{1,0},{2,3},{3,2},{4,5},{5,4},{6,7},{7,6},{8,9},{9,8},{10,11... | collective-permute-start | bytes 1105928 | tf_op jit(solution)/shard_map/ppermute | solution.py:914
  117.1 2.7 %all-to-all-start.4 = ((f32[32,8,256]{2,1,0:T(8,128)}), f32[32,8,256]{2,1,0:T(8,128)S(1)}, u32[]{:S(2)}, u32[]{:S(2)}) async-start(f32[32,8,256]{2,1,0:T(8,128)} %get-tuple-element.102), calls=%async_computation.4 | async-start | bytes 524288 | tf_op jit(solution)/shard_map/all_to_all | solution.py:880
  124.4 4.1 %collective-permute-done.16.other_ref = f32[2,360,128]{2,1,0:T(8,128)S(1)} collective-permute-done((f32[2,360,128]{2,1,0:T(8,128)S(1)}, f32[2,360,128]{2,1,0:T(8,128)S(1)}, u32[]{:S(2)}, u32[]{:S(2)}) %collective-permute-start.16) | collective-permute-done | bytes 368672 | tf_op jit(solution)/shard_map/ppermute | solution.py:914
  (81 shorter events, 39.6 us)
Async XLA Ops:
  0.6 25.9 %copy-start = (f32[2,4,3,5]{3,1,2,0:T(4,128)S(1)}, f32[2,4,3,5]{3,1,2,0:T(4,128)}, u32[]{:S(2)}) copy-start(f32[2,4,3,5]{3,1,2,0:T(4,128)} %param.15) | copy-start | bytes 1444
  1.7 11.7 %collective-permute-start = (f32[2,360,128]{2,1,0:T(8,128)S(1)}, f32[2,360,128]{2,1,0:T(8,128)S(1)}, u32[]{:S(2)}, u32[]{:S(2)}) collective-permute-start(f32[2,360,128]{2,1,0:T(8,128)S(1)} %constant_dynamic-slice_fusion.1), channel_id=1, source_target_pairs={{0,1},{1,0},{2,3},{3,2},{4,5},{5,4},{6,7},{7,6},{8,9},{9,8},{10,11... | collective-permute-start | bytes 1105928 | tf_op jit(solution)/shard_map/ppermute | solution.py:914
  16.1 20.7 %all-to-all-start = ((f32[32,16,256]{2,1,0:T(8,128)}), f32[32,16,256]{2,1,0:T(8,128)S(1)}, u32[]{:S(2)}, u32[]{:S(2)}) async-start(f32[32,16,256]{2,1,0:T(8,128)} %bitcast.2), calls=%async_computation | async-start | bytes 1048576 | tf_op jit(solution)/shard_map/all_to_all | solution.py:880
  22.2 27.9 %collective-permute-start.5 = (f32[2,720,128]{2,1,0:T(8,128)}, f32[2,720,128]{2,1,0:T(8,128)S(1)}, u32[]{:S(2)}, u32[]{:S(2)}) collective-permute-start(f32[2,720,128]{2,1,0:T(8,128)} %get-tuple-element.70.own_ref), channel_id=1, source_target_pairs={{4,0},{8,4},{12,8},{16,12},{20,16},{24,20},{28,24},{5,1},{9,5},{13... | collective-permute-start | bytes 2211848 | tf_op jit(solution)/shard_map/ppermute | solution.py:911
  23.5 26.6 %collective-permute-start.4 = (f32[2,720,128]{2,1,0:T(8,128)}, f32[2,720,128]{2,1,0:T(8,128)S(1)}, u32[]{:S(2)}, u32[]{:S(2)}) collective-permute-start(f32[2,720,128]{2,1,0:T(8,128)} %get-tuple-element.70.own_ref), channel_id=1, source_target_pairs={{0,4},{4,8},{8,12},{12,16},{16,20},{20,24},{24,28},{1,5},{5,9},{9,... | collective-permute-start | bytes 2211848 | tf_op jit(solution)/shard_map/ppermute | solution.py:911
  27.5 11.8 %collective-permute-start.1 = (f32[2,16,128]{2,1,0:T(8,128)S(1)}, f32[2,16,128]{2,1,0:T(8,128)S(1)}, u32[]{:S(2)}, u32[]{:S(2)}) collective-permute-start(f32[2,16,128]{2,1,0:T(8,128)S(1)} %pad_maximum_fusion), channel_id=1, source_target_pairs={{0,2},{1,3},{2,0},{3,1},{4,6},{5,7},{6,4},{7,5},{8,10},{9,11},{10,... | collective-permute-start | bytes 49160 | tf_op jit(solution)/shard_map/ppermute | solution.py:914
  30.2 9.5 %collective-permute-start.2 = (f32[1,360,128]{2,1,0:T(8,128)S(1)}, f32[1,360,128]{2,1,0:T(8,128)S(1)}, u32[]{:S(2)}, u32[]{:S(2)}) collective-permute-start(f32[1,360,128]{2,1,0:T(8,128)S(1)} %get-tuple-element.112), channel_id=1, source_target_pairs={{0,1},{1,0},{2,3},{3,2},{4,5},{5,4},{6,7},{7,6},{8,9},{9,8},{10,11... | collective-permute-start | bytes 552968 | tf_op jit(solution)/shard_map/ppermute | solution.py:914
  39.7 19.1 %copy-start.1 = (f32[1,360,128]{2,1,0:T(8,128)}, f32[1,360,128]{2,1,0:T(8,128)S(1)}, u32[]{:S(2)}) copy-start(f32[1,360,128]{2,1,0:T(8,128)S(1)} %collective-permute-done.2.first_ref.first_hbm) | copy-start | bytes 552964
  39.7 19.1 %all-to-all-start.1 = ((f32[32,16,256]{2,1,0:T(8,128)}), f32[32,16,256]{2,1,0:T(8,128)S(1)}, u32[]{:S(2)}, u32[]{:S(2)}) async-start(f32[32,16,256]{2,1,0:T(8,128)} %get-tuple-element.72), calls=%async_computation.1 | async-start | bytes 1048576 | tf_op jit(solution)/shard_map/all_to_all | solution.py:880
  43.9 6.2 %collective-permute-start.7 = (f32[2,48,128]{2,1,0:T(8,128)S(1)}, f32[2,48,128]{2,1,0:T(8,128)S(1)}, u32[]{:S(2)}, u32[]{:S(2)}) collective-permute-start(f32[2,48,128]{2,1,0:T(8,128)S(1)} %select_maximum_fusion.middle_ref), channel_id=1, source_target_pairs={{4,0},{8,4},{12,8},{16,12},{20,16},{24,20},{28,24},{5,1},{9,5},{13... | collective-permute-start | bytes 147464 | tf_op jit(solution)/shard_map/ppermute | solution.py:911
  45.2 4.9 %collective-permute-start.6 = (f32[2,48,128]{2,1,0:T(8,128)S(1)}, f32[2,48,128]{2,1,0:T(8,128)S(1)}, u32[]{:S(2)}, u32[]{:S(2)}) collective-permute-start(f32[2,48,128]{2,1,0:T(8,128)S(1)} %select_maximum_fusion.middle_ref), channel_id=1, source_target_pairs={{0,4},{4,8},{8,12},{12,16},{16,20},{20,24},{24,28},{1,5},{5,9},{9,... | collective-permute-start | bytes 147464 | tf_op jit(solution)/shard_map/ppermute | solution.py:911
  48.2 10.6 %collective-permute-start.3 = (f32[1,360,128]{2,1,0:T(8,128)S(1)}, f32[1,360,128]{2,1,0:T(8,128)S(1)}, u32[]{:S(2)}, u32[]{:S(2)}) collective-permute-start(f32[1,360,128]{2,1,0:T(8,128)S(1)} %get-tuple-element.111), channel_id=1, source_target_pairs={{0,1},{1,0},{2,3},{3,2},{4,5},{5,4},{6,7},{7,6},{8,9},{9,8},{10,11... | collective-permute-start | bytes 552968 | tf_op jit(solution)/shard_map/ppermute | solution.py:914
  63.3 19.4 %all-to-all-start.2 = ((f32[32,16,256]{2,1,0:T(8,128)}), f32[32,16,256]{2,1,0:T(8,128)S(1)}, u32[]{:S(2)}, u32[]{:S(2)}) async-start(f32[32,16,256]{2,1,0:T(8,128)} %bitcast.7), calls=%async_computation.2 | async-start | bytes 1048576 | tf_op jit(solution)/shard_map/all_to_all | solution.py:880
  68.0 18.4 %collective-permute-start.11 = (f32[2,720,128]{2,1,0:T(8,128)}, f32[2,720,128]{2,1,0:T(8,128)S(1)}, u32[]{:S(2)}, u32[]{:S(2)}) collective-permute-start(f32[2,720,128]{2,1,0:T(8,128)} %get-tuple-element.85.own_ref), channel_id=1, source_target_pairs={{4,0},{8,4},{12,8},{16,12},{20,16},{24,20},{28,24},{5,1},{9,5},{13... | collective-permute-start | bytes 2211848 | tf_op jit(solution)/shard_map/ppermute | solution.py:956
  70.4 15.9 %collective-permute-start.10 = (f32[1,720,128]{2,1,0:T(8,128)S(1)}, f32[1,720,128]{2,1,0:T(8,128)S(1)}, u32[]{:S(2)}, u32[]{:S(2)}) collective-permute-start(f32[1,720,128]{2,1,0:T(8,128)S(1)} %get-tuple-element.106), channel_id=1, source_target_pairs={{0,4},{4,8},{8,12},{12,16},{16,20},{20,24},{24,28},{1,5},{5,9},{9,... | collective-permute-start | bytes 1105928 | tf_op jit(solution)/shard_map/ppermute | solution.py:955
  74.2 12.1 %collective-permute-start.8 = (f32[2,16,128]{2,1,0:T(8,128)S(1)}, f32[2,16,128]{2,1,0:T(8,128)S(1)}, u32[]{:S(2)}, u32[]{:S(2)}) collective-permute-start(f32[2,16,128]{2,1,0:T(8,128)S(1)} %pad_maximum_fusion.1), channel_id=1, source_target_pairs={{0,2},{1,3},{2,0},{3,1},{4,6},{5,7},{6,4},{7,5},{8,10},{9,11},{10,... | collective-permute-start | bytes 49160 | tf_op jit(solution)/shard_map/ppermute | solution.py:914
  76.9 9.4 %collective-permute-start.9 = (f32[1,360,128]{2,1,0:T(8,128)S(1)}, f32[1,360,128]{2,1,0:T(8,128)S(1)}, u32[]{:S(2)}, u32[]{:S(2)}) collective-permute-start(f32[1,360,128]{2,1,0:T(8,128)S(1)} %copy-done.11), channel_id=1, source_target_pairs={{0,1},{1,0},{2,3},{3,2},{4,5},{5,4},{6,7},{7,6},{8,9},{9,8},{10,11... | collective-permute-start | bytes 552968 | tf_op jit(solution)/shard_map/ppermute | solution.py:914
  86.4 25.9 %all-to-all-start.3 = ((f32[32,24,256]{2,1,0:T(8,128)}), f32[32,24,256]{2,1,0:T(8,128)S(1)}, u32[]{:S(2)}, u32[]{:S(2)}) async-start(f32[32,24,256]{2,1,0:T(8,128)} %shard_map.165), calls=%async_computation.3 | async-start | bytes 1572864 | tf_op jit(solution)/shard_map/all_to_all | solution.py:880
  92.7 10.1 %collective-permute-start.12 = (f32[1,720,128]{2,1,0:T(8,128)S(1)}, f32[1,720,128]{2,1,0:T(8,128)S(1)}, u32[]{:S(2)}, u32[]{:S(2)}) collective-permute-start(f32[1,720,128]{2,1,0:T(8,128)S(1)} %get-tuple-element.105), channel_id=1, source_target_pairs={{0,4},{4,8},{8,12},{12,16},{16,20},{20,24},{24,28},{1,5},{5,9},{9,... | collective-permute-start | bytes 1105928 | tf_op jit(solution)/shard_map/ppermute | solution.py:955
  94.9 19.2 %collective-permute-start.15 = (f32[1,360,128]{2,1,0:T(8,128)}, f32[1,360,128]{2,1,0:T(8,128)S(1)}, u32[]{:S(2)}, u32[]{:S(2)}) collective-permute-start(f32[1,360,128]{2,1,0:T(8,128)} %get-tuple-element.98), channel_id=1, source_target_pairs={{0,1},{1,0},{2,3},{3,2},{4,5},{5,4},{6,7},{7,6},{8,9},{9,8},{10,11... | collective-permute-start | bytes 552968 | tf_op jit(solution)/shard_map/ppermute | solution.py:914
  96.6 6.2 %collective-permute-start.14 = (f32[2,16,128]{2,1,0:T(8,128)S(1)}, f32[2,16,128]{2,1,0:T(8,128)S(1)}, u32[]{:S(2)}, u32[]{:S(2)}) collective-permute-start(f32[2,16,128]{2,1,0:T(8,128)S(1)} %collective-permute-done.8.middle_ref), channel_id=1, source_target_pairs={{4,0},{8,4},{12,8},{16,12},{20,16},{24,20},{28,24},{5,1},{9,5},{13... | collective-permute-start | bytes 49160 | tf_op jit(solution)/shard_map/ppermute | solution.py:911
  97.9 4.9 %collective-permute-start.13 = (f32[2,16,128]{2,1,0:T(8,128)S(1)}, f32[2,16,128]{2,1,0:T(8,128)S(1)}, u32[]{:S(2)}, u32[]{:S(2)}) collective-permute-start(f32[2,16,128]{2,1,0:T(8,128)S(1)} %collective-permute-done.8.middle_ref), channel_id=1, source_target_pairs={{0,4},{4,8},{8,12},{12,16},{16,20},{20,24},{24,28},{1,5},{5,9},{9,... | collective-permute-start | bytes 49160 | tf_op jit(solution)/shard_map/ppermute | solution.py:911
  114.1 14.4 %collective-permute-start.16 = (f32[2,360,128]{2,1,0:T(8,128)S(1)}, f32[2,360,128]{2,1,0:T(8,128)S(1)}, u32[]{:S(2)}, u32[]{:S(2)}) collective-permute-start(f32[2,360,128]{2,1,0:T(8,128)S(1)} %get-tuple-element.101), channel_id=1, source_target_pairs={{0,1},{1,0},{2,3},{3,2},{4,5},{5,4},{6,7},{7,6},{8,9},{9,8},{10,11... | collective-permute-start | bytes 1105928 | tf_op jit(solution)/shard_map/ppermute | solution.py:914
  117.1 14.3 %all-to-all-start.4 = ((f32[32,8,256]{2,1,0:T(8,128)}), f32[32,8,256]{2,1,0:T(8,128)S(1)}, u32[]{:S(2)}, u32[]{:S(2)}) async-start(f32[32,8,256]{2,1,0:T(8,128)} %get-tuple-element.102), calls=%async_computation.4 | async-start | bytes 524288 | tf_op jit(solution)/shard_map/all_to_all | solution.py:880
  (12 other events, 95.5 us)
